TPU v7x, 32 devices: a whole 2x2x4 slice. The times are simulated.
32 devices in a mesh: sec: 4 (over z), depth: 4 (over y, x), segment: 2 (over core).
Axes of the slice: x: 2, y: 2, z: 4, core: 2. Of those that a mesh axis runs over, the one named last changes fastest.
Arguments:
- fields: float32 [2, 9, 8, 64, 128], P('segment', None, 'sec', 'depth'), may hold values from -6 to 6
- block_ids: int32 [2, 8, 64, 128], P('segment', 'sec', 'depth'), may hold values from 0 to 15
- buoyancy: float32 [16], replicated, may hold values from 0.5 to 1
- lame_lambda: float32 [16], replicated, may hold values from 0.2 to 0.6
- lame_mu: float32 [16], replicated, may hold values from 0.1 to 0.3
- moments: float32 [6, 16384], P(None, ('sec', 'depth')), may hold values from -12 to 12
- moment_owner: int32 [16384, 1], P(('sec', 'depth')), may hold values from 0 to 3; in each aligned block of 1024 rows (0 to 1023, 1024 to 2047, ...) at most 512 rows name the same one
- moment_cells: int32 [16384], P(('sec', 'depth')), may hold values from 0 to 4095
- drm_rows: int32 [32768], P(('sec', 'depth')), may hold values from 0 to 4095
Outputs:
- final_fields: float32 [2, 9, 8, 64, 128], P('segment', None, 'sec', 'depth')
Inputs may be any that keep to these rules, and one draw needn't show every extreme that they name: `moment_owner`: in the entries of one section and slab at most 512 name the same section, a bound that some block reaches of them.
All inputs are finite; a program needn't handle non-finite values.
Results may differ from a plain program's by a relative error of at most 0.00002.
Values sent between devices are 32-bit elements; how exact they have to be, the bound alone decides.
No kernel may reach another device: no remote copies, remote signals or barrier semaphores. Data moves between devices by JAX's collectives and lax.ppermute only.
A program may use at most 64 MiB of HBM per device.

v0:
```python
import jax
import jax.numpy as jnp
from jax import lax
from jax.sharding import PartitionSpec as P

STEPS = 4


HALF_STEP = 0.5


def passed_along(block, axis, distance):
    devices = range(lax.axis_size(axis))
    route = [(i - distance, i) for i in devices if i - distance in devices]
    return lax.ppermute(block, axis, route)


def lookup(block_ids, table):
    result = jnp.zeros(block_ids.shape, jnp.float32)
    for entry in range(table.shape[0]):
        result = result + jnp.where(block_ids == entry, table[entry], jnp.float32(0.0))
    return result


def back_diff(field, before_rim, axis):
    count = field.shape[axis]
    before = jnp.concatenate([before_rim, lax.slice_in_dim(field, 0, count - 1, axis=axis)], axis)
    return field - before


def fore_diff(field, after_rim, axis):
    count = field.shape[axis]
    after = jnp.concatenate([lax.slice_in_dim(field, 1, count, axis=axis), after_rim], axis)
    return after - field


def stress_rims(state):
    xplane = jnp.stack([state[:, 3, -1:], state[:, 8, -1:], state[:, 7, -1:]], axis=1)
    zplane = jnp.stack([state[:, 7, :, -1:], state[:, 6, :, -1:], state[:, 5, :, -1:]], axis=1)
    x_rims = passed_along(xplane, "sec", 1)
    z_rims = passed_along(zplane, "depth", 1)
    return (x_rims, z_rims)


def velocity_rims(newv):
    xplane = newv[:, :, :1]
    zplane = newv[:, :, :, :1]
    x_rims = passed_along(xplane, "sec", -1)
    z_rims = passed_along(zplane, "depth", -1)
    return (x_rims, z_rims)


def couple(newv, oldv, rows_here):
    shape_one = newv.shape[1:]
    increment = (newv[0] - oldv[0]).reshape(3, -1)[:, rows_here]
    arrived = passed_along(increment, "segment", 1)
    basin = newv[0].reshape(3, -1).at[:, rows_here].add(arrived)
    return basin.reshape((1,) + shape_one)


def advance(state, buoy, lam, shear, rows_here):
    x_rims, z_rims = stress_rims(state)
    vx, vy, vz = (state[:, 0], state[:, 1], state[:, 2])
    sxx, syy, szz, syz, sxz, sxy = (state[:, k] for k in range(3, 9))
    y_zero = jnp.zeros_like(sxx[..., :1])
    nvx = vx + HALF_STEP * buoy * (
        back_diff(sxx, x_rims[:, 0], 1)
        + back_diff(sxy, y_zero, 3)
        + back_diff(sxz, z_rims[:, 0], 2)
    )
    nvy = vy + HALF_STEP * buoy * (
        back_diff(sxy, x_rims[:, 1], 1)
        + back_diff(syy, y_zero, 3)
        + back_diff(syz, z_rims[:, 1], 2)
    )
    nvz = vz + HALF_STEP * buoy * (
        back_diff(sxz, x_rims[:, 2], 1)
        + back_diff(syz, y_zero, 3)
        + back_diff(szz, z_rims[:, 2], 2)
    )
    newv = couple(jnp.stack([nvx, nvy, nvz], axis=1), state[:, :3], rows_here)
    vx_rims, vz_rims = velocity_rims(newv)
    vx, vy, vz = (newv[:, 0], newv[:, 1], newv[:, 2])
    exx = fore_diff(vx, vx_rims[:, 0], 1)
    eyy = fore_diff(vy, y_zero, 3)
    ezz = fore_diff(vz, vz_rims[:, 2], 2)
    trace = exx + eyy + ezz
    sxx = sxx + HALF_STEP * (lam * trace + 2.0 * shear * exx)
    syy = syy + HALF_STEP * (lam * trace + 2.0 * shear * eyy)
    szz = szz + HALF_STEP * (lam * trace + 2.0 * shear * ezz)
    syz = syz + HALF_STEP * shear * (fore_diff(vy, vz_rims[:, 1], 2) + fore_diff(vz, y_zero, 3))
    sxz = sxz + HALF_STEP * shear * (
        fore_diff(vx, vz_rims[:, 0], 2) + fore_diff(vz, vx_rims[:, 2], 1)
    )
    sxy = sxy + HALF_STEP * shear * (fore_diff(vx, y_zero, 3) + fore_diff(vy, vx_rims[:, 1], 1))
    return jnp.stack([vx, vy, vz, sxx, syy, szz, syz, sxz, sxy], axis=1)


def on_device(
    fields, block_ids, buoyancy, lame_lambda, lame_mu, moments, moment_owner, moment_cells, drm_rows
):
    sections = lax.axis_size("sec")
    segment_pos = lax.axis_index("segment")
    width_x, width_z, width_y = (fields.shape[2], fields.shape[3], fields.shape[4])
    cells_here = width_x * width_z * width_y
    capacity = 2 * moment_cells.shape[0] // sections
    owner = moment_owner[:, 0]
    marks = (owner[:, None] == jnp.arange(sections, dtype=jnp.int32)[None, :]).astype(jnp.int32)
    ranks = jnp.cumsum(marks, axis=0) - 1
    slot = jnp.sum(ranks * marks, axis=1)
    parcels = jnp.zeros((sections, 6, capacity), jnp.float32).at[owner, :, slot].set(moments.T)
    targets = jnp.full((sections, capacity), -1, jnp.int32).at[owner, slot].set(moment_cells)
    parcels, targets = (
        lax.all_to_all(parcels, "sec", split_axis=0, concat_axis=0, tiled=True),
        lax.all_to_all(targets, "sec", split_axis=0, concat_axis=0, tiled=True),
    )
    values = jnp.transpose(parcels, (1, 0, 2)).reshape(6, -1)
    places = targets.reshape(-1)
    places = jnp.where(places >= 0, places, cells_here)
    values = values * (segment_pos == 0).astype(jnp.float32)
    stress = fields[0, 3:].reshape(6, -1).at[:, places].add(values, mode="drop")
    state = jnp.concatenate(
        [fields[:, :3], stress.reshape(1, 6, width_x, width_z, width_y)], axis=1
    )
    block_here = block_ids[:, None]
    block_here = block_here[:, 0]
    buoy = lookup(block_here, buoyancy)
    lam = lookup(block_here, lame_lambda)
    shear = lookup(block_here, lame_mu)
    for step in range(STEPS):
        state = advance(state, buoy, lam, shear, drm_rows)
    return state


def solution(mesh):
    in_specs = (
        P("segment", None, "sec", "depth", None),
        P("segment", "sec", "depth", None),
        P(),
        P(),
        P(),
        P(None, ("sec", "depth")),
        P(("sec", "depth"), None),
        P(("sec", "depth")),
        P(("sec", "depth")),
    )
    out_specs = P("segment", None, "sec", "depth", None)
    return jax.shard_map(
        on_device, mesh=mesh, in_specs=in_specs, out_specs=out_specs, check_vma=False
    )
```

profile of v0, /device:TPU:13, one launch (start us, length us, event | category | flops | bytes accessed | tf_op | source)
XLA Modules:
  0.0 320.9 jit_solution(12817840987889373268)
XLA Ops:
  5.3 5.0 %scatter_custom_fusion.5 = s32[2048]{0:T(1024)} fusion(s32[1024]{0:T(1024)S(1)} %broadcast_select_fusion, s32[1024]{0:T(1024)} %param.16, s32[]{:T(128)} %constant.13.clone.1), kind=kCustom, calls=%fused_computation.247 | custom fusion | bytes 8704
  10.3 4.8 %all-to-all-start = ((s32[4,1,512]{2,1,0:T(1,128)}), s32[4,1,512]{2,1,0:T(1,128)S(1)}, u32[]{:S(2)}, u32[]{:S(2)}) async-start(s32[4,1,512]{2,1,0:T(1,128)} %bitcast.22), calls=%async_computation | async-start | bytes 16384 | tf_op jit(solution)/shard_map/all_to_all | solution.py:115
  27.6 4.5 %all-to-all-start.1 = ((f32[4,6,512]{2,1,0:T(8,128)}), f32[4,6,512]{2,1,0:T(8,128)S(1)}, u32[]{:S(2)}, u32[]{:S(2)}) async-start(f32[4,6,512]{2,1,0:T(8,128)} %bitcast.27), calls=%async_computation.1 | async-start | bytes 131072 | tf_op jit(solution)/shard_map/all_to_all | solution.py:114
  32.2 3.7 %all-to-all-done.1 = f32[4,6,512]{2,1,0:T(8,128)S(1)} async-done(((f32[4,6,512]{2,1,0:T(8,128)}), f32[4,6,512]{2,1,0:T(8,128)S(1)}, u32[]{:S(2)}, u32[]{:S(2)}) %all-to-all-start.1) | async-done | bytes 49184 | tf_op jit(solution)/shard_map/all_to_all | solution.py:114
  36.3 12.2 %scatter_fusion = f32[6,4096]{0,1:T(8,128)S(1)} fusion(f32[6,4096]{0,1:T(8,128)S(1)} %bitcast.403, s32[2048]{0:T(1024)S(1)} %bitcast.510, f32[2048,6]{1,0:T(8,128)S(1)} %copy.985), kind=kCustom, calls=%fused_computation.4 | custom fusion | flops 12288 | bytes 155648 | tf_op jit(solution)/shard_map/scatter-add | solution.py:121
  50.7 7.3 %fusion.100 = (f32[1,1,2,16,128]{1,4,3,2,0:T(8,128)}, f32[1,1,2,16,128]{1,4,3,2,0:T(8,128)}, f32[1,1,2,16,128]{1,4,3,2,0:T(8,128)}, f32[1,1,2,16,128]{1,4,3,2,0:...) fusion(f32[1,6,2,16,128]{1,4,3,2,0:T(8,128)S(1)} %bitcast.406), kind=kLoop, calls=%fused_computation.260 | loop fusion | bytes 196608 | tf_op jit(solution)/shard_map/slice | solution.py:64
  77.6 10.7 %fusion.7 = (f32[1,2,16,128]{3,2,1,0:T(8,128)S(1)}, f32[1,2,16,128]{3,2,1,0:T(8,128)S(1)}, pred[1,2,16,128]{3,2,1,0:T(8,128)(4,1)S(1)}, pred[1,2,16,128]{3,2,1,0...) fusion(f32[1,1,16,128]{3,2,1,0:T(8,128)S(1)} %slice.921, ...), kind=kLoop, calls=%fused_computation.39 | loop fusion | flops 233472 | bytes 229312 | tf_op jit(solution)/shard_map/add | solution.py:66
  92.3 7.0 %gather_fusion = f32[2048,3]{1,0:T(8,128)S(1)} fusion(f32[3,4096]{0,1:T(8,128)} %bitcast_subtract_fusion, s32[2048]{0:T(1024)S(1)} %get-tuple-element.103), kind=kCustom, calls=%fused_computation | custom fusion | bytes 57344 | tf_op jit(solution)/shard_map/gather | solution.py:55
  105.3 12.2 %scatter_fusion.1 = f32[3,4096]{0,1:T(8,128)S(1)} fusion(f32[3,4096]{0,1:T(8,128)S(1)} %copy.993, s32[2048]{0:T(1024)S(1)} %get-tuple-element.104, f32[2048,3]{1,0:T(8,128)S(1)} %copy.994), kind=kCustom, calls=%fused_computation.5 | custom fusion | flops 6144 | bytes 81920 | tf_op jit(solution)/shard_map/scatter-add | solution.py:57
  120.7 3.9 %fusion.99 = (f32[1,1,2,16,128]{1,4,3,2,0:T(8,128)}, f32[1,1,2,16,128]{1,4,3,2,0:T(8,128)}, f32[1,1,2,16,128]{1,4,3,2,0:T(8,128)}) fusion(f32[1,3,2,16,128]{1,4,3,2,0:T(8,128)S(1)} %bitcast.408), kind=kLoop, calls=%fused_computation.259 | loop fusion | bytes 98304 | tf_op jit(solution)/shard_map/slice | solution.py:83
  136.5 20.8 %multiply_add_fusion.6 = (f32[1,2,16,128]{3,2,1,0:T(8,128)S(1)}, f32[1,2,16,128]{3,2,1,0:T(8,128)S(1)}, f32[1,2,16,128]{3,2,1,0:T(8,128)S(1)}, f32[1,2,16,128]{3,2,1,0:T(8,128)S(1)}) fusion(f32[1,2,16,127]{3,2,1,0:T(8,128)S(1)} %slice.948, f32[1,1,2,16,128]{4,3,2,1,0:T(8,128)S(1)} %copy.1061, f32[1,1,2,16,128]{4,3,2,1,0:T(8,128)S(1)} %copy.1056, ...), kind=kLoop, calls=%fused_computation.188 | loop fusion | flops 307200 | bytes 245760 | tf_op jit(solution)/shard_map/add | solution.py:89
  170.0 7.2 %gather_fusion.1 = f32[2048,3]{1,0:T(8,128)S(1)} fusion(f32[3,4096]{0,1:T(8,128)} %sub.511, s32[2048]{0:T(1024)S(1)} %get-tuple-element.103), kind=kCustom, calls=%fused_computation.1 | custom fusion | bytes 57344 | tf_op jit(solution)/shard_map/gather | solution.py:55
  182.6 12.2 %scatter_fusion.2 = f32[3,4096]{0,1:T(8,128)S(1)} fusion(f32[3,4096]{0,1:T(8,128)S(1)} %copy-done, s32[2048]{0:T(1024)S(1)} %get-tuple-element.104, f32[2048,3]{1,0:T(8,128)S(1)} %copy.1007), kind=kCustom, calls=%fused_computation.6 | custom fusion | flops 6144 | bytes 81920 | tf_op jit(solution)/shard_map/scatter-add | solution.py:57
  195.0 4.2 %collective-permute-start.9 = (f32[1,3,2,1,128]{4,2,3,1,0:T(2,128)S(1)}, f32[1,3,2,1,128]{4,2,3,1,0:T(2,128)S(1)}, u32[]{:S(2)}, u32[]{:S(2)}) collective-permute-start(f32[1,3,2,1,128]{4,2,3,1,0:T(2,128)S(1)} %copy.1071), channel_id=1, source_target_pairs={{2,0},{4,2},{6,4},{3,1},{5,3},{7,5},{10,8},{12,10},{14,12},{11,9},... | collective-permute-start | bytes 9224 | tf_op jit(solution)/shard_map/ppermute | solution.py:15
  199.1 3.9 %fusion.98 = (f32[1,1,2,16,128]{1,4,3,2,0:T(8,128)}, f32[1,1,2,16,128]{1,4,3,2,0:T(8,128)}, f32[1,1,2,16,128]{1,4,3,2,0:T(8,128)}) fusion(f32[1,3,2,16,128]{1,4,3,2,0:T(8,128)S(1)} %bitcast.411), kind=kLoop, calls=%fused_computation.258 | loop fusion | bytes 98304 | tf_op jit(solution)/shard_map/slice | solution.py:83
  227.1 7.2 %gather_fusion.2 = f32[2048,3]{1,0:T(8,128)S(1)} fusion(f32[3,4096]{0,1:T(8,128)} %sub.530, s32[2048]{0:T(1024)S(1)} %get-tuple-element.103), kind=kCustom, calls=%fused_computation.2 | custom fusion | bytes 57344 | tf_op jit(solution)/shard_map/gather | solution.py:55
  235.9 3.4 %collective-permute-done.12 = f32[3,2048]{1,0:T(4,128)S(1)} collective-permute-done((f32[3,2048]{1,0:T(4,128)S(1)}, f32[3,2048]{1,0:T(4,128)S(1)}, u32[]{:S(2)}, u32[]{:S(2)}) %collective-permute-start.12) | collective-permute-done | bytes 24608 | tf_op jit(solution)/shard_map/ppermute | solution.py:15
  239.7 12.2 %scatter_fusion.3 = f32[3,4096]{0,1:T(8,128)S(1)} fusion(f32[3,4096]{0,1:T(8,128)S(1)} %copy-done.1, s32[2048]{0:T(1024)S(1)} %get-tuple-element.104, f32[2048,3]{1,0:T(8,128)S(1)} %copy.1020), kind=kCustom, calls=%fused_computation.7 | custom fusion | flops 6144 | bytes 81920 | tf_op jit(solution)/shard_map/scatter-add | solution.py:57
  252.0 4.5 %collective-permute-start.14 = (f32[1,3,2,1,128]{4,2,3,1,0:T(2,128)S(1)}, f32[1,3,2,1,128]{4,2,3,1,0:T(2,128)S(1)}, u32[]{:S(2)}, u32[]{:S(2)}) collective-permute-start(f32[1,3,2,1,128]{4,2,3,1,0:T(2,128)S(1)} %copy.1079), channel_id=1, source_target_pairs={{2,0},{4,2},{6,4},{3,1},{5,3},{7,5},{10,8},{12,10},{14,12},{11,9},... | collective-permute-start | bytes 9224 | tf_op jit(solution)/shard_map/ppermute | solution.py:15
  256.6 3.9 %fusion.97 = (f32[1,1,2,16,128]{1,4,3,2,0:T(8,128)}, f32[1,1,2,16,128]{1,4,3,2,0:T(8,128)}, f32[1,1,2,16,128]{1,4,3,2,0:T(8,128)}) fusion(f32[1,3,2,16,128]{1,4,3,2,0:T(8,128)S(1)} %bitcast.414), kind=kLoop, calls=%fused_computation.257 | loop fusion | bytes 98304 | tf_op jit(solution)/shard_map/slice | solution.py:83
  284.5 7.2 %gather_fusion.3 = f32[2048,3]{1,0:T(8,128)S(1)} fusion(f32[3,4096]{0,1:T(8,128)} %sub.549, s32[2048]{0:T(1024)S(1)} %get-tuple-element.103), kind=kCustom, calls=%fused_computation.3 | custom fusion | bytes 57344 | tf_op jit(solution)/shard_map/gather | solution.py:55
  293.3 3.4 %collective-permute-done.17 = f32[3,2048]{1,0:T(4,128)S(1)} collective-permute-done((f32[3,2048]{1,0:T(4,128)S(1)}, f32[3,2048]{1,0:T(4,128)S(1)}, u32[]{:S(2)}, u32[]{:S(2)}) %collective-permute-start.17) | collective-permute-done | bytes 24608 | tf_op jit(solution)/shard_map/ppermute | solution.py:15
  297.1 12.2 %scatter_fusion.4 = f32[3,4096]{0,1:T(8,128)S(1)} fusion(f32[3,4096]{0,1:T(8,128)S(1)} %copy-done.2, s32[2048]{0:T(1024)S(1)} %get-tuple-element.104, f32[2048,3]{1,0:T(8,128)S(1)} %copy.1033), kind=kCustom, calls=%fused_computation.8 | custom fusion | flops 6144 | bytes 81920 | tf_op jit(solution)/shard_map/scatter-add | solution.py:57
  310.1 4.5 %collective-permute-start.19 = (f32[1,3,2,1,128]{4,2,3,1,0:T(2,128)S(1)}, f32[1,3,2,1,128]{4,2,3,1,0:T(2,128)S(1)}, u32[]{:S(2)}, u32[]{:S(2)}) collective-permute-start(f32[1,3,2,1,128]{4,2,3,1,0:T(2,128)S(1)} %copy.1083), channel_id=1, source_target_pairs={{2,0},{4,2},{6,4},{3,1},{5,3},{7,5},{10,8},{12,10},{14,12},{11,9},... | collective-permute-start | bytes 9224 | tf_op jit(solution)/shard_map/ppermute | solution.py:15
  (250 shorter events, 141.1 us)
Async XLA Ops:
  0.0 25.0 %slice-start = ((f32[1,9,2,16,128]{4,3,2,1,0:T(8,128)}), f32[1,6,2,16,128]{4,3,2,1,0:T(8,128)S(1)}, s32[]{:S(2)}) async-start(f32[1,9,2,16,128]{4,3,2,1,0:T(8,128)} %param.9), calls=%async_computation.2 | async-start | bytes 196608 | tf_op jit(solution)/shard_map/slice | solution.py:121
  10.3 17.3 %all-to-all-start = ((s32[4,1,512]{2,1,0:T(1,128)}), s32[4,1,512]{2,1,0:T(1,128)S(1)}, u32[]{:S(2)}, u32[]{:S(2)}) async-start(s32[4,1,512]{2,1,0:T(1,128)} %bitcast.22), calls=%async_computation | async-start | bytes 16384 | tf_op jit(solution)/shard_map/all_to_all | solution.py:115
  27.6 8.3 %all-to-all-start.1 = ((f32[4,6,512]{2,1,0:T(8,128)}), f32[4,6,512]{2,1,0:T(8,128)S(1)}, u32[]{:S(2)}, u32[]{:S(2)}) async-start(f32[4,6,512]{2,1,0:T(8,128)} %bitcast.27), calls=%async_computation.1 | async-start | bytes 131072 | tf_op jit(solution)/shard_map/all_to_all | solution.py:114
  61.7 15.8 %collective-permute-start.1 = (f32[1,3,2,1,128]{4,3,2,1,0:T(1,128)S(1)}, f32[1,3,2,1,128]{4,3,2,1,0:T(1,128)S(1)}, u32[]{:S(2)}, u32[]{:S(2)}) collective-permute-start(f32[1,3,2,1,128]{4,3,2,1,0:T(1,128)S(1)} %pad_maximum_fusion.8), channel_id=1, source_target_pairs={{0,2},{2,4},{4,6},{1,3},{3,5},{5,7},{8,10},{10,12},{12,14},{9,11},... | collective-permute-start | bytes 9224 | tf_op jit(solution)/shard_map/ppermute | solution.py:15
  64.9 12.7 %collective-permute-start = (f32[1,3,1,16,128]{4,3,2,1,0:T(8,128)S(1)}, f32[1,3,1,16,128]{4,3,2,1,0:T(8,128)S(1)}, u32[]{:S(2)}, u32[]{:S(2)}) collective-permute-start(f32[1,3,1,16,128]{4,3,2,1,0:T(8,128)S(1)} %pad_maximum_fusion.4), channel_id=1, source_target_pairs={{0,8},{8,16},{16,24},{1,9},{9,17},{17,25},{2,10},{10,18},{18,26},{... | collective-permute-start | bytes 73736 | tf_op jit(solution)/shard_map/ppermute | solution.py:15
  99.7 5.2 %collective-permute-start.2 = (f32[3,2048]{1,0:T(4,128)S(1)}, f32[3,2048]{1,0:T(4,128)S(1)}, u32[]{:S(2)}, u32[]{:S(2)}) collective-permute-start(f32[3,2048]{1,0:T(4,128)S(1)} %copy.992), channel_id=1, source_target_pairs={{0,1},{2,3},{4,5},{6,7},{8,9},{10,11},{12,13},{14,15},{16,17},{18,... | collective-permute-start | bytes 73736 | tf_op jit(solution)/shard_map/ppermute | solution.py:15
  117.6 17.6 %collective-permute-start.4 = (f32[1,3,2,1,128]{4,2,3,1,0:T(2,128)S(1)}, f32[1,3,2,1,128]{4,2,3,1,0:T(2,128)S(1)}, u32[]{:S(2)}, u32[]{:S(2)}) collective-permute-start(f32[1,3,2,1,128]{4,2,3,1,0:T(2,128)S(1)} %copy.1063), channel_id=1, source_target_pairs={{2,0},{4,2},{6,4},{3,1},{5,3},{7,5},{10,8},{12,10},{14,12},{11,9},... | collective-permute-start | bytes 9224 | tf_op jit(solution)/shard_map/ppermute | solution.py:15
  131.9 4.6 %collective-permute-start.3 = (f32[1,3,1,16,128]{4,3,2,1,0:T(8,128)S(1)}, f32[1,3,1,16,128]{4,3,2,1,0:T(8,128)S(1)}, u32[]{:S(2)}, u32[]{:S(2)}) collective-permute-start(f32[1,3,1,16,128]{4,3,2,1,0:T(8,128)S(1)} %copy.1060), channel_id=1, source_target_pairs={{8,0},{16,8},{24,16},{9,1},{17,9},{25,17},{10,2},{18,10},{26,18},{... | collective-permute-start | bytes 73736 | tf_op jit(solution)/shard_map/ppermute | solution.py:15
  157.5 5.2 %collective-permute-start.6 = (f32[1,3,2,1,128]{4,2,3,1,0:T(2,128)S(1)}, f32[1,3,2,1,128]{4,2,3,1,0:T(2,128)S(1)}, u32[]{:S(2)}, u32[]{:S(2)}) collective-permute-start(f32[1,3,2,1,128]{4,2,3,1,0:T(2,128)S(1)} %pad_maximum_fusion.9), channel_id=1, source_target_pairs={{0,2},{2,4},{4,6},{1,3},{3,5},{5,7},{8,10},{10,12},{12,14},{9,11},... | collective-permute-start | bytes 9224 | tf_op jit(solution)/shard_map/ppermute | solution.py:15
  159.7 4.9 %collective-permute-start.5 = (f32[1,3,1,16,128]{4,3,2,1,0:T(8,128)S(1)}, f32[1,3,1,16,128]{4,3,2,1,0:T(8,128)S(1)}, u32[]{:S(2)}, u32[]{:S(2)}) collective-permute-start(f32[1,3,1,16,128]{4,3,2,1,0:T(8,128)S(1)} %pad_maximum_fusion.5), channel_id=1, source_target_pairs={{0,8},{8,16},{16,24},{1,9},{9,17},{17,25},{2,10},{10,18},{18,26},{... | collective-permute-start | bytes 73736 | tf_op jit(solution)/shard_map/ppermute | solution.py:15
  177.5 4.7 %collective-permute-start.7 = (f32[3,2048]{1,0:T(4,128)S(1)}, f32[3,2048]{1,0:T(4,128)S(1)}, u32[]{:S(2)}, u32[]{:S(2)}) collective-permute-start(f32[3,2048]{1,0:T(4,128)S(1)} %copy.1005), channel_id=1, source_target_pairs={{0,1},{2,3},{4,5},{6,7},{8,9},{10,11},{12,13},{14,15},{16,17},{18,... | collective-permute-start | bytes 73736 | tf_op jit(solution)/shard_map/ppermute | solution.py:15
  195.0 17.4 %collective-permute-start.9 = (f32[1,3,2,1,128]{4,2,3,1,0:T(2,128)S(1)}, f32[1,3,2,1,128]{4,2,3,1,0:T(2,128)S(1)}, u32[]{:S(2)}, u32[]{:S(2)}) collective-permute-start(f32[1,3,2,1,128]{4,2,3,1,0:T(2,128)S(1)} %copy.1071), channel_id=1, source_target_pairs={{2,0},{4,2},{6,4},{3,1},{5,3},{7,5},{10,8},{12,10},{14,12},{11,9},... | collective-permute-start | bytes 9224 | tf_op jit(solution)/shard_map/ppermute | solution.py:15
  210.4 4.6 %collective-permute-start.8 = (f32[1,3,1,16,128]{4,3,2,1,0:T(8,128)S(1)}, f32[1,3,1,16,128]{4,3,2,1,0:T(8,128)S(1)}, u32[]{:S(2)}, u32[]{:S(2)}) collective-permute-start(f32[1,3,1,16,128]{4,3,2,1,0:T(8,128)S(1)} %copy.1068), channel_id=1, source_target_pairs={{8,0},{16,8},{24,16},{9,1},{17,9},{25,17},{10,2},{18,10},{26,18},{... | collective-permute-start | bytes 73736 | tf_op jit(solution)/shard_map/ppermute | solution.py:15
  215.1 5.2 %collective-permute-start.11 = (f32[1,3,2,1,128]{4,2,3,1,0:T(2,128)S(1)}, f32[1,3,2,1,128]{4,2,3,1,0:T(2,128)S(1)}, u32[]{:S(2)}, u32[]{:S(2)}) collective-permute-start(f32[1,3,2,1,128]{4,2,3,1,0:T(2,128)S(1)} %pad_maximum_fusion.10), channel_id=1, source_target_pairs={{0,2},{2,4},{4,6},{1,3},{3,5},{5,7},{8,10},{10,12},{12,14},{9,11},... | collective-permute-start | bytes 9224 | tf_op jit(solution)/shard_map/ppermute | solution.py:15
  217.1 4.6 %collective-permute-start.10 = (f32[1,3,1,16,128]{4,3,2,1,0:T(8,128)S(1)}, f32[1,3,1,16,128]{4,3,2,1,0:T(8,128)S(1)}, u32[]{:S(2)}, u32[]{:S(2)}) collective-permute-start(f32[1,3,1,16,128]{4,3,2,1,0:T(8,128)S(1)} %pad_maximum_fusion.6), channel_id=1, source_target_pairs={{0,8},{8,16},{16,24},{1,9},{9,17},{17,25},{2,10},{10,18},{18,26},{... | collective-permute-start | bytes 73736 | tf_op jit(solution)/shard_map/ppermute | solution.py:15
  227.0 12.6 %copy-start.1 = (f32[3,4096]{0,1:T(8,128)S(1)}, f32[3,4096]{0,1:T(8,128)}, u32[]{:S(2)}) copy-start(f32[3,4096]{0,1:T(8,128)} %copy.1019) | copy-start | bytes 147460
  234.6 4.7 %collective-permute-start.12 = (f32[3,2048]{1,0:T(4,128)S(1)}, f32[3,2048]{1,0:T(4,128)S(1)}, u32[]{:S(2)}, u32[]{:S(2)}) collective-permute-start(f32[3,2048]{1,0:T(4,128)S(1)} %copy.1018), channel_id=1, source_target_pairs={{0,1},{2,3},{4,5},{6,7},{8,9},{10,11},{12,13},{14,15},{16,17},{18,... | collective-permute-start | bytes 73736 | tf_op jit(solution)/shard_map/ppermute | solution.py:15
  252.0 17.7 %collective-permute-start.14 = (f32[1,3,2,1,128]{4,2,3,1,0:T(2,128)S(1)}, f32[1,3,2,1,128]{4,2,3,1,0:T(2,128)S(1)}, u32[]{:S(2)}, u32[]{:S(2)}) collective-permute-start(f32[1,3,2,1,128]{4,2,3,1,0:T(2,128)S(1)} %copy.1079), channel_id=1, source_target_pairs={{2,0},{4,2},{6,4},{3,1},{5,3},{7,5},{10,8},{12,10},{14,12},{11,9},... | collective-permute-start | bytes 9224 | tf_op jit(solution)/shard_map/ppermute | solution.py:15
  267.8 4.6 %collective-permute-start.13 = (f32[1,3,1,16,128]{4,3,2,1,0:T(8,128)S(1)}, f32[1,3,1,16,128]{4,3,2,1,0:T(8,128)S(1)}, u32[]{:S(2)}, u32[]{:S(2)}) collective-permute-start(f32[1,3,1,16,128]{4,3,2,1,0:T(8,128)S(1)} %copy.1076), channel_id=1, source_target_pairs={{8,0},{16,8},{24,16},{9,1},{17,9},{25,17},{10,2},{18,10},{26,18},{... | collective-permute-start | bytes 73736 | tf_op jit(solution)/shard_map/ppermute | solution.py:15
  272.5 5.2 %collective-permute-start.16 = (f32[1,3,2,1,128]{4,2,3,1,0:T(2,128)S(1)}, f32[1,3,2,1,128]{4,2,3,1,0:T(2,128)S(1)}, u32[]{:S(2)}, u32[]{:S(2)}) collective-permute-start(f32[1,3,2,1,128]{4,2,3,1,0:T(2,128)S(1)} %pad_maximum_fusion.11), channel_id=1, source_target_pairs={{0,2},{2,4},{4,6},{1,3},{3,5},{5,7},{8,10},{10,12},{12,14},{9,11},... | collective-permute-start | bytes 9224 | tf_op jit(solution)/shard_map/ppermute | solution.py:15
  274.5 4.6 %collective-permute-start.15 = (f32[1,3,1,16,128]{4,3,2,1,0:T(8,128)S(1)}, f32[1,3,1,16,128]{4,3,2,1,0:T(8,128)S(1)}, u32[]{:S(2)}, u32[]{:S(2)}) collective-permute-start(f32[1,3,1,16,128]{4,3,2,1,0:T(8,128)S(1)} %pad_maximum_fusion.7), channel_id=1, source_target_pairs={{0,8},{8,16},{16,24},{1,9},{9,17},{17,25},{2,10},{10,18},{18,26},{... | collective-permute-start | bytes 73736 | tf_op jit(solution)/shard_map/ppermute | solution.py:15
  292.0 4.7 %collective-permute-start.17 = (f32[3,2048]{1,0:T(4,128)S(1)}, f32[3,2048]{1,0:T(4,128)S(1)}, u32[]{:S(2)}, u32[]{:S(2)}) collective-permute-start(f32[3,2048]{1,0:T(4,128)S(1)} %copy.1031), channel_id=1, source_target_pairs={{0,1},{2,3},{4,5},{6,7},{8,9},{10,11},{12,13},{14,15},{16,17},{18,... | collective-permute-start | bytes 73736 | tf_op jit(solution)/shard_map/ppermute | solution.py:15
  310.1 6.8 %collective-permute-start.19 = (f32[1,3,2,1,128]{4,2,3,1,0:T(2,128)S(1)}, f32[1,3,2,1,128]{4,2,3,1,0:T(2,128)S(1)}, u32[]{:S(2)}, u32[]{:S(2)}) collective-permute-start(f32[1,3,2,1,128]{4,2,3,1,0:T(2,128)S(1)} %copy.1083), channel_id=1, source_target_pairs={{2,0},{4,2},{6,4},{3,1},{5,3},{7,5},{10,8},{12,10},{14,12},{11,9},... | collective-permute-start | bytes 9224 | tf_op jit(solution)/shard_map/ppermute | solution.py:15
  314.9 4.6 %collective-permute-start.18 = (f32[1,3,1,16,128]{4,3,2,1,0:T(8,128)S(1)}, f32[1,3,1,16,128]{4,3,2,1,0:T(8,128)S(1)}, u32[]{:S(2)}, u32[]{:S(2)}) collective-permute-start(f32[1,3,1,16,128]{4,3,2,1,0:T(8,128)S(1)} %slice.1068), channel_id=1, source_target_pairs={{8,0},{16,8},{24,16},{9,1},{17,9},{25,17},{10,2},{18,10},{26,18},{... | collective-permute-start | bytes 73736 | tf_op jit(solution)/shard_map/ppermute | solution.py:15
  (9 other events, 57.8 us)
where the time goes:
time: 324 us; the launch traced here: 321 us
  local copies, waits for them, and re-layouts  116 us (36%)
  other arithmetic  113 us (35%)
  starting transfers between devices  57.8 us (18%)
  waiting for transfers between devices  33.7 us (10%)
    scatter-add x4, other arithmetic, couple(): basin = newv[0].reshape(3, -1).at[:, rows_here].add(arrived)  49 us
    ppermute x20, starting transfers between devices, passed_along(): return lax.ppermute(block, axis, route)  48.5 us
    unnamed x50, local copies, waits for them, and re-layouts  45.4 us
    ppermute x20, waiting for transfers between devices, passed_along(): return lax.ppermute(block, axis, route)  30 us
    gather x8, local copies, waits for them, and re-layouts, couple(): increment = (newv[0] - oldv[0]).reshape(3, -1)[:, rows_here]  30 us
    add x3, other arithmetic, advance(): syy = syy + HALF_STEP * (lam * trace + 2.0 * shear * eyy)  20.9 us
    sub x4, other arithmetic, couple(): increment = (newv[0] - oldv[0]).reshape(3, -1)[:, rows_here]  12.6 us
    scatter-add x1, other arithmetic, on_device(): stress = fields[0, 3:].reshape(6, -1).at[:, places].add(values, mode='drop')  12.2 us
  transfers between devices with their start and end apart: 22, of which 15 were waited for; matrix products, arithmetic and copies ran while one was open for 18% of the time, Pallas kernels for 0%

commit v1 on v0

v1 whole, which is shorter than its diff:
```python
import functools

import jax
import jax.numpy as jnp
from jax import lax
from jax.experimental import pallas as pl
from jax.experimental.pallas import tpu as pltpu
from jax.sharding import PartitionSpec as P

STEPS = 4
MARGIN = 8
F32 = jnp.float32
BF16 = jnp.bfloat16
NT = (((1,), (1,)), ((), ()))


def one_hot(index, count):
    rows = lax.broadcasted_iota(jnp.int32, (count, index.shape[-1]), 0)
    return jnp.where(rows == index, F32(1.0), F32(0.0)).astype(BF16)


def split3(value):
    high = value.astype(BF16)
    rest = value - high.astype(F32)
    mid = rest.astype(BF16)
    low = (rest - mid.astype(F32)).astype(BF16)
    return high, mid, low


def pack_kernel(fields, ids, moments, cells, rows, payload, entries):
    cx, cz, cy = fields.shape[2:]
    payload[0:9] = fields[0]
    payload[9] = (ids[0] + 1).astype(F32)
    lines = [rows[i : i + 1, :] for i in range(rows.shape[0])]
    line = jnp.concatenate(lines, axis=1)
    high = one_hot(line // cy, cx * cz)
    low = one_hot(line % cy, cy)
    count = lax.dot_general(high, low, NT, preferred_element_type=F32)
    payload[10] = count.reshape(cx, cz, cy)
    entries[0:6] = moments[...]
    width = cells.shape[1]
    for i in range(cells.shape[0]):
        entries[6:7, i * width : (i + 1) * width] = cells[i : i + 1, :].astype(F32)
        entries[7:8, i * width : (i + 1) * width] = jnp.zeros((1, width), F32)


def moment_kernel(sizes, entries, window, acc):
    cx, cz, cy, reach, sections, slabs = sizes
    planes = window.shape[1]
    section = lax.axis_index("sec")
    slab = lax.axis_index("depth")
    first_plane = (section - reach) * cx
    window[...] = jnp.zeros_like(window)

    def gather(depth_index, first_row, row_count, at_row):
        acc[0 : 6 * planes * row_count, :] = jnp.zeros((6 * planes * row_count, cy), F32)

        @pl.loop(0, sections)
        def _(source):
            block = entries[source * slabs + depth_index]
            cell = block[6:7, :].astype(jnp.int32)
            row = cell // cy
            z = row % cz - first_row
            plane = row // cz - first_plane
            inside = (z >= 0) & (z < row_count)
            place = jnp.where(inside, plane * row_count + z, -1)
            high = one_hot(place, planes * row_count)
            low = one_hot(cell % cy, cy)
            parts = split3(block[0:6, :])
            for comp in range(6):
                total = jnp.zeros((planes * row_count, cy), F32)
                for part in parts:
                    total = total + lax.dot_general(
                        high * part[comp : comp + 1, :], low, NT, preferred_element_type=F32
                    )
                span = slice(comp * planes * row_count, (comp + 1) * planes * row_count)
                acc[span, :] = acc[span, :] + total

        for comp in range(6):
            span = slice(comp * planes * row_count, (comp + 1) * planes * row_count)
            window[comp, :, at_row : at_row + row_count, :] = acc[span, :].reshape(
                planes, row_count, cy
            )

    gather(slab, 0, cz, MARGIN)

    @pl.when(slab > 0)
    def _():
        gather(slab - 1, cz - MARGIN, MARGIN, 0)

    @pl.when(slab < slabs - 1)
    def _():
        gather(slab + 1, 0, MARGIN, MARGIN + cz)


def step_kernel(sizes, gathered, window, buoyancy, lame_lambda, lame_mu, out, state, coef, sem):
    cx, cz, cy, reach, sections, slabs = sizes
    planes, rows = state.shape[2], state.shape[3]
    section = lax.axis_index("sec")
    slab = lax.axis_index("depth")
    segment = lax.axis_index("segment")
    state[...] = jnp.zeros_like(state)

    def pieces(act):
        for i in range(2 * reach + 1):
            source = section - reach + i
            for k, (first, count, at) in enumerate(
                ((cz - MARGIN, MARGIN, 0), (0, cz, MARGIN), (0, MARGIN, MARGIN + cz))
            ):
                depth = slab - 1 + k

                @pl.when((source >= 0) & (source < sections) & (depth >= 0) & (depth < slabs))
                def _():
                    for model in range(2):
                        device = (source * slabs + depth) * 2 + model
                        act(
                            pltpu.make_async_copy(
                                gathered.at[device, :, :, pl.ds(first, count), :],
                                state.at[model, :, pl.ds(i * cx, cx), pl.ds(at, count), :],
                                sem.at[i, k, model],
                            )
                        )

    pieces(lambda copy: copy.start())
    pieces(lambda copy: copy.wait())

    @pl.loop(0, planes)
    def _(x):
        for model in range(2):
            ids = state[model, 9, x]
            found = [jnp.zeros((rows, cy), F32)] * 3
            for entry in range(buoyancy.shape[0]):
                hit = ids == F32(entry + 1)
                found = [
                    jnp.where(hit, F32(0.5) * table[entry], value)
                    for table, value in zip((buoyancy, lame_lambda, lame_mu), found)
                ]
            for number in range(3):
                coef[model, number, x] = found[number]
        for comp in range(6):
            state[0, 3 + comp, x] = state[0, 3 + comp, x] + window[comp, x]

    lane = lax.broadcasted_iota(jnp.int32, (rows, cy), 1)
    first_lane, last_lane = lane == 0, lane == cy - 1

    def back_y(f):
        return f - jnp.where(first_lane, F32(0.0), pltpu.roll(f, 1, 1))

    def back_z(f):
        return f - pltpu.roll(f, 1, 0)

    def fore_y(f):
        return jnp.where(last_lane, F32(0.0), pltpu.roll(f, cy - 1, 1)) - f

    def fore_z(f):
        return pltpu.roll(f, rows - 1, 0) - f

    own = reach * cx
    for step in range(STEPS):
        left = STEPS - 1 - step
        low, high = own - left, own + cx + left

        @pl.loop(low, high + 1)
        def _(x):
            inc = [None, None]
            for model in range(2):
                sxx, syy, szz, syz, sxz, sxy = (state[model, 3 + k, x] for k in range(6))
                sxx_p, sxz_p, sxy_p = (state[model, k, x - 1] for k in (3, 7, 8))
                hb = coef[model, 0, x]
                inc[model] = (
                    hb * ((sxx - sxx_p) + back_y(sxy) + back_z(sxz)),
                    hb * ((sxy - sxy_p) + back_y(syy) + back_z(syz)),
                    hb * ((sxz - sxz_p) + back_y(syz) + back_z(szz)),
                )
            times = state[1, 10, x]
            for k in range(3):
                state[0, k, x] = state[0, k, x] + inc[0][k]
                state[1, k, x] = (state[1, k, x] + inc[1][k]) + times * inc[0][k]

        @pl.loop(low, high)
        def _(x):
            for model in range(2):
                vx, vy, vz = (state[model, k, x] for k in range(3))
                vx_n, vy_n, vz_n = (state[model, k, x + 1] for k in range(3))
                hl, hm = coef[model, 1, x], coef[model, 2, x]
                exx, eyy, ezz = vx_n - vx, fore_y(vy), fore_z(vz)
                pressure = hl * (exx + eyy + ezz)
                twice = hm + hm
                state[model, 3, x] = state[model, 3, x] + (pressure + twice * exx)
                state[model, 4, x] = state[model, 4, x] + (pressure + twice * eyy)
                state[model, 5, x] = state[model, 5, x] + (pressure + twice * ezz)
                state[model, 6, x] = state[model, 6, x] + hm * (fore_z(vy) + fore_y(vz))
                state[model, 7, x] = state[model, 7, x] + hm * (fore_z(vx) + (vz_n - vz))
                state[model, 8, x] = state[model, 8, x] + hm * (fore_y(vx) + (vy_n - vy))

    out[0] = state[segment, 0:9, own : own + cx, MARGIN : MARGIN + cz, :]


VMEM = pl.BlockSpec(memory_space=pltpu.VMEM)
SMEM = pl.BlockSpec(memory_space=pltpu.SMEM)
ANY = pl.BlockSpec(memory_space=pl.ANY)
LIMIT = pltpu.CompilerParams(vmem_limit_bytes=40 * 2**20)


def on_device(
    fields, block_ids, buoyancy, lame_lambda, lame_mu, moments, moment_owner, moment_cells, drm_rows
):
    sections, slabs = lax.axis_size("sec"), lax.axis_size("depth")
    cx, cz, cy = fields.shape[2:]
    cells_here = cx * cz * cy
    count = moment_cells.shape[0]
    reach = -(-STEPS // cx)
    planes, rows = (2 * reach + 1) * cx, cz + 2 * MARGIN
    sizes = (cx, cz, cy, reach, sections, slabs)
    cells = (moment_owner[:, 0] * cells_here + moment_cells).reshape(-1, cy)
    payload, entries = pl.pallas_call(
        pack_kernel,
        out_shape=(
            jax.ShapeDtypeStruct((11, cx, cz, cy), F32),
            jax.ShapeDtypeStruct((8, count), F32),
        ),
        in_specs=[VMEM] * 5,
        out_specs=(VMEM, VMEM),
        compiler_params=LIMIT,
        name="pack",
    )(fields, block_ids, moments, cells, drm_rows.reshape(-1, cy))
    all_entries = lax.all_gather(entries, ("sec", "depth"))
    gathered = lax.all_gather(payload, ("sec", "depth", "segment"))
    window = pl.pallas_call(
        functools.partial(moment_kernel, sizes),
        out_shape=jax.ShapeDtypeStruct((6, planes, rows, cy), F32),
        in_specs=[VMEM],
        out_specs=VMEM,
        scratch_shapes=[pltpu.VMEM((6 * planes * max(cz, MARGIN), cy), F32)],
        compiler_params=LIMIT,
        name="moments_in_window",
    )(all_entries)
    return pl.pallas_call(
        functools.partial(step_kernel, sizes),
        out_shape=jax.ShapeDtypeStruct(fields.shape, F32),
        in_specs=[ANY, VMEM, SMEM, SMEM, SMEM],
        out_specs=VMEM,
        scratch_shapes=[
            pltpu.VMEM((2, 11, planes, rows, cy), F32),
            pltpu.VMEM((2, 3, planes, rows, cy), F32),
            pltpu.SemaphoreType.DMA((2 * reach + 1, 3, 2)),
        ],
        compiler_params=LIMIT,
        name="steps",
    )(gathered, window, buoyancy, lame_lambda, lame_mu)


def solution(mesh):
    in_specs = (
        P("segment", None, "sec", "depth", None),
        P("segment", "sec", "depth", None),
        P(),
        P(),
        P(),
        P(None, ("sec", "depth")),
        P(("sec", "depth"), None),
        P(("sec", "depth")),
        P(("sec", "depth")),
    )
    out_specs = P("segment", None, "sec", "depth", None)
    return jax.shard_map(
        on_device, mesh=mesh, in_specs=in_specs, out_specs=out_specs, check_vma=False
    )
```

time: 324 us -> 103 us (0.32)
  other arithmetic: 113 us -> 1.38 us
  local copies, waits for them, and re-layouts: 116 us -> 7.68 us
  starting transfers between devices: 57.8 us -> 0.01 us
  Pallas kernels: 0 us -> 30.2 us
  blocking collectives: 0 us -> 28.1 us
  between operations: 1.08 us -> 13.4 us
  waiting for transfers between devices: 33.7 us -> 21.4 us
    scatter-add x5 -> x0, other arithmetic: 61.2 us -> none  [the longest x4 49 us: couple(): basin = newv[0].reshape(3, -1).at[:, rows_here].add(arrived)]
    ppermute x20 -> x0, starting transfers between devices: 48.5 us -> none  [passed_along(): return lax.ppermute(block, axis, route)]
    unnamed x50 -> x16, local copies, waits for them, and re-layouts: 45.4 us -> 7.68 us
    add x15 -> x0, other arithmetic: 32.3 us -> none  [the longest x3 20.9 us: advance(): syy = syy + HALF_STEP * (lam * trace + 2.0 * shear * eyy)]
    pallas_call x0 -> x3, Pallas kernels: none -> 30.2 us  [the longest x1 21.6 us: on_device(): pl.pallas_call(functools.partial(moment_kernel, sizes), out_shape=jax.Sha...]
    slice x97 -> x0, local copies, waits for them, and re-layouts: 30.1 us -> none  [the longest x3 11.7 us: advance(): vx, vy, vz = (newv[:, 0], newv[:, 1], newv[:, 2])]
    ppermute x20 -> x0, waiting for transfers between devices: 30 us -> none  [passed_along(): return lax.ppermute(block, axis, route)]
    gather x8 -> x0, local copies, waits for them, and re-layouts: 30 us -> none  [couple(): increment = (newv[0] - oldv[0]).reshape(3, -1)[:, rows_here]]
  transfers between devices with their start and end apart: 22 -> 1, of which waited for: 15 -> 1; matrix products, arithmetic and copies ran while one was open for 18% -> 0% of each run, Pallas kernels for 0% -> 21%
where the time goes in v1:
time: 103 us; the launch traced here: 102 us
  Pallas kernels  30.2 us (29%)
  blocking collectives  28.1 us (27%)
  waiting for transfers between devices  21.4 us (21%)
  between operations  13.4 us (13%)
  local copies, waits for them, and re-layouts  7.68 us (7%)
  other arithmetic  1.38 us (1%)
    all_gather x1, blocking collectives, on_device(): all_entries = lax.all_gather(entries, ('sec', 'depth'))  28.1 us
    pallas_call x1, Pallas kernels, on_device(): pl.pallas_call(functools.partial(moment_kernel, sizes), out_shape=jax.Sha...  21.6 us
    all_gather x1, waiting for transfers between devices, on_device(): gathered = lax.all_gather(payload, ('sec', 'depth', 'segment'))  21.4 us
    unnamed x16, local copies, waits for them, and re-layouts  7.68 us
    pallas_call x1, Pallas kernels, on_device(): pl.pallas_call(functools.partial(step_kernel, sizes), out_shape=jax.Shape...  7.66 us
  transfers between devices with their start and end apart: 1, of which 1 were waited for; matrix products, arithmetic and copies ran while one was open for 0% of the time, Pallas kernels for 21%

profile of v1, /device:TPU:13, one launch (start us, length us, event | category | flops | bytes accessed | tf_op | source)
XLA Modules:
  0.0 102.2 jit_solution(9421133904406654550)
XLA Ops:
  6.5 0.0 all-gather.4.cloned.1.call-start
  6.5 0.7 broadcast_multiply_fusion
  7.2 0.7 add_bitcast_fusion.cells
  7.9 0.0 copy-start.1
  7.9 0.9 copy-done.1
  8.8 0.0 copy-start.2
  8.8 0.8 copy-done.2
  9.6 0.0 copy-start.3
  9.6 0.7 copy-done.3
  10.3 0.0 copy-start.4
  10.3 0.7 copy-done.4
  11.0 1.0 pack.1
  12.0 0.0 all-gather.4.cloned.1.call-update
  12.0 28.1 %all-gather.1 = f32[128,1024]{1,0:T(8,128)S(1)} all-gather(f32[8,1024]{1,0:T(8,128)S(1)} %get-tuple-element.8), channel_id=3, replica_groups=mesh['sec'=4,'depth'=4,'segment'=2] {'sec','depth'}, dimensions={0}, use_global_device_ids=true | all-gather | bytes 557056 | tf_op jit(solution)/shard_map/all_gather | solution.py:227
  40.1 21.6 %moments_in_window.1.window = f32[6,10,32,128]{3,2,1,0:T(8,128)S(1)} custom-call(f32[16,8,1024]{2,1,0:T(8,128)S(1)} %bitcast.7), custom_call_target="tpu_custom_call" | custom-call | tf_op jit(solution)/shard_map/moments_in_window/pallas_call | solution.py:229
  61.7 21.4 %all-gather.4.cloned.1.call-done = f32[352,2,16,128]{3,2,1,0:T(8,128)} async-done(((f32[11,2,16,128]{3,2,1,0:T(8,128)}), f32[352,2,16,128]{3,2,1,0:T(8,128)}) %all-gather.4.cloned.1.call-update) | async-done | bytes 5767184 | tf_op jit(solution)/shard_map/all_gather | solution.py:228
  83.1 0.0 copy-start
  83.1 2.6 %copy-done = f32[352,2,16,128]{3,2,1,0:T(8,128)S(1)} copy-done((f32[352,2,16,128]{3,2,1,0:T(8,128)S(1)}, f32[352,2,16,128]{3,2,1,0:T(8,128)}, u32[]{:S(2)}) %copy-start) | copy-done | bytes 5767192
  85.7 0.0 copy-start.5
  85.7 0.7 copy-done.5
  86.4 0.0 copy-start.6
  86.4 0.7 copy-done.6
  87.0 0.7 copy-done.7
  87.7 7.7 %steps.1 = f32[1,9,2,16,128]{4,3,2,1,0:T(8,128)} custom-call(f32[32,11,2,16,128]{4,3,2,1,0:T(8,128)S(1)} %bitcast.6, f32[6,10,32,128]{3,2,1,0:T(8,128)S(1)} %moments_in_window.1.window, f32[16]{0:T(128)S(1)} %copy-done.5, f32[16]{0:T(128)S(1)} %copy-done.6, f32[16]{0:T(128)S(1)} %copy-done.7), custom_call_target="tpu_custom_call" | custom-call | tf_op jit(solution)/shard_map/steps/pallas_call | solution.py:238
  (1 shorter events, 0.0 us)
Async XLA Ops:
  6.5 76.5 %all-gather.4.cloned.1.call-start = ((), (), s32[]{:S(2)}) async-start(), calls=%async_computation | async-start | bytes 5947392 | tf_op jit(solution)/shard_map/all_gather | solution.py:228
  7.9 0.9 copy-start.1
  8.8 0.8 copy-start.2
  9.6 0.7 copy-start.3
  10.3 0.7 copy-start.4
  83.1 2.6 %copy-start = (f32[352,2,16,128]{3,2,1,0:T(8,128)S(1)}, f32[352,2,16,128]{3,2,1,0:T(8,128)}, u32[]{:S(2)}) copy-start(f32[352,2,16,128]{3,2,1,0:T(8,128)} %all-gather.4.cloned.1.call-done) | copy-start | bytes 17301508
  85.7 0.7 copy-start.5
  86.4 0.7 copy-start.6
  87.0 0.7 copy-start.7
Sparse Core Ops, SparseCore 0:
  12.1 70.9 all-gather.3

commit v2 on v1

v2 whole, which is shorter than its diff:
```python
import functools

import jax
import jax.numpy as jnp
from jax import lax
from jax.experimental import pallas as pl
from jax.experimental.pallas import tpu as pltpu
from jax.sharding import PartitionSpec as P

STEPS = 4
F32 = jnp.float32
BF16 = jnp.bfloat16
NT = (((1,), (1,)), ((), ()))


def one_hot(index, count):
    rows = lax.broadcasted_iota(jnp.int32, (count, index.shape[-1]), 0)
    return jnp.where(rows == index, F32(1.0), F32(0.0))


def split3(value):
    high = value.astype(BF16).astype(F32)
    rest = value - high
    mid = rest.astype(BF16).astype(F32)
    return high, mid, rest - mid


def copy_all(sem, pairs):
    copies = [pltpu.make_async_copy(a, b, sem.at[i]) for i, (a, b) in enumerate(pairs)]
    for copy in copies:
        copy.start()
    for copy in copies:
        copy.wait()


def in_line(rows):
    return jnp.concatenate([rows[i : i + 1, :] for i in range(rows.shape[0])], axis=1)


def aux_kernel(ids_in, moments_in, owner_in, cells_in, rows_in, aux, ids, moments, owner, cells, rows, sem):
    copy_all(
        sem,
        [(ids_in, ids), (moments_in, moments), (owner_in, owner), (cells_in, cells), (rows_in, rows)],
    )
    cx, cz, cy = ids.shape[1:]
    lines = cx * cz
    aux[0:lines] = (ids[0] + 1).astype(F32).reshape(lines, cy)
    line = in_line(rows[...])
    high = one_hot(line // cy, lines).astype(BF16)
    low = one_hot(line % cy, cy).astype(BF16)
    aux[lines : 2 * lines] = lax.dot_general(high, low, NT, preferred_element_type=F32)
    for i in range(cells.shape[0]):
        at = 2 * lines + 8 * i
        aux[at : at + 6] = moments[:, i * cy : (i + 1) * cy]
        aux[at + 6 : at + 7] = owner[i : i + 1, :].astype(F32)
        aux[at + 7 : at + 8] = cells[i : i + 1, :].astype(F32)


def widen_kernel(cx, sections, *refs):
    fields, left, right = refs[0:3]
    auxes = refs[3 : 3 + sections]
    wide, top, bottom = refs[3 + sections : 6 + sections]
    block, aux, acc, sem = refs[6 + sections :]
    section = lax.axis_index("sec")
    segment = lax.axis_index("segment")
    comps, planes, cz, cy = wide.shape
    lines = cx * cz
    copy_all(
        sem,
        [(fields.at[0], block.at[:, pl.ds(cx, cx)])]
        + [(left.at[0], block.at[:, pl.ds(0, cx)]), (right.at[0], block.at[:, pl.ds(2 * cx, cx)])]
        + [(auxes[i], aux.at[i]) for i in range(sections)],
    )
    wide[0:9] = block[...]
    zeros = jnp.zeros((2, cx, cz, cy), F32)
    before, after = aux[sections - 1, 0 : 2 * lines], aux[1 % sections, 0 : 2 * lines]
    wide[9:11, 0:cx] = jnp.where(section > 0, before.reshape(2, cx, cz, cy), zeros)
    wide[9:11, cx : 2 * cx] = aux[0, 0 : 2 * lines].reshape(2, cx, cz, cy)
    wide[9:11, 2 * cx :] = jnp.where(section < sections - 1, after.reshape(2, cx, cz, cy), zeros)

    @pl.when(segment == 0)
    def _():
        half = planes * cz // 2
        acc[...] = jnp.zeros_like(acc)

        @pl.loop(0, sections)
        def _(source):
            groups = (aux.shape[1] - 2 * lines) // 8
            chunk = [aux[source, pl.ds(2 * lines + 8 * i, 8)] for i in range(groups)]
            entries = jnp.concatenate(chunk, axis=1)
            owner = entries[6:7].astype(jnp.int32)
            cell = entries[7:8].astype(jnp.int32)
            plane = (owner - section + 1) * cx + cell // (cz * cy)
            line = plane * cz + (cell // cy) % cz
            upper = line >= half
            high = one_hot(jnp.where(upper, line - half, line), half)
            low = one_hot(jnp.where(upper, cell % cy + cy, cell % cy), 2 * cy).astype(BF16)
            for part in split3(entries[0:6]):
                spread = [(high * part[c : c + 1]).astype(BF16) for c in range(6)]
                acc[...] += lax.dot_general(
                    jnp.concatenate(spread, axis=0), low, NT, preferred_element_type=F32
                )

        for c in range(6):
            span = slice(c * half, (c + 1) * half)
            for k in range(2):
                at = slice(k * planes // 2, (k + 1) * planes // 2)
                extra = acc[span, k * cy : (k + 1) * cy].reshape(planes // 2, cz, cy)
                wide[3 + c, at] = wide[3 + c, at] + extra

    for x in range(planes):
        top[:, x * STEPS : (x + 1) * STEPS] = wide[:, x, cz - STEPS :]
        bottom[:, x * STEPS : (x + 1) * STEPS] = wide[:, x, 0:STEPS]


def advance(cx, steps, state, coef, times):
    planes, rows, cy = state.shape[2:]
    lane = lax.broadcasted_iota(jnp.int32, (rows, cy), 1)
    first_lane, last_lane = lane == 0, lane == cy - 1

    def back_y(f):
        return f - jnp.where(first_lane, F32(0.0), pltpu.roll(f, 1, 1))

    def back_z(f):
        return f - pltpu.roll(f, 1, 0)

    def fore_y(f):
        return jnp.where(last_lane, F32(0.0), pltpu.roll(f, cy - 1, 1)) - f

    def fore_z(f):
        return pltpu.roll(f, rows - 1, 0) - f

    for step in range(steps):
        left = steps - 1 - step
        low, high = cx - left, 2 * cx + left

        @pl.loop(low, high + 1)
        def _(x):
            inc = [None, None]
            for model in range(2):
                sxx, syy, szz, syz, sxz, sxy = (state[model, 3 + k, x] for k in range(6))
                sxx_p, sxz_p, sxy_p = (state[model, k, x - 1] for k in (3, 7, 8))
                hb = coef[model, 0, x]
                inc[model] = (
                    hb * ((sxx - sxx_p) + back_y(sxy) + back_z(sxz)),
                    hb * ((sxy - sxy_p) + back_y(syy) + back_z(syz)),
                    hb * ((sxz - sxz_p) + back_y(syz) + back_z(szz)),
                )
            for k in range(3):
                state[0, k, x] = state[0, k, x] + inc[0][k]
                state[1, k, x] = (state[1, k, x] + inc[1][k]) + times[x] * inc[0][k]

        @pl.loop(low, high)
        def _(x):
            for model in range(2):
                vx, vy, vz = (state[model, k, x] for k in range(3))
                vx_n, vy_n, vz_n = (state[model, k, x + 1] for k in range(3))
                hl, hm = coef[model, 1, x], coef[model, 2, x]
                exx, eyy, ezz = vx_n - vx, fore_y(vy), fore_z(vz)
                pressure = hl * (exx + eyy + ezz)
                twice = hm + hm
                state[model, 3, x] = state[model, 3, x] + (pressure + twice * exx)
                state[model, 4, x] = state[model, 4, x] + (pressure + twice * eyy)
                state[model, 5, x] = state[model, 5, x] + (pressure + twice * ezz)
                state[model, 6, x] = state[model, 6, x] + hm * (fore_z(vy) + fore_y(vz))
                state[model, 7, x] = state[model, 7, x] + hm * (fore_z(vx) + (vz_n - vz))
                state[model, 8, x] = state[model, 8, x] + hm * (fore_y(vx) + (vy_n - vy))


def first_kernel(
    cx, steps, wide, above, below, r_wide, r_above, r_below, buoyancy, lame_lambda, lame_mu,
    sent, both, coef, times, mid, ends, state, tables, sem,
):
    segment = lax.axis_index("segment")
    planes, cz, cy = mid.shape[2:]
    rows = state.shape[3]
    copy_all(
        sem,
        [(wide, mid.at[0]), (above, ends.at[0, 0]), (below, ends.at[0, 1])]
        + [(r_wide, mid.at[1]), (r_above, ends.at[1, 0]), (r_below, ends.at[1, 1])]
        + [(t, tables.at[i]) for i, t in enumerate((buoyancy, lame_lambda, lame_mu))],
    )

    def join(model, source, first, count):
        for x in range(planes):
            span = slice(x * STEPS, (x + 1) * STEPS)
            to = state.at[model, first : first + count, x]
            at = slice(first, first + count)
            to[:, 0:STEPS] = ends[source, 0, at, span]
            to[:, STEPS : STEPS + cz] = mid[source, at, x]
            to[:, STEPS + cz :] = ends[source, 1, at, span]

    join(segment, 0, 0, 11)

    @pl.when(segment == 1)
    def _():
        join(0, 1, 0, 11)

    @pl.loop(0, planes)
    def _(x):
        for model in range(2):
            ids = state[model, 9, x]
            found = [jnp.zeros((rows, cy), F32)] * 3
            for entry in range(tables.shape[1]):
                hit = ids == F32(entry + 1)
                found = [
                    jnp.where(hit, F32(0.5) * tables[i, entry], found[i]) for i in range(3)
                ]
            for i in range(3):
                coef[model, i, x] = found[i]
        times[x] = state[1, 10, x]

    advance(cx, steps, state, coef, times)
    both[...] = state[:, 0:9, cx : 2 * cx]
    sent[...] = state[segment, 0:9, cx : 2 * cx]


def next_kernel(cx, steps, last, both_in, left, right, r_left, r_right, coef_in, times_in, *refs):
    segment = lax.axis_index("segment")
    sent, both = refs[0:2]
    state, coef, times, sem = refs[-4:]
    near = slice(0, cx), slice(2 * cx, 3 * cx)
    copy_all(
        sem,
        [(both_in, state.at[:, :, pl.ds(cx, cx)]), (coef_in, coef), (times_in, times)]
        + [(left, state.at[segment, :, pl.ds(0, cx)])]
        + [(right, state.at[segment, :, pl.ds(2 * cx, cx)])],
    )

    @pl.when(segment == 1)
    def _():
        copy_all(
            sem,
            [(r_left, state.at[0, :, pl.ds(0, cx)]), (r_right, state.at[0, :, pl.ds(2 * cx, cx)])],
        )

    advance(cx, steps, state, coef, times)
    if last:
        rows = state.shape[3]
        sent[0] = state[segment, :, cx : 2 * cx, STEPS : rows - STEPS]
    else:
        sent[...] = state[segment, :, cx : 2 * cx]
        both[...] = state[:, :, cx : 2 * cx]


VMEM = pl.BlockSpec(memory_space=pltpu.VMEM)
ANY = pl.BlockSpec(memory_space=pl.ANY)
LIMIT = pltpu.CompilerParams(vmem_limit_bytes=40 * 2**20)


def call(kernel, name, operands, outs, scratch, copies):
    return pl.pallas_call(
        kernel,
        out_shape=[jax.ShapeDtypeStruct(shape, F32) for shape in outs],
        in_specs=[ANY] * len(operands),
        out_specs=[VMEM] * len(outs),
        scratch_shapes=scratch + [pltpu.SemaphoreType.DMA((copies,))],
        compiler_params=LIMIT,
        name=name,
    )(*operands)


def on_device(
    fields, block_ids, buoyancy, lame_lambda, lame_mu, moments, moment_owner, moment_cells, drm_rows
):
    sections, slabs = lax.axis_size("sec"), lax.axis_size("depth")
    cx, cz, cy = fields.shape[2:]
    planes, rows = 3 * cx, cz + 2 * STEPS
    around = range(sections)

    def along(block, axis, distance):
        size = lax.axis_size(axis)
        route = [(i, i + distance) for i in range(size) if 0 <= i + distance < size]
        return lax.ppermute(block, axis, route)

    def to_basin(block, axis, distance):
        size = lax.axis_size(axis)
        route = [
            (2 * i, 2 * (i + distance) + 1) for i in range(size) if 0 <= i + distance < size
        ]
        return lax.ppermute(block, (axis, "segment"), route)

    owner = moment_owner.reshape(-1, cy)
    cells = moment_cells.reshape(-1, cy)
    boundary = drm_rows.reshape(-1, cy)
    left, right = along(fields, "sec", 1), along(fields, "sec", -1)
    ids_and_entries = (block_ids, moments, owner, cells, boundary)
    aux_shape = (2 * cx * cz + 8 * cells.shape[0], cy)
    (aux,) = call(
        aux_kernel,
        "ids_counts_entries",
        ids_and_entries,
        [aux_shape],
        [pltpu.VMEM(a.shape, a.dtype) for a in ids_and_entries],
        len(ids_and_entries),
    )
    auxes = [aux] + [
        lax.ppermute(aux, "sec", [((i + k) % sections, i) for i in around]) for k in around[1:]
    ]
    wide, top, bottom = call(
        functools.partial(widen_kernel, cx, sections),
        "widen_and_moments",
        (fields, left, right, *auxes),
        [(11, planes, cz, cy), (11, planes * STEPS, cy), (11, planes * STEPS, cy)],
        [
            pltpu.VMEM((9, planes, cz, cy), F32),
            pltpu.VMEM((sections, *aux_shape), F32),
            pltpu.VMEM((6 * planes * cz // 2, 2 * cy), F32),
        ],
        3 + sections,
    )
    above, below = along(top, "depth", 1), along(bottom, "depth", -1)
    r_wide = lax.ppermute(wide, "segment", [(0, 1)])
    r_above, r_below = to_basin(top, "depth", 1), to_basin(bottom, "depth", -1)
    plan = [cx] * (STEPS // cx) + [STEPS % cx] * (STEPS % cx > 0)
    window = pltpu.VMEM((2, 9, planes, rows, cy), F32)
    block_shape = (9, cx, rows, cy)
    coef_shape, times_shape = (2, 3, planes, rows, cy), (planes, rows, cy)
    sent, both, coef, times = call(
        functools.partial(first_kernel, cx, plan[0]),
        "first_steps",
        (wide, above, below, r_wide, r_above, r_below, buoyancy, lame_lambda, lame_mu),
        [block_shape, (2, *block_shape), coef_shape, times_shape],
        [
            pltpu.VMEM((2, 11, planes, cz, cy), F32),
            pltpu.VMEM((2, 2, 11, planes * STEPS, cy), F32),
            pltpu.VMEM((2, 11, planes, rows, cy), F32),
            pltpu.SMEM((3, buoyancy.shape[0]), F32),
        ],
        9,
    )
    for number, steps in enumerate(plan[1:]):
        last = number == len(plan) - 2
        left, right = along(sent, "sec", 1), along(sent, "sec", -1)
        r_left, r_right = to_basin(sent, "sec", 1), to_basin(sent, "sec", -1)
        outs = [fields.shape] if last else [block_shape, (2, *block_shape)]
        got = call(
            functools.partial(next_kernel, cx, steps, last),
            "next_steps",
            (both, left, right, r_left, r_right, coef, times),
            outs,
            [window, pltpu.VMEM(coef_shape, F32), pltpu.VMEM(times_shape, F32)],
            5,
        )
        sent, both = got[0], got[-1]
    return sent


def solution(mesh):
    in_specs = (
        P("segment", None, "sec", "depth", None),
        P("segment", "sec", "depth", None),
        P(),
        P(),
        P(),
        P(None, ("sec", "depth")),
        P(("sec", "depth"), None),
        P(("sec", "depth")),
        P(("sec", "depth")),
    )
    out_specs = P("segment", None, "sec", "depth", None)
    return jax.shard_map(
        on_device, mesh=mesh, in_specs=in_specs, out_specs=out_specs, check_vma=False
    )
```

time: 103 us -> 56.8 us (0.55)
  the two profiles are of different devices: /device:TPU:13 before, /device:TPU:18 now
where the time goes in v2:
time: 56.8 us; the launch traced here: 56.2 us
  starting transfers between devices  27 us (48%)
  waiting for transfers between devices  15.4 us (27%)
  Pallas kernels  9.87 us (17%)
  local copies, waits for them, and re-layouts  3.78 us (7%)
    ppermute x6, starting transfers between devices, along(): return lax.ppermute(block, axis, route)  17.1 us
    ppermute x6, waiting for transfers between devices, along(): return lax.ppermute(block, axis, route)  11.3 us
    pallas_call x4, Pallas kernels, call(): pl.pallas_call(kernel, out_shape=[jax.ShapeDtypeStruct(shape, F32) for sh...  9.87 us
    ppermute x4, starting transfers between devices, to_basin(): return lax.ppermute(block, (axis, 'segment'), route)  5.33 us
    unnamed x18, local copies, waits for them, and re-layouts  3.78 us
    ppermute x3, waiting for transfers between devices, on_device(): lax.ppermute(aux, 'sec', [((i + k) % sections, i) for i in around])  3.63 us
    ppermute x3, starting transfers between devices, on_device(): lax.ppermute(aux, 'sec', [((i + k) % sections, i) for i in around])  3.17 us
    ppermute x1, starting transfers between devices, on_device(): r_wide = lax.ppermute(wide, 'segment', [(0, 1)])  1.32 us
  transfers between devices with their start and end apart: 14, of which 7 were waited for; matrix products, arithmetic and copies ran while one was open for 0% of the time, Pallas kernels for 1%

profile of v2, /device:TPU:18, one launch (start us, length us, event | category | flops | bytes accessed | tf_op | source)
XLA Modules:
  0.0 56.2 jit_solution(5227313198508255400)
XLA Ops:
  0.0 3.6 %collective-permute-start = (f32[1,9,2,16,128]{4,3,2,1,0:T(8,128)}, f32[1,9,2,16,128]{4,3,2,1,0:T(8,128)S(1)}, u32[]{:S(2)}, u32[]{:S(2)}) collective-permute-start(f32[1,9,2,16,128]{4,3,2,1,0:T(8,128)} %refs_0_.1), channel_id=1, source_target_pairs={{0,8},{8,16},{16,24},{1,9},{9,17},{17,25},{2,10},{10,18},{18,26},{... | collective-permute-start | bytes 442376 | tf_op jit(solution)/shard_map/ppermute | solution.py:274
  3.6 2.4 %collective-permute-start.1 = (f32[1,9,2,16,128]{4,3,2,1,0:T(8,128)}, f32[1,9,2,16,128]{4,3,2,1,0:T(8,128)S(1)}, u32[]{:S(2)}, u32[]{:S(2)}) collective-permute-start(f32[1,9,2,16,128]{4,3,2,1,0:T(8,128)} %refs_0_.1), channel_id=1, source_target_pairs={{8,0},{16,8},{24,16},{9,1},{17,9},{25,17},{10,2},{18,10},{26,18},{... | collective-permute-start | bytes 442376 | tf_op jit(solution)/shard_map/ppermute | solution.py:274
  6.0 0.7 %copy-done.1 = f32[6,1024]{1,0:T(8,128)S(1)} copy-done((f32[6,1024]{1,0:T(8,128)S(1)}, f32[6,1024]{1,0:T(8,128)}, u32[]{:S(2)}) %copy-start.1) | copy-done | bytes 24600
  6.8 0.7 %copy-done.2 = s32[1,2,16,128]{3,2,1,0:T(8,128)S(1)} copy-done((s32[1,2,16,128]{3,2,1,0:T(8,128)S(1)}, s32[1,2,16,128]{3,2,1,0:T(8,128)}, u32[]{:S(2)}) %copy-start.2) | copy-done | bytes 16408
  9.3 1.6 %collective-permute-start.4 = (f32[128,128]{1,0:T(8,128)S(1)}, f32[128,128]{1,0:T(8,128)S(1)}, u32[]{:S(2)}, u32[]{:S(2)}) collective-permute-start(f32[128,128]{1,0:T(8,128)S(1)} %ids_counts_entries.1.refs_3_), channel_id=1, source_target_pairs={{24,0},{0,8},{8,16},{16,24},{25,1},{1,9},{9,17},{17,25},{26,2},{2,... | collective-permute-start | bytes 196616 | tf_op jit(solution)/shard_map/ppermute | solution.py:298
  11.2 1.2 %collective-permute-start.2 = (f32[128,128]{1,0:T(8,128)S(1)}, f32[128,128]{1,0:T(8,128)S(1)}, u32[]{:S(2)}, u32[]{:S(2)}) collective-permute-start(f32[128,128]{1,0:T(8,128)S(1)} %ids_counts_entries.1.refs_3_), channel_id=1, source_target_pairs={{8,0},{16,8},{24,16},{0,24},{9,1},{17,9},{25,17},{1,25},{10,2},{18... | collective-permute-start | bytes 196616 | tf_op jit(solution)/shard_map/ppermute | solution.py:298
  12.5 1.9 %collective-permute-done.4.refs_6_ = f32[128,128]{1,0:T(8,128)S(1)} collective-permute-done((f32[128,128]{1,0:T(8,128)S(1)}, f32[128,128]{1,0:T(8,128)S(1)}, u32[]{:S(2)}, u32[]{:S(2)}) %collective-permute-start.4) | collective-permute-done | bytes 65568 | tf_op jit(solution)/shard_map/ppermute | solution.py:298
  14.4 1.7 %collective-permute-done.3.refs_5_ = f32[128,128]{1,0:T(8,128)S(1)} collective-permute-done((f32[128,128]{1,0:T(8,128)S(1)}, f32[128,128]{1,0:T(8,128)S(1)}, u32[]{:S(2)}, u32[]{:S(2)}) %collective-permute-start.3) | collective-permute-done | bytes 65568 | tf_op jit(solution)/shard_map/ppermute | solution.py:298
  16.1 0.9 %copy-done = f32[1,9,2,16,128]{4,3,2,1,0:T(8,128)S(1)} copy-done((f32[1,9,2,16,128]{4,3,2,1,0:T(8,128)S(1)}, f32[1,9,2,16,128]{4,3,2,1,0:T(8,128)}, u32[]{:S(2)}) %copy-start) | copy-done | bytes 147480
  17.0 3.6 %widen_and_moments.1 = (f32[11,6,16,128]{3,2,1,0:T(8,128)S(1)}, f32[11,24,128]{2,1,0:T(8,128)S(1)}, f32[11,24,128]{2,1,0:T(8,128)S(1)}) custom-call(f32[1,9,2,16,128]{4,3,2,1,0:T(8,128)S(1)} %copy-done, f32[1,9,2,16,128]{4,3,2,1,0:T(8,128)S(1)} %collective-permute-done.refs_1_, f32[1,9,2,16,128]{4,3,2,1,0:T(8,128)S(1)} %collective-permute-done.1.refs_2_, ...), custom_call_target="tpu_custom_call" | custom-call | tf_op jit(solution)/shard_map/widen_and_moments/pallas_call | solution.py:252
  20.6 1.3 %collective-permute-start.7 = (f32[11,6,16,128]{3,2,1,0:T(8,128)S(1)}, f32[11,6,16,128]{3,2,1,0:T(8,128)S(1)}, u32[]{:S(2)}, u32[]{:S(2)}) collective-permute-start(f32[11,6,16,128]{3,2,1,0:T(8,128)S(1)} %get-tuple-element.12.wide), channel_id=1, source_target_pairs={{0,1},{2,3},{4,5},{6,7},{8,9},{10,11},{12,13},{14,15},{16,17},{18,... | collective-permute-start | bytes 1622024 | tf_op jit(solution)/shard_map/ppermute | solution.py:313
  21.9 1.4 %collective-permute-start.8 = (f32[11,24,128]{2,1,0:T(8,128)S(1)}, f32[11,24,128]{2,1,0:T(8,128)S(1)}, u32[]{:S(2)}, u32[]{:S(2)}) collective-permute-start(f32[11,24,128]{2,1,0:T(8,128)S(1)} %get-tuple-element.13), channel_id=1, source_target_pairs={{0,3},{2,5},{4,7},{8,11},{10,13},{12,15},{16,19},{18,21},{20,23},{... | collective-permute-start | bytes 405512 | tf_op jit(solution)/shard_map/ppermute | solution.py:281
  23.4 3.4 %collective-permute-start.5 = (f32[11,24,128]{2,1,0:T(8,128)S(1)}, f32[11,24,128]{2,1,0:T(8,128)S(1)}, u32[]{:S(2)}, u32[]{:S(2)}) collective-permute-start(f32[11,24,128]{2,1,0:T(8,128)S(1)} %get-tuple-element.13), channel_id=1, source_target_pairs={{0,2},{2,4},{4,6},{1,3},{3,5},{5,7},{8,10},{10,12},{12,14},{9,11},... | collective-permute-start | bytes 405512 | tf_op jit(solution)/shard_map/ppermute | solution.py:274
  26.8 1.3 %collective-permute-start.9 = (f32[11,24,128]{2,1,0:T(8,128)S(1)}, f32[11,24,128]{2,1,0:T(8,128)S(1)}, u32[]{:S(2)}, u32[]{:S(2)}) collective-permute-start(f32[11,24,128]{2,1,0:T(8,128)S(1)} %get-tuple-element.14), channel_id=1, source_target_pairs={{2,1},{4,3},{6,5},{10,9},{12,11},{14,13},{18,17},{20,19},{22,21},{... | collective-permute-start | bytes 405512 | tf_op jit(solution)/shard_map/ppermute | solution.py:281
  28.1 1.9 %collective-permute-start.6 = (f32[11,24,128]{2,1,0:T(8,128)S(1)}, f32[11,24,128]{2,1,0:T(8,128)S(1)}, u32[]{:S(2)}, u32[]{:S(2)}) collective-permute-start(f32[11,24,128]{2,1,0:T(8,128)S(1)} %get-tuple-element.14), channel_id=1, source_target_pairs={{2,0},{4,2},{6,4},{3,1},{5,3},{7,5},{10,8},{12,10},{14,12},{11,9},... | collective-permute-start | bytes 405512 | tf_op jit(solution)/shard_map/ppermute | solution.py:274
  30.8 5.2 %collective-permute-done.6.below = f32[11,24,128]{2,1,0:T(8,128)S(1)} collective-permute-done((f32[11,24,128]{2,1,0:T(8,128)S(1)}, f32[11,24,128]{2,1,0:T(8,128)S(1)}, u32[]{:S(2)}, u32[]{:S(2)}) %collective-permute-start.6) | collective-permute-done | bytes 135200 | tf_op jit(solution)/shard_map/ppermute | solution.py:274
  35.9 3.4 %first_steps.1 = (f32[9,2,24,128]{3,2,1,0:T(8,128)S(1)}, f32[2,9,2,24,128]{4,3,2,1,0:T(8,128)S(1)}, f32[2,3,6,24,128]{4,3,2,1,0:T(8,128)S(1)}, f32[6,24,128]{2,1,0:T(8,128)S(1)}) custom-call(f32[11,6,16,128]{3,2,1,0:T(8,128)S(1)} %get-tuple-element.12.wide, f32[11,24,128]{2,1,0:T(8,128)S(1)} %collective-permute-done.5.above, ...), custom_call_target="tpu_custom_call" | custom-call | tf_op jit(solution)/shard_map/first_steps/pallas_call | solution.py:252
  39.3 1.3 %collective-permute-start.13 = (f32[9,2,24,128]{3,2,1,0:T(8,128)S(1)}, f32[9,2,24,128]{3,2,1,0:T(8,128)S(1)}, u32[]{:S(2)}, u32[]{:S(2)}) collective-permute-start(f32[9,2,24,128]{3,2,1,0:T(8,128)S(1)} %get-tuple-element.16), channel_id=1, source_target_pairs={{8,1},{16,9},{24,17},{10,3},{18,11},{26,19},{12,5},{20,13},{28,21}... | collective-permute-start | bytes 663560 | tf_op jit(solution)/shard_map/ppermute | solution.py:281
  40.6 1.3 %collective-permute-start.12 = (f32[9,2,24,128]{3,2,1,0:T(8,128)S(1)}, f32[9,2,24,128]{3,2,1,0:T(8,128)S(1)}, u32[]{:S(2)}, u32[]{:S(2)}) collective-permute-start(f32[9,2,24,128]{3,2,1,0:T(8,128)S(1)} %get-tuple-element.16), channel_id=1, source_target_pairs={{0,9},{8,17},{16,25},{2,11},{10,19},{18,27},{4,13},{12,21},{20,29}... | collective-permute-start | bytes 663560 | tf_op jit(solution)/shard_map/ppermute | solution.py:281
  42.0 3.9 %collective-permute-start.11 = (f32[9,2,24,128]{3,2,1,0:T(8,128)S(1)}, f32[9,2,24,128]{3,2,1,0:T(8,128)S(1)}, u32[]{:S(2)}, u32[]{:S(2)}) collective-permute-start(f32[9,2,24,128]{3,2,1,0:T(8,128)S(1)} %get-tuple-element.16), channel_id=1, source_target_pairs={{8,0},{16,8},{24,16},{9,1},{17,9},{25,17},{10,2},{18,10},{26,18},{... | collective-permute-start | bytes 663560 | tf_op jit(solution)/shard_map/ppermute | solution.py:274
  45.9 1.9 %collective-permute-start.10 = (f32[9,2,24,128]{3,2,1,0:T(8,128)S(1)}, f32[9,2,24,128]{3,2,1,0:T(8,128)S(1)}, u32[]{:S(2)}, u32[]{:S(2)}) collective-permute-start(f32[9,2,24,128]{3,2,1,0:T(8,128)S(1)} %get-tuple-element.16), channel_id=1, source_target_pairs={{0,8},{8,16},{16,24},{1,9},{9,17},{17,25},{2,10},{10,18},{18,26},{... | collective-permute-start | bytes 663560 | tf_op jit(solution)/shard_map/ppermute | solution.py:274
  47.9 3.0 %collective-permute-done.11.right = f32[9,2,24,128]{3,2,1,0:T(8,128)S(1)} collective-permute-done((f32[9,2,24,128]{3,2,1,0:T(8,128)S(1)}, f32[9,2,24,128]{3,2,1,0:T(8,128)S(1)}, u32[]{:S(2)}, u32[]{:S(2)}) %collective-permute-start.11) | collective-permute-done | bytes 221216 | tf_op jit(solution)/shard_map/ppermute | solution.py:274
  50.8 2.9 %collective-permute-done.10.left = f32[9,2,24,128]{3,2,1,0:T(8,128)S(1)} collective-permute-done((f32[9,2,24,128]{3,2,1,0:T(8,128)S(1)}, f32[9,2,24,128]{3,2,1,0:T(8,128)S(1)}, u32[]{:S(2)}, u32[]{:S(2)}) %collective-permute-start.10) | collective-permute-done | bytes 221216 | tf_op jit(solution)/shard_map/ppermute | solution.py:274
  53.7 2.5 %next_steps.1 = f32[1,9,2,16,128]{4,3,2,1,0:T(8,128)} custom-call(f32[2,9,2,24,128]{4,3,2,1,0:T(8,128)S(1)} %get-tuple-element.15.both_in, f32[9,2,24,128]{3,2,1,0:T(8,128)S(1)} %collective-permute-done.10.left, f32[9,2,24,128]{3,2,1,0:T(8,128)S(1)} %collective-permute-done.11.right, f32[9,2,24,128]{3,2,1,0:T(8,128)S(1)} %collective-permute-done.12.r_left, ...), custom_call_target="tpu_custom_call" | custom-call | tf_op jit(solution)/shard_map/next_steps/pallas_call | solution.py:252
  (26 shorter events, 2.9 us)
Async XLA Ops:
  0.0 6.0 %copy-start.4 = (s32[1024,1]{0,1:T(1,128)S(1)}, s32[1024,1]{0,1:T(1,128)}, u32[]{:S(2)}) copy-start(s32[1024,1]{0,1:T(1,128)} %param.15) | copy-start | bytes 12292
  0.0 16.1 %collective-permute-start = (f32[1,9,2,16,128]{4,3,2,1,0:T(8,128)}, f32[1,9,2,16,128]{4,3,2,1,0:T(8,128)S(1)}, u32[]{:S(2)}, u32[]{:S(2)}) collective-permute-start(f32[1,9,2,16,128]{4,3,2,1,0:T(8,128)} %refs_0_.1), channel_id=1, source_target_pairs={{0,8},{8,16},{16,24},{1,9},{9,17},{17,25},{2,10},{10,18},{18,26},{... | collective-permute-start | bytes 442376 | tf_op jit(solution)/shard_map/ppermute | solution.py:274
  3.6 12.5 %collective-permute-start.1 = (f32[1,9,2,16,128]{4,3,2,1,0:T(8,128)}, f32[1,9,2,16,128]{4,3,2,1,0:T(8,128)S(1)}, u32[]{:S(2)}, u32[]{:S(2)}) collective-permute-start(f32[1,9,2,16,128]{4,3,2,1,0:T(8,128)} %refs_0_.1), channel_id=1, source_target_pairs={{8,0},{16,8},{24,16},{9,1},{17,9},{25,17},{10,2},{18,10},{26,18},{... | collective-permute-start | bytes 442376 | tf_op jit(solution)/shard_map/ppermute | solution.py:274
  6.0 0.8 %copy-start.1 = (f32[6,1024]{1,0:T(8,128)S(1)}, f32[6,1024]{1,0:T(8,128)}, u32[]{:S(2)}) copy-start(f32[6,1024]{1,0:T(8,128)} %moments_in.1) | copy-start | bytes 73732
  6.8 0.7 %copy-start.2 = (s32[1,2,16,128]{3,2,1,0:T(8,128)S(1)}, s32[1,2,16,128]{3,2,1,0:T(8,128)}, u32[]{:S(2)}) copy-start(s32[1,2,16,128]{3,2,1,0:T(8,128)} %ids_in.1) | copy-start | bytes 49156
  7.5 0.7 %copy-start.3 = (s32[2048]{0:T(1024)S(1)}, s32[2048]{0:T(1024)}, u32[]{:S(2)}) copy-start(s32[2048]{0:T(1024)} %param.17) | copy-start | bytes 24580
  8.2 0.7 %copy-start.5 = (s32[1024]{0:T(1024)S(1)}, s32[1024]{0:T(1024)}, u32[]{:S(2)}) copy-start(s32[1024]{0:T(1024)} %param.16) | copy-start | bytes 12292
  9.3 5.1 %collective-permute-start.4 = (f32[128,128]{1,0:T(8,128)S(1)}, f32[128,128]{1,0:T(8,128)S(1)}, u32[]{:S(2)}, u32[]{:S(2)}) collective-permute-start(f32[128,128]{1,0:T(8,128)S(1)} %ids_counts_entries.1.refs_3_), channel_id=1, source_target_pairs={{24,0},{0,8},{8,16},{16,24},{25,1},{1,9},{9,17},{17,25},{26,2},{2,... | collective-permute-start | bytes 196616 | tf_op jit(solution)/shard_map/ppermute | solution.py:298
  10.9 5.2 %collective-permute-start.3 = (f32[128,128]{1,0:T(8,128)S(1)}, f32[128,128]{1,0:T(8,128)S(1)}, u32[]{:S(2)}, u32[]{:S(2)}) collective-permute-start(f32[128,128]{1,0:T(8,128)S(1)} %ids_counts_entries.1.refs_3_), channel_id=1, source_target_pairs={{16,0},{24,8},{0,16},{8,24},{17,1},{25,9},{1,17},{9,25},{18,2},{26... | collective-permute-start | bytes 196616 | tf_op jit(solution)/shard_map/ppermute | solution.py:298
  11.2 4.8 %collective-permute-start.2 = (f32[128,128]{1,0:T(8,128)S(1)}, f32[128,128]{1,0:T(8,128)S(1)}, u32[]{:S(2)}, u32[]{:S(2)}) collective-permute-start(f32[128,128]{1,0:T(8,128)S(1)} %ids_counts_entries.1.refs_3_), channel_id=1, source_target_pairs={{8,0},{16,8},{24,16},{0,24},{9,1},{17,9},{25,17},{1,25},{10,2},{18... | collective-permute-start | bytes 196616 | tf_op jit(solution)/shard_map/ppermute | solution.py:298
  16.1 0.9 %copy-start = (f32[1,9,2,16,128]{4,3,2,1,0:T(8,128)S(1)}, f32[1,9,2,16,128]{4,3,2,1,0:T(8,128)}, u32[]{:S(2)}) copy-start(f32[1,9,2,16,128]{4,3,2,1,0:T(8,128)} %refs_0_.1) | copy-start | bytes 442372
  20.6 15.3 %collective-permute-start.7 = (f32[11,6,16,128]{3,2,1,0:T(8,128)S(1)}, f32[11,6,16,128]{3,2,1,0:T(8,128)S(1)}, u32[]{:S(2)}, u32[]{:S(2)}) collective-permute-start(f32[11,6,16,128]{3,2,1,0:T(8,128)S(1)} %get-tuple-element.12.wide), channel_id=1, source_target_pairs={{0,1},{2,3},{4,5},{6,7},{8,9},{10,11},{12,13},{14,15},{16,17},{18,... | collective-permute-start | bytes 1622024 | tf_op jit(solution)/shard_map/ppermute | solution.py:313
  21.9 14.0 %copy-start.6 = (f32[16]{0:T(128)S(1)}, f32[16]{0:T(128)}, u32[]{:S(2)}) copy-start(f32[16]{0:T(128)} %buoyancy.1) | copy-start | bytes 196
  21.9 14.0 %copy-start.7 = (f32[16]{0:T(128)S(1)}, f32[16]{0:T(128)}, u32[]{:S(2)}) copy-start(f32[16]{0:T(128)} %lame_lambda.1) | copy-start | bytes 196
  21.9 14.0 %copy-start.8 = (f32[16]{0:T(128)S(1)}, f32[16]{0:T(128)}, u32[]{:S(2)}) copy-start(f32[16]{0:T(128)} %lame_mu.1) | copy-start | bytes 196
  21.9 8.1 %collective-permute-start.8 = (f32[11,24,128]{2,1,0:T(8,128)S(1)}, f32[11,24,128]{2,1,0:T(8,128)S(1)}, u32[]{:S(2)}, u32[]{:S(2)}) collective-permute-start(f32[11,24,128]{2,1,0:T(8,128)S(1)} %get-tuple-element.13), channel_id=1, source_target_pairs={{0,3},{2,5},{4,7},{8,11},{10,13},{12,15},{16,19},{18,21},{20,23},{... | collective-permute-start | bytes 405512 | tf_op jit(solution)/shard_map/ppermute | solution.py:281
  23.4 6.9 %collective-permute-start.5 = (f32[11,24,128]{2,1,0:T(8,128)S(1)}, f32[11,24,128]{2,1,0:T(8,128)S(1)}, u32[]{:S(2)}, u32[]{:S(2)}) collective-permute-start(f32[11,24,128]{2,1,0:T(8,128)S(1)} %get-tuple-element.13), channel_id=1, source_target_pairs={{0,2},{2,4},{4,6},{1,3},{3,5},{5,7},{8,10},{10,12},{12,14},{9,11},... | collective-permute-start | bytes 405512 | tf_op jit(solution)/shard_map/ppermute | solution.py:274
  26.8 4.0 %collective-permute-start.9 = (f32[11,24,128]{2,1,0:T(8,128)S(1)}, f32[11,24,128]{2,1,0:T(8,128)S(1)}, u32[]{:S(2)}, u32[]{:S(2)}) collective-permute-start(f32[11,24,128]{2,1,0:T(8,128)S(1)} %get-tuple-element.14), channel_id=1, source_target_pairs={{2,1},{4,3},{6,5},{10,9},{12,11},{14,13},{18,17},{20,19},{22,21},{... | collective-permute-start | bytes 405512 | tf_op jit(solution)/shard_map/ppermute | solution.py:281
  28.1 7.8 %collective-permute-start.6 = (f32[11,24,128]{2,1,0:T(8,128)S(1)}, f32[11,24,128]{2,1,0:T(8,128)S(1)}, u32[]{:S(2)}, u32[]{:S(2)}) collective-permute-start(f32[11,24,128]{2,1,0:T(8,128)S(1)} %get-tuple-element.14), channel_id=1, source_target_pairs={{2,0},{4,2},{6,4},{3,1},{5,3},{7,5},{10,8},{12,10},{14,12},{11,9},... | collective-permute-start | bytes 405512 | tf_op jit(solution)/shard_map/ppermute | solution.py:274
  39.3 8.5 %collective-permute-start.13 = (f32[9,2,24,128]{3,2,1,0:T(8,128)S(1)}, f32[9,2,24,128]{3,2,1,0:T(8,128)S(1)}, u32[]{:S(2)}, u32[]{:S(2)}) collective-permute-start(f32[9,2,24,128]{3,2,1,0:T(8,128)S(1)} %get-tuple-element.16), channel_id=1, source_target_pairs={{8,1},{16,9},{24,17},{10,3},{18,11},{26,19},{12,5},{20,13},{28,21}... | collective-permute-start | bytes 663560 | tf_op jit(solution)/shard_map/ppermute | solution.py:281
  40.6 7.2 %collective-permute-start.12 = (f32[9,2,24,128]{3,2,1,0:T(8,128)S(1)}, f32[9,2,24,128]{3,2,1,0:T(8,128)S(1)}, u32[]{:S(2)}, u32[]{:S(2)}) collective-permute-start(f32[9,2,24,128]{3,2,1,0:T(8,128)S(1)} %get-tuple-element.16), channel_id=1, source_target_pairs={{0,9},{8,17},{16,25},{2,11},{10,19},{18,27},{4,13},{12,21},{20,29}... | collective-permute-start | bytes 663560 | tf_op jit(solution)/shard_map/ppermute | solution.py:281
  42.0 8.9 %collective-permute-start.11 = (f32[9,2,24,128]{3,2,1,0:T(8,128)S(1)}, f32[9,2,24,128]{3,2,1,0:T(8,128)S(1)}, u32[]{:S(2)}, u32[]{:S(2)}) collective-permute-start(f32[9,2,24,128]{3,2,1,0:T(8,128)S(1)} %get-tuple-element.16), channel_id=1, source_target_pairs={{8,0},{16,8},{24,16},{9,1},{17,9},{25,17},{10,2},{18,10},{26,18},{... | collective-permute-start | bytes 663560 | tf_op jit(solution)/shard_map/ppermute | solution.py:274
  45.9 7.8 %collective-permute-start.10 = (f32[9,2,24,128]{3,2,1,0:T(8,128)S(1)}, f32[9,2,24,128]{3,2,1,0:T(8,128)S(1)}, u32[]{:S(2)}, u32[]{:S(2)}) collective-permute-start(f32[9,2,24,128]{3,2,1,0:T(8,128)S(1)} %get-tuple-element.16), channel_id=1, source_target_pairs={{0,8},{8,16},{16,24},{1,9},{9,17},{17,25},{2,10},{10,18},{18,26},{... | collective-permute-start | bytes 663560 | tf_op jit(solution)/shard_map/ppermute | solution.py:274

commit v3 on v2

v3 whole, which is shorter than its diff:
```python
import functools

import jax
import jax.numpy as jnp
from jax import lax
from jax.experimental import pallas as pl
from jax.experimental.pallas import tpu as pltpu
from jax.sharding import PartitionSpec as P

STEPS = 4
F32 = jnp.float32
BF16 = jnp.bfloat16
NT = (((1,), (1,)), ((), ()))


def one_hot(index, count):
    rows = lax.broadcasted_iota(jnp.int32, (count, index.shape[-1]), 0)
    return jnp.where(rows == index, F32(1.0), F32(0.0))


def split3(value):
    high = value.astype(BF16).astype(F32)
    rest = value - high
    mid = rest.astype(BF16).astype(F32)
    return high, mid, rest - mid


def copy_all(sem, pairs):
    copies = [pltpu.make_async_copy(a, b, sem.at[i]) for i, (a, b) in enumerate(pairs)]
    for copy in copies:
        copy.start()
    for copy in copies:
        copy.wait()


def in_line(rows):
    return jnp.concatenate([rows[i : i + 1, :] for i in range(rows.shape[0])], axis=1)


def pack_kernel(layout, fields_in, ids_in, moments_in, owner_in, cells_in, rows_in, packed, entries, *scratch):
    cx, cz, cy = layout
    ids, moments, owner, cells, rows, sem = scratch
    lines = cx * cz
    copies = [(ids_in, ids), (moments_in, moments), (owner_in, owner), (cells_in, cells), (rows_in, rows)]
    copies += [
        (fields_in.at[0, k, x], packed.at[pl.ds((k * cx + x) * cz, cz)])
        for k in range(9)
        for x in range(cx)
    ]
    copy_all(sem, copies)
    packed[9 * lines : 10 * lines] = (ids[0] + 1).astype(F32).reshape(lines, cy)
    line = in_line(rows[...])
    high = one_hot(line // cy, lines).astype(BF16)
    low = one_hot(line % cy, cy).astype(BF16)
    packed[10 * lines : 11 * lines] = lax.dot_general(high, low, NT, preferred_element_type=F32)
    for i in range(cells.shape[0]):
        at = 8 * i
        entries[at : at + 6] = moments[:, i * cy : (i + 1) * cy]
        entries[at + 6 : at + 7] = owner[i : i + 1, :].astype(F32)
        entries[at + 7 : at + 8] = cells[i : i + 1, :].astype(F32)
    packed[11 * lines :] = entries[...]


def widen_kernel(layout, *refs):
    cx, cz, cy = layout
    packs, others = refs[0:3], refs[3:-6]
    kept, swapped, near, far, wide, acc = refs[-6:]
    section = lax.axis_index("sec")
    segment = lax.axis_index("segment")
    planes = 3 * cx
    lines = cx * cz
    for i, pack in enumerate(packs):
        wide[:, i * cx : (i + 1) * cx] = pack[0 : 11 * lines].reshape(11, cx, cz, cy)

    @pl.when(segment == 0)
    def _():
        half = planes * cz // 2
        acc[...] = jnp.zeros_like(acc)
        for entries in [pack.at[pl.ds(11 * lines, pack.shape[0] - 11 * lines)] for pack in packs] + list(others):
            groups = entries.shape[0] // 8
            chunk = [entries[8 * i : 8 * i + 8] for i in range(groups)]
            entry = jnp.concatenate(chunk, axis=1)
            owner = entry[6:7].astype(jnp.int32)
            cell = entry[7:8].astype(jnp.int32)
            plane = (owner - section + 1) * cx + cell // (cz * cy)
            line = plane * cz + (cell // cy) % cz
            upper = line >= half
            high = one_hot(jnp.where(upper, line - half, line), half)
            low = one_hot(jnp.where(upper, cell % cy + cy, cell % cy), 2 * cy).astype(BF16)
            for part in split3(entry[0:6]):
                spread = [(high * part[c : c + 1]).astype(BF16) for c in range(6)]
                acc[...] += lax.dot_general(
                    jnp.concatenate(spread, axis=0), low, NT, preferred_element_type=F32
                )

        for c in range(6):
            span = slice(c * half, (c + 1) * half)
            for k in range(2):
                at = slice(k * planes // 2, (k + 1) * planes // 2)
                extra = acc[span, k * cy : (k + 1) * cy].reshape(planes // 2, cz, cy)
                wide[3 + c, at] = wide[3 + c, at] + extra

    def cut(to, first, count):
        for x in range(planes):
            to[:, x * count : (x + 1) * count] = wide[:, x, first : first + count]

    reach = cz // 2 + STEPS

    @pl.when(segment == 0)
    def _():
        cut(kept, 0, reach)
        cut(swapped, cz - reach, reach)
        cut(near, cz - STEPS, STEPS)
        cut(far, 0, STEPS)

    @pl.when(segment == 1)
    def _():
        cut(kept, cz - reach, reach)
        cut(swapped, 0, reach)
        cut(near, 0, STEPS)
        cut(far, cz - STEPS, STEPS)


def advance(cx, steps, state, coef, times):
    planes, rows, cy = state.shape[2:]
    lane = lax.broadcasted_iota(jnp.int32, (rows, cy), 1)
    first_lane, last_lane = lane == 0, lane == cy - 1

    def back_y(f):
        return f - jnp.where(first_lane, F32(0.0), pltpu.roll(f, 1, 1))

    def back_z(f):
        return f - pltpu.roll(f, 1, 0)

    def fore_y(f):
        return jnp.where(last_lane, F32(0.0), pltpu.roll(f, cy - 1, 1)) - f

    def fore_z(f):
        return pltpu.roll(f, rows - 1, 0) - f

    for step in range(steps):
        left = steps - 1 - step
        low, high = cx - left, 2 * cx + left

        @pl.loop(low, high + 1)
        def _(x):
            inc = [None, None]
            for model in range(2):
                sxx, syy, szz, syz, sxz, sxy = (state[model, 3 + k, x] for k in range(6))
                sxx_p, sxz_p, sxy_p = (state[model, k, x - 1] for k in (3, 7, 8))
                hb = coef[model, 0, x]
                inc[model] = (
                    hb * ((sxx - sxx_p) + back_y(sxy) + back_z(sxz)),
                    hb * ((sxy - sxy_p) + back_y(syy) + back_z(syz)),
                    hb * ((sxz - sxz_p) + back_y(syz) + back_z(szz)),
                )
            for k in range(3):
                state[0, k, x] = state[0, k, x] + inc[0][k]
                state[1, k, x] = (state[1, k, x] + inc[1][k]) + times[x] * inc[0][k]

        @pl.loop(low, high)
        def _(x):
            for model in range(2):
                vx, vy, vz = (state[model, k, x] for k in range(3))
                vx_n, vy_n, vz_n = (state[model, k, x + 1] for k in range(3))
                hl, hm = coef[model, 1, x], coef[model, 2, x]
                exx, eyy, ezz = vx_n - vx, fore_y(vy), fore_z(vz)
                pressure = hl * (exx + eyy + ezz)
                twice = hm + hm
                state[model, 3, x] = state[model, 3, x] + (pressure + twice * exx)
                state[model, 4, x] = state[model, 4, x] + (pressure + twice * eyy)
                state[model, 5, x] = state[model, 5, x] + (pressure + twice * ezz)
                state[model, 6, x] = state[model, 6, x] + hm * (fore_z(vy) + fore_y(vz))
                state[model, 7, x] = state[model, 7, x] + hm * (fore_z(vx) + (vz_n - vz))
                state[model, 8, x] = state[model, 8, x] + hm * (fore_y(vx) + (vy_n - vy))


def first_kernel(
    cx, steps, kept, swapped, near, far, buoyancy, lame_lambda, lame_mu,
    sent, both, coef, times, state, tables, sem,
):
    segment = lax.axis_index("segment")
    planes, rows, cy = state.shape[2:]
    reach = rows - STEPS
    copy_all(sem, [(t, tables.at[i]) for i, t in enumerate((buoyancy, lame_lambda, lame_mu))])

    def join(model, body, halo, upper):
        for x in range(planes):
            inner, outer = slice(x * reach, (x + 1) * reach), slice(x * STEPS, (x + 1) * STEPS)
            if upper:
                state[model, :, x, 0:STEPS] = halo[:, outer]
                state[model, :, x, STEPS:] = body[:, inner]
            else:
                state[model, :, x, 0:reach] = body[:, inner]
                state[model, :, x, reach:] = halo[:, outer]

    @pl.when(segment == 0)
    def _():
        join(0, kept, near, True)
        join(1, swapped, far, True)

    @pl.when(segment == 1)
    def _():
        join(1, kept, near, False)
        join(0, swapped, far, False)

    @pl.loop(0, planes)
    def _(x):
        for model in range(2):
            ids = state[model, 9, x]
            found = [jnp.zeros((rows, cy), F32)] * 3
            for entry in range(tables.shape[1]):
                hit = ids == F32(entry + 1)
                found = [
                    jnp.where(hit, F32(0.5) * tables[i, entry], found[i]) for i in range(3)
                ]
            for i in range(3):
                coef[model, i, x] = found[i]
        times[x] = state[1, 10, x]

    advance(cx, steps, state, coef, times)
    both[...] = state[:, 0:9, cx : 2 * cx]
    cut_edges(cx, steps, state, sent)


def cut_edges(cx, done, state, sent):
    rows = state.shape[3]
    count = rows - 2 * done
    for x in range(cx):
        sent[:, :, x * count : (x + 1) * count] = state[:, 0:9, cx + x, done : rows - done]


def next_kernel(cx, done, steps, both_in, left, right, coef, times, *refs):
    segment = lax.axis_index("segment")
    first, second, state = refs
    rows = state.shape[3]
    count = rows - 2 * done
    state[:, :, cx : 2 * cx] = both_in[...]
    for x in range(cx):
        span = slice(x * count, (x + 1) * count)
        state[:, :, x, done : rows - done] = left[:, :, span]
        state[:, :, 2 * cx + x, done : rows - done] = right[:, :, span]
    advance(cx, steps, state, coef, times)
    if done + steps == STEPS:
        first[...] = state[segment, :, cx : 2 * cx, STEPS : rows - STEPS]
        second[...] = state[1 - segment, :, cx : 2 * cx, STEPS : rows - STEPS]
    else:
        first[...] = state[:, :, cx : 2 * cx]
        cut_edges(cx, done + steps, state, second)


def home_kernel(mine, brought, out):
    half = mine.shape[2]
    segment = lax.axis_index("segment")

    @pl.when(segment == 0)
    def _():
        out[0, :, :, 0:half] = mine[...]
        out[0, :, :, half:] = brought[...]

    @pl.when(segment == 1)
    def _():
        out[0, :, :, half:] = mine[...]
        out[0, :, :, 0:half] = brought[...]


VMEM = pl.BlockSpec(memory_space=pltpu.VMEM)
HBM = pl.BlockSpec(memory_space=pltpu.HBM)
LIMIT = pltpu.CompilerParams(vmem_limit_bytes=40 * 2**20)


def call(kernel, name, in_hbm, in_vmem, outs, scratch, copies=0):
    sems = [pltpu.SemaphoreType.DMA((copies,))] * (copies > 0)
    return pl.pallas_call(
        kernel,
        out_shape=[jax.ShapeDtypeStruct(shape, F32) for shape in outs],
        in_specs=[VMEM] * len(in_vmem) + [HBM] * len(in_hbm),
        out_specs=[VMEM] * len(outs),
        scratch_shapes=scratch + sems,
        compiler_params=LIMIT,
        name=name,
    )(*in_vmem, *in_hbm)


def on_device(
    fields, block_ids, buoyancy, lame_lambda, lame_mu, moments, moment_owner, moment_cells, drm_rows
):
    sections, slabs = lax.axis_size("sec"), lax.axis_size("depth")
    layout = cx, cz, cy = fields.shape[2:]
    planes = 3 * cx
    reach, rows = cz // 2 + STEPS, cz // 2 + 2 * STEPS
    plan = [cx] * (STEPS // cx) + [STEPS % cx] * (STEPS % cx > 0)

    def along_x(block, distance):
        route = [(i, i + distance) for i in range(sections) if 0 <= i + distance < sections]
        return lax.ppermute(block, "sec", route)

    def halo(block, core_zero_goes, flip):
        route = []
        for i in range(slabs):
            for core in range(2):
                to = i + (core_zero_goes if core == 0 else -core_zero_goes)
                if 0 <= to < slabs:
                    route.append((2 * i + core, 2 * to + (1 - core if flip else core)))
        return lax.ppermute(block, ("depth", "segment"), route)

    def swap(block):
        return lax.ppermute(block, "segment", [(0, 1), (1, 0)])

    owner = moment_owner.reshape(-1, cy)
    cells = moment_cells.reshape(-1, cy)
    boundary = drm_rows.reshape(-1, cy)
    small = (block_ids, moments, owner, cells, boundary)
    lines = cx * cz
    entry_lines = 8 * cells.shape[0]
    packed, entries = call(
        functools.partial(pack_kernel, layout),
        "pack",
        (fields, *small),
        (),
        [(11 * lines + entry_lines, cy), (entry_lines, cy)],
        [pltpu.VMEM(a.shape, a.dtype) for a in small],
        len(small) + 9 * cx,
    )
    routes = [
        [((i + k) % sections, i) for i in range(sections)] for k in range(2, sections - 1)
    ] + [[(0, sections - 1), (sections - 1, 0)]] * (sections > 2)
    others = [lax.ppermute(entries, "sec", route) for route in routes]
    left, right = along_x(packed, 1), along_x(packed, -1)
    kept, swapped, near, far = call(
        functools.partial(widen_kernel, layout),
        "widen_and_moments",
        (),
        (left, packed, right, *others),
        [(11, planes * reach, cy)] * 2 + [(11, planes * STEPS, cy)] * 2,
        [pltpu.VMEM((11, planes, cz, cy), F32), pltpu.VMEM((6 * planes * cz // 2, 2 * cy), F32)],
    )
    near, far, swapped = halo(near, 1, False), halo(far, -1, True), swap(swapped)
    both_shape = (2, 9, cx, rows, cy)
    coef_shape, times_shape = (2, 3, planes, rows, cy), (planes, rows, cy)

    def edge_shape(done):
        return (2, 9, cx * (rows - 2 * done), cy)

    done = plan[0]
    sent, both, coef, times = call(
        functools.partial(first_kernel, cx, plan[0]),
        "first_steps",
        (buoyancy, lame_lambda, lame_mu),
        (kept, swapped, near, far),
        [edge_shape(done), both_shape, coef_shape, times_shape],
        [
            pltpu.VMEM((2, 11, planes, rows, cy), F32),
            pltpu.SMEM((3, buoyancy.shape[0]), F32),
        ],
        3,
    )
    for steps in plan[1:]:
        left, right = along_x(sent, 1), along_x(sent, -1)
        after = done + steps
        half_block = (9, cx, cz // 2, cy)
        both, sent = call(
            functools.partial(next_kernel, cx, done, steps),
            "next_steps",
            (),
            (both, left, right, coef, times),
            [half_block] * 2 if after == STEPS else [both_shape, edge_shape(after)],
            [pltpu.VMEM((2, 9, planes, rows, cy), F32)],
        )
        done = after
    (out,) = call(home_kernel, "home", (), (both, swap(sent)), [fields.shape], [])
    return out


def solution(mesh):
    in_specs = (
        P("segment", None, "sec", "depth", None),
        P("segment", "sec", "depth", None),
        P(),
        P(),
        P(),
        P(None, ("sec", "depth")),
        P(("sec", "depth"), None),
        P(("sec", "depth")),
        P(("sec", "depth")),
    )
    out_specs = P("segment", None, "sec", "depth", None)
    return jax.shard_map(
        on_device, mesh=mesh, in_specs=in_specs, out_specs=out_specs, check_vma=False
    )
```

time: 56.8 us -> 51 us (0.90)
  the two profiles are of different devices: /device:TPU:18 before, /device:TPU:13 now
where the time goes in v3:
time: 51 us; the launch traced here: 50 us
  starting transfers between devices  27.9 us (55%)
  waiting for transfers between devices  12.3 us (24%)
  Pallas kernels  5.25 us (10%)
  local copies, waits for them, and re-layouts  4.47 us (9%)
    ppermute x4, starting transfers between devices, along_x(): return lax.ppermute(block, 'sec', route)  10.6 us
    ppermute x2, starting transfers between devices, swap(): return lax.ppermute(block, 'segment', [(0, 1), (1, 0)])  7.93 us
    pallas_call x5, Pallas kernels, call(): pl.pallas_call(kernel, out_shape=[jax.ShapeDtypeStruct(shape, F32) for sh...  5.25 us
    ppermute x4, waiting for transfers between devices, along_x(): return lax.ppermute(block, 'sec', route)  5.1 us
    ppermute x2, starting transfers between devices, halo(): return lax.ppermute(block, ('depth', 'segment'), route)  5.1 us
    ppermute x2, waiting for transfers between devices, halo(): return lax.ppermute(block, ('depth', 'segment'), route)  4.7 us
    unnamed x18, local copies, waits for them, and re-layouts  4.47 us
    ppermute x2, starting transfers between devices, on_device(): others = [lax.ppermute(entries, 'sec', route) for route in routes]  4.23 us
  transfers between devices with their start and end apart: 10, of which 6 were waited for; matrix products, arithmetic and copies ran while one was open for 0% of the time, Pallas kernels for 0%

profile of v3, /device:TPU:13, one launch (start us, length us, event | category | flops | bytes accessed | tf_op | source)
XLA Modules:
  0.0 50.0 jit_solution(5961102532909159657)
XLA Ops:
  0.0 0.7 %copy-done.4 = s32[1024,1]{0,1:T(1,128)S(1)} copy-done((s32[1024,1]{0,1:T(1,128)S(1)}, s32[1024,1]{0,1:T(1,128)}, u32[]{:S(2)}) %copy-start.4) | copy-done | bytes 4120
  0.7 0.9 %copy-done = f32[1,9,2,16,128]{4,3,2,1,0:T(8,128)S(1)} copy-done((f32[1,9,2,16,128]{4,3,2,1,0:T(8,128)S(1)}, f32[1,9,2,16,128]{4,3,2,1,0:T(8,128)}, u32[]{:S(2)}) %copy-start) | copy-done | bytes 147480
  1.6 0.8 %copy-done.1 = f32[6,1024]{1,0:T(8,128)S(1)} copy-done((f32[6,1024]{1,0:T(8,128)S(1)}, f32[6,1024]{1,0:T(8,128)}, u32[]{:S(2)}) %copy-start.1) | copy-done | bytes 24600
  2.4 0.7 %copy-done.2 = s32[1,2,16,128]{3,2,1,0:T(8,128)S(1)} copy-done((s32[1,2,16,128]{3,2,1,0:T(8,128)S(1)}, s32[1,2,16,128]{3,2,1,0:T(8,128)}, u32[]{:S(2)}) %copy-start.2) | copy-done | bytes 16408
  3.1 0.7 %copy-done.3 = s32[2048]{0:T(1024)S(1)} copy-done((s32[2048]{0:T(1024)S(1)}, s32[2048]{0:T(1024)}, u32[]{:S(2)}) %copy-start.3) | copy-done | bytes 8216
  3.8 0.7 %copy-done.5 = s32[1024]{0:T(1024)S(1)} copy-done((s32[1024]{0:T(1024)S(1)}, s32[1024]{0:T(1024)}, u32[]{:S(2)}) %copy-start.5) | copy-done | bytes 4120
  4.5 0.8 %pack.1 = (f32[416,128]{1,0:T(8,128)S(1)}, f32[64,128]{1,0:T(8,128)S(1)}) custom-call(f32[1,9,2,16,128]{4,3,2,1,0:T(8,128)S(1)} %copy-done, s32[1,2,16,128]{3,2,1,0:T(8,128)S(1)} %copy-done.2, f32[6,1024]{1,0:T(8,128)S(1)} %copy-done.1, s32[8,128]{1,0:T(8,128)S(1)} %bitcast.4, s32[8,128]{1,0:T(8,128)S(1)} %bitcast.5, s32[16,128]{1,0:T(8,128)S(1)} %bitcast.3), custom_call_target="tpu_custom_call" | custom-call | tf_op jit(solution)/shard_map/pack/pallas_call | solution.py:274
  5.3 2.1 %collective-permute-start.1 = (f32[416,128]{1,0:T(8,128)S(1)}, f32[416,128]{1,0:T(8,128)S(1)}, u32[]{:S(2)}, u32[]{:S(2)}) collective-permute-start(f32[416,128]{1,0:T(8,128)S(1)} %get-tuple-element.17.refs_1_), channel_id=1, source_target_pairs={{8,0},{16,8},{24,16},{9,1},{17,9},{25,17},{10,2},{18,10},{26,18},{... | collective-permute-start | bytes 638984 | tf_op jit(solution)/shard_map/ppermute | solution.py:296
  7.4 3.2 %collective-permute-start = (f32[416,128]{1,0:T(8,128)S(1)}, f32[416,128]{1,0:T(8,128)S(1)}, u32[]{:S(2)}, u32[]{:S(2)}) collective-permute-start(f32[416,128]{1,0:T(8,128)S(1)} %get-tuple-element.17.refs_1_), channel_id=1, source_target_pairs={{0,8},{8,16},{16,24},{1,9},{9,17},{17,25},{2,10},{10,18},{18,26},{... | collective-permute-start | bytes 638984 | tf_op jit(solution)/shard_map/ppermute | solution.py:296
  11.2 3.6 %collective-permute-start.2 = (f32[64,128]{1,0:T(8,128)S(1)}, f32[64,128]{1,0:T(8,128)S(1)}, u32[]{:S(2)}, u32[]{:S(2)}) collective-permute-start(f32[64,128]{1,0:T(8,128)S(1)} %get-tuple-element.18), channel_id=1, source_target_pairs={{16,0},{24,8},{0,16},{8,24},{17,1},{25,9},{1,17},{9,25},{18,2},{26... | collective-permute-start | bytes 98312 | tf_op jit(solution)/shard_map/ppermute | solution.py:328
  14.8 1.6 %collective-permute-done.2.refs_3_ = f32[64,128]{1,0:T(8,128)S(1)} collective-permute-done((f32[64,128]{1,0:T(8,128)S(1)}, f32[64,128]{1,0:T(8,128)S(1)}, u32[]{:S(2)}, u32[]{:S(2)}) %collective-permute-start.2) | collective-permute-done | bytes 32800 | tf_op jit(solution)/shard_map/ppermute | solution.py:328
  16.5 5.2 %collective-permute-start.4 = (f32[11,72,128]{2,1,0:T(8,128)S(1)}, f32[11,72,128]{2,1,0:T(8,128)S(1)}, u32[]{:S(2)}, u32[]{:S(2)}) collective-permute-start(f32[11,72,128]{2,1,0:T(8,128)S(1)} %get-tuple-element.20), channel_id=1, source_target_pairs={{0,1},{1,0},{2,3},{3,2},{4,5},{5,4},{6,7},{7,6},{8,9},{9,8},{10,11... | collective-permute-start | bytes 1216520 | tf_op jit(solution)/shard_map/ppermute | solution.py:308
  21.7 3.1 %collective-permute-start.5 = (f32[11,24,128]{2,1,0:T(8,128)S(1)}, f32[11,24,128]{2,1,0:T(8,128)S(1)}, u32[]{:S(2)}, u32[]{:S(2)}) collective-permute-start(f32[11,24,128]{2,1,0:T(8,128)S(1)} %get-tuple-element.21), channel_id=1, source_target_pairs={{0,2},{2,4},{3,1},{4,6},{5,3},{7,5},{8,10},{10,12},{11,9},{12,14},... | collective-permute-start | bytes 405512 | tf_op jit(solution)/shard_map/ppermute | solution.py:305
  24.8 2.1 %collective-permute-start.6 = (f32[11,24,128]{2,1,0:T(8,128)S(1)}, f32[11,24,128]{2,1,0:T(8,128)S(1)}, u32[]{:S(2)}, u32[]{:S(2)}) collective-permute-start(f32[11,24,128]{2,1,0:T(8,128)S(1)} %get-tuple-element.22), channel_id=1, source_target_pairs={{1,2},{2,1},{3,4},{4,3},{5,6},{6,5},{9,10},{10,9},{11,12},{12,11},... | collective-permute-start | bytes 405512 | tf_op jit(solution)/shard_map/ppermute | solution.py:305
  26.9 0.9 %collective-permute-done.5.near = f32[11,24,128]{2,1,0:T(8,128)S(1)} collective-permute-done((f32[11,24,128]{2,1,0:T(8,128)S(1)}, f32[11,24,128]{2,1,0:T(8,128)S(1)}, u32[]{:S(2)}, u32[]{:S(2)}) %collective-permute-start.5) | collective-permute-done | bytes 135200 | tf_op jit(solution)/shard_map/ppermute | solution.py:305
  27.7 3.8 %collective-permute-done.6.far = f32[11,24,128]{2,1,0:T(8,128)S(1)} collective-permute-done((f32[11,24,128]{2,1,0:T(8,128)S(1)}, f32[11,24,128]{2,1,0:T(8,128)S(1)}, u32[]{:S(2)}, u32[]{:S(2)}) %collective-permute-start.6) | collective-permute-done | bytes 135200 | tf_op jit(solution)/shard_map/ppermute | solution.py:305
  31.6 2.3 %first_steps.1 = (f32[2,9,24,128]{3,2,1,0:T(8,128)S(1)}, f32[2,9,2,16,128]{4,3,2,1,0:T(8,128)S(1)}, f32[2,3,6,16,128]{4,3,2,1,0:T(8,128)S(1)}, f32[6,16,128]{2,1,0:T(8,128)S(1)}) custom-call(f32[11,72,128]{2,1,0:T(8,128)S(1)} %get-tuple-element.19.kept, f32[11,72,128]{2,1,0:T(8,128)S(1)} %collective-permute-done.4.swapped, ...), custom_call_target="tpu_custom_call" | custom-call | tf_op jit(solution)/shard_map/first_steps/pallas_call | solution.py:274
  33.9 3.4 %collective-permute-start.8 = (f32[2,9,24,128]{3,2,1,0:T(8,128)S(1)}, f32[2,9,24,128]{3,2,1,0:T(8,128)S(1)}, u32[]{:S(2)}, u32[]{:S(2)}) collective-permute-start(f32[2,9,24,128]{3,2,1,0:T(8,128)S(1)} %get-tuple-element.24), channel_id=1, source_target_pairs={{8,0},{16,8},{24,16},{9,1},{17,9},{25,17},{10,2},{18,10},{26,18},{... | collective-permute-start | bytes 663560 | tf_op jit(solution)/shard_map/ppermute | solution.py:296
  37.4 1.9 %collective-permute-start.7 = (f32[2,9,24,128]{3,2,1,0:T(8,128)S(1)}, f32[2,9,24,128]{3,2,1,0:T(8,128)S(1)}, u32[]{:S(2)}, u32[]{:S(2)}) collective-permute-start(f32[2,9,24,128]{3,2,1,0:T(8,128)S(1)} %get-tuple-element.24), channel_id=1, source_target_pairs={{0,8},{8,16},{16,24},{1,9},{9,17},{17,25},{2,10},{10,18},{18,26},{... | collective-permute-start | bytes 663560 | tf_op jit(solution)/shard_map/ppermute | solution.py:296
  39.3 1.9 %collective-permute-done.8.right = f32[2,9,24,128]{3,2,1,0:T(8,128)S(1)} collective-permute-done((f32[2,9,24,128]{3,2,1,0:T(8,128)S(1)}, f32[2,9,24,128]{3,2,1,0:T(8,128)S(1)}, u32[]{:S(2)}, u32[]{:S(2)}) %collective-permute-start.8) | collective-permute-done | bytes 221216 | tf_op jit(solution)/shard_map/ppermute | solution.py:296
  41.2 3.2 %collective-permute-done.7.left = f32[2,9,24,128]{3,2,1,0:T(8,128)S(1)} collective-permute-done((f32[2,9,24,128]{3,2,1,0:T(8,128)S(1)}, f32[2,9,24,128]{3,2,1,0:T(8,128)S(1)}, u32[]{:S(2)}, u32[]{:S(2)}) %collective-permute-start.7) | collective-permute-done | bytes 221216 | tf_op jit(solution)/shard_map/ppermute | solution.py:296
  44.4 1.3 %next_steps.1 = (f32[9,2,8,128]{3,2,1,0:T(8,128)S(1)}, f32[9,2,8,128]{3,2,1,0:T(8,128)S(1)}) custom-call(f32[2,9,2,16,128]{4,3,2,1,0:T(8,128)S(1)} %get-tuple-element.23.both_in, f32[2,9,24,128]{3,2,1,0:T(8,128)S(1)} %collective-permute-done.7.left, f32[2,9,24,128]{3,2,1,0:T(8,128)S(1)} %collective-permute-done.8.right, ...), custom_call_target="tpu_custom_call" | custom-call | tf_op jit(solution)/shard_map/next_steps/pallas_call | solution.py:274
  45.7 2.8 %collective-permute-start.9 = (f32[9,2,8,128]{3,2,1,0:T(8,128)S(1)}, f32[9,2,8,128]{3,2,1,0:T(8,128)S(1)}, u32[]{:S(2)}, u32[]{:S(2)}) collective-permute-start(f32[9,2,8,128]{3,2,1,0:T(8,128)S(1)} %get-tuple-element.28), channel_id=1, source_target_pairs={{0,1},{1,0},{2,3},{3,2},{4,5},{5,4},{6,7},{7,6},{8,9},{9,8},{10,11... | collective-permute-start | bytes 221192 | tf_op jit(solution)/shard_map/ppermute | solution.py:308
  48.5 0.9 %collective-permute-done.9.brought = f32[9,2,8,128]{3,2,1,0:T(8,128)S(1)} collective-permute-done((f32[9,2,8,128]{3,2,1,0:T(8,128)S(1)}, f32[9,2,8,128]{3,2,1,0:T(8,128)S(1)}, u32[]{:S(2)}, u32[]{:S(2)}) %collective-permute-start.9) | collective-permute-done | bytes 73760 | tf_op jit(solution)/shard_map/ppermute | solution.py:308
  (19 shorter events, 1.5 us)
Async XLA Ops:
  0.0 0.7 %copy-start.4 = (s32[1024,1]{0,1:T(1,128)S(1)}, s32[1024,1]{0,1:T(1,128)}, u32[]{:S(2)}) copy-start(s32[1024,1]{0,1:T(1,128)} %param.15) | copy-start | bytes 12292
  0.7 0.9 %copy-start = (f32[1,9,2,16,128]{4,3,2,1,0:T(8,128)S(1)}, f32[1,9,2,16,128]{4,3,2,1,0:T(8,128)}, u32[]{:S(2)}) copy-start(f32[1,9,2,16,128]{4,3,2,1,0:T(8,128)} %fields_in.1) | copy-start | bytes 442372
  1.6 0.8 %copy-start.1 = (f32[6,1024]{1,0:T(8,128)S(1)}, f32[6,1024]{1,0:T(8,128)}, u32[]{:S(2)}) copy-start(f32[6,1024]{1,0:T(8,128)} %moments_in.1) | copy-start | bytes 73732
  2.4 0.7 %copy-start.2 = (s32[1,2,16,128]{3,2,1,0:T(8,128)S(1)}, s32[1,2,16,128]{3,2,1,0:T(8,128)}, u32[]{:S(2)}) copy-start(s32[1,2,16,128]{3,2,1,0:T(8,128)} %ids_in.1) | copy-start | bytes 49156
  3.1 0.7 %copy-start.3 = (s32[2048]{0:T(1024)S(1)}, s32[2048]{0:T(1024)}, u32[]{:S(2)}) copy-start(s32[2048]{0:T(1024)} %param.17) | copy-start | bytes 24580
  3.8 0.7 %copy-start.5 = (s32[1024]{0:T(1024)S(1)}, s32[1024]{0:T(1024)}, u32[]{:S(2)}) copy-start(s32[1024]{0:T(1024)} %param.16) | copy-start | bytes 12292
  5.3 11.1 %collective-permute-start.1 = (f32[416,128]{1,0:T(8,128)S(1)}, f32[416,128]{1,0:T(8,128)S(1)}, u32[]{:S(2)}, u32[]{:S(2)}) collective-permute-start(f32[416,128]{1,0:T(8,128)S(1)} %get-tuple-element.17.refs_1_), channel_id=1, source_target_pairs={{8,0},{16,8},{24,16},{9,1},{17,9},{25,17},{10,2},{18,10},{26,18},{... | collective-permute-start | bytes 638984 | tf_op jit(solution)/shard_map/ppermute | solution.py:296
  7.4 9.0 %collective-permute-start = (f32[416,128]{1,0:T(8,128)S(1)}, f32[416,128]{1,0:T(8,128)S(1)}, u32[]{:S(2)}, u32[]{:S(2)}) collective-permute-start(f32[416,128]{1,0:T(8,128)S(1)} %get-tuple-element.17.refs_1_), channel_id=1, source_target_pairs={{0,8},{8,16},{16,24},{1,9},{9,17},{17,25},{2,10},{10,18},{18,26},{... | collective-permute-start | bytes 638984 | tf_op jit(solution)/shard_map/ppermute | solution.py:296
  10.6 4.2 %collective-permute-start.3 = (f32[64,128]{1,0:T(8,128)S(1)}, f32[64,128]{1,0:T(8,128)S(1)}, u32[]{:S(2)}, u32[]{:S(2)}) collective-permute-start(f32[64,128]{1,0:T(8,128)S(1)} %get-tuple-element.18), channel_id=1, source_target_pairs={{0,24},{24,0},{1,25},{25,1},{2,26},{26,2},{3,27},{27,3},{4,28},{28... | collective-permute-start | bytes 98312 | tf_op jit(solution)/shard_map/ppermute | solution.py:328
  11.2 5.1 %collective-permute-start.2 = (f32[64,128]{1,0:T(8,128)S(1)}, f32[64,128]{1,0:T(8,128)S(1)}, u32[]{:S(2)}, u32[]{:S(2)}) collective-permute-start(f32[64,128]{1,0:T(8,128)S(1)} %get-tuple-element.18), channel_id=1, source_target_pairs={{16,0},{24,8},{0,16},{8,24},{17,1},{25,9},{1,17},{9,25},{18,2},{26... | collective-permute-start | bytes 98312 | tf_op jit(solution)/shard_map/ppermute | solution.py:328
  16.5 15.0 %collective-permute-start.4 = (f32[11,72,128]{2,1,0:T(8,128)S(1)}, f32[11,72,128]{2,1,0:T(8,128)S(1)}, u32[]{:S(2)}, u32[]{:S(2)}) collective-permute-start(f32[11,72,128]{2,1,0:T(8,128)S(1)} %get-tuple-element.20), channel_id=1, source_target_pairs={{0,1},{1,0},{2,3},{3,2},{4,5},{5,4},{6,7},{7,6},{8,9},{9,8},{10,11... | collective-permute-start | bytes 1216520 | tf_op jit(solution)/shard_map/ppermute | solution.py:308
  21.7 6.0 %collective-permute-start.5 = (f32[11,24,128]{2,1,0:T(8,128)S(1)}, f32[11,24,128]{2,1,0:T(8,128)S(1)}, u32[]{:S(2)}, u32[]{:S(2)}) collective-permute-start(f32[11,24,128]{2,1,0:T(8,128)S(1)} %get-tuple-element.21), channel_id=1, source_target_pairs={{0,2},{2,4},{3,1},{4,6},{5,3},{7,5},{8,10},{10,12},{11,9},{12,14},... | collective-permute-start | bytes 405512 | tf_op jit(solution)/shard_map/ppermute | solution.py:305
  24.8 6.8 %copy-start.6 = (f32[16]{0:T(128)S(1)}, f32[16]{0:T(128)}, u32[]{:S(2)}) copy-start(f32[16]{0:T(128)} %buoyancy.1) | copy-start | bytes 196
  24.8 6.8 %copy-start.7 = (f32[16]{0:T(128)S(1)}, f32[16]{0:T(128)}, u32[]{:S(2)}) copy-start(f32[16]{0:T(128)} %lame_lambda.1) | copy-start | bytes 196
  24.8 6.8 %copy-start.8 = (f32[16]{0:T(128)S(1)}, f32[16]{0:T(128)}, u32[]{:S(2)}) copy-start(f32[16]{0:T(128)} %lame_mu.1) | copy-start | bytes 196
  24.8 6.8 %collective-permute-start.6 = (f32[11,24,128]{2,1,0:T(8,128)S(1)}, f32[11,24,128]{2,1,0:T(8,128)S(1)}, u32[]{:S(2)}, u32[]{:S(2)}) collective-permute-start(f32[11,24,128]{2,1,0:T(8,128)S(1)} %get-tuple-element.22), channel_id=1, source_target_pairs={{1,2},{2,1},{3,4},{4,3},{5,6},{6,5},{9,10},{10,9},{11,12},{12,11},... | collective-permute-start | bytes 405512 | tf_op jit(solution)/shard_map/ppermute | solution.py:305
  33.9 7.3 %collective-permute-start.8 = (f32[2,9,24,128]{3,2,1,0:T(8,128)S(1)}, f32[2,9,24,128]{3,2,1,0:T(8,128)S(1)}, u32[]{:S(2)}, u32[]{:S(2)}) collective-permute-start(f32[2,9,24,128]{3,2,1,0:T(8,128)S(1)} %get-tuple-element.24), channel_id=1, source_target_pairs={{8,0},{16,8},{24,16},{9,1},{17,9},{25,17},{10,2},{18,10},{26,18},{... | collective-permute-start | bytes 663560 | tf_op jit(solution)/shard_map/ppermute | solution.py:296
  37.4 7.0 %collective-permute-start.7 = (f32[2,9,24,128]{3,2,1,0:T(8,128)S(1)}, f32[2,9,24,128]{3,2,1,0:T(8,128)S(1)}, u32[]{:S(2)}, u32[]{:S(2)}) collective-permute-start(f32[2,9,24,128]{3,2,1,0:T(8,128)S(1)} %get-tuple-element.24), channel_id=1, source_target_pairs={{0,8},{8,16},{16,24},{1,9},{9,17},{17,25},{2,10},{10,18},{18,26},{... | collective-permute-start | bytes 663560 | tf_op jit(solution)/shard_map/ppermute | solution.py:296
  45.7 3.7 %collective-permute-start.9 = (f32[9,2,8,128]{3,2,1,0:T(8,128)S(1)}, f32[9,2,8,128]{3,2,1,0:T(8,128)S(1)}, u32[]{:S(2)}, u32[]{:S(2)}) collective-permute-start(f32[9,2,8,128]{3,2,1,0:T(8,128)S(1)} %get-tuple-element.28), channel_id=1, source_target_pairs={{0,1},{1,0},{2,3},{3,2},{4,5},{5,4},{6,7},{7,6},{8,9},{9,8},{10,11... | collective-permute-start | bytes 221192 | tf_op jit(solution)/shard_map/ppermute | solution.py:308

commit v4 on v3

--- a/solution.py
+++ b/solution.py
@@ -58,25 +58,19 @@
         entries[at : at + 6] = moments[:, i * cy : (i + 1) * cy]
         entries[at + 6 : at + 7] = owner[i : i + 1, :].astype(F32)
         entries[at + 7 : at + 8] = cells[i : i + 1, :].astype(F32)
-    packed[11 * lines :] = entries[...]
-
-
-def widen_kernel(layout, *refs):
+
+
+def moment_kernel(layout, *refs):
     cx, cz, cy = layout
-    packs, others = refs[0:3], refs[3:-6]
-    kept, swapped, near, far, wide, acc = refs[-6:]
+    blocks, dense, acc = refs[:-2], refs[-2], refs[-1]
     section = lax.axis_index("sec")
-    segment = lax.axis_index("segment")
     planes = 3 * cx
-    lines = cx * cz
-    for i, pack in enumerate(packs):
-        wide[:, i * cx : (i + 1) * cx] = pack[0 : 11 * lines].reshape(11, cx, cz, cy)
-
-    @pl.when(segment == 0)
-    def _():
-        half = planes * cz // 2
+    half = planes * cz // 2
+
+    @pl.when(lax.axis_index("segment") == 0)
+    def _():
         acc[...] = jnp.zeros_like(acc)
-        for entries in [pack.at[pl.ds(11 * lines, pack.shape[0] - 11 * lines)] for pack in packs] + list(others):
+        for entries in blocks:
             groups = entries.shape[0] // 8
             chunk = [entries[8 * i : 8 * i + 8] for i in range(groups)]
             entry = jnp.concatenate(chunk, axis=1)
@@ -92,13 +86,39 @@
                 acc[...] += lax.dot_general(
                     jnp.concatenate(spread, axis=0), low, NT, preferred_element_type=F32
                 )
-
         for c in range(6):
-            span = slice(c * half, (c + 1) * half)
             for k in range(2):
                 at = slice(k * planes // 2, (k + 1) * planes // 2)
-                extra = acc[span, k * cy : (k + 1) * cy].reshape(planes // 2, cz, cy)
-                wide[3 + c, at] = wide[3 + c, at] + extra
+                got = acc[c * half : (c + 1) * half, k * cy : (k + 1) * cy]
+                dense[c, at] = got.reshape(planes // 2, cz, cy)
+
+
+def by_parity(even, odd, act):
+    parity = lax.axis_index("sec") % 2
+
+    @pl.when(parity == 0)
+    def _():
+        act(*even)
+
+    @pl.when(parity == 1)
+    def _():
+        act(*odd)
+
+
+def widen_kernel(layout, packed, first, second, dense, kept, swapped, near, far, wide):
+    cx, cz, cy = layout
+    segment = lax.axis_index("segment")
+    planes = 3 * cx
+
+    def place(left, right):
+        for i, pack in enumerate((left, packed, right)):
+            wide[:, i * cx : (i + 1) * cx] = pack[...].reshape(11, cx, cz, cy)
+
+    by_parity((second, first), (first, second), place)
+
+    @pl.when(segment == 0)
+    def _():
+        wide[3:9] = wide[3:9] + dense[...]
 
     def cut(to, first, count):
         for x in range(planes):
@@ -121,7 +141,7 @@
         cut(far, cz - STEPS, STEPS)
 
 
-def advance(cx, steps, state, coef, times):
+def advance(cx, steps, state, coef, times, given_top=False):
     planes, rows, cy = state.shape[2:]
     lane = lax.broadcasted_iota(jnp.int32, (rows, cy), 1)
     first_lane, last_lane = lane == 0, lane == cy - 1
@@ -138,25 +158,25 @@
     def fore_z(f):
         return pltpu.roll(f, rows - 1, 0) - f
 
+    def velocity(x):
+        inc = [None, None]
+        for model in range(2):
+            sxx, syy, szz, syz, sxz, sxy = (state[model, 3 + k, x] for k in range(6))
+            sxx_p, sxz_p, sxy_p = (state[model, k, x - 1] for k in (3, 7, 8))
+            hb = coef[model, 0, x]
+            inc[model] = (
+                hb * ((sxx - sxx_p) + back_y(sxy) + back_z(sxz)),
+                hb * ((sxy - sxy_p) + back_y(syy) + back_z(syz)),
+                hb * ((sxz - sxz_p) + back_y(syz) + back_z(szz)),
+            )
+        for k in range(3):
+            state[0, k, x] = state[0, k, x] + inc[0][k]
+            state[1, k, x] = (state[1, k, x] + inc[1][k]) + times[x] * inc[0][k]
+
     for step in range(steps):
         left = steps - 1 - step
         low, high = cx - left, 2 * cx + left
-
-        @pl.loop(low, high + 1)
-        def _(x):
-            inc = [None, None]
-            for model in range(2):
-                sxx, syy, szz, syz, sxz, sxy = (state[model, 3 + k, x] for k in range(6))
-                sxx_p, sxz_p, sxy_p = (state[model, k, x - 1] for k in (3, 7, 8))
-                hb = coef[model, 0, x]
-                inc[model] = (
-                    hb * ((sxx - sxx_p) + back_y(sxy) + back_z(sxz)),
-                    hb * ((sxy - sxy_p) + back_y(syy) + back_z(syz)),
-                    hb * ((sxz - sxz_p) + back_y(syz) + back_z(szz)),
-                )
-            for k in range(3):
-                state[0, k, x] = state[0, k, x] + inc[0][k]
-                state[1, k, x] = (state[1, k, x] + inc[1][k]) + times[x] * inc[0][k]
+        pl.loop(low, high + 1 - (given_top and step == 0))(velocity)
 
         @pl.loop(low, high)
         def _(x):
@@ -174,10 +194,12 @@
                 state[model, 7, x] = state[model, 7, x] + hm * (fore_z(vx) + (vz_n - vz))
                 state[model, 8, x] = state[model, 8, x] + hm * (fore_y(vx) + (vy_n - vy))
 
+    return velocity
+
 
 def first_kernel(
     cx, steps, kept, swapped, near, far, buoyancy, lame_lambda, lame_mu,
-    sent, both, coef, times, state, tables, sem,
+    to_first, to_second, both, coef, times, state, tables, sem,
 ):
     segment = lax.axis_index("segment")
     planes, rows, cy = state.shape[2:]
@@ -218,35 +240,71 @@
                 coef[model, i, x] = found[i]
         times[x] = state[1, 10, x]
 
-    advance(cx, steps, state, coef, times)
+    velocity = advance(cx, steps, state, coef, times)
     both[...] = state[:, 0:9, cx : 2 * cx]
-    cut_edges(cx, steps, state, sent)
-
-
-def cut_edges(cx, done, state, sent):
+    cut_edges(cx, steps, velocity, state, to_first, to_second)
+
+
+def cut_edges(cx, done, velocity, state, to_first, to_second):
     rows = state.shape[3]
+    at = slice(done, rows - done)
     count = rows - 2 * done
-    for x in range(cx):
-        sent[:, :, x * count : (x + 1) * count] = state[:, 0:9, cx + x, done : rows - done]
-
-
-def next_kernel(cx, done, steps, both_in, left, right, coef, times, *refs):
+
+    def put(to, place, x, comps):
+        for k in comps:
+            to[:, place * count : (place + 1) * count] = state[:, k, x, at]
+            place += 1
+        return place
+
+    def rightward(to):
+        place = 0
+        for x in range(1, cx):
+            place = put(to, place, cx + x, range(9))
+        put(to, place, cx, (3, 7, 8))
+
+    def leftward(to):
+        place = 0
+        for x in range(cx - 1):
+            place = put(to, place, cx + x, range(9))
+        put(to, place, 2 * cx - 1, range(3))
+
+    by_parity((to_second, to_first), (to_first, to_second), lambda left, right: rightward(right))
+    velocity(2 * cx - 1)
+    by_parity((to_second, to_first), (to_first, to_second), lambda left, right: leftward(left))
+
+
+def next_kernel(cx, done, steps, both_in, from_first, from_second, coef, times, *refs):
     segment = lax.axis_index("segment")
-    first, second, state = refs
+    state = refs[-1]
     rows = state.shape[3]
+    at = slice(done, rows - done)
     count = rows - 2 * done
     state[:, :, cx : 2 * cx] = both_in[...]
-    for x in range(cx):
-        span = slice(x * count, (x + 1) * count)
-        state[:, :, x, done : rows - done] = left[:, :, span]
-        state[:, :, 2 * cx + x, done : rows - done] = right[:, :, span]
-    advance(cx, steps, state, coef, times)
+
+    def get(edge, place, x, comps):
+        for k in comps:
+            state[:, k, x, at] = edge[:, place * count : (place + 1) * count]
+            place += 1
+        return place
+
+    def place_edges(left, right):
+        place = 0
+        for x in range(1, cx):
+            place = get(left, place, x, range(9))
+        get(left, place, 0, (3, 7, 8))
+        place = 0
+        for x in range(cx - 1):
+            place = get(right, place, 2 * cx + x, range(9))
+        get(right, place, 3 * cx - 1, range(3))
+
+    by_parity((from_second, from_first), (from_first, from_second), place_edges)
+    velocity = advance(cx, steps, state, coef, times, given_top=True)
     if done + steps == STEPS:
-        first[...] = state[segment, :, cx : 2 * cx, STEPS : rows - STEPS]
-        second[...] = state[1 - segment, :, cx : 2 * cx, STEPS : rows - STEPS]
+        refs[0][...] = state[segment, :, cx : 2 * cx, STEPS : rows - STEPS]
+        refs[1][...] = state[1 - segment, :, cx : 2 * cx, STEPS : rows - STEPS]
     else:
-        first[...] = state[:, :, cx : 2 * cx]
-        cut_edges(cx, done + steps, state, second)
+        refs[2][...] = state[:, :, cx : 2 * cx]
+        cut_edges(cx, done + steps, velocity, state, refs[0], refs[1])
 
 
 def home_kernel(mine, brought, out):
@@ -266,10 +324,9 @@
 
 VMEM = pl.BlockSpec(memory_space=pltpu.VMEM)
 HBM = pl.BlockSpec(memory_space=pltpu.HBM)
-LIMIT = pltpu.CompilerParams(vmem_limit_bytes=40 * 2**20)
-
-
-def call(kernel, name, in_hbm, in_vmem, outs, scratch, copies=0):
+
+
+def call(kernel, name, in_hbm, in_vmem, outs, scratch, copies=0, limit=40 * 2**20, flops=10**7):
     sems = [pltpu.SemaphoreType.DMA((copies,))] * (copies > 0)
     return pl.pallas_call(
         kernel,
@@ -277,7 +334,8 @@
         in_specs=[VMEM] * len(in_vmem) + [HBM] * len(in_hbm),
         out_specs=[VMEM] * len(outs),
         scratch_shapes=scratch + sems,
-        compiler_params=LIMIT,
+        compiler_params=pltpu.CompilerParams(vmem_limit_bytes=limit),
+        cost_estimate=pl.CostEstimate(flops=flops, bytes_accessed=2**20, transcendentals=0),
         name=name,
     )(*in_vmem, *in_hbm)
 
@@ -289,11 +347,14 @@
     layout = cx, cz, cy = fields.shape[2:]
     planes = 3 * cx
     reach, rows = cz // 2 + STEPS, cz // 2 + 2 * STEPS
-    plan = [cx] * (STEPS // cx) + [STEPS % cx] * (STEPS % cx > 0)
-
-    def along_x(block, distance):
-        route = [(i, i + distance) for i in range(sections) if 0 <= i + distance < sections]
-        return lax.ppermute(block, "sec", route)
+    assert cx > 1 and STEPS % cx == 0
+
+    def pairs(block, start):
+        route = [(i, i + 1) for i in range(start, sections - 1, 2)]
+        return lax.ppermute(block, "sec", route + [(j, i) for i, j in route])
+
+    def other(section, k):
+        return section ^ k if sections & (sections - 1) == 0 else (section + k) % sections
 
     def halo(block, core_zero_goes, flip):
         route = []
@@ -318,57 +379,71 @@
         "pack",
         (fields, *small),
         (),
-        [(11 * lines + entry_lines, cy), (entry_lines, cy)],
+        [(11 * lines, cy), (entry_lines, cy)],
         [pltpu.VMEM(a.shape, a.dtype) for a in small],
         len(small) + 9 * cx,
-    )
-    routes = [
-        [((i + k) % sections, i) for i in range(sections)] for k in range(2, sections - 1)
-    ] + [[(0, sections - 1), (sections - 1, 0)]] * (sections > 2)
-    others = [lax.ppermute(entries, "sec", route) for route in routes]
-    left, right = along_x(packed, 1), along_x(packed, -1)
+        limit=64 * 2**20,
+    )
+    blocks = [entries] + [
+        lax.ppermute(
+            entries, ("sec", "segment"), [(2 * other(i, k), 2 * i) for i in range(sections)]
+        )
+        for k in range(1, sections)
+    ]
+    first, second = pairs(packed, 0), pairs(packed, 1)
+    half = planes * cz // 2
+    (dense,) = call(
+        functools.partial(moment_kernel, layout),
+        "moments",
+        (),
+        blocks,
+        [(6, planes, cz, cy)],
+        [pltpu.VMEM((6 * half, 2 * cy), F32)],
+        flops=2 * 18 * half * 2 * cy * sections * moments.shape[1],
+    )
     kept, swapped, near, far = call(
         functools.partial(widen_kernel, layout),
-        "widen_and_moments",
+        "widen",
         (),
-        (left, packed, right, *others),
+        (packed, first, second, dense),
         [(11, planes * reach, cy)] * 2 + [(11, planes * STEPS, cy)] * 2,
-        [pltpu.VMEM((11, planes, cz, cy), F32), pltpu.VMEM((6 * planes * cz // 2, 2 * cy), F32)],
+        [pltpu.VMEM((11, planes, cz, cy), F32)],
     )
     near, far, swapped = halo(near, 1, False), halo(far, -1, True), swap(swapped)
     both_shape = (2, 9, cx, rows, cy)
     coef_shape, times_shape = (2, 3, planes, rows, cy), (planes, rows, cy)
 
     def edge_shape(done):
-        return (2, 9, cx * (rows - 2 * done), cy)
-
-    done = plan[0]
-    sent, both, coef, times = call(
-        functools.partial(first_kernel, cx, plan[0]),
+        return (2, (9 * (cx - 1) + 3) * (rows - 2 * done), cy)
+
+    done = cx
+    to_first, to_second, both, coef, times = call(
+        functools.partial(first_kernel, cx, cx),
         "first_steps",
         (buoyancy, lame_lambda, lame_mu),
         (kept, swapped, near, far),
-        [edge_shape(done), both_shape, coef_shape, times_shape],
+        [edge_shape(done)] * 2 + [both_shape, coef_shape, times_shape],
         [
             pltpu.VMEM((2, 11, planes, rows, cy), F32),
             pltpu.SMEM((3, buoyancy.shape[0]), F32),
         ],
         3,
     )
-    for steps in plan[1:]:
-        left, right = along_x(sent, 1), along_x(sent, -1)
-        after = done + steps
+    while done < STEPS:
+        first, second = pairs(to_first, 0), pairs(to_second, 1)
+        after = done + cx
         half_block = (9, cx, cz // 2, cy)
-        both, sent = call(
-            functools.partial(next_kernel, cx, done, steps),
+        got = call(
+            functools.partial(next_kernel, cx, done, cx),
             "next_steps",
             (),
-            (both, left, right, coef, times),
-            [half_block] * 2 if after == STEPS else [both_shape, edge_shape(after)],
+            (both, first, second, coef, times),
+            [half_block] * 2 if after == STEPS else [edge_shape(after)] * 2 + [both_shape],
             [pltpu.VMEM((2, 9, planes, rows, cy), F32)],
         )
+        to_first, to_second, both = got[0], got[1], got[-1]
         done = after
-    (out,) = call(home_kernel, "home", (), (both, swap(sent)), [fields.shape], [])
+    (out,) = call(home_kernel, "home", (), (to_first, swap(to_second)), [fields.shape], [])
     return out
 
 

time: 51 us -> 46.3 us (0.908); the launches traced: 50 us -> 45.9 us
  local copies, waits for them, and re-layouts: 4.47 us -> 0.78 us
  starting transfers between devices: 27.9 us -> 24.5 us
  waiting for transfers between devices: 12.3 us -> 14 us
  Pallas kernels: 5.25 us -> 6.51 us
    ppermute x6 -> x7, starting transfers between devices: 14.9 us -> 7.66 us  [the longest x4 5.67 us: pairs(): return lax.ppermute(block, 'sec', route + [(j, i) for i, j in route])]
    ppermute x2, starting transfers between devices: 7.93 us -> 11.7 us  [swap(): return lax.ppermute(block, 'segment', [(0, 1), (1, 0)])]
    unnamed x18 -> x10, local copies, waits for them, and re-layouts: 4.47 us -> 0.78 us
    ppermute x6 -> x7, waiting for transfers between devices: 6.67 us -> 8.34 us  [the longest x4 8.34 us: pairs(): return lax.ppermute(block, 'sec', route + [(j, i) for i, j in route])]
    pallas_call x5 -> x6, Pallas kernels: 5.25 us -> 6.51 us  [call(): pl.pallas_call(kernel, out_shape=[jax.ShapeDtypeStruct(shape, F32) for sh...]
  transfers between devices with their start and end apart: 10 -> 11, of which waited for: 6 -> 7; matrix products, arithmetic and copies ran while one was open for 0% -> 0% of each run, Pallas kernels for 0% -> 0%
where the time goes in v4:
time: 46.3 us; the launch traced here: 45.9 us
  starting transfers between devices  24.5 us (53%)
  waiting for transfers between devices  14 us (30%)
  Pallas kernels  6.51 us (14%)
  local copies, waits for them, and re-layouts  0.78 us (2%)
    ppermute x2, starting transfers between devices, swap(): return lax.ppermute(block, 'segment', [(0, 1), (1, 0)])  11.7 us
    ppermute x4, waiting for transfers between devices, pairs(): return lax.ppermute(block, 'sec', route + [(j, i) for i, j in route])  8.34 us
    pallas_call x6, Pallas kernels, call(): pl.pallas_call(kernel, out_shape=[jax.ShapeDtypeStruct(shape, F32) for sh...  6.51 us
    ppermute x4, starting transfers between devices, pairs(): return lax.ppermute(block, 'sec', route + [(j, i) for i, j in route])  5.67 us
    ppermute x2, starting transfers between devices, halo(): return lax.ppermute(block, ('depth', 'segment'), route)  5.1 us
    ppermute x2, waiting for transfers between devices, halo(): return lax.ppermute(block, ('depth', 'segment'), route)  4.7 us
    ppermute x3, starting transfers between devices, on_device(): lax.ppermute(entries, ('sec', 'segment'), [(2 * other(i, k), 2 * i) for i...  1.99 us
  transfers between devices with their start and end apart: 11, of which 7 were waited for; matrix products, arithmetic and copies ran while one was open for 0% of the time, Pallas kernels for 0%

profile of v4, /device:TPU:13, one launch (start us, length us, event | category | flops | bytes accessed | tf_op | source)
XLA Modules:
  0.0 45.9 jit_solution(8696752348848995253)
XLA Ops:
  0.0 2.1 %pack.1 = (f32[352,128]{1,0:T(8,128)}, f32[64,128]{1,0:T(8,128)}) custom-call(f32[1,9,2,16,128]{4,3,2,1,0:T(8,128)} %fields_in.1, s32[1,2,16,128]{3,2,1,0:T(8,128)} %ids_in.1, f32[6,1024]{1,0:T(8,128)} %moments_in.1, s32[8,128]{1,0:T(8,128)} %bitcast.4, s32[8,128]{1,0:T(8,128)} %bitcast.5, s32[16,128]{1,0:T(8,128)} %bitcast.3), custom_call_target="tpu_custom_call" | custom-call | flops 10000000 | bytes 1048576 | tf_op jit(solution)/shard_map/pack/pallas_call | solution.py:331
  2.1 0.7 %collective-permute-start.4 = (f32[64,128]{1,0:T(8,128)}, f32[64,128]{1,0:T(8,128)S(1)}, u32[]{:S(2)}, u32[]{:S(2)}) collective-permute-start(f32[64,128]{1,0:T(8,128)} %get-tuple-element.19.refs_0_), channel_id=1, source_target_pairs={{24,0},{16,8},{8,16},{0,24},{26,2},{18,10},{10,18},{2,26},{28,4},{... | collective-permute-start | bytes 98312 | tf_op jit(solution)/shard_map/ppermute | solution.py:388
  2.7 0.7 %collective-permute-start.3 = (f32[64,128]{1,0:T(8,128)}, f32[64,128]{1,0:T(8,128)S(1)}, u32[]{:S(2)}, u32[]{:S(2)}) collective-permute-start(f32[64,128]{1,0:T(8,128)} %get-tuple-element.19.refs_0_), channel_id=1, source_target_pairs={{16,0},{24,8},{0,16},{8,24},{18,2},{26,10},{2,18},{10,26},{20,4},{... | collective-permute-start | bytes 98312 | tf_op jit(solution)/shard_map/ppermute | solution.py:388
  3.4 0.7 %collective-permute-start.2 = (f32[64,128]{1,0:T(8,128)}, f32[64,128]{1,0:T(8,128)S(1)}, u32[]{:S(2)}, u32[]{:S(2)}) collective-permute-start(f32[64,128]{1,0:T(8,128)} %get-tuple-element.19.refs_0_), channel_id=1, source_target_pairs={{8,0},{0,8},{24,16},{16,24},{10,2},{2,10},{26,18},{18,26},{12,4},{... | collective-permute-start | bytes 98312 | tf_op jit(solution)/shard_map/ppermute | solution.py:388
  4.1 3.3 %collective-permute-start.1 = (f32[352,128]{1,0:T(8,128)}, f32[352,128]{1,0:T(8,128)S(1)}, u32[]{:S(2)}, u32[]{:S(2)}) collective-permute-start(f32[352,128]{1,0:T(8,128)} %get-tuple-element.18.packed), channel_id=1, source_target_pairs={{8,16},{16,8},{9,17},{17,9},{10,18},{18,10},{11,19},{19,11},{12,20... | collective-permute-start | bytes 540680 | tf_op jit(solution)/shard_map/ppermute | solution.py:354
  7.4 0.1 collective-permute-start
  7.6 0.7 %copy-done.4 = f32[64,128]{1,0:T(8,128)S(1)} copy-done((f32[64,128]{1,0:T(8,128)S(1)}, f32[64,128]{1,0:T(8,128)}, u32[]{:S(2)}) %copy-start.4) | copy-done | bytes 32792
  8.3 2.5 %collective-permute-done.1.second = f32[352,128]{1,0:T(8,128)S(1)} collective-permute-done((f32[352,128]{1,0:T(8,128)}, f32[352,128]{1,0:T(8,128)S(1)}, u32[]{:S(2)}, u32[]{:S(2)}) %collective-permute-start.1) | collective-permute-done | bytes 180256 | tf_op jit(solution)/shard_map/ppermute | solution.py:354
  10.8 1.9 %collective-permute-done.first = f32[352,128]{1,0:T(8,128)S(1)} collective-permute-done((f32[352,128]{1,0:T(8,128)}, f32[352,128]{1,0:T(8,128)S(1)}, u32[]{:S(2)}, u32[]{:S(2)}) %collective-permute-start) | collective-permute-done | bytes 180256 | tf_op jit(solution)/shard_map/ppermute | solution.py:354
  12.7 0.2 widen.1
  12.8 9.3 %collective-permute-start.5 = (f32[11,72,128]{2,1,0:T(8,128)S(1)}, f32[11,72,128]{2,1,0:T(8,128)S(1)}, u32[]{:S(2)}, u32[]{:S(2)}) collective-permute-start(f32[11,72,128]{2,1,0:T(8,128)S(1)} %get-tuple-element.21), channel_id=1, source_target_pairs={{0,1},{1,0},{2,3},{3,2},{4,5},{5,4},{6,7},{7,6},{8,9},{9,8},{10,11... | collective-permute-start | bytes 1216520 | tf_op jit(solution)/shard_map/ppermute | solution.py:369
  22.1 3.0 %collective-permute-start.6 = (f32[11,24,128]{2,1,0:T(8,128)S(1)}, f32[11,24,128]{2,1,0:T(8,128)S(1)}, u32[]{:S(2)}, u32[]{:S(2)}) collective-permute-start(f32[11,24,128]{2,1,0:T(8,128)S(1)} %get-tuple-element.22), channel_id=1, source_target_pairs={{0,2},{2,4},{3,1},{4,6},{5,3},{7,5},{8,10},{10,12},{11,9},{12,14},... | collective-permute-start | bytes 405512 | tf_op jit(solution)/shard_map/ppermute | solution.py:366
  25.2 2.1 %collective-permute-start.7 = (f32[11,24,128]{2,1,0:T(8,128)S(1)}, f32[11,24,128]{2,1,0:T(8,128)S(1)}, u32[]{:S(2)}, u32[]{:S(2)}) collective-permute-start(f32[11,24,128]{2,1,0:T(8,128)S(1)} %get-tuple-element.23), channel_id=1, source_target_pairs={{1,2},{2,1},{3,4},{4,3},{5,6},{6,5},{9,10},{10,9},{11,12},{12,11},... | collective-permute-start | bytes 405512 | tf_op jit(solution)/shard_map/ppermute | solution.py:366
  27.3 0.9 %collective-permute-done.6.near = f32[11,24,128]{2,1,0:T(8,128)S(1)} collective-permute-done((f32[11,24,128]{2,1,0:T(8,128)S(1)}, f32[11,24,128]{2,1,0:T(8,128)S(1)}, u32[]{:S(2)}, u32[]{:S(2)}) %collective-permute-start.6) | collective-permute-done | bytes 135200 | tf_op jit(solution)/shard_map/ppermute | solution.py:366
  28.1 3.8 %collective-permute-done.7.far = f32[11,24,128]{2,1,0:T(8,128)S(1)} collective-permute-done((f32[11,24,128]{2,1,0:T(8,128)S(1)}, f32[11,24,128]{2,1,0:T(8,128)S(1)}, u32[]{:S(2)}, u32[]{:S(2)}) %collective-permute-start.7) | collective-permute-done | bytes 135200 | tf_op jit(solution)/shard_map/ppermute | solution.py:366
  32.0 2.4 %first_steps.1 = (f32[2,144,128]{2,1,0:T(8,128)S(1)}, f32[2,144,128]{2,1,0:T(8,128)S(1)}, f32[2,9,2,16,128]{4,3,2,1,0:T(8,128)S(1)}, f32[2,3,6,16,128]{4,3,2,1,0:T(8,128)S(1)}, f32[6,16,128]{2,1,0:T(8,128)S(1)}) custom-call(f32[11,72,128]{2,1,0:T(8,128)S(1)} %get-tuple-element.20.kept, f32[11,72,128]{2,1,0:T(8,128)S(1)} %collective-permute-done.5.swapped, ...), custom_call_target="tpu_custom_call" | custom-call | flops 10000000 | bytes 1048576 | tf_op jit(solution)/shard_map/first_steps/pallas_call | solution.py:331
  34.4 0.1 collective-permute-start.8
  34.5 2.2 %collective-permute-start.9 = (f32[2,144,128]{2,1,0:T(8,128)S(1)}, f32[2,144,128]{2,1,0:T(8,128)S(1)}, u32[]{:S(2)}, u32[]{:S(2)}) collective-permute-start(f32[2,144,128]{2,1,0:T(8,128)S(1)} %get-tuple-element.26), channel_id=1, source_target_pairs={{8,16},{16,8},{9,17},{17,9},{10,18},{18,10},{11,19},{19,11},{12,20... | collective-permute-start | bytes 442376 | tf_op jit(solution)/shard_map/ppermute | solution.py:354
  36.7 1.8 %collective-permute-done.8.from_first = f32[2,144,128]{2,1,0:T(8,128)S(1)} collective-permute-done((f32[2,144,128]{2,1,0:T(8,128)S(1)}, f32[2,144,128]{2,1,0:T(8,128)S(1)}, u32[]{:S(2)}, u32[]{:S(2)}) %collective-permute-start.8) | collective-permute-done | bytes 147488 | tf_op jit(solution)/shard_map/ppermute | solution.py:354
  38.5 2.2 %collective-permute-done.9.from_second = f32[2,144,128]{2,1,0:T(8,128)S(1)} collective-permute-done((f32[2,144,128]{2,1,0:T(8,128)S(1)}, f32[2,144,128]{2,1,0:T(8,128)S(1)}, u32[]{:S(2)}, u32[]{:S(2)}) %collective-permute-start.9) | collective-permute-done | bytes 147488 | tf_op jit(solution)/shard_map/ppermute | solution.py:354
  40.7 1.2 %next_steps.1 = (f32[9,2,8,128]{3,2,1,0:T(8,128)S(1)}, f32[9,2,8,128]{3,2,1,0:T(8,128)S(1)}) custom-call(f32[2,9,2,16,128]{4,3,2,1,0:T(8,128)S(1)} %get-tuple-element.24.both_in, f32[2,144,128]{2,1,0:T(8,128)S(1)} %collective-permute-done.8.from_first, f32[2,144,128]{2,1,0:T(8,128)S(1)} %collective-permute-done.9.from_second, ...), custom_call_target="tpu_custom_call" | custom-call | flops 10000000 | bytes 1048576 | tf_op jit(solution)/shard_map/next_steps/pallas_call | solution.py:331
  41.9 2.4 %collective-permute-start.10 = (f32[9,2,8,128]{3,2,1,0:T(8,128)S(1)}, f32[9,2,8,128]{3,2,1,0:T(8,128)S(1)}, u32[]{:S(2)}, u32[]{:S(2)}) collective-permute-start(f32[9,2,8,128]{3,2,1,0:T(8,128)S(1)} %get-tuple-element.30), channel_id=1, source_target_pairs={{0,1},{1,0},{2,3},{3,2},{4,5},{5,4},{6,7},{7,6},{8,9},{9,8},{10,11... | collective-permute-start | bytes 221192 | tf_op jit(solution)/shard_map/ppermute | solution.py:369
  44.3 0.9 %collective-permute-done.10.brought = f32[9,2,8,128]{3,2,1,0:T(8,128)S(1)} collective-permute-done((f32[9,2,8,128]{3,2,1,0:T(8,128)S(1)}, f32[9,2,8,128]{3,2,1,0:T(8,128)S(1)}, u32[]{:S(2)}, u32[]{:S(2)}) %collective-permute-start.10) | collective-permute-done | bytes 73760 | tf_op jit(solution)/shard_map/ppermute | solution.py:369
  45.2 0.7 %home.1 = f32[1,9,2,16,128]{4,3,2,1,0:T(8,128)} custom-call(f32[9,2,8,128]{3,2,1,0:T(8,128)S(1)} %get-tuple-element.29.mine, f32[9,2,8,128]{3,2,1,0:T(8,128)S(1)} %collective-permute-done.10.brought), custom_call_target="tpu_custom_call" | custom-call | flops 10000000 | bytes 1048576 | tf_op jit(solution)/shard_map/home/pallas_call | solution.py:331
  (14 shorter events, 0.0 us)
Async XLA Ops:
  2.1 5.4 %collective-permute-start.4 = (f32[64,128]{1,0:T(8,128)}, f32[64,128]{1,0:T(8,128)S(1)}, u32[]{:S(2)}, u32[]{:S(2)}) collective-permute-start(f32[64,128]{1,0:T(8,128)} %get-tuple-element.19.refs_0_), channel_id=1, source_target_pairs={{24,0},{16,8},{8,16},{0,24},{26,2},{18,10},{10,18},{2,26},{28,4},{... | collective-permute-start | bytes 98312 | tf_op jit(solution)/shard_map/ppermute | solution.py:388
  2.7 4.8 %collective-permute-start.3 = (f32[64,128]{1,0:T(8,128)}, f32[64,128]{1,0:T(8,128)S(1)}, u32[]{:S(2)}, u32[]{:S(2)}) collective-permute-start(f32[64,128]{1,0:T(8,128)} %get-tuple-element.19.refs_0_), channel_id=1, source_target_pairs={{16,0},{24,8},{0,16},{8,24},{18,2},{26,10},{2,18},{10,26},{20,4},{... | collective-permute-start | bytes 98312 | tf_op jit(solution)/shard_map/ppermute | solution.py:388
  3.4 4.1 %collective-permute-start.2 = (f32[64,128]{1,0:T(8,128)}, f32[64,128]{1,0:T(8,128)S(1)}, u32[]{:S(2)}, u32[]{:S(2)}) collective-permute-start(f32[64,128]{1,0:T(8,128)} %get-tuple-element.19.refs_0_), channel_id=1, source_target_pairs={{8,0},{0,8},{24,16},{16,24},{10,2},{2,10},{26,18},{18,26},{12,4},{... | collective-permute-start | bytes 98312 | tf_op jit(solution)/shard_map/ppermute | solution.py:388
  4.1 8.6 %copy-start = (f32[352,128]{1,0:T(8,128)S(1)}, f32[352,128]{1,0:T(8,128)}, u32[]{:S(2)}) copy-start(f32[352,128]{1,0:T(8,128)} %get-tuple-element.18.packed) | copy-start | bytes 540676
  4.1 6.7 %collective-permute-start.1 = (f32[352,128]{1,0:T(8,128)}, f32[352,128]{1,0:T(8,128)S(1)}, u32[]{:S(2)}, u32[]{:S(2)}) collective-permute-start(f32[352,128]{1,0:T(8,128)} %get-tuple-element.18.packed), channel_id=1, source_target_pairs={{8,16},{16,8},{9,17},{17,9},{10,18},{18,10},{11,19},{19,11},{12,20... | collective-permute-start | bytes 540680 | tf_op jit(solution)/shard_map/ppermute | solution.py:354
  7.4 5.2 %collective-permute-start = (f32[352,128]{1,0:T(8,128)}, f32[352,128]{1,0:T(8,128)S(1)}, u32[]{:S(2)}, u32[]{:S(2)}) collective-permute-start(f32[352,128]{1,0:T(8,128)} %get-tuple-element.18.packed), channel_id=1, source_target_pairs={{0,8},{16,24},{8,0},{24,16},{1,9},{17,25},{9,1},{25,17},{2,10},{18... | collective-permute-start | bytes 540680 | tf_op jit(solution)/shard_map/ppermute | solution.py:354
  7.6 0.8 %copy-start.4 = (f32[64,128]{1,0:T(8,128)S(1)}, f32[64,128]{1,0:T(8,128)}, u32[]{:S(2)}) copy-start(f32[64,128]{1,0:T(8,128)} %get-tuple-element.19.refs_0_) | copy-start | bytes 98308
  12.8 19.1 %collective-permute-start.5 = (f32[11,72,128]{2,1,0:T(8,128)S(1)}, f32[11,72,128]{2,1,0:T(8,128)S(1)}, u32[]{:S(2)}, u32[]{:S(2)}) collective-permute-start(f32[11,72,128]{2,1,0:T(8,128)S(1)} %get-tuple-element.21), channel_id=1, source_target_pairs={{0,1},{1,0},{2,3},{3,2},{4,5},{5,4},{6,7},{7,6},{8,9},{9,8},{10,11... | collective-permute-start | bytes 1216520 | tf_op jit(solution)/shard_map/ppermute | solution.py:369
  22.1 6.0 %collective-permute-start.6 = (f32[11,24,128]{2,1,0:T(8,128)S(1)}, f32[11,24,128]{2,1,0:T(8,128)S(1)}, u32[]{:S(2)}, u32[]{:S(2)}) collective-permute-start(f32[11,24,128]{2,1,0:T(8,128)S(1)} %get-tuple-element.22), channel_id=1, source_target_pairs={{0,2},{2,4},{3,1},{4,6},{5,3},{7,5},{8,10},{10,12},{11,9},{12,14},... | collective-permute-start | bytes 405512 | tf_op jit(solution)/shard_map/ppermute | solution.py:366
  25.2 6.8 %copy-start.1 = (f32[16]{0:T(128)S(1)}, f32[16]{0:T(128)}, u32[]{:S(2)}) copy-start(f32[16]{0:T(128)} %buoyancy.1) | copy-start | bytes 196
  25.2 6.8 %copy-start.2 = (f32[16]{0:T(128)S(1)}, f32[16]{0:T(128)}, u32[]{:S(2)}) copy-start(f32[16]{0:T(128)} %lame_lambda.1) | copy-start | bytes 196
  25.2 6.8 %copy-start.3 = (f32[16]{0:T(128)S(1)}, f32[16]{0:T(128)}, u32[]{:S(2)}) copy-start(f32[16]{0:T(128)} %lame_mu.1) | copy-start | bytes 196
  25.2 6.8 %collective-permute-start.7 = (f32[11,24,128]{2,1,0:T(8,128)S(1)}, f32[11,24,128]{2,1,0:T(8,128)S(1)}, u32[]{:S(2)}, u32[]{:S(2)}) collective-permute-start(f32[11,24,128]{2,1,0:T(8,128)S(1)} %get-tuple-element.23), channel_id=1, source_target_pairs={{1,2},{2,1},{3,4},{4,3},{5,6},{6,5},{9,10},{10,9},{11,12},{12,11},... | collective-permute-start | bytes 405512 | tf_op jit(solution)/shard_map/ppermute | solution.py:366
  34.4 4.1 %collective-permute-start.8 = (f32[2,144,128]{2,1,0:T(8,128)S(1)}, f32[2,144,128]{2,1,0:T(8,128)S(1)}, u32[]{:S(2)}, u32[]{:S(2)}) collective-permute-start(f32[2,144,128]{2,1,0:T(8,128)S(1)} %get-tuple-element.25), channel_id=1, source_target_pairs={{0,8},{16,24},{8,0},{24,16},{1,9},{17,25},{9,1},{25,17},{2,10},{18... | collective-permute-start | bytes 442376 | tf_op jit(solution)/shard_map/ppermute | solution.py:354
  34.5 6.2 %collective-permute-start.9 = (f32[2,144,128]{2,1,0:T(8,128)S(1)}, f32[2,144,128]{2,1,0:T(8,128)S(1)}, u32[]{:S(2)}, u32[]{:S(2)}) collective-permute-start(f32[2,144,128]{2,1,0:T(8,128)S(1)} %get-tuple-element.26), channel_id=1, source_target_pairs={{8,16},{16,8},{9,17},{17,9},{10,18},{18,10},{11,19},{19,11},{12,20... | collective-permute-start | bytes 442376 | tf_op jit(solution)/shard_map/ppermute | solution.py:354
  41.9 3.3 %collective-permute-start.10 = (f32[9,2,8,128]{3,2,1,0:T(8,128)S(1)}, f32[9,2,8,128]{3,2,1,0:T(8,128)S(1)}, u32[]{:S(2)}, u32[]{:S(2)}) collective-permute-start(f32[9,2,8,128]{3,2,1,0:T(8,128)S(1)} %get-tuple-element.30), channel_id=1, source_target_pairs={{0,1},{1,0},{2,3},{3,2},{4,5},{5,4},{6,7},{7,6},{8,9},{9,8},{10,11... | collective-permute-start | bytes 221192 | tf_op jit(solution)/shard_map/ppermute | solution.py:369

commit v5 on v4

--- a/solution.py
+++ b/solution.py
@@ -42,17 +42,14 @@
     ids, moments, owner, cells, rows, sem = scratch
     lines = cx * cz
     copies = [(ids_in, ids), (moments_in, moments), (owner_in, owner), (cells_in, cells), (rows_in, rows)]
-    copies += [
-        (fields_in.at[0, k, x], packed.at[pl.ds((k * cx + x) * cz, cz)])
-        for k in range(9)
-        for x in range(cx)
-    ]
+    copies += [(fields_in.at[0], packed.at[pl.ds(0, 9)])]
     copy_all(sem, copies)
-    packed[9 * lines : 10 * lines] = (ids[0] + 1).astype(F32).reshape(lines, cy)
+    packed[9] = (ids[0] + 1).astype(F32)
     line = in_line(rows[...])
     high = one_hot(line // cy, lines).astype(BF16)
     low = one_hot(line % cy, cy).astype(BF16)
-    packed[10 * lines : 11 * lines] = lax.dot_general(high, low, NT, preferred_element_type=F32)
+    count = lax.dot_general(high, low, NT, preferred_element_type=F32)
+    packed[10] = count.reshape(cx, cz, cy)
     for i in range(cells.shape[0]):
         at = 8 * i
         entries[at : at + 6] = moments[:, i * cy : (i + 1) * cy]
@@ -62,15 +59,19 @@
 
 def moment_kernel(layout, *refs):
     cx, cz, cy = layout
-    blocks, dense, acc = refs[:-2], refs[-2], refs[-1]
+    blocks, own_in, dense, acc, own, sem = refs[:-5], *refs[-5:]
     section = lax.axis_index("sec")
     planes = 3 * cx
     half = planes * cz // 2
 
     @pl.when(lax.axis_index("segment") == 0)
     def _():
+        copy = pltpu.make_async_copy(own_in, own, sem.at[0])
+        copy.start()
         acc[...] = jnp.zeros_like(acc)
-        for entries in blocks:
+        for entries in (*blocks, own):
+            if entries is own:
+                copy.wait()
             groups = entries.shape[0] // 8
             chunk = [entries[8 * i : 8 * i + 8] for i in range(groups)]
             entry = jnp.concatenate(chunk, axis=1)
@@ -112,7 +113,7 @@
 
     def place(left, right):
         for i, pack in enumerate((left, packed, right)):
-            wide[:, i * cx : (i + 1) * cx] = pack[...].reshape(11, cx, cz, cy)
+            wide[:, i * cx : (i + 1) * cx] = pack[...]
 
     by_parity((second, first), (first, second), place)
 
@@ -124,21 +125,37 @@
         for x in range(planes):
             to[:, x * count : (x + 1) * count] = wide[:, x, first : first + count]
 
+    def cut_halo(to, upward):
+        spans, lines = halo_rows(cx, upward)
+        for x, at, rows in spans:
+            first = cz - rows if upward else 0
+            for k in range(11):
+                to[k * lines + at : k * lines + at + rows] = wide[k, x, first : first + rows]
+
     reach = cz // 2 + STEPS
 
     @pl.when(segment == 0)
     def _():
         cut(kept, 0, reach)
         cut(swapped, cz - reach, reach)
-        cut(near, cz - STEPS, STEPS)
-        cut(far, 0, STEPS)
+        cut_halo(near, True)
+        cut_halo(far, False)
 
     @pl.when(segment == 1)
     def _():
         cut(kept, cz - reach, reach)
         cut(swapped, 0, reach)
-        cut(near, 0, STEPS)
-        cut(far, cz - STEPS, STEPS)
+        cut_halo(near, False)
+        cut_halo(far, True)
+
+
+def halo_rows(cx, upward):
+    found, at = [], 0
+    for x in range(3 * cx):
+        beyond = max(0, cx - x) if upward else max(0, x - 2 * cx + 1)
+        found.append((x, at, STEPS - beyond))
+        at += STEPS - beyond
+    return found, at
 
 
 def advance(cx, steps, state, coef, times, given_top=False):
@@ -207,14 +224,15 @@
     copy_all(sem, [(t, tables.at[i]) for i, t in enumerate((buoyancy, lame_lambda, lame_mu))])
 
     def join(model, body, halo, upper):
-        for x in range(planes):
-            inner, outer = slice(x * reach, (x + 1) * reach), slice(x * STEPS, (x + 1) * STEPS)
-            if upper:
-                state[model, :, x, 0:STEPS] = halo[:, outer]
-                state[model, :, x, STEPS:] = body[:, inner]
-            else:
-                state[model, :, x, 0:reach] = body[:, inner]
-                state[model, :, x, reach:] = halo[:, outer]
+        spans, lines = halo_rows(cx, upper)
+        for x, at, count in spans:
+            inner = slice(x * reach, (x + 1) * reach)
+            first = STEPS if upper else 0
+            state[model, :, x, first : first + reach] = body[:, inner]
+            first = STEPS - count if upper else reach
+            for k in range(11):
+                outer = slice(k * lines + at, k * lines + at + count)
+                state[model, k, x, first : first + count] = halo[outer]
 
     @pl.when(segment == 0)
     def _():
@@ -372,33 +390,32 @@
     cells = moment_cells.reshape(-1, cy)
     boundary = drm_rows.reshape(-1, cy)
     small = (block_ids, moments, owner, cells, boundary)
-    lines = cx * cz
     entry_lines = 8 * cells.shape[0]
     packed, entries = call(
         functools.partial(pack_kernel, layout),
         "pack",
         (fields, *small),
         (),
-        [(11 * lines, cy), (entry_lines, cy)],
+        [(11, cx, cz, cy), (entry_lines, cy)],
         [pltpu.VMEM(a.shape, a.dtype) for a in small],
-        len(small) + 9 * cx,
+        len(small) + 1,
         limit=64 * 2**20,
     )
-    blocks = [entries] + [
-        lax.ppermute(
-            entries, ("sec", "segment"), [(2 * other(i, k), 2 * i) for i in range(sections)]
-        )
+    blocks = [
+        lax.ppermute(entries, "sec", [(other(i, k), i) for i in range(sections)])
         for k in range(1, sections)
     ]
     first, second = pairs(packed, 0), pairs(packed, 1)
     half = planes * cz // 2
+    halo_lines = -(-11 * halo_rows(cx, True)[1] // 8) * 8
     (dense,) = call(
         functools.partial(moment_kernel, layout),
         "moments",
-        (),
+        (entries,),
         blocks,
         [(6, planes, cz, cy)],
-        [pltpu.VMEM((6 * half, 2 * cy), F32)],
+        [pltpu.VMEM((6 * half, 2 * cy), F32), pltpu.VMEM((entry_lines, cy), F32)],
+        1,
         flops=2 * 18 * half * 2 * cy * sections * moments.shape[1],
     )
     kept, swapped, near, far = call(
@@ -406,7 +423,7 @@
         "widen",
         (),
         (packed, first, second, dense),
-        [(11, planes * reach, cy)] * 2 + [(11, planes * STEPS, cy)] * 2,
+        [(11, planes * reach, cy)] * 2 + [(halo_lines, cy)] * 2,
         [pltpu.VMEM((11, planes, cz, cy), F32)],
     )
     near, far, swapped = halo(near, 1, False), halo(far, -1, True), swap(swapped)

time: 46.3 us -> 40.6 us (0.88)
  starting transfers between devices: 24.5 us -> 19.6 us
  waiting for transfers between devices: 14 us -> 13.2 us
    ppermute x2, starting transfers between devices: 11.7 us -> 5.26 us  [swap(): return lax.ppermute(block, 'segment', [(0, 1), (1, 0)])]
    ppermute x3, starting transfers between devices: 1.99 us -> 3.56 us  [on_device(): lax.ppermute(entries, 'sec', [(other(i, k), i) for i in range(sections)])]
    ppermute x4, waiting for transfers between devices: 8.34 us -> 7.76 us  [pairs(): return lax.ppermute(block, 'sec', route + [(j, i) for i, j in route])]
where the time goes in v5:
time: 40.6 us; the launch traced here: 40.2 us
  starting transfers between devices  19.6 us (48%)
  waiting for transfers between devices  13.2 us (33%)
  Pallas kernels  6.47 us (16%)
  local copies, waits for them, and re-layouts  0.78 us (2%)
    ppermute x4, waiting for transfers between devices, pairs(): return lax.ppermute(block, 'sec', route + [(j, i) for i, j in route])  7.76 us
    pallas_call x6, Pallas kernels, call(): pl.pallas_call(kernel, out_shape=[jax.ShapeDtypeStruct(shape, F32) for sh...  6.47 us
    ppermute x4, starting transfers between devices, pairs(): return lax.ppermute(block, 'sec', route + [(j, i) for i, j in route])  5.69 us
    ppermute x2, starting transfers between devices, swap(): return lax.ppermute(block, 'segment', [(0, 1), (1, 0)])  5.26 us
    ppermute x2, starting transfers between devices, halo(): return lax.ppermute(block, ('depth', 'segment'), route)  5.1 us
    ppermute x2, waiting for transfers between devices, halo(): return lax.ppermute(block, ('depth', 'segment'), route)  4.52 us
    ppermute x3, starting transfers between devices, on_device(): lax.ppermute(entries, 'sec', [(other(i, k), i) for i in range(sections)])  3.56 us
    ppermute x2, waiting for transfers between devices, swap(): return lax.ppermute(block, 'segment', [(0, 1), (1, 0)])  0.92 us
  transfers between devices with their start and end apart: 11, of which 7 were waited for; matrix products, arithmetic and copies ran while one was open for 0% of the time, Pallas kernels for 0%

profile of v5, /device:TPU:13, one launch (start us, length us, event | category | flops | bytes accessed | tf_op | source)
XLA Modules:
  0.0 40.2 jit_solution(12290135663177123202)
XLA Ops:
  0.0 2.0 %pack.1 = (f32[11,2,16,128]{3,2,1,0:T(8,128)}, f32[64,128]{1,0:T(8,128)}) custom-call(f32[1,9,2,16,128]{4,3,2,1,0:T(8,128)} %fields_in.1, s32[1,2,16,128]{3,2,1,0:T(8,128)} %ids_in.1, f32[6,1024]{1,0:T(8,128)} %moments_in.1, s32[8,128]{1,0:T(8,128)} %bitcast.4, s32[8,128]{1,0:T(8,128)} %bitcast.5, s32[16,128]{1,0:T(8,128)} %bitcast.3), custom_call_target="tpu_custom_call" | custom-call | flops 10000000 | bytes 1048576 | tf_op jit(solution)/shard_map/pack/pallas_call | solution.py:349
  2.0 1.4 %collective-permute-start.4 = (f32[64,128]{1,0:T(8,128)}, f32[64,128]{1,0:T(8,128)S(1)}, u32[]{:S(2)}, u32[]{:S(2)}) collective-permute-start(f32[64,128]{1,0:T(8,128)} %get-tuple-element.19.refs_3_), channel_id=1, source_target_pairs={{24,0},{16,8},{8,16},{0,24},{25,1},{17,9},{9,17},{1,25},{26,2},{18... | collective-permute-start | bytes 98312 | tf_op jit(solution)/shard_map/ppermute | solution.py:405
  3.4 1.1 %collective-permute-start.3 = (f32[64,128]{1,0:T(8,128)}, f32[64,128]{1,0:T(8,128)S(1)}, u32[]{:S(2)}, u32[]{:S(2)}) collective-permute-start(f32[64,128]{1,0:T(8,128)} %get-tuple-element.19.refs_3_), channel_id=1, source_target_pairs={{16,0},{24,8},{0,16},{8,24},{17,1},{25,9},{1,17},{9,25},{18,2},{26... | collective-permute-start | bytes 98312 | tf_op jit(solution)/shard_map/ppermute | solution.py:405
  4.5 1.1 %collective-permute-start.2 = (f32[64,128]{1,0:T(8,128)}, f32[64,128]{1,0:T(8,128)S(1)}, u32[]{:S(2)}, u32[]{:S(2)}) collective-permute-start(f32[64,128]{1,0:T(8,128)} %get-tuple-element.19.refs_3_), channel_id=1, source_target_pairs={{8,0},{0,8},{24,16},{16,24},{9,1},{1,9},{25,17},{17,25},{10,2},{2,... | collective-permute-start | bytes 98312 | tf_op jit(solution)/shard_map/ppermute | solution.py:405
  5.6 3.2 %collective-permute-start.1 = (f32[11,2,16,128]{3,2,1,0:T(8,128)}, f32[11,2,16,128]{3,2,1,0:T(8,128)S(1)}, u32[]{:S(2)}, u32[]{:S(2)}) collective-permute-start(f32[11,2,16,128]{3,2,1,0:T(8,128)} %get-tuple-element.18.packed), channel_id=1, source_target_pairs={{8,16},{16,8},{9,17},{17,9},{10,18},{18,10},{11,19},{19,11},{12,20... | collective-permute-start | bytes 540680 | tf_op jit(solution)/shard_map/ppermute | solution.py:372
  8.8 0.1 collective-permute-start
  8.9 0.7 %copy-done.4 = f32[64,128]{1,0:T(8,128)S(1)} copy-done((f32[64,128]{1,0:T(8,128)S(1)}, f32[64,128]{1,0:T(8,128)}, u32[]{:S(2)}) %copy-start.4) | copy-done | bytes 32792
  9.7 2.9 %collective-permute-done.1.second = f32[11,2,16,128]{3,2,1,0:T(8,128)S(1)} collective-permute-done((f32[11,2,16,128]{3,2,1,0:T(8,128)}, f32[11,2,16,128]{3,2,1,0:T(8,128)S(1)}, u32[]{:S(2)}, u32[]{:S(2)}) %collective-permute-start.1) | collective-permute-done | bytes 180256 | tf_op jit(solution)/shard_map/ppermute | solution.py:372
  12.6 1.1 %collective-permute-done.first = f32[11,2,16,128]{3,2,1,0:T(8,128)S(1)} collective-permute-done((f32[11,2,16,128]{3,2,1,0:T(8,128)}, f32[11,2,16,128]{3,2,1,0:T(8,128)S(1)}, u32[]{:S(2)}, u32[]{:S(2)}) %collective-permute-start) | collective-permute-done | bytes 180256 | tf_op jit(solution)/shard_map/ppermute | solution.py:372
  13.7 0.2 widen.1
  13.9 2.5 %collective-permute-start.5 = (f32[11,72,128]{2,1,0:T(8,128)S(1)}, f32[11,72,128]{2,1,0:T(8,128)S(1)}, u32[]{:S(2)}, u32[]{:S(2)}) collective-permute-start(f32[11,72,128]{2,1,0:T(8,128)S(1)} %get-tuple-element.21), channel_id=1, source_target_pairs={{0,1},{1,0},{2,3},{3,2},{4,5},{5,4},{6,7},{7,6},{8,9},{9,8},{10,11... | collective-permute-start | bytes 1216520 | tf_op jit(solution)/shard_map/ppermute | solution.py:387
  16.4 3.1 %collective-permute-start.6 = (f32[232,128]{1,0:T(8,128)S(1)}, f32[232,128]{1,0:T(8,128)S(1)}, u32[]{:S(2)}, u32[]{:S(2)}) collective-permute-start(f32[232,128]{1,0:T(8,128)S(1)} %get-tuple-element.22), channel_id=1, source_target_pairs={{0,2},{2,4},{3,1},{4,6},{5,3},{7,5},{8,10},{10,12},{11,9},{12,14},... | collective-permute-start | bytes 356360 | tf_op jit(solution)/shard_map/ppermute | solution.py:384
  19.5 2.1 %collective-permute-start.7 = (f32[232,128]{1,0:T(8,128)S(1)}, f32[232,128]{1,0:T(8,128)S(1)}, u32[]{:S(2)}, u32[]{:S(2)}) collective-permute-start(f32[232,128]{1,0:T(8,128)S(1)} %get-tuple-element.23), channel_id=1, source_target_pairs={{1,2},{2,1},{3,4},{4,3},{5,6},{6,5},{9,10},{10,9},{11,12},{12,11},... | collective-permute-start | bytes 356360 | tf_op jit(solution)/shard_map/ppermute | solution.py:384
  21.5 0.5 %collective-permute-done.6.near = f32[232,128]{1,0:T(8,128)S(1)} collective-permute-done((f32[232,128]{1,0:T(8,128)S(1)}, f32[232,128]{1,0:T(8,128)S(1)}, u32[]{:S(2)}, u32[]{:S(2)}) %collective-permute-start.6) | collective-permute-done | bytes 118816 | tf_op jit(solution)/shard_map/ppermute | solution.py:384
  22.0 4.1 %collective-permute-done.7.far = f32[232,128]{1,0:T(8,128)S(1)} collective-permute-done((f32[232,128]{1,0:T(8,128)S(1)}, f32[232,128]{1,0:T(8,128)S(1)}, u32[]{:S(2)}, u32[]{:S(2)}) %collective-permute-start.7) | collective-permute-done | bytes 118816 | tf_op jit(solution)/shard_map/ppermute | solution.py:384
  26.1 2.4 %first_steps.1 = (f32[2,144,128]{2,1,0:T(8,128)S(1)}, f32[2,144,128]{2,1,0:T(8,128)S(1)}, f32[2,9,2,16,128]{4,3,2,1,0:T(8,128)S(1)}, f32[2,3,6,16,128]{4,3,2,1,0:T(8,128)S(1)}, f32[6,16,128]{2,1,0:T(8,128)S(1)}) custom-call(f32[11,72,128]{2,1,0:T(8,128)S(1)} %get-tuple-element.20.kept, f32[11,72,128]{2,1,0:T(8,128)S(1)} %collective-permute-done.5.swapped, ...), custom_call_target="tpu_custom_call" | custom-call | flops 10000000 | bytes 1048576 | tf_op jit(solution)/shard_map/first_steps/pallas_call | solution.py:349
  28.5 0.2 collective-permute-start.8
  28.7 2.2 %collective-permute-start.9 = (f32[2,144,128]{2,1,0:T(8,128)S(1)}, f32[2,144,128]{2,1,0:T(8,128)S(1)}, u32[]{:S(2)}, u32[]{:S(2)}) collective-permute-start(f32[2,144,128]{2,1,0:T(8,128)S(1)} %get-tuple-element.26), channel_id=1, source_target_pairs={{8,16},{16,8},{9,17},{17,9},{10,18},{18,10},{11,19},{19,11},{12,20... | collective-permute-start | bytes 442376 | tf_op jit(solution)/shard_map/ppermute | solution.py:372
  30.9 1.6 %collective-permute-done.8.from_first = f32[2,144,128]{2,1,0:T(8,128)S(1)} collective-permute-done((f32[2,144,128]{2,1,0:T(8,128)S(1)}, f32[2,144,128]{2,1,0:T(8,128)S(1)}, u32[]{:S(2)}, u32[]{:S(2)}) %collective-permute-start.8) | collective-permute-done | bytes 147488 | tf_op jit(solution)/shard_map/ppermute | solution.py:372
  32.5 2.1 %collective-permute-done.9.from_second = f32[2,144,128]{2,1,0:T(8,128)S(1)} collective-permute-done((f32[2,144,128]{2,1,0:T(8,128)S(1)}, f32[2,144,128]{2,1,0:T(8,128)S(1)}, u32[]{:S(2)}, u32[]{:S(2)}) %collective-permute-start.9) | collective-permute-done | bytes 147488 | tf_op jit(solution)/shard_map/ppermute | solution.py:372
  34.6 1.2 %next_steps.1 = (f32[9,2,8,128]{3,2,1,0:T(8,128)S(1)}, f32[9,2,8,128]{3,2,1,0:T(8,128)S(1)}) custom-call(f32[2,9,2,16,128]{4,3,2,1,0:T(8,128)S(1)} %get-tuple-element.24.both_in, f32[2,144,128]{2,1,0:T(8,128)S(1)} %collective-permute-done.8.from_first, f32[2,144,128]{2,1,0:T(8,128)S(1)} %collective-permute-done.9.from_second, ...), custom_call_target="tpu_custom_call" | custom-call | flops 10000000 | bytes 1048576 | tf_op jit(solution)/shard_map/next_steps/pallas_call | solution.py:349
  35.8 2.8 %collective-permute-start.10 = (f32[9,2,8,128]{3,2,1,0:T(8,128)S(1)}, f32[9,2,8,128]{3,2,1,0:T(8,128)S(1)}, u32[]{:S(2)}, u32[]{:S(2)}) collective-permute-start(f32[9,2,8,128]{3,2,1,0:T(8,128)S(1)} %get-tuple-element.30), channel_id=1, source_target_pairs={{0,1},{1,0},{2,3},{3,2},{4,5},{5,4},{6,7},{7,6},{8,9},{9,8},{10,11... | collective-permute-start | bytes 221192 | tf_op jit(solution)/shard_map/ppermute | solution.py:387
  38.6 0.9 %collective-permute-done.10.brought = f32[9,2,8,128]{3,2,1,0:T(8,128)S(1)} collective-permute-done((f32[9,2,8,128]{3,2,1,0:T(8,128)S(1)}, f32[9,2,8,128]{3,2,1,0:T(8,128)S(1)}, u32[]{:S(2)}, u32[]{:S(2)}) %collective-permute-start.10) | collective-permute-done | bytes 73760 | tf_op jit(solution)/shard_map/ppermute | solution.py:387
  39.5 0.7 %home.1 = f32[1,9,2,16,128]{4,3,2,1,0:T(8,128)} custom-call(f32[9,2,8,128]{3,2,1,0:T(8,128)S(1)} %get-tuple-element.29.mine, f32[9,2,8,128]{3,2,1,0:T(8,128)S(1)} %collective-permute-done.10.brought), custom_call_target="tpu_custom_call" | custom-call | flops 10000000 | bytes 1048576 | tf_op jit(solution)/shard_map/home/pallas_call | solution.py:349
  (14 shorter events, 0.0 us)
Async XLA Ops:
  2.0 6.9 %collective-permute-start.4 = (f32[64,128]{1,0:T(8,128)}, f32[64,128]{1,0:T(8,128)S(1)}, u32[]{:S(2)}, u32[]{:S(2)}) collective-permute-start(f32[64,128]{1,0:T(8,128)} %get-tuple-element.19.refs_3_), channel_id=1, source_target_pairs={{24,0},{16,8},{8,16},{0,24},{25,1},{17,9},{9,17},{1,25},{26,2},{18... | collective-permute-start | bytes 98312 | tf_op jit(solution)/shard_map/ppermute | solution.py:405
  3.4 5.5 %collective-permute-start.3 = (f32[64,128]{1,0:T(8,128)}, f32[64,128]{1,0:T(8,128)S(1)}, u32[]{:S(2)}, u32[]{:S(2)}) collective-permute-start(f32[64,128]{1,0:T(8,128)} %get-tuple-element.19.refs_3_), channel_id=1, source_target_pairs={{16,0},{24,8},{0,16},{8,24},{17,1},{25,9},{1,17},{9,25},{18,2},{26... | collective-permute-start | bytes 98312 | tf_op jit(solution)/shard_map/ppermute | solution.py:405
  4.5 4.4 %collective-permute-start.2 = (f32[64,128]{1,0:T(8,128)}, f32[64,128]{1,0:T(8,128)S(1)}, u32[]{:S(2)}, u32[]{:S(2)}) collective-permute-start(f32[64,128]{1,0:T(8,128)} %get-tuple-element.19.refs_3_), channel_id=1, source_target_pairs={{8,0},{0,8},{24,16},{16,24},{9,1},{1,9},{25,17},{17,25},{10,2},{2,... | collective-permute-start | bytes 98312 | tf_op jit(solution)/shard_map/ppermute | solution.py:405
  5.6 8.1 %copy-start = (f32[11,2,16,128]{3,2,1,0:T(8,128)S(1)}, f32[11,2,16,128]{3,2,1,0:T(8,128)}, u32[]{:S(2)}) copy-start(f32[11,2,16,128]{3,2,1,0:T(8,128)} %get-tuple-element.18.packed) | copy-start | bytes 540676
  5.6 7.0 %collective-permute-start.1 = (f32[11,2,16,128]{3,2,1,0:T(8,128)}, f32[11,2,16,128]{3,2,1,0:T(8,128)S(1)}, u32[]{:S(2)}, u32[]{:S(2)}) collective-permute-start(f32[11,2,16,128]{3,2,1,0:T(8,128)} %get-tuple-element.18.packed), channel_id=1, source_target_pairs={{8,16},{16,8},{9,17},{17,9},{10,18},{18,10},{11,19},{19,11},{12,20... | collective-permute-start | bytes 540680 | tf_op jit(solution)/shard_map/ppermute | solution.py:372
  8.8 4.9 %collective-permute-start = (f32[11,2,16,128]{3,2,1,0:T(8,128)}, f32[11,2,16,128]{3,2,1,0:T(8,128)S(1)}, u32[]{:S(2)}, u32[]{:S(2)}) collective-permute-start(f32[11,2,16,128]{3,2,1,0:T(8,128)} %get-tuple-element.18.packed), channel_id=1, source_target_pairs={{0,8},{16,24},{8,0},{24,16},{1,9},{17,25},{9,1},{25,17},{2,10},{18... | collective-permute-start | bytes 540680 | tf_op jit(solution)/shard_map/ppermute | solution.py:372
  8.9 0.8 %copy-start.4 = (f32[64,128]{1,0:T(8,128)S(1)}, f32[64,128]{1,0:T(8,128)}, u32[]{:S(2)}) copy-start(f32[64,128]{1,0:T(8,128)} %get-tuple-element.19.refs_3_) | copy-start | bytes 98308
  13.9 12.1 %collective-permute-start.5 = (f32[11,72,128]{2,1,0:T(8,128)S(1)}, f32[11,72,128]{2,1,0:T(8,128)S(1)}, u32[]{:S(2)}, u32[]{:S(2)}) collective-permute-start(f32[11,72,128]{2,1,0:T(8,128)S(1)} %get-tuple-element.21), channel_id=1, source_target_pairs={{0,1},{1,0},{2,3},{3,2},{4,5},{5,4},{6,7},{7,6},{8,9},{9,8},{10,11... | collective-permute-start | bytes 1216520 | tf_op jit(solution)/shard_map/ppermute | solution.py:387
  16.4 5.6 %collective-permute-start.6 = (f32[232,128]{1,0:T(8,128)S(1)}, f32[232,128]{1,0:T(8,128)S(1)}, u32[]{:S(2)}, u32[]{:S(2)}) collective-permute-start(f32[232,128]{1,0:T(8,128)S(1)} %get-tuple-element.22), channel_id=1, source_target_pairs={{0,2},{2,4},{3,1},{4,6},{5,3},{7,5},{8,10},{10,12},{11,9},{12,14},... | collective-permute-start | bytes 356360 | tf_op jit(solution)/shard_map/ppermute | solution.py:384
  19.4 6.6 %copy-start.1 = (f32[16]{0:T(128)S(1)}, f32[16]{0:T(128)}, u32[]{:S(2)}) copy-start(f32[16]{0:T(128)} %buoyancy.1) | copy-start | bytes 196
  19.4 6.6 %copy-start.2 = (f32[16]{0:T(128)S(1)}, f32[16]{0:T(128)}, u32[]{:S(2)}) copy-start(f32[16]{0:T(128)} %lame_lambda.1) | copy-start | bytes 196
  19.4 6.6 %copy-start.3 = (f32[16]{0:T(128)S(1)}, f32[16]{0:T(128)}, u32[]{:S(2)}) copy-start(f32[16]{0:T(128)} %lame_mu.1) | copy-start | bytes 196
  19.5 6.6 %collective-permute-start.7 = (f32[232,128]{1,0:T(8,128)S(1)}, f32[232,128]{1,0:T(8,128)S(1)}, u32[]{:S(2)}, u32[]{:S(2)}) collective-permute-start(f32[232,128]{1,0:T(8,128)S(1)} %get-tuple-element.23), channel_id=1, source_target_pairs={{1,2},{2,1},{3,4},{4,3},{5,6},{6,5},{9,10},{10,9},{11,12},{12,11},... | collective-permute-start | bytes 356360 | tf_op jit(solution)/shard_map/ppermute | solution.py:384
  28.5 4.1 %collective-permute-start.8 = (f32[2,144,128]{2,1,0:T(8,128)S(1)}, f32[2,144,128]{2,1,0:T(8,128)S(1)}, u32[]{:S(2)}, u32[]{:S(2)}) collective-permute-start(f32[2,144,128]{2,1,0:T(8,128)S(1)} %get-tuple-element.25), channel_id=1, source_target_pairs={{0,8},{16,24},{8,0},{24,16},{1,9},{17,25},{9,1},{25,17},{2,10},{18... | collective-permute-start | bytes 442376 | tf_op jit(solution)/shard_map/ppermute | solution.py:372
  28.7 5.9 %collective-permute-start.9 = (f32[2,144,128]{2,1,0:T(8,128)S(1)}, f32[2,144,128]{2,1,0:T(8,128)S(1)}, u32[]{:S(2)}, u32[]{:S(2)}) collective-permute-start(f32[2,144,128]{2,1,0:T(8,128)S(1)} %get-tuple-element.26), channel_id=1, source_target_pairs={{8,16},{16,8},{9,17},{17,9},{10,18},{18,10},{11,19},{19,11},{12,20... | collective-permute-start | bytes 442376 | tf_op jit(solution)/shard_map/ppermute | solution.py:372
  35.8 3.7 %collective-permute-start.10 = (f32[9,2,8,128]{3,2,1,0:T(8,128)S(1)}, f32[9,2,8,128]{3,2,1,0:T(8,128)S(1)}, u32[]{:S(2)}, u32[]{:S(2)}) collective-permute-start(f32[9,2,8,128]{3,2,1,0:T(8,128)S(1)} %get-tuple-element.30), channel_id=1, source_target_pairs={{0,1},{1,0},{2,3},{3,2},{4,5},{5,4},{6,7},{7,6},{8,9},{9,8},{10,11... | collective-permute-start | bytes 221192 | tf_op jit(solution)/shard_map/ppermute | solution.py:387

commit v6 on v5

--- a/solution.py
+++ b/solution.py
@@ -39,39 +39,41 @@
 
 def pack_kernel(layout, fields_in, ids_in, moments_in, owner_in, cells_in, rows_in, packed, entries, *scratch):
     cx, cz, cy = layout
-    ids, moments, owner, cells, rows, sem = scratch
-    lines = cx * cz
-    copies = [(ids_in, ids), (moments_in, moments), (owner_in, owner), (cells_in, cells), (rows_in, rows)]
-    copies += [(fields_in.at[0], packed.at[pl.ds(0, 9)])]
-    copy_all(sem, copies)
-    packed[9] = (ids[0] + 1).astype(F32)
+    ids, moments, owner, cells, rows, extra, lines, sem = scratch
+    arguments = [(ids_in, ids), (moments_in, moments), (owner_in, owner), (cells_in, cells), (rows_in, rows)]
+    fields = pltpu.make_async_copy(fields_in.at[0], packed.at[pl.ds(0, 9)], sem.at[5])
+    fields.start()
+    copy_all(sem, arguments)
+    for i in range(cells.shape[0]):
+        at = 8 * i
+        lines[at : at + 6] = moments[:, i * cy : (i + 1) * cy]
+        lines[at + 6 : at + 7] = owner[i : i + 1, :].astype(F32)
+        lines[at + 7 : at + 8] = cells[i : i + 1, :].astype(F32)
+    sent = pltpu.make_async_copy(lines, entries, sem.at[6])
+    sent.start()
+    extra[0] = (ids[0] + 1).astype(F32)
     line = in_line(rows[...])
-    high = one_hot(line // cy, lines).astype(BF16)
+    high = one_hot(line // cy, cx * cz).astype(BF16)
     low = one_hot(line % cy, cy).astype(BF16)
     count = lax.dot_general(high, low, NT, preferred_element_type=F32)
-    packed[10] = count.reshape(cx, cz, cy)
-    for i in range(cells.shape[0]):
-        at = 8 * i
-        entries[at : at + 6] = moments[:, i * cy : (i + 1) * cy]
-        entries[at + 6 : at + 7] = owner[i : i + 1, :].astype(F32)
-        entries[at + 7 : at + 8] = cells[i : i + 1, :].astype(F32)
+    extra[1] = count.reshape(cx, cz, cy)
+    added = pltpu.make_async_copy(extra, packed.at[pl.ds(9, 2)], sem.at[7])
+    added.start()
+    for copy in (fields, sent, added):
+        copy.wait()
 
 
 def moment_kernel(layout, *refs):
     cx, cz, cy = layout
-    blocks, own_in, dense, acc, own, sem = refs[:-5], *refs[-5:]
+    blocks, dense, acc = refs[:-2], *refs[-2:]
     section = lax.axis_index("sec")
     planes = 3 * cx
     half = planes * cz // 2
 
     @pl.when(lax.axis_index("segment") == 0)
     def _():
-        copy = pltpu.make_async_copy(own_in, own, sem.at[0])
-        copy.start()
         acc[...] = jnp.zeros_like(acc)
-        for entries in (*blocks, own):
-            if entries is own:
-                copy.wait()
+        for entries in blocks:
             groups = entries.shape[0] // 8
             chunk = [entries[8 * i : 8 * i + 8] for i in range(groups)]
             entry = jnp.concatenate(chunk, axis=1)
@@ -122,14 +124,16 @@
         wide[3:9] = wide[3:9] + dense[...]
 
     def cut(to, first, count):
+        comps = to.shape[0]
         for x in range(planes):
-            to[:, x * count : (x + 1) * count] = wide[:, x, first : first + count]
+            to[:, x * count : (x + 1) * count] = wide[0:comps, x, first : first + count]
 
     def cut_halo(to, upward):
         spans, lines = halo_rows(cx, upward)
+        comps = to.shape[0] // lines
         for x, at, rows in spans:
             first = cz - rows if upward else 0
-            for k in range(11):
+            for k in range(comps):
                 to[k * lines + at : k * lines + at + rows] = wide[k, x, first : first + rows]
 
     reach = cz // 2 + STEPS
@@ -147,6 +151,10 @@
         cut(swapped, 0, reach)
         cut_halo(near, False)
         cut_halo(far, True)
+
+
+def hold_kernel(block, after, same):
+    pass
 
 
 def halo_rows(cx, upward):
@@ -215,24 +223,31 @@
 
 
 def first_kernel(
-    cx, steps, kept, swapped, near, far, buoyancy, lame_lambda, lame_mu,
+    cx, steps, kept, near, far, swapped, buoyancy, lame_lambda, lame_mu,
     to_first, to_second, both, coef, times, state, tables, sem,
 ):
     segment = lax.axis_index("segment")
     planes, rows, cy = state.shape[2:]
     reach = rows - STEPS
-    copy_all(sem, [(t, tables.at[i]) for i, t in enumerate((buoyancy, lame_lambda, lame_mu))])
+    copies = [
+        pltpu.make_async_copy(table, tables.at[i], sem.at[i])
+        for i, table in enumerate((buoyancy, lame_lambda, lame_mu))
+    ]
+    for copy in copies:
+        copy.start()
 
     def join(model, body, halo, upper):
         spans, lines = halo_rows(cx, upper)
         for x, at, count in spans:
             inner = slice(x * reach, (x + 1) * reach)
-            first = STEPS if upper else 0
-            state[model, :, x, first : first + reach] = body[:, inner]
-            first = STEPS - count if upper else reach
-            for k in range(11):
-                outer = slice(k * lines + at, k * lines + at + count)
-                state[model, k, x, first : first + count] = halo[outer]
+            to = slice(STEPS, rows) if upper else slice(0, reach)
+            edge = slice(STEPS - count, STEPS) if upper else slice(reach, reach + count)
+            state[model, :, x, to] = body[0:10, inner]
+            for k in range(10):
+                state[model, k, x, edge] = halo[k * lines + at : k * lines + at + count]
+            if body.shape[0] == 11:
+                times[x, to] = body[10, inner]
+                times[x, edge] = halo[10 * lines + at : 10 * lines + at + count]
 
     @pl.when(segment == 0)
     def _():
@@ -243,6 +258,9 @@
     def _():
         join(1, kept, near, False)
         join(0, swapped, far, False)
+
+    for copy in copies:
+        copy.wait()
 
     @pl.loop(0, planes)
     def _(x):
@@ -256,7 +274,6 @@
                 ]
             for i in range(3):
                 coef[model, i, x] = found[i]
-        times[x] = state[1, 10, x]
 
     velocity = advance(cx, steps, state, coef, times)
     both[...] = state[:, 0:9, cx : 2 * cx]
@@ -342,15 +359,16 @@
 
 VMEM = pl.BlockSpec(memory_space=pltpu.VMEM)
 HBM = pl.BlockSpec(memory_space=pltpu.HBM)
-
-
-def call(kernel, name, in_hbm, in_vmem, outs, scratch, copies=0, limit=40 * 2**20, flops=10**7):
+ANY = pl.BlockSpec(memory_space=pl.ANY)
+
+
+def call(kernel, name, in_hbm, in_vmem, outs, scratch, copies=0, limit=40 * 2**20, flops=10**7, out_space=VMEM):
     sems = [pltpu.SemaphoreType.DMA((copies,))] * (copies > 0)
     return pl.pallas_call(
         kernel,
         out_shape=[jax.ShapeDtypeStruct(shape, F32) for shape in outs],
         in_specs=[VMEM] * len(in_vmem) + [HBM] * len(in_hbm),
-        out_specs=[VMEM] * len(outs),
+        out_specs=[out_space] * len(outs),
         scratch_shapes=scratch + sems,
         compiler_params=pltpu.CompilerParams(vmem_limit_bytes=limit),
         cost_estimate=pl.CostEstimate(flops=flops, bytes_accessed=2**20, transcendentals=0),
@@ -397,9 +415,11 @@
         (fields, *small),
         (),
         [(11, cx, cz, cy), (entry_lines, cy)],
-        [pltpu.VMEM(a.shape, a.dtype) for a in small],
-        len(small) + 1,
+        [pltpu.VMEM(a.shape, a.dtype) for a in small]
+        + [pltpu.VMEM((2, cx, cz, cy), F32), pltpu.VMEM((entry_lines, cy), F32)],
+        8,
         limit=64 * 2**20,
+        out_space=HBM,
     )
     blocks = [
         lax.ppermute(entries, "sec", [(other(i, k), i) for i in range(sections)])
@@ -407,15 +427,17 @@
     ]
     first, second = pairs(packed, 0), pairs(packed, 1)
     half = planes * cz // 2
-    halo_lines = -(-11 * halo_rows(cx, True)[1] // 8) * 8
+
+    def halo_shape(comps):
+        return (-(-comps * halo_rows(cx, True)[1] // 8) * 8, cy)
+
     (dense,) = call(
         functools.partial(moment_kernel, layout),
         "moments",
-        (entries,),
-        blocks,
+        (),
+        [entries, *blocks],
         [(6, planes, cz, cy)],
-        [pltpu.VMEM((6 * half, 2 * cy), F32), pltpu.VMEM((entry_lines, cy), F32)],
-        1,
+        [pltpu.VMEM((6 * half, 2 * cy), F32)],
         flops=2 * 18 * half * 2 * cy * sections * moments.shape[1],
     )
     kept, swapped, near, far = call(
@@ -423,10 +445,19 @@
         "widen",
         (),
         (packed, first, second, dense),
-        [(11, planes * reach, cy)] * 2 + [(halo_lines, cy)] * 2,
+        [(11, planes * reach, cy), (10, planes * reach, cy), halo_shape(11), halo_shape(10)],
         [pltpu.VMEM((11, planes, cz, cy), F32)],
     )
-    near, far, swapped = halo(near, 1, False), halo(far, -1, True), swap(swapped)
+    near, far = halo(near, 1, False), halo(far, -1, True)
+    swapped = pl.pallas_call(
+        hold_kernel,
+        out_shape=jax.ShapeDtypeStruct(swapped.shape, F32),
+        in_specs=[ANY, ANY],
+        out_specs=ANY,
+        input_output_aliases={0: 0},
+        name="hold",
+    )(swapped, near)
+    swapped = swap(swapped)
     both_shape = (2, 9, cx, rows, cy)
     coef_shape, times_shape = (2, 3, planes, rows, cy), (planes, rows, cy)
 
@@ -438,10 +469,10 @@
         functools.partial(first_kernel, cx, cx),
         "first_steps",
         (buoyancy, lame_lambda, lame_mu),
-        (kept, swapped, near, far),
+        (kept, near, far, swapped),
         [edge_shape(done)] * 2 + [both_shape, coef_shape, times_shape],
         [
-            pltpu.VMEM((2, 11, planes, rows, cy), F32),
+            pltpu.VMEM((2, 10, planes, rows, cy), F32),
             pltpu.SMEM((3, buoyancy.shape[0]), F32),
         ],
         3,

time: 40.6 us -> 50 us (1.23)
  Pallas kernels: 6.47 us -> 9.9 us
  waiting for transfers between devices: 13.2 us -> 15.9 us
  local copies, waits for them, and re-layouts: 0.78 us -> 3.04 us
  starting transfers between devices: 19.6 us -> 20.7 us
    pallas_call x6, Pallas kernels: 6.47 us -> 9.9 us  [call(): pl.pallas_call(kernel, out_shape=[jax.ShapeDtypeStruct(shape, F32) for sh...]
    unnamed x10 -> x16, local copies, waits for them, and re-layouts: 0.78 us -> 3.04 us
    ppermute x2, waiting for transfers between devices: 4.52 us -> 6.73 us  [halo(): return lax.ppermute(block, ('depth', 'segment'), route)]
    ppermute x2, starting transfers between devices: 5.26 us -> 6.26 us  [swap(): return lax.ppermute(block, 'segment', [(0, 1), (1, 0)])]
where the time goes in v6:
time: 50 us; the launch traced here: 49.7 us
  starting transfers between devices  20.7 us (41%)
  waiting for transfers between devices  15.9 us (32%)
  Pallas kernels  9.9 us (20%)
  local copies, waits for them, and re-layouts  3.04 us (6%)
    pallas_call x6, Pallas kernels, call(): pl.pallas_call(kernel, out_shape=[jax.ShapeDtypeStruct(shape, F32) for sh...  9.9 us
    ppermute x4, waiting for transfers between devices, pairs(): return lax.ppermute(block, 'sec', route + [(j, i) for i, j in route])  8.24 us
    ppermute x2, waiting for transfers between devices, halo(): return lax.ppermute(block, ('depth', 'segment'), route)  6.73 us
    ppermute x2, starting transfers between devices, swap(): return lax.ppermute(block, 'segment', [(0, 1), (1, 0)])  6.26 us
    ppermute x4, starting transfers between devices, pairs(): return lax.ppermute(block, 'sec', route + [(j, i) for i, j in route])  5.55 us
    ppermute x2, starting transfers between devices, halo(): return lax.ppermute(block, ('depth', 'segment'), route)  5.3 us
    ppermute x3, starting transfers between devices, on_device(): lax.ppermute(entries, 'sec', [(other(i, k), i) for i in range(sections)])  3.56 us
    unnamed x16, local copies, waits for them, and re-layouts  3.04 us
  transfers between devices with their start and end apart: 11, of which 7 were waited for; matrix products, arithmetic and copies ran while one was open for 0% of the time, Pallas kernels for 0%

profile of v6, /device:TPU:13, one launch (start us, length us, event | category | flops | bytes accessed | tf_op | source)
XLA Modules:
  0.0 49.7 jit_solution(2905354229054048830)
XLA Ops:
  0.0 5.6 %pack.1 = (f32[11,2,16,128]{3,2,1,0:T(8,128)}, f32[64,128]{1,0:T(8,128)}) custom-call(f32[1,9,2,16,128]{4,3,2,1,0:T(8,128)} %fields_in.1, s32[1,2,16,128]{3,2,1,0:T(8,128)} %ids_in.1, f32[6,1024]{1,0:T(8,128)} %moments_in.1, s32[8,128]{1,0:T(8,128)} %bitcast.4, s32[8,128]{1,0:T(8,128)} %bitcast.5, s32[16,128]{1,0:T(8,128)} %bitcast.3), custom_call_target="tpu_custom_call" | custom-call | flops 10000000 | bytes 1048576 | tf_op jit(solution)/shard_map/pack/pallas_call | solution.py:367
  5.6 1.4 %collective-permute-start.4 = (f32[64,128]{1,0:T(8,128)}, f32[64,128]{1,0:T(8,128)S(1)}, u32[]{:S(2)}, u32[]{:S(2)}) collective-permute-start(f32[64,128]{1,0:T(8,128)} %get-tuple-element.19.refs_0_), channel_id=1, source_target_pairs={{24,0},{16,8},{8,16},{0,24},{25,1},{17,9},{9,17},{1,25},{26,2},{18... | collective-permute-start | bytes 98312 | tf_op jit(solution)/shard_map/ppermute | solution.py:425
  7.0 1.1 %collective-permute-start.3 = (f32[64,128]{1,0:T(8,128)}, f32[64,128]{1,0:T(8,128)S(1)}, u32[]{:S(2)}, u32[]{:S(2)}) collective-permute-start(f32[64,128]{1,0:T(8,128)} %get-tuple-element.19.refs_0_), channel_id=1, source_target_pairs={{16,0},{24,8},{0,16},{8,24},{17,1},{25,9},{1,17},{9,25},{18,2},{26... | collective-permute-start | bytes 98312 | tf_op jit(solution)/shard_map/ppermute | solution.py:425
  8.1 1.1 %collective-permute-start.2 = (f32[64,128]{1,0:T(8,128)}, f32[64,128]{1,0:T(8,128)S(1)}, u32[]{:S(2)}, u32[]{:S(2)}) collective-permute-start(f32[64,128]{1,0:T(8,128)} %get-tuple-element.19.refs_0_), channel_id=1, source_target_pairs={{8,0},{0,8},{24,16},{16,24},{9,1},{1,9},{25,17},{17,25},{10,2},{2,... | collective-permute-start | bytes 98312 | tf_op jit(solution)/shard_map/ppermute | solution.py:425
  9.2 3.2 %collective-permute-start.1 = (f32[11,2,16,128]{3,2,1,0:T(8,128)}, f32[11,2,16,128]{3,2,1,0:T(8,128)S(1)}, u32[]{:S(2)}, u32[]{:S(2)}) collective-permute-start(f32[11,2,16,128]{3,2,1,0:T(8,128)} %get-tuple-element.18.packed), channel_id=1, source_target_pairs={{8,16},{16,8},{9,17},{17,9},{10,18},{18,10},{11,19},{19,11},{12,20... | collective-permute-start | bytes 540680 | tf_op jit(solution)/shard_map/ppermute | solution.py:390
  12.6 0.7 %copy-done.7 = f32[64,128]{1,0:T(8,128)S(1)} copy-done((f32[64,128]{1,0:T(8,128)S(1)}, f32[64,128]{1,0:T(8,128)}, u32[]{:S(2)}) %copy-start.7) | copy-done | bytes 32792
  13.3 2.9 %collective-permute-done.1.second = f32[11,2,16,128]{3,2,1,0:T(8,128)S(1)} collective-permute-done((f32[11,2,16,128]{3,2,1,0:T(8,128)}, f32[11,2,16,128]{3,2,1,0:T(8,128)S(1)}, u32[]{:S(2)}, u32[]{:S(2)}) %collective-permute-start.1) | collective-permute-done | bytes 180256 | tf_op jit(solution)/shard_map/ppermute | solution.py:390
  16.2 1.1 %collective-permute-done.first = f32[11,2,16,128]{3,2,1,0:T(8,128)S(1)} collective-permute-done((f32[11,2,16,128]{3,2,1,0:T(8,128)}, f32[11,2,16,128]{3,2,1,0:T(8,128)S(1)}, u32[]{:S(2)}, u32[]{:S(2)}) %collective-permute-start) | collective-permute-done | bytes 180256 | tf_op jit(solution)/shard_map/ppermute | solution.py:390
  17.5 0.7 %copy-done.2 = f32[10,72,128]{2,1,0:T(8,128)} copy-done((f32[10,72,128]{2,1,0:T(8,128)}, f32[10,72,128]{2,1,0:T(8,128)S(1)}, u32[]{:S(2)}) %copy-start.2) | copy-done | bytes 368664
  18.2 3.0 %collective-permute-start.5 = (f32[232,128]{1,0:T(8,128)S(1)}, f32[232,128]{1,0:T(8,128)S(1)}, u32[]{:S(2)}, u32[]{:S(2)}) collective-permute-start(f32[232,128]{1,0:T(8,128)S(1)} %get-tuple-element.21), channel_id=1, source_target_pairs={{0,2},{2,4},{3,1},{4,6},{5,3},{7,5},{8,10},{10,12},{11,9},{12,14},... | collective-permute-start | bytes 356360 | tf_op jit(solution)/shard_map/ppermute | solution.py:402
  21.3 2.5 %collective-permute-done.5.after.near = f32[232,128]{1,0:T(8,128)S(1)} collective-permute-done((f32[232,128]{1,0:T(8,128)S(1)}, f32[232,128]{1,0:T(8,128)S(1)}, u32[]{:S(2)}, u32[]{:S(2)}) %collective-permute-start.5) | collective-permute-done | bytes 118816 | tf_op jit(solution)/shard_map/ppermute | solution.py:402
  23.8 0.6 %copy-done = f32[232,128]{1,0:T(8,128)} copy-done((f32[232,128]{1,0:T(8,128)}, f32[232,128]{1,0:T(8,128)S(1)}, u32[]{:S(2)}) %copy-start) | copy-done | bytes 118808
  24.5 4.4 %collective-permute-start.7 = (f32[10,72,128]{2,1,0:T(8,128)}, f32[10,72,128]{2,1,0:T(8,128)S(1)}, u32[]{:S(2)}, u32[]{:S(2)}) collective-permute-start(f32[10,72,128]{2,1,0:T(8,128)} %hold.1), channel_id=1, source_target_pairs={{0,1},{1,0},{2,3},{3,2},{4,5},{5,4},{6,7},{7,6},{8,9},{9,8},{10,11... | collective-permute-start | bytes 1105928 | tf_op jit(solution)/shard_map/ppermute | solution.py:405
  28.9 2.3 %collective-permute-start.6 = (f32[216,128]{1,0:T(8,128)S(1)}, f32[216,128]{1,0:T(8,128)S(1)}, u32[]{:S(2)}, u32[]{:S(2)}) collective-permute-start(f32[216,128]{1,0:T(8,128)S(1)} %get-tuple-element.22), channel_id=1, source_target_pairs={{1,2},{2,1},{3,4},{4,3},{5,6},{6,5},{9,10},{10,9},{11,12},{12,11},... | collective-permute-start | bytes 331784 | tf_op jit(solution)/shard_map/ppermute | solution.py:402
  31.2 4.2 %collective-permute-done.6.far = f32[216,128]{1,0:T(8,128)S(1)} collective-permute-done((f32[216,128]{1,0:T(8,128)S(1)}, f32[216,128]{1,0:T(8,128)S(1)}, u32[]{:S(2)}, u32[]{:S(2)}) %collective-permute-start.6) | collective-permute-done | bytes 110624 | tf_op jit(solution)/shard_map/ppermute | solution.py:402
  35.4 0.9 %copy-done.1 = f32[232,128]{1,0:T(8,128)S(1)} copy-done((f32[232,128]{1,0:T(8,128)S(1)}, f32[232,128]{1,0:T(8,128)}, u32[]{:S(2)}) %copy-start.1) | copy-done | bytes 118808
  36.3 2.3 %first_steps.1 = (f32[2,144,128]{2,1,0:T(8,128)S(1)}, f32[2,144,128]{2,1,0:T(8,128)S(1)}, f32[2,9,2,16,128]{4,3,2,1,0:T(8,128)S(1)}, f32[2,3,6,16,128]{4,3,2,1,0:T(8,128)S(1)}, f32[6,16,128]{2,1,0:T(8,128)S(1)}) custom-call(f32[11,72,128]{2,1,0:T(8,128)S(1)} %get-tuple-element.20.kept, f32[232,128]{1,0:T(8,128)S(1)} %copy-done.1, ...), custom_call_target="tpu_custom_call" | custom-call | flops 10000000 | bytes 1048576 | tf_op jit(solution)/shard_map/first_steps/pallas_call | solution.py:367
  38.7 2.2 %collective-permute-start.9 = (f32[2,144,128]{2,1,0:T(8,128)S(1)}, f32[2,144,128]{2,1,0:T(8,128)S(1)}, u32[]{:S(2)}, u32[]{:S(2)}) collective-permute-start(f32[2,144,128]{2,1,0:T(8,128)S(1)} %get-tuple-element.26), channel_id=1, source_target_pairs={{8,16},{16,8},{9,17},{17,9},{10,18},{18,10},{11,19},{19,11},{12,20... | collective-permute-start | bytes 442376 | tf_op jit(solution)/shard_map/ppermute | solution.py:390
  40.9 2.5 %collective-permute-done.8.from_first = f32[2,144,128]{2,1,0:T(8,128)S(1)} collective-permute-done((f32[2,144,128]{2,1,0:T(8,128)S(1)}, f32[2,144,128]{2,1,0:T(8,128)S(1)}, u32[]{:S(2)}, u32[]{:S(2)}) %collective-permute-start.8) | collective-permute-done | bytes 147488 | tf_op jit(solution)/shard_map/ppermute | solution.py:390
  43.4 1.6 %collective-permute-done.9.from_second = f32[2,144,128]{2,1,0:T(8,128)S(1)} collective-permute-done((f32[2,144,128]{2,1,0:T(8,128)S(1)}, f32[2,144,128]{2,1,0:T(8,128)S(1)}, u32[]{:S(2)}, u32[]{:S(2)}) %collective-permute-start.9) | collective-permute-done | bytes 147488 | tf_op jit(solution)/shard_map/ppermute | solution.py:390
  45.1 1.2 %next_steps.1 = (f32[9,2,8,128]{3,2,1,0:T(8,128)S(1)}, f32[9,2,8,128]{3,2,1,0:T(8,128)S(1)}) custom-call(f32[2,9,2,16,128]{4,3,2,1,0:T(8,128)S(1)} %get-tuple-element.24.both_in, f32[2,144,128]{2,1,0:T(8,128)S(1)} %collective-permute-done.8.from_first, f32[2,144,128]{2,1,0:T(8,128)S(1)} %collective-permute-done.9.from_second, ...), custom_call_target="tpu_custom_call" | custom-call | flops 10000000 | bytes 1048576 | tf_op jit(solution)/shard_map/next_steps/pallas_call | solution.py:367
  46.3 1.8 %collective-permute-start.10 = (f32[9,2,8,128]{3,2,1,0:T(8,128)S(1)}, f32[9,2,8,128]{3,2,1,0:T(8,128)S(1)}, u32[]{:S(2)}, u32[]{:S(2)}) collective-permute-start(f32[9,2,8,128]{3,2,1,0:T(8,128)S(1)} %get-tuple-element.30), channel_id=1, source_target_pairs={{0,1},{1,0},{2,3},{3,2},{4,5},{5,4},{6,7},{7,6},{8,9},{9,8},{10,11... | collective-permute-start | bytes 221192 | tf_op jit(solution)/shard_map/ppermute | solution.py:405
  48.1 0.9 %collective-permute-done.10.brought = f32[9,2,8,128]{3,2,1,0:T(8,128)S(1)} collective-permute-done((f32[9,2,8,128]{3,2,1,0:T(8,128)S(1)}, f32[9,2,8,128]{3,2,1,0:T(8,128)S(1)}, u32[]{:S(2)}, u32[]{:S(2)}) %collective-permute-start.10) | collective-permute-done | bytes 73760 | tf_op jit(solution)/shard_map/ppermute | solution.py:405
  49.0 0.7 %home.1 = f32[1,9,2,16,128]{4,3,2,1,0:T(8,128)} custom-call(f32[9,2,8,128]{3,2,1,0:T(8,128)S(1)} %get-tuple-element.29.mine, f32[9,2,8,128]{3,2,1,0:T(8,128)S(1)} %collective-permute-done.10.brought), custom_call_target="tpu_custom_call" | custom-call | flops 10000000 | bytes 1048576 | tf_op jit(solution)/shard_map/home/pallas_call | solution.py:367
  (21 shorter events, 0.3 us)
Async XLA Ops:
  5.6 6.9 %collective-permute-start.4 = (f32[64,128]{1,0:T(8,128)}, f32[64,128]{1,0:T(8,128)S(1)}, u32[]{:S(2)}, u32[]{:S(2)}) collective-permute-start(f32[64,128]{1,0:T(8,128)} %get-tuple-element.19.refs_0_), channel_id=1, source_target_pairs={{24,0},{16,8},{8,16},{0,24},{25,1},{17,9},{9,17},{1,25},{26,2},{18... | collective-permute-start | bytes 98312 | tf_op jit(solution)/shard_map/ppermute | solution.py:425
  7.0 5.5 %collective-permute-start.3 = (f32[64,128]{1,0:T(8,128)}, f32[64,128]{1,0:T(8,128)S(1)}, u32[]{:S(2)}, u32[]{:S(2)}) collective-permute-start(f32[64,128]{1,0:T(8,128)} %get-tuple-element.19.refs_0_), channel_id=1, source_target_pairs={{16,0},{24,8},{0,16},{8,24},{17,1},{25,9},{1,17},{9,25},{18,2},{26... | collective-permute-start | bytes 98312 | tf_op jit(solution)/shard_map/ppermute | solution.py:425
  8.1 4.4 %collective-permute-start.2 = (f32[64,128]{1,0:T(8,128)}, f32[64,128]{1,0:T(8,128)S(1)}, u32[]{:S(2)}, u32[]{:S(2)}) collective-permute-start(f32[64,128]{1,0:T(8,128)} %get-tuple-element.19.refs_0_), channel_id=1, source_target_pairs={{8,0},{0,8},{24,16},{16,24},{9,1},{1,9},{25,17},{17,25},{10,2},{2,... | collective-permute-start | bytes 98312 | tf_op jit(solution)/shard_map/ppermute | solution.py:425
  9.2 8.1 %copy-start.3 = (f32[11,2,16,128]{3,2,1,0:T(8,128)S(1)}, f32[11,2,16,128]{3,2,1,0:T(8,128)}, u32[]{:S(2)}) copy-start(f32[11,2,16,128]{3,2,1,0:T(8,128)} %get-tuple-element.18.packed) | copy-start | bytes 540676
  9.2 7.0 %collective-permute-start.1 = (f32[11,2,16,128]{3,2,1,0:T(8,128)}, f32[11,2,16,128]{3,2,1,0:T(8,128)S(1)}, u32[]{:S(2)}, u32[]{:S(2)}) collective-permute-start(f32[11,2,16,128]{3,2,1,0:T(8,128)} %get-tuple-element.18.packed), channel_id=1, source_target_pairs={{8,16},{16,8},{9,17},{17,9},{10,18},{18,10},{11,19},{19,11},{12,20... | collective-permute-start | bytes 540680 | tf_op jit(solution)/shard_map/ppermute | solution.py:390
  12.4 4.9 %collective-permute-start = (f32[11,2,16,128]{3,2,1,0:T(8,128)}, f32[11,2,16,128]{3,2,1,0:T(8,128)S(1)}, u32[]{:S(2)}, u32[]{:S(2)}) collective-permute-start(f32[11,2,16,128]{3,2,1,0:T(8,128)} %get-tuple-element.18.packed), channel_id=1, source_target_pairs={{0,8},{16,24},{8,0},{24,16},{1,9},{17,25},{9,1},{25,17},{2,10},{18... | collective-permute-start | bytes 540680 | tf_op jit(solution)/shard_map/ppermute | solution.py:390
  12.5 0.8 %copy-start.7 = (f32[64,128]{1,0:T(8,128)S(1)}, f32[64,128]{1,0:T(8,128)}, u32[]{:S(2)}) copy-start(f32[64,128]{1,0:T(8,128)} %get-tuple-element.19.refs_0_) | copy-start | bytes 98308
  17.5 0.7 %copy-start.2 = (f32[10,72,128]{2,1,0:T(8,128)}, f32[10,72,128]{2,1,0:T(8,128)S(1)}, u32[]{:S(2)}) copy-start(f32[10,72,128]{2,1,0:T(8,128)S(1)} %get-tuple-element.23.block) | copy-start | bytes 1105924
  18.2 5.6 %collective-permute-start.5 = (f32[232,128]{1,0:T(8,128)S(1)}, f32[232,128]{1,0:T(8,128)S(1)}, u32[]{:S(2)}, u32[]{:S(2)}) collective-permute-start(f32[232,128]{1,0:T(8,128)S(1)} %get-tuple-element.21), channel_id=1, source_target_pairs={{0,2},{2,4},{3,1},{4,6},{5,3},{7,5},{8,10},{10,12},{11,9},{12,14},... | collective-permute-start | bytes 356360 | tf_op jit(solution)/shard_map/ppermute | solution.py:402
  23.8 0.6 %copy-start = (f32[232,128]{1,0:T(8,128)}, f32[232,128]{1,0:T(8,128)S(1)}, u32[]{:S(2)}) copy-start(f32[232,128]{1,0:T(8,128)S(1)} %collective-permute-done.5.after.near) | copy-start | bytes 356356
  24.5 10.9 %collective-permute-start.7 = (f32[10,72,128]{2,1,0:T(8,128)}, f32[10,72,128]{2,1,0:T(8,128)S(1)}, u32[]{:S(2)}, u32[]{:S(2)}) collective-permute-start(f32[10,72,128]{2,1,0:T(8,128)} %hold.1), channel_id=1, source_target_pairs={{0,1},{1,0},{2,3},{3,2},{4,5},{5,4},{6,7},{7,6},{8,9},{9,8},{10,11... | collective-permute-start | bytes 1105928 | tf_op jit(solution)/shard_map/ppermute | solution.py:405
  28.9 6.5 %copy-start.4 = (f32[16]{0:T(128)S(1)}, f32[16]{0:T(128)}, u32[]{:S(2)}) copy-start(f32[16]{0:T(128)} %buoyancy.1) | copy-start | bytes 196
  28.9 6.5 %copy-start.5 = (f32[16]{0:T(128)S(1)}, f32[16]{0:T(128)}, u32[]{:S(2)}) copy-start(f32[16]{0:T(128)} %lame_lambda.1) | copy-start | bytes 196
  28.9 6.5 %copy-start.6 = (f32[16]{0:T(128)S(1)}, f32[16]{0:T(128)}, u32[]{:S(2)}) copy-start(f32[16]{0:T(128)} %lame_mu.1) | copy-start | bytes 196
  28.9 6.5 %collective-permute-start.6 = (f32[216,128]{1,0:T(8,128)S(1)}, f32[216,128]{1,0:T(8,128)S(1)}, u32[]{:S(2)}, u32[]{:S(2)}) collective-permute-start(f32[216,128]{1,0:T(8,128)S(1)} %get-tuple-element.22), channel_id=1, source_target_pairs={{1,2},{2,1},{3,4},{4,3},{5,6},{6,5},{9,10},{10,9},{11,12},{12,11},... | collective-permute-start | bytes 331784 | tf_op jit(solution)/shard_map/ppermute | solution.py:402
  35.4 0.9 %copy-start.1 = (f32[232,128]{1,0:T(8,128)S(1)}, f32[232,128]{1,0:T(8,128)}, u32[]{:S(2)}) copy-start(f32[232,128]{1,0:T(8,128)} %copy-done) | copy-start | bytes 356356
  38.6 4.8 %collective-permute-start.8 = (f32[2,144,128]{2,1,0:T(8,128)S(1)}, f32[2,144,128]{2,1,0:T(8,128)S(1)}, u32[]{:S(2)}, u32[]{:S(2)}) collective-permute-start(f32[2,144,128]{2,1,0:T(8,128)S(1)} %get-tuple-element.25), channel_id=1, source_target_pairs={{0,8},{16,24},{8,0},{24,16},{1,9},{17,25},{9,1},{25,17},{2,10},{18... | collective-permute-start | bytes 442376 | tf_op jit(solution)/shard_map/ppermute | solution.py:390
  38.7 6.4 %collective-permute-start.9 = (f32[2,144,128]{2,1,0:T(8,128)S(1)}, f32[2,144,128]{2,1,0:T(8,128)S(1)}, u32[]{:S(2)}, u32[]{:S(2)}) collective-permute-start(f32[2,144,128]{2,1,0:T(8,128)S(1)} %get-tuple-element.26), channel_id=1, source_target_pairs={{8,16},{16,8},{9,17},{17,9},{10,18},{18,10},{11,19},{19,11},{12,20... | collective-permute-start | bytes 442376 | tf_op jit(solution)/shard_map/ppermute | solution.py:390
  46.3 2.7 %collective-permute-start.10 = (f32[9,2,8,128]{3,2,1,0:T(8,128)S(1)}, f32[9,2,8,128]{3,2,1,0:T(8,128)S(1)}, u32[]{:S(2)}, u32[]{:S(2)}) collective-permute-start(f32[9,2,8,128]{3,2,1,0:T(8,128)S(1)} %get-tuple-element.30), channel_id=1, source_target_pairs={{0,1},{1,0},{2,3},{3,2},{4,5},{5,4},{6,7},{7,6},{8,9},{9,8},{10,11... | collective-permute-start | bytes 221192 | tf_op jit(solution)/shard_map/ppermute | solution.py:405

commit v7 on v4

v7 whole, which is shorter than its diff:
```python
import functools

import jax
import jax.numpy as jnp
from jax import lax
from jax.experimental import pallas as pl
from jax.experimental.pallas import tpu as pltpu
from jax.sharding import PartitionSpec as P

STEPS = 4
F32 = jnp.float32
BF16 = jnp.bfloat16
NT = (((1,), (1,)), ((), ()))


def one_hot(index, count):
    rows = lax.broadcasted_iota(jnp.int32, (count, index.shape[-1]), 0)
    return jnp.where(rows == index, F32(1.0), F32(0.0))


def split3(value):
    high = value.astype(BF16).astype(F32)
    rest = value - high
    mid = rest.astype(BF16).astype(F32)
    return high, mid, rest - mid


def copy_all(sem, pairs):
    copies = [pltpu.make_async_copy(a, b, sem.at[i]) for i, (a, b) in enumerate(pairs)]
    for copy in copies:
        copy.start()
    for copy in copies:
        copy.wait()


def in_line(rows):
    return jnp.concatenate([rows[i : i + 1, :] for i in range(rows.shape[0])], axis=1)


def reach_of(cz):
    return cz // 2 + STEPS


def pack_kernel(
    fields_in, ids_in, moments_in, owner_in, cells_in, rows_in, buoyancy, lame_lambda, lame_mu,
    entries, kept, given, fields, ids, moments, owner, cells, rows, wide, tables, sem,
):
    cx, cz, cy = ids.shape[1:]
    arguments = [(fields_in, fields), (ids_in, ids), (moments_in, moments), (owner_in, owner)]
    arguments += [(cells_in, cells), (rows_in, rows)]
    arguments += [(t, tables.at[i]) for i, t in enumerate((buoyancy, lame_lambda, lame_mu))]
    copy_all(sem, arguments)
    for i in range(cells.shape[0]):
        at = 8 * i
        entries[at : at + 6] = moments[:, i * cy : (i + 1) * cy]
        entries[at + 6 : at + 7] = owner[i : i + 1, :].astype(F32)
        entries[at + 7 : at + 8] = cells[i : i + 1, :].astype(F32)
    wide[0] = (ids[0] + 1).astype(F32)
    line = in_line(rows[...])
    high = one_hot(line // cy, cx * cz).astype(BF16)
    low = one_hot(line % cy, cy).astype(BF16)
    count = lax.dot_general(high, low, NT, preferred_element_type=F32)
    wide[1] = count.reshape(cx, cz, cy)
    reach = reach_of(cz)
    lines = 11 * cx * reach
    lane = lax.broadcasted_iota(jnp.int32, (1, cy), 1)
    for i in range(3):
        found = jnp.zeros((1, cy), F32)
        for entry in range(tables.shape[1]):
            found = jnp.where(lane == entry + 1, F32(0.5) * tables[i, entry], found)
        kept[lines + i : lines + i + 1] = found
    kept[lines + 3 : lines + 8] = jnp.zeros((5, cy), F32)
    kept[lines + 8 :] = entries[...]

    def cut(first, other):
        for x in range(cx):
            at = slice(x * reach, (x + 1) * reach)
            for k in range(11):
                source = fields.at[0, k] if k < 9 else wide.at[k - 9]
                line = (k * cx + x) * reach
                kept[line : line + reach] = source[x, first : first + reach]
            given[0:9, at] = fields[0, :, x, other : other + reach]
            given[9, at] = wide[0, x, other : other + reach]

    @pl.when(lax.axis_index("segment") == 0)
    def _():
        cut(0, cz - reach)

    @pl.when(lax.axis_index("segment") == 1)
    def _():
        cut(cz - reach, 0)


def add_moments(layout, blocks, acc):
    cx, cz, cy = layout
    section = lax.axis_index("sec")
    half = cx * cz // 2
    for entries in blocks:
        chunk = [entries[8 * i : 8 * i + 8] for i in range(entries.shape[0] // 8)]
        entry = jnp.concatenate(chunk, axis=1)
        owner = entry[6:7].astype(jnp.int32)
        cell = entry[7:8].astype(jnp.int32)
        line = jnp.where(owner == section, cell // cy, -1)
        upper = line >= half
        high = one_hot(jnp.where(upper, line - half, line), half)
        low = one_hot(jnp.where(upper, cell % cy + cy, cell % cy), 2 * cy).astype(BF16)
        for part in split3(entry[0:6]):
            spread = [(high * part[c : c + 1]).astype(BF16) for c in range(6)]
            acc[...] += lax.dot_general(
                jnp.concatenate(spread, axis=0), low, NT, preferred_element_type=F32
            )


def own_kernel(layout, kept, out, tables, acc):
    lines = out.shape[0] * out.shape[1]
    out[...] = kept[0:lines].reshape(out.shape)
    tables[...] = kept[lines : lines + 8]
    acc[...] = jnp.zeros_like(acc)
    add_moments(layout, [kept.at[pl.ds(lines + 8, kept.shape[0] - lines - 8)]], acc)


def join_kernel(layout, *refs):
    cx, cz, cy = layout
    kept, got, started, blocks = refs[0], refs[1], refs[2], refs[3:-5]
    body, count, edge, acc, dense = refs[-5:]
    reach = reach_of(cz)
    half = cx * cz // 2
    acc[...] = started[...]
    add_moments(layout, blocks, acc)
    for c in range(6):
        for k in range(2):
            added = acc[c * half : (c + 1) * half, k * cy : (k + 1) * cy]
            dense[c, k * half : (k + 1) * half] = added
    count[...] = kept[10]

    def join(mine, first, sent):
        body[mine] = kept[0:10]
        body[1 - mine] = got[...]
        for x in range(cx):
            at = slice(x * reach, (x + 1) * reach)
            added = dense[:, x * cz + first : x * cz + first + reach]
            body[0, 3:9, at] = body[0, 3:9, at] + added
        for x in range(cx):
            row = x * reach + sent
            for k in range(21):
                at = slice((k * cx + x) * STEPS, (k * cx + x + 1) * STEPS)
                if k < 20:
                    edge[at] = body[k // 10, k % 10, row : row + STEPS]
                else:
                    edge[at] = count[row : row + STEPS]

    @pl.when(lax.axis_index("segment") == 0)
    def _():
        join(0, 0, 0)

    @pl.when(lax.axis_index("segment") == 1)
    def _():
        join(1, cz - reach, reach - STEPS)


def by_parity(even, odd, act):
    parity = lax.axis_index("sec") % 2

    @pl.when(parity == 0)
    def _():
        act(*even)

    @pl.when(parity == 1)
    def _():
        act(*odd)


def advance(cx, steps, state, coef, times, given_top=False):
    planes, rows, cy = state.shape[2:]
    lane = lax.broadcasted_iota(jnp.int32, (rows, cy), 1)
    first_lane, last_lane = lane == 0, lane == cy - 1

    def back_y(f):
        return f - jnp.where(first_lane, F32(0.0), pltpu.roll(f, 1, 1))

    def back_z(f):
        return f - pltpu.roll(f, 1, 0)

    def fore_y(f):
        return jnp.where(last_lane, F32(0.0), pltpu.roll(f, cy - 1, 1)) - f

    def fore_z(f):
        return pltpu.roll(f, rows - 1, 0) - f

    def velocity(x):
        inc = [None, None]
        for model in range(2):
            sxx, syy, szz, syz, sxz, sxy = (state[model, 3 + k, x] for k in range(6))
            sxx_p, sxz_p, sxy_p = (state[model, k, x - 1] for k in (3, 7, 8))
            hb = coef[model, 0, x]
            inc[model] = (
                hb * ((sxx - sxx_p) + back_y(sxy) + back_z(sxz)),
                hb * ((sxy - sxy_p) + back_y(syy) + back_z(syz)),
                hb * ((sxz - sxz_p) + back_y(syz) + back_z(szz)),
            )
        for k in range(3):
            state[0, k, x] = state[0, k, x] + inc[0][k]
            state[1, k, x] = (state[1, k, x] + inc[1][k]) + times[x] * inc[0][k]

    for step in range(steps):
        left = steps - 1 - step
        low, high = cx - left, 2 * cx + left
        pl.loop(low, high + 1 - (given_top and step == 0))(velocity)

        @pl.loop(low, high)
        def _(x):
            for model in range(2):
                vx, vy, vz = (state[model, k, x] for k in range(3))
                vx_n, vy_n, vz_n = (state[model, k, x + 1] for k in range(3))
                hl, hm = coef[model, 1, x], coef[model, 2, x]
                exx, eyy, ezz = vx_n - vx, fore_y(vy), fore_z(vz)
                pressure = hl * (exx + eyy + ezz)
                twice = hm + hm
                state[model, 3, x] = state[model, 3, x] + (pressure + twice * exx)
                state[model, 4, x] = state[model, 4, x] + (pressure + twice * eyy)
                state[model, 5, x] = state[model, 5, x] + (pressure + twice * ezz)
                state[model, 6, x] = state[model, 6, x] + hm * (fore_z(vy) + fore_y(vz))
                state[model, 7, x] = state[model, 7, x] + hm * (fore_z(vx) + (vz_n - vz))
                state[model, 8, x] = state[model, 8, x] + hm * (fore_y(vx) + (vy_n - vy))

    return velocity


def look_up(tables, ids):
    lanes = ids.astype(jnp.int32)
    wide = [jnp.broadcast_to(tables[i : i + 1], ids.shape) for i in range(3)]
    return [jnp.take_along_axis(table, lanes, axis=1) for table in wide]


def edge_units(cx, with_ids):
    right, left = [], []
    for model in range(2):
        whole = list(range(10 if with_ids else 9)) + [10] * (with_ids and model == 1)
        for x in range(cx - 1):
            right += [(model, what, x + 1) for what in whole]
            left += [(model, what, x) for what in whole]
        right += [(model, what, 0) for what in (3, 7, 8)]
        left += [(model, what, cx - 1) for what in range(3)]
    return right, left


def cut_edges(cx, done, with_ids, velocity, state, ids, times, to_first, to_second):
    rows = state.shape[3]
    at = slice(done, rows - done)
    count = rows - 2 * done
    right_units, left_units = edge_units(cx, with_ids)

    def put(to, units):
        for i, (model, what, x) in enumerate(units):
            line = slice(i * count, (i + 1) * count)
            if what == 10:
                to[line] = times[cx + x, at]
            elif what == 9:
                to[line] = ids[model, cx + x, at]
            else:
                to[line] = state[model, what, cx + x, at]

    holders = (to_second, to_first), (to_first, to_second)
    by_parity(*holders, lambda left, right: put(right, right_units))
    velocity(2 * cx - 1)
    by_parity(*holders, lambda left, right: put(left, left_units))


def planes_kernel(
    cx, body, count, halo, tables,
    to_first, to_second, both, coef_out, times_out, state, ids, coef, times,
):
    rows = state.shape[3]
    reach = rows - STEPS

    def join(main, edge):
        for x in range(cx):
            inner = slice(x * reach, (x + 1) * reach)
            for k in range(21):
                outer = halo[(k * cx + x) * STEPS : (k * cx + x + 1) * STEPS]
                model, what = k // 10, k % 10
                if k == 20:
                    times[cx + x, main] = count[inner]
                    times[cx + x, edge] = outer
                elif what == 9:
                    ids[model, cx + x, main] = body[model, what, inner]
                    ids[model, cx + x, edge] = outer
                else:
                    state[model, what, cx + x, main] = body[model, what, inner]
                    state[model, what, cx + x, edge] = outer

    @pl.when(lax.axis_index("segment") == 0)
    def _():
        join(slice(STEPS, rows), slice(0, STEPS))

    @pl.when(lax.axis_index("segment") == 1)
    def _():
        join(slice(0, reach), slice(reach, rows))

    for model in range(2):
        for x in range(cx, 2 * cx):
            for i, found in enumerate(look_up(tables, ids[model, x])):
                coef[model, i, x] = found
    own = slice(cx, 2 * cx)
    both[...] = state[:, :, own]
    coef_out[...] = coef[:, :, own]
    times_out[...] = times[own]
    velocity = advance(cx, 0, state, coef, times)
    cut_edges(cx, 0, True, velocity, state, ids, times, to_first, to_second)


def next_kernel(cx, done, *refs):
    first = done == 0
    both_in, from_first, from_second, coef_in, times_in = refs[0:5]
    if first:
        tables = refs[5]
        state, ids, coef, times = refs[-4:]
    else:
        state, coef, times = refs[-1], coef_in, times_in
    outs = refs[6 if first else 5 :]
    segment = lax.axis_index("segment")
    rows = state.shape[3]
    at = slice(done, rows - done)
    count = rows - 2 * done
    own = slice(cx, 2 * cx)
    state[:, :, own] = both_in[...]
    right_units, left_units = edge_units(cx, first)

    def get(edge, units, start):
        for i, (model, what, x) in enumerate(units):
            line = edge[i * count : (i + 1) * count]
            if what == 10:
                times[start + x, at] = line
            elif what == 9:
                ids[model, start + x, at] = line
            else:
                state[model, what, start + x, at] = line

    def place(left, right):
        get(left, right_units, 0)
        get(right, left_units, 2 * cx)

    by_parity((from_second, from_first), (from_first, from_second), place)
    if first:
        coef[:, :, own] = coef_in[...]
        times[own] = times_in[...]
        for model in range(2):
            for x in (*range(1, cx), *range(2 * cx, 3 * cx - 1)):
                for i, found in enumerate(look_up(tables, ids[model, x])):
                    coef[model, i, x] = found
    velocity = advance(cx, cx, state, coef, times, given_top=True)
    if done + cx == STEPS:
        outs[0][...] = state[segment, :, own, STEPS : rows - STEPS]
        outs[1][...] = state[1 - segment, :, own, STEPS : rows - STEPS]
    else:
        outs[2][...] = state[:, :, own]
        if first:
            outs[3][...] = coef[...]
            outs[4][...] = times[...]
        cut_edges(cx, done + cx, False, velocity, state, None, times, outs[0], outs[1])


def home_kernel(mine, brought, out):
    half = mine.shape[2]
    segment = lax.axis_index("segment")

    @pl.when(segment == 0)
    def _():
        out[0, :, :, 0:half] = mine[...]
        out[0, :, :, half:] = brought[...]

    @pl.when(segment == 1)
    def _():
        out[0, :, :, half:] = mine[...]
        out[0, :, :, 0:half] = brought[...]


VMEM = pl.BlockSpec(memory_space=pltpu.VMEM)
HBM = pl.BlockSpec(memory_space=pltpu.HBM)


def call(kernel, name, in_vmem, in_hbm, outs, scratch, copies=0, limit=40 * 2**20, flops=10**7):
    sems = [pltpu.SemaphoreType.DMA((copies,))] * (copies > 0)
    return pl.pallas_call(
        kernel,
        out_shape=[jax.ShapeDtypeStruct(shape, F32) for shape in outs],
        in_specs=[VMEM] * len(in_vmem) + [HBM] * len(in_hbm),
        out_specs=[VMEM] * len(outs),
        scratch_shapes=[pltpu.VMEM(s, F32) if isinstance(s, tuple) else s for s in scratch] + sems,
        compiler_params=pltpu.CompilerParams(vmem_limit_bytes=limit),
        cost_estimate=pl.CostEstimate(flops=flops, bytes_accessed=2**20, transcendentals=0),
        name=name,
    )(*in_vmem, *in_hbm)


def on_device(
    fields, block_ids, buoyancy, lame_lambda, lame_mu, moments, moment_owner, moment_cells, drm_rows
):
    sections, slabs = lax.axis_size("sec"), lax.axis_size("depth")
    layout = cx, cz, cy = fields.shape[2:]
    reach, rows = reach_of(cz), cz // 2 + 2 * STEPS
    assert cx > 1 and STEPS % cx == 0

    def pairs(block, start):
        route = [(i, i + 1) for i in range(start, sections - 1, 2)]
        return lax.ppermute(block, "sec", route + [(j, i) for i, j in route])

    def other(section, k):
        return section ^ k if sections & (sections - 1) == 0 else (section + k) % sections

    def along_depth(block):
        down = [(2 * i + 1, 2 * (i + 1)) for i in range(slabs - 1)]
        return lax.ppermute(block, ("depth", "segment"), down + [(j, i) for i, j in down])

    def swap(block):
        return lax.ppermute(block, "segment", [(0, 1), (1, 0)])

    owner = moment_owner.reshape(-1, cy)
    cells = moment_cells.reshape(-1, cy)
    arguments = (fields, block_ids, moments, owner, cells, drm_rows.reshape(-1, cy))
    entry_lines = 8 * cells.shape[0]
    entries, kept, given = call(
        pack_kernel,
        "pack",
        (),
        (*arguments, buoyancy, lame_lambda, lame_mu),
        [(entry_lines, cy), (11 * cx * reach + 8 + entry_lines, cy), (10, cx * reach, cy)],
        [pltpu.VMEM(a.shape, a.dtype) for a in arguments]
        + [(2, cx, cz, cy), pltpu.SMEM((3, buoyancy.shape[0]), F32)],
        len(arguments) + 3,
        limit=64 * 2**20,
    )
    blocks = [
        lax.ppermute(entries, "sec", [(other(i, k), i) for i in range(sections)])
        for k in range(1, sections)
    ]
    got = swap(given)
    acc_shape = (6 * cx * cz // 2, 2 * cy)
    kept, tables, started = call(
        functools.partial(own_kernel, layout),
        "own_moments",
        (kept,),
        (),
        [(11, cx * reach, cy), (8, cy), acc_shape],
        [],
        flops=10**9,
    )
    body, count, edge = call(
        functools.partial(join_kernel, layout),
        "join_and_moments",
        (kept, got, started, *blocks),
        (),
        [(2, 10, cx * reach, cy), (cx * reach, cy), (21 * cx * STEPS, cy)],
        [acc_shape, (6, cx * cz, cy)],
    )
    halo = along_depth(edge)
    own = (cx, rows, cy)
    window = (3 * cx, rows, cy)

    def edges(done):
        units = edge_units(cx, done == 0)[0]
        return [(len(units) * (rows - 2 * done), cy)] * 2

    to_first, to_second, both, coef, times = call(
        functools.partial(planes_kernel, cx),
        "own_planes",
        (body, count, halo, tables),
        (),
        edges(0) + [(2, 9, *own), (2, 3, *own), own],
        [(2, 9, *window), (2, *window), (2, 3, *window), window],
    )
    for done in range(0, STEPS, cx):
        from_first, from_second = pairs(to_first, 0), pairs(to_second, 1)
        first, last = done == 0, done + cx == STEPS
        outs = [(9, cx, cz // 2, cy)] * 2 if last else edges(done + cx) + [(2, 9, *own)]
        if first:
            outs = outs + [(2, 3, *window), window]
        space = [(2, 9, *window)]
        if first:
            space += [(2, *window), (2, 3, *window), window]
        done_now = call(
            functools.partial(next_kernel, cx, done),
            "steps",
            (both, from_first, from_second, coef, times) + (tables,) * first,
            (),
            outs,
            space,
        )
        to_first, to_second = done_now[0:2]
        if first:
            coef, times = done_now[3:5]
        both = done_now[-1] if not first else done_now[2]
    (out,) = call(home_kernel, "home", (to_first, swap(to_second)), (), [fields.shape], [])
    return out


def solution(mesh):
    in_specs = (
        P("segment", None, "sec", "depth", None),
        P("segment", "sec", "depth", None),
        P(),
        P(),
        P(),
        P(None, ("sec", "depth")),
        P(("sec", "depth"), None),
        P(("sec", "depth")),
        P(("sec", "depth")),
    )
    out_specs = P("segment", None, "sec", "depth", None)
    return jax.shard_map(
        on_device, mesh=mesh, in_specs=in_specs, out_specs=out_specs, check_vma=False
    )
```

time: 46.3 us -> 41.1 us (0.89)
  starting transfers between devices: 24.5 us -> 18.4 us
  Pallas kernels: 6.51 us -> 7.98 us
  waiting for transfers between devices: 14 us -> 12.9 us
    ppermute x2, starting transfers between devices: 11.7 us -> 4.11 us  [swap(): return lax.ppermute(block, 'segment', [(0, 1), (1, 0)])]
    pallas_call x6 -> x7, Pallas kernels: 6.51 us -> 7.98 us  [call(): pl.pallas_call(kernel, out_shape=[jax.ShapeDtypeStruct(shape, F32) for sh...]
    ppermute x5 -> x4, waiting for transfers between devices: 4.7 us -> 3.7 us  [the longest x1 2.45 us: along_depth(): lax.ppermute(block, ('depth', 'segment'), down + [(j, i) for i, j in down])]
    ppermute x4, starting transfers between devices: 5.67 us -> 6.61 us  [pairs(): return lax.ppermute(block, 'sec', route + [(j, i) for i, j in route])]
    ppermute x5 -> x4, starting transfers between devices: 7.09 us -> 7.65 us  [the longest x1 4.14 us: along_depth(): lax.ppermute(block, ('depth', 'segment'), down + [(j, i) for i, j in down])]
  transfers between devices with their start and end apart: 11 -> 10, of which waited for: 7 -> 8; matrix products, arithmetic and copies ran while one was open for 0% -> 0% of each run, Pallas kernels for 0% -> 2%
where the time goes in v7:
time: 41.1 us; the launch traced here: 40.3 us
  starting transfers between devices  18.4 us (45%)
  waiting for transfers between devices  12.9 us (31%)
  Pallas kernels  7.98 us (19%)
  local copies, waits for them, and re-layouts  0.92 us (2%)
    ppermute x4, waiting for transfers between devices, pairs(): return lax.ppermute(block, 'sec', route + [(j, i) for i, j in route])  8.33 us
    pallas_call x7, Pallas kernels, call(): pl.pallas_call(kernel, out_shape=[jax.ShapeDtypeStruct(shape, F32) for sh...  7.98 us
    ppermute x4, starting transfers between devices, pairs(): return lax.ppermute(block, 'sec', route + [(j, i) for i, j in route])  6.61 us
    ppermute x1, starting transfers between devices, along_depth(): lax.ppermute(block, ('depth', 'segment'), down + [(j, i) for i, j in down])  4.14 us
    ppermute x2, starting transfers between devices, swap(): return lax.ppermute(block, 'segment', [(0, 1), (1, 0)])  4.11 us
    ppermute x3, starting transfers between devices, on_device(): lax.ppermute(entries, 'sec', [(other(i, k), i) for i in range(sections)])  3.51 us
    ppermute x1, waiting for transfers between devices, along_depth(): lax.ppermute(block, ('depth', 'segment'), down + [(j, i) for i, j in down])  2.45 us
    ppermute x3, waiting for transfers between devices, on_device(): lax.ppermute(entries, 'sec', [(other(i, k), i) for i in range(sections)])  1.25 us
  transfers between devices with their start and end apart: 10, of which 8 were waited for; matrix products, arithmetic and copies ran while one was open for 0% of the time, Pallas kernels for 2%

profile of v7, /device:TPU:13, one launch (start us, length us, event | category | flops | bytes accessed | tf_op | source)
XLA Modules:
  0.0 40.3 jit_solution(11938809791267576554)
XLA Ops:
  0.0 2.1 %pack.1 = (f32[64,128]{1,0:T(8,128)}, f32[336,128]{1,0:T(8,128)}, f32[10,24,128]{2,1,0:T(8,128)}) custom-call(f32[1,9,2,16,128]{4,3,2,1,0:T(8,128)} %fields_in.1, s32[1,2,16,128]{3,2,1,0:T(8,128)} %ids_in.1, f32[6,1024]{1,0:T(8,128)} %moments_in.1, s32[8,128]{1,0:T(8,128)} %bitcast.4, s32[8,128]{1,0:T(8,128)} %bitcast.5, s32[16,128]{1,0:T(8,128)} %bitcast.3, ...), custom_call_target="tpu_custom_call" | custom-call | flops 10000000 | bytes 1048576 | tf_op jit(solution)/shard_map/pack/pallas_call | solution.py:384
  2.1 0.7 %collective-permute-start = (f32[10,24,128]{2,1,0:T(8,128)}, f32[10,24,128]{2,1,0:T(8,128)S(1)}, u32[]{:S(2)}, u32[]{:S(2)}) collective-permute-start(f32[10,24,128]{2,1,0:T(8,128)} %get-tuple-element.28), channel_id=1, source_target_pairs={{0,1},{1,0},{2,3},{3,2},{4,5},{5,4},{6,7},{7,6},{8,9},{9,8},{10,11... | collective-permute-start | bytes 368648 | tf_op jit(solution)/shard_map/ppermute | solution.py:416
  2.8 1.3 %collective-permute-start.3 = (f32[64,128]{1,0:T(8,128)}, f32[64,128]{1,0:T(8,128)S(1)}, u32[]{:S(2)}, u32[]{:S(2)}) collective-permute-start(f32[64,128]{1,0:T(8,128)} %get-tuple-element.30), channel_id=1, source_target_pairs={{24,0},{16,8},{8,16},{0,24},{25,1},{17,9},{9,17},{1,25},{26,2},{18... | collective-permute-start | bytes 98312 | tf_op jit(solution)/shard_map/ppermute | solution.py:434
  4.1 1.0 %collective-permute-start.2 = (f32[64,128]{1,0:T(8,128)}, f32[64,128]{1,0:T(8,128)S(1)}, u32[]{:S(2)}, u32[]{:S(2)}) collective-permute-start(f32[64,128]{1,0:T(8,128)} %get-tuple-element.30), channel_id=1, source_target_pairs={{16,0},{24,8},{0,16},{8,24},{17,1},{25,9},{1,17},{9,25},{18,2},{26... | collective-permute-start | bytes 98312 | tf_op jit(solution)/shard_map/ppermute | solution.py:434
  5.1 1.2 %collective-permute-start.1 = (f32[64,128]{1,0:T(8,128)}, f32[64,128]{1,0:T(8,128)S(1)}, u32[]{:S(2)}, u32[]{:S(2)}) collective-permute-start(f32[64,128]{1,0:T(8,128)} %get-tuple-element.30), channel_id=1, source_target_pairs={{8,0},{0,8},{24,16},{16,24},{9,1},{1,9},{25,17},{17,25},{10,2},{2,... | collective-permute-start | bytes 98312 | tf_op jit(solution)/shard_map/ppermute | solution.py:434
  6.3 0.9 %copy-done = f32[336,128]{1,0:T(8,128)S(1)} copy-done((f32[336,128]{1,0:T(8,128)S(1)}, f32[336,128]{1,0:T(8,128)}, u32[]{:S(2)}) %copy-start) | copy-done | bytes 172056
  7.2 0.6 %own_moments.1 = (f32[11,24,128]{2,1,0:T(8,128)S(1)}, f32[8,128]{1,0:T(8,128)S(1)}, f32[96,256]{1,0:T(8,128)S(1)}) custom-call(f32[336,128]{1,0:T(8,128)S(1)} %copy-done), custom_call_target="tpu_custom_call" | custom-call | flops 1000000000 | bytes 1048576 | tf_op jit(solution)/shard_map/own_moments/pallas_call | solution.py:384
  8.0 1.2 %collective-permute-done.1.refs_3_ = f32[64,128]{1,0:T(8,128)S(1)} collective-permute-done((f32[64,128]{1,0:T(8,128)}, f32[64,128]{1,0:T(8,128)S(1)}, u32[]{:S(2)}, u32[]{:S(2)}) %collective-permute-start.1) | collective-permute-done | bytes 32800 | tf_op jit(solution)/shard_map/ppermute | solution.py:434
  9.1 1.7 %join_and_moments.1 = (f32[2,10,24,128]{3,2,1,0:T(8,128)S(1)}, f32[24,128]{1,0:T(8,128)S(1)}, f32[168,128]{1,0:T(8,128)S(1)}) custom-call(f32[11,24,128]{2,1,0:T(8,128)S(1)} %get-tuple-element.27.refs_0_, f32[10,24,128]{2,1,0:T(8,128)S(1)} %collective-permute-done.refs_1_, f32[96,256]{1,0:T(8,128)S(1)} %get-tuple-element.29.refs_2_, ...), custom_call_target="tpu_custom_call" | custom-call | flops 10000000 | bytes 1048576 | tf_op jit(solution)/shard_map/join_and_moments/pallas_call | solution.py:384
  10.8 4.1 %collective-permute-start.4 = (f32[168,128]{1,0:T(8,128)S(1)}, f32[168,128]{1,0:T(8,128)S(1)}, u32[]{:S(2)}, u32[]{:S(2)}) collective-permute-start(f32[168,128]{1,0:T(8,128)S(1)} %get-tuple-element.33), channel_id=1, source_target_pairs={{1,2},{3,4},{5,6},{2,1},{4,3},{6,5},{9,10},{11,12},{13,14},{10,9},... | collective-permute-start | bytes 258056 | tf_op jit(solution)/shard_map/ppermute | solution.py:413
  15.0 2.4 %collective-permute-done.4.halo = f32[168,128]{1,0:T(8,128)S(1)} collective-permute-done((f32[168,128]{1,0:T(8,128)S(1)}, f32[168,128]{1,0:T(8,128)S(1)}, u32[]{:S(2)}, u32[]{:S(2)}) %collective-permute-start.4) | collective-permute-done | bytes 86048 | tf_op jit(solution)/shard_map/ppermute | solution.py:413
  17.4 0.3 own_planes.1
  17.7 1.4 %collective-permute-start.5 = (f32[432,128]{1,0:T(8,128)S(1)}, f32[432,128]{1,0:T(8,128)S(1)}, u32[]{:S(2)}, u32[]{:S(2)}) collective-permute-start(f32[432,128]{1,0:T(8,128)S(1)} %get-tuple-element.36), channel_id=1, source_target_pairs={{0,8},{16,24},{8,0},{24,16},{1,9},{17,25},{9,1},{25,17},{2,10},{18... | collective-permute-start | bytes 663560 | tf_op jit(solution)/shard_map/ppermute | solution.py:406
  19.2 2.5 %collective-permute-start.6 = (f32[432,128]{1,0:T(8,128)S(1)}, f32[432,128]{1,0:T(8,128)S(1)}, u32[]{:S(2)}, u32[]{:S(2)}) collective-permute-start(f32[432,128]{1,0:T(8,128)S(1)} %get-tuple-element.37), channel_id=1, source_target_pairs={{8,16},{16,8},{9,17},{17,9},{10,18},{18,10},{11,19},{19,11},{12,20... | collective-permute-start | bytes 663560 | tf_op jit(solution)/shard_map/ppermute | solution.py:406
  21.6 1.8 %collective-permute-done.5.refs_1_ = f32[432,128]{1,0:T(8,128)S(1)} collective-permute-done((f32[432,128]{1,0:T(8,128)S(1)}, f32[432,128]{1,0:T(8,128)S(1)}, u32[]{:S(2)}, u32[]{:S(2)}) %collective-permute-start.5) | collective-permute-done | bytes 221216 | tf_op jit(solution)/shard_map/ppermute | solution.py:406
  23.4 3.0 %collective-permute-done.6.refs_2_ = f32[432,128]{1,0:T(8,128)S(1)} collective-permute-done((f32[432,128]{1,0:T(8,128)S(1)}, f32[432,128]{1,0:T(8,128)S(1)}, u32[]{:S(2)}, u32[]{:S(2)}) %collective-permute-start.6) | collective-permute-done | bytes 221216 | tf_op jit(solution)/shard_map/ppermute | solution.py:406
  26.4 1.5 %steps.2 = (f32[288,128]{1,0:T(8,128)S(1)}, f32[288,128]{1,0:T(8,128)S(1)}, f32[2,9,2,16,128]{4,3,2,1,0:T(8,128)S(1)}, f32[2,3,6,16,128]{4,3,2,1,0:T(8,128)S(1)}, f32[6,16,128]{2,1,0:T(8,128)S(1)}) custom-call(f32[2,9,2,16,128]{4,3,2,1,0:T(8,128)S(1)} %get-tuple-element.35.refs_0_, f32[432,128]{1,0:T(8,128)S(1)} %collective-permute-done.5.refs_1_, ...), custom_call_target="tpu_custom_call" | custom-call | flops 10000000 | bytes 1048576 | tf_op jit(solution)/shard_map/steps/pallas_call | solution.py:384
  28.0 2.6 %collective-permute-start.8 = (f32[288,128]{1,0:T(8,128)S(1)}, f32[288,128]{1,0:T(8,128)S(1)}, u32[]{:S(2)}, u32[]{:S(2)}) collective-permute-start(f32[288,128]{1,0:T(8,128)S(1)} %get-tuple-element.42), channel_id=1, source_target_pairs={{8,16},{16,8},{9,17},{17,9},{10,18},{18,10},{11,19},{19,11},{12,20... | collective-permute-start | bytes 442376 | tf_op jit(solution)/shard_map/ppermute | solution.py:406
  30.6 1.4 %collective-permute-done.7.refs_1_ = f32[288,128]{1,0:T(8,128)S(1)} collective-permute-done((f32[288,128]{1,0:T(8,128)S(1)}, f32[288,128]{1,0:T(8,128)S(1)}, u32[]{:S(2)}, u32[]{:S(2)}) %collective-permute-start.7) | collective-permute-done | bytes 147488 | tf_op jit(solution)/shard_map/ppermute | solution.py:406
  31.9 2.2 %collective-permute-done.8.refs_2_ = f32[288,128]{1,0:T(8,128)S(1)} collective-permute-done((f32[288,128]{1,0:T(8,128)S(1)}, f32[288,128]{1,0:T(8,128)S(1)}, u32[]{:S(2)}, u32[]{:S(2)}) %collective-permute-start.8) | collective-permute-done | bytes 147488 | tf_op jit(solution)/shard_map/ppermute | solution.py:406
  34.1 1.2 %steps.3 = (f32[9,2,8,128]{3,2,1,0:T(8,128)S(1)}, f32[9,2,8,128]{3,2,1,0:T(8,128)S(1)}) custom-call(f32[2,9,2,16,128]{4,3,2,1,0:T(8,128)S(1)} %get-tuple-element.40.refs_0_, f32[288,128]{1,0:T(8,128)S(1)} %collective-permute-done.7.refs_1_, f32[288,128]{1,0:T(8,128)S(1)} %collective-permute-done.8.refs_2_, ...), custom_call_target="tpu_custom_call" | custom-call | flops 10000000 | bytes 1048576 | tf_op jit(solution)/shard_map/steps/pallas_call | solution.py:384
  35.3 3.4 %collective-permute-start.9 = (f32[9,2,8,128]{3,2,1,0:T(8,128)S(1)}, f32[9,2,8,128]{3,2,1,0:T(8,128)S(1)}, u32[]{:S(2)}, u32[]{:S(2)}) collective-permute-start(f32[9,2,8,128]{3,2,1,0:T(8,128)S(1)} %get-tuple-element.46), channel_id=1, source_target_pairs={{0,1},{1,0},{2,3},{3,2},{4,5},{5,4},{6,7},{7,6},{8,9},{9,8},{10,11... | collective-permute-start | bytes 221192 | tf_op jit(solution)/shard_map/ppermute | solution.py:416
  38.7 0.9 %collective-permute-done.9.brought = f32[9,2,8,128]{3,2,1,0:T(8,128)S(1)} collective-permute-done((f32[9,2,8,128]{3,2,1,0:T(8,128)S(1)}, f32[9,2,8,128]{3,2,1,0:T(8,128)S(1)}, u32[]{:S(2)}, u32[]{:S(2)}) %collective-permute-start.9) | collective-permute-done | bytes 73760 | tf_op jit(solution)/shard_map/ppermute | solution.py:416
  39.6 0.7 %home.1 = f32[1,9,2,16,128]{4,3,2,1,0:T(8,128)} custom-call(f32[9,2,8,128]{3,2,1,0:T(8,128)S(1)} %get-tuple-element.45.mine, f32[9,2,8,128]{3,2,1,0:T(8,128)S(1)} %collective-permute-done.9.brought), custom_call_target="tpu_custom_call" | custom-call | flops 10000000 | bytes 1048576 | tf_op jit(solution)/shard_map/home/pallas_call | solution.py:384
  (5 shorter events, 0.2 us)
Async XLA Ops:
  2.1 7.1 %collective-permute-start = (f32[10,24,128]{2,1,0:T(8,128)}, f32[10,24,128]{2,1,0:T(8,128)S(1)}, u32[]{:S(2)}, u32[]{:S(2)}) collective-permute-start(f32[10,24,128]{2,1,0:T(8,128)} %get-tuple-element.28), channel_id=1, source_target_pairs={{0,1},{1,0},{2,3},{3,2},{4,5},{5,4},{6,7},{7,6},{8,9},{9,8},{10,11... | collective-permute-start | bytes 368648 | tf_op jit(solution)/shard_map/ppermute | solution.py:416
  2.8 5.1 %collective-permute-start.3 = (f32[64,128]{1,0:T(8,128)}, f32[64,128]{1,0:T(8,128)S(1)}, u32[]{:S(2)}, u32[]{:S(2)}) collective-permute-start(f32[64,128]{1,0:T(8,128)} %get-tuple-element.30), channel_id=1, source_target_pairs={{24,0},{16,8},{8,16},{0,24},{25,1},{17,9},{9,17},{1,25},{26,2},{18... | collective-permute-start | bytes 98312 | tf_op jit(solution)/shard_map/ppermute | solution.py:434
  4.1 3.9 %collective-permute-start.2 = (f32[64,128]{1,0:T(8,128)}, f32[64,128]{1,0:T(8,128)S(1)}, u32[]{:S(2)}, u32[]{:S(2)}) collective-permute-start(f32[64,128]{1,0:T(8,128)} %get-tuple-element.30), channel_id=1, source_target_pairs={{16,0},{24,8},{0,16},{8,24},{17,1},{25,9},{1,17},{9,25},{18,2},{26... | collective-permute-start | bytes 98312 | tf_op jit(solution)/shard_map/ppermute | solution.py:434
  5.1 4.0 %collective-permute-start.1 = (f32[64,128]{1,0:T(8,128)}, f32[64,128]{1,0:T(8,128)S(1)}, u32[]{:S(2)}, u32[]{:S(2)}) collective-permute-start(f32[64,128]{1,0:T(8,128)} %get-tuple-element.30), channel_id=1, source_target_pairs={{8,0},{0,8},{24,16},{16,24},{9,1},{1,9},{25,17},{17,25},{10,2},{2,... | collective-permute-start | bytes 98312 | tf_op jit(solution)/shard_map/ppermute | solution.py:434
  6.3 0.9 %copy-start = (f32[336,128]{1,0:T(8,128)S(1)}, f32[336,128]{1,0:T(8,128)}, u32[]{:S(2)}) copy-start(f32[336,128]{1,0:T(8,128)} %get-tuple-element.26.kept) | copy-start | bytes 516100
  10.8 6.6 %collective-permute-start.4 = (f32[168,128]{1,0:T(8,128)S(1)}, f32[168,128]{1,0:T(8,128)S(1)}, u32[]{:S(2)}, u32[]{:S(2)}) collective-permute-start(f32[168,128]{1,0:T(8,128)S(1)} %get-tuple-element.33), channel_id=1, source_target_pairs={{1,2},{3,4},{5,6},{2,1},{4,3},{6,5},{9,10},{11,12},{13,14},{10,9},... | collective-permute-start | bytes 258056 | tf_op jit(solution)/shard_map/ppermute | solution.py:413
  17.7 5.7 %collective-permute-start.5 = (f32[432,128]{1,0:T(8,128)S(1)}, f32[432,128]{1,0:T(8,128)S(1)}, u32[]{:S(2)}, u32[]{:S(2)}) collective-permute-start(f32[432,128]{1,0:T(8,128)S(1)} %get-tuple-element.36), channel_id=1, source_target_pairs={{0,8},{16,24},{8,0},{24,16},{1,9},{17,25},{9,1},{25,17},{2,10},{18... | collective-permute-start | bytes 663560 | tf_op jit(solution)/shard_map/ppermute | solution.py:406
  19.2 7.3 %collective-permute-start.6 = (f32[432,128]{1,0:T(8,128)S(1)}, f32[432,128]{1,0:T(8,128)S(1)}, u32[]{:S(2)}, u32[]{:S(2)}) collective-permute-start(f32[432,128]{1,0:T(8,128)S(1)} %get-tuple-element.37), channel_id=1, source_target_pairs={{8,16},{16,8},{9,17},{17,9},{10,18},{18,10},{11,19},{19,11},{12,20... | collective-permute-start | bytes 663560 | tf_op jit(solution)/shard_map/ppermute | solution.py:406
  27.9 4.1 %collective-permute-start.7 = (f32[288,128]{1,0:T(8,128)S(1)}, f32[288,128]{1,0:T(8,128)S(1)}, u32[]{:S(2)}, u32[]{:S(2)}) collective-permute-start(f32[288,128]{1,0:T(8,128)S(1)} %get-tuple-element.41), channel_id=1, source_target_pairs={{0,8},{16,24},{8,0},{24,16},{1,9},{17,25},{9,1},{25,17},{2,10},{18... | collective-permute-start | bytes 442376 | tf_op jit(solution)/shard_map/ppermute | solution.py:406
  28.0 6.2 %collective-permute-start.8 = (f32[288,128]{1,0:T(8,128)S(1)}, f32[288,128]{1,0:T(8,128)S(1)}, u32[]{:S(2)}, u32[]{:S(2)}) collective-permute-start(f32[288,128]{1,0:T(8,128)S(1)} %get-tuple-element.42), channel_id=1, source_target_pairs={{8,16},{16,8},{9,17},{17,9},{10,18},{18,10},{11,19},{19,11},{12,20... | collective-permute-start | bytes 442376 | tf_op jit(solution)/shard_map/ppermute | solution.py:406
  35.3 4.3 %collective-permute-start.9 = (f32[9,2,8,128]{3,2,1,0:T(8,128)S(1)}, f32[9,2,8,128]{3,2,1,0:T(8,128)S(1)}, u32[]{:S(2)}, u32[]{:S(2)}) collective-permute-start(f32[9,2,8,128]{3,2,1,0:T(8,128)S(1)} %get-tuple-element.46), channel_id=1, source_target_pairs={{0,1},{1,0},{2,3},{3,2},{4,5},{5,4},{6,7},{7,6},{8,9},{9,8},{10,11... | collective-permute-start | bytes 221192 | tf_op jit(solution)/shard_map/ppermute | solution.py:416

commit v8 on v7

--- a/solution.py
+++ b/solution.py
@@ -119,10 +119,22 @@
     add_moments(layout, [kept.at[pl.ds(lines + 8, kept.shape[0] - lines - 8)]], acc)
 
 
+def by_core(act):
+    segment = lax.axis_index("segment")
+
+    @pl.when(segment == 0)
+    def _():
+        act(0, lambda reach: slice(STEPS, STEPS + reach), lambda reach: slice(0, STEPS))
+
+    @pl.when(segment == 1)
+    def _():
+        act(1, lambda reach: slice(0, reach), lambda reach: slice(reach, reach + STEPS))
+
+
 def join_kernel(layout, *refs):
     cx, cz, cy = layout
-    kept, got, started, blocks = refs[0], refs[1], refs[2], refs[3:-5]
-    body, count, edge, acc, dense = refs[-5:]
+    kept, got, started, blocks = refs[0], refs[1], refs[2], refs[3:-6]
+    state, ids, times, edge, acc, dense = refs[-6:]
     reach = reach_of(cz)
     half = cx * cz // 2
     acc[...] = started[...]
@@ -131,31 +143,34 @@
         for k in range(2):
             added = acc[c * half : (c + 1) * half, k * cy : (k + 1) * cy]
             dense[c, k * half : (k + 1) * half] = added
-    count[...] = kept[10]
-
-    def join(mine, first, sent):
-        body[mine] = kept[0:10]
-        body[1 - mine] = got[...]
+
+    def join(mine, main, outer):
+        main, outer = main(reach), outer(reach)
+        first = 0 if mine == 0 else cz - reach
+        last = main.start if mine == 0 else main.stop - STEPS
+        gone = slice(last, last + STEPS)
         for x in range(cx):
             at = slice(x * reach, (x + 1) * reach)
+            for model in range(2):
+                rows = kept if model == mine else got
+                state[model, :, x, main] = rows[0:9, at]
+                ids[model, x, main] = rows[9, at]
             added = dense[:, x * cz + first : x * cz + first + reach]
-            body[0, 3:9, at] = body[0, 3:9, at] + added
-        for x in range(cx):
-            row = x * reach + sent
+            state[0, 3:9, x, main] = state[0, 3:9, x, main] + added
+            times[x, main] = kept[10, at]
+            state[:, :, x, outer] = jnp.zeros((2, 9, STEPS, cy), F32)
+            ids[:, x, outer] = jnp.zeros((2, STEPS, cy), F32)
+            times[x, outer] = jnp.zeros((STEPS, cy), F32)
             for k in range(21):
-                at = slice((k * cx + x) * STEPS, (k * cx + x + 1) * STEPS)
-                if k < 20:
-                    edge[at] = body[k // 10, k % 10, row : row + STEPS]
+                line = slice((k * cx + x) * STEPS, (k * cx + x + 1) * STEPS)
+                if k == 20:
+                    edge[line] = times[x, gone]
+                elif k % 10 == 9:
+                    edge[line] = ids[k // 10, x, gone]
                 else:
-                    edge[at] = count[row : row + STEPS]
-
-    @pl.when(lax.axis_index("segment") == 0)
-    def _():
-        join(0, 0, 0)
-
-    @pl.when(lax.axis_index("segment") == 1)
-    def _():
-        join(1, cz - reach, reach - STEPS)
+                    edge[line] = state[k // 10, k % 10, x, gone]
+
+    by_core(join)
 
 
 def by_parity(even, odd, act):
@@ -244,14 +259,13 @@
     return right, left
 
 
-def cut_edges(cx, done, with_ids, velocity, state, ids, times, to_first, to_second):
-    rows = state.shape[3]
-    at = slice(done, rows - done)
-    count = rows - 2 * done
+def cut_edges(cx, rows_of, with_ids, velocity, state, ids, times, to_first, to_second):
     right_units, left_units = edge_units(cx, with_ids)
 
-    def put(to, units):
+    def put(to, units, new_plane):
         for i, (model, what, x) in enumerate(units):
+            at = rows_of(x == new_plane)
+            count = at.stop - at.start
             line = slice(i * count, (i + 1) * count)
             if what == 10:
                 to[line] = times[cx + x, at]
@@ -261,73 +275,94 @@
                 to[line] = state[model, what, cx + x, at]
 
     holders = (to_second, to_first), (to_first, to_second)
-    by_parity(*holders, lambda left, right: put(right, right_units))
+    by_parity(*holders, lambda left, right: put(right, right_units, -1))
     velocity(2 * cx - 1)
-    by_parity(*holders, lambda left, right: put(left, left_units))
-
-
-def planes_kernel(
-    cx, body, count, halo, tables,
+    by_parity(*holders, lambda left, right: put(left, left_units, cx - 1))
+
+
+def outer_rows(mine, outer):
+    def rows_of(new):
+        shift = 1 if new and mine == 0 else 0
+        return slice(outer.start + shift, outer.stop + shift)
+
+    return rows_of
+
+
+def coefficients(cx, planes, tables, ids, coef):
+    for model in range(2):
+        for x in planes:
+            for i, found in enumerate(look_up(tables, ids[model, x])):
+                coef[model, i, x] = found
+
+
+def inner_kernel(cx, own_state, own_ids, own_times, tables, to_first, to_second, state, ids, coef, times):
+    own = slice(cx, 2 * cx)
+    reach = state.shape[3] - STEPS
+    state[:, :, own], ids[:, own], times[own] = own_state[...], own_ids[...], own_times[...]
+    coefficients(cx, range(2 * cx - 1, 2 * cx), tables, ids, coef)
+    velocity = advance(cx, 0, state, coef, times)
+
+    def cut(mine, main, outer):
+        rows_of = lambda new: main(reach)
+        cut_edges(cx, rows_of, True, velocity, state, ids, times, to_first, to_second)
+
+    by_core(cut)
+
+
+def outer_kernel(
+    cx, own_state, own_ids, own_times, halo, tables,
     to_first, to_second, both, coef_out, times_out, state, ids, coef, times,
 ):
-    rows = state.shape[3]
-    reach = rows - STEPS
-
-    def join(main, edge):
+    own = slice(cx, 2 * cx)
+    reach = state.shape[3] - STEPS
+    state[:, :, own], ids[:, own], times[own] = own_state[...], own_ids[...], own_times[...]
+
+    def join(mine, main, outer):
         for x in range(cx):
-            inner = slice(x * reach, (x + 1) * reach)
             for k in range(21):
-                outer = halo[(k * cx + x) * STEPS : (k * cx + x + 1) * STEPS]
-                model, what = k // 10, k % 10
+                line = halo[(k * cx + x) * STEPS : (k * cx + x + 1) * STEPS]
                 if k == 20:
-                    times[cx + x, main] = count[inner]
-                    times[cx + x, edge] = outer
-                elif what == 9:
-                    ids[model, cx + x, main] = body[model, what, inner]
-                    ids[model, cx + x, edge] = outer
+                    times[cx + x, outer(reach)] = line
+                elif k % 10 == 9:
+                    ids[k // 10, cx + x, outer(reach)] = line
                 else:
-                    state[model, what, cx + x, main] = body[model, what, inner]
-                    state[model, what, cx + x, edge] = outer
-
-    @pl.when(lax.axis_index("segment") == 0)
-    def _():
-        join(slice(STEPS, rows), slice(0, STEPS))
-
-    @pl.when(lax.axis_index("segment") == 1)
-    def _():
-        join(slice(0, reach), slice(reach, rows))
-
-    for model in range(2):
-        for x in range(cx, 2 * cx):
-            for i, found in enumerate(look_up(tables, ids[model, x])):
-                coef[model, i, x] = found
-    own = slice(cx, 2 * cx)
+                    state[k // 10, k % 10, cx + x, outer(reach)] = line
+
+    by_core(join)
+    coefficients(cx, range(cx, 2 * cx), tables, ids, coef)
     both[...] = state[:, :, own]
     coef_out[...] = coef[:, :, own]
     times_out[...] = times[own]
     velocity = advance(cx, 0, state, coef, times)
-    cut_edges(cx, 0, True, velocity, state, ids, times, to_first, to_second)
+
+    def cut(mine, main, outer):
+        rows_of = outer_rows(mine, outer(reach))
+        cut_edges(cx, rows_of, True, velocity, state, ids, times, to_first, to_second)
+
+    by_core(cut)
 
 
 def next_kernel(cx, done, *refs):
     first = done == 0
-    both_in, from_first, from_second, coef_in, times_in = refs[0:5]
+    parts = 2 if first else 1
+    both_in, coef_in, times_in = refs[0:3]
+    edges, refs = refs[3 : 3 + 2 * parts], refs[3 + 2 * parts :]
     if first:
-        tables = refs[5]
+        tables, outs = refs[0], refs[1:]
         state, ids, coef, times = refs[-4:]
     else:
+        ids, outs = None, refs
         state, coef, times = refs[-1], coef_in, times_in
-    outs = refs[6 if first else 5 :]
     segment = lax.axis_index("segment")
     rows = state.shape[3]
-    at = slice(done, rows - done)
-    count = rows - 2 * done
     own = slice(cx, 2 * cx)
     state[:, :, own] = both_in[...]
     right_units, left_units = edge_units(cx, first)
 
-    def get(edge, units, start):
+    def get(edge, units, start, rows_of, new_plane):
         for i, (model, what, x) in enumerate(units):
+            at = rows_of(x == new_plane)
+            count = at.stop - at.start
             line = edge[i * count : (i + 1) * count]
             if what == 10:
                 times[start + x, at] = line
@@ -336,18 +371,26 @@
             else:
                 state[model, what, start + x, at] = line
 
-    def place(left, right):
-        get(left, right_units, 0)
-        get(right, left_units, 2 * cx)
-
-    by_parity((from_second, from_first), (from_first, from_second), place)
+    def place(rows_of, pair):
+        def put(left, right):
+            get(left, right_units, 0, rows_of, -1)
+            get(right, left_units, 2 * cx, rows_of, cx - 1)
+
+        by_parity((pair[1], pair[0]), pair, put)
+
     if first:
+
+        def place_both(mine, main, outer):
+            reach = rows - STEPS
+            place(lambda new: main(reach), edges[0:2])
+            place(outer_rows(mine, outer(reach)), edges[2:4])
+
+        by_core(place_both)
         coef[:, :, own] = coef_in[...]
         times[own] = times_in[...]
-        for model in range(2):
-            for x in (*range(1, cx), *range(2 * cx, 3 * cx - 1)):
-                for i, found in enumerate(look_up(tables, ids[model, x])):
-                    coef[model, i, x] = found
+        coefficients(cx, (*range(1, cx), *range(2 * cx, 3 * cx - 1)), tables, ids, coef)
+    else:
+        place(lambda new: slice(done, rows - done), edges)
     velocity = advance(cx, cx, state, coef, times, given_top=True)
     if done + cx == STEPS:
         outs[0][...] = state[segment, :, own, STEPS : rows - STEPS]
@@ -357,7 +400,8 @@
         if first:
             outs[3][...] = coef[...]
             outs[4][...] = times[...]
-        cut_edges(cx, done + cx, False, velocity, state, None, times, outs[0], outs[1])
+        left = slice(done + cx, rows - done - cx)
+        cut_edges(cx, lambda new: left, False, velocity, state, None, times, outs[0], outs[1])
 
 
 def home_kernel(mine, brought, out):
@@ -445,51 +489,66 @@
         [],
         flops=10**9,
     )
-    body, count, edge = call(
+    own = (cx, rows, cy)
+    window = (3 * cx, rows, cy)
+    state, ids, times, edge = call(
         functools.partial(join_kernel, layout),
         "join_and_moments",
         (kept, got, started, *blocks),
         (),
-        [(2, 10, cx * reach, cy), (cx * reach, cy), (21 * cx * STEPS, cy)],
+        [(2, 9, *own), (2, *own), own, (21 * cx * STEPS, cy)],
         [acc_shape, (6, cx * cz, cy)],
     )
     halo = along_depth(edge)
-    own = (cx, rows, cy)
-    window = (3 * cx, rows, cy)
-
-    def edges(done):
-        units = edge_units(cx, done == 0)[0]
-        return [(len(units) * (rows - 2 * done), cy)] * 2
-
-    to_first, to_second, both, coef, times = call(
-        functools.partial(planes_kernel, cx),
-        "own_planes",
-        (body, count, halo, tables),
+    work = [(2, 9, *window), (2, *window), (2, 3, *window), window]
+
+    def edges(count, with_ids):
+        return [(len(edge_units(cx, with_ids)[0]) * count, cy)] * 2
+
+    def exchange(pair):
+        return [pairs(pair[0], 0), pairs(pair[1], 1)]
+
+    inner = call(
+        functools.partial(inner_kernel, cx),
+        "inner_edges",
+        (state, ids, times, tables),
         (),
-        edges(0) + [(2, 9, *own), (2, 3, *own), own],
-        [(2, 9, *window), (2, *window), (2, 3, *window), window],
-    )
+        edges(reach, True),
+        work,
+        flops=10**9,
+    )
+    got_edges = exchange(inner)
+    *outer, both, coef, times = call(
+        functools.partial(outer_kernel, cx),
+        "outer_edges",
+        (state, ids, times, halo, tables),
+        (),
+        edges(STEPS, True) + [(2, 9, *own), (2, 3, *own), own],
+        work,
+        flops=4 * 10**9,
+    )
+    got_edges += exchange(outer)
     for done in range(0, STEPS, cx):
-        from_first, from_second = pairs(to_first, 0), pairs(to_second, 1)
         first, last = done == 0, done + cx == STEPS
-        outs = [(9, cx, cz // 2, cy)] * 2 if last else edges(done + cx) + [(2, 9, *own)]
-        if first:
-            outs = outs + [(2, 3, *window), window]
-        space = [(2, 9, *window)]
-        if first:
-            space += [(2, *window), (2, 3, *window), window]
-        done_now = call(
+        after = done + cx
+        outs = [(9, cx, cz // 2, cy)] * 2
+        if not last:
+            outs = edges(rows - 2 * after, False) + [(2, 9, *own)]
+            outs += [(2, 3, *window), window] * first
+        pair = call(
             functools.partial(next_kernel, cx, done),
             "steps",
-            (both, from_first, from_second, coef, times) + (tables,) * first,
+            (both, coef, times, *got_edges) + (tables,) * first,
             (),
             outs,
-            space,
+            work if first else work[0:1],
         )
-        to_first, to_second = done_now[0:2]
-        if first:
-            coef, times = done_now[3:5]
-        both = done_now[-1] if not first else done_now[2]
+        if not last:
+            got_edges = exchange(pair[0:2])
+            both = pair[2]
+            if first:
+                coef, times = pair[3:5]
+    to_first, to_second = pair[0:2]
     (out,) = call(home_kernel, "home", (to_first, swap(to_second)), (), [fields.shape], [])
     return out
 

time: 41.1 us -> 38.5 us (0.937); the launches traced: 40.3 us -> 38.3 us
  waiting for transfers between devices: 12.9 us -> 8.63 us
  starting transfers between devices: 18.4 us -> 20.3 us
    ppermute x4 -> x6, starting transfers between devices: 6.61 us -> 9.4 us  [pairs(): return lax.ppermute(block, 'sec', route + [(j, i) for i, j in route])]
    ppermute x1, waiting for transfers between devices: 2.45 us -> 0.01 us  [along_depth(): lax.ppermute(block, ('depth', 'segment'), down + [(j, i) for i, j in down])]
    ppermute x4 -> x6, waiting for transfers between devices: 8.33 us -> 6.46 us  [pairs(): return lax.ppermute(block, 'sec', route + [(j, i) for i, j in route])]
    ppermute x2, starting transfers between devices: 4.11 us -> 3.29 us  [swap(): return lax.ppermute(block, 'segment', [(0, 1), (1, 0)])]
    pallas_call x7 -> x8, Pallas kernels: 7.98 us -> 8.27 us  [call(): pl.pallas_call(kernel, out_shape=[jax.ShapeDtypeStruct(shape, F32) for sh...]
  transfers between devices with their start and end apart: 10 -> 12, of which waited for: 8 -> 7; matrix products, arithmetic and copies ran while one was open for 0% -> 0% of each run, Pallas kernels for 2% -> 3%
where the time goes in v8:
time: 38.5 us; the launch traced here: 38.3 us
  starting transfers between devices  20.3 us (53%)
  waiting for transfers between devices  8.63 us (22%)
  Pallas kernels  8.27 us (21%)
  local copies, waits for them, and re-layouts  0.92 us (2%)
    ppermute x6, starting transfers between devices, pairs(): return lax.ppermute(block, 'sec', route + [(j, i) for i, j in route])  9.4 us
    pallas_call x8, Pallas kernels, call(): pl.pallas_call(kernel, out_shape=[jax.ShapeDtypeStruct(shape, F32) for sh...  8.27 us
    ppermute x6, waiting for transfers between devices, pairs(): return lax.ppermute(block, 'sec', route + [(j, i) for i, j in route])  6.46 us
    ppermute x1, starting transfers between devices, along_depth(): lax.ppermute(block, ('depth', 'segment'), down + [(j, i) for i, j in down])  4.14 us
    ppermute x3, starting transfers between devices, on_device(): lax.ppermute(entries, 'sec', [(other(i, k), i) for i in range(sections)])  3.51 us
    ppermute x2, starting transfers between devices, swap(): return lax.ppermute(block, 'segment', [(0, 1), (1, 0)])  3.29 us
    ppermute x3, waiting for transfers between devices, on_device(): lax.ppermute(entries, 'sec', [(other(i, k), i) for i in range(sections)])  1.25 us
    unnamed x2, local copies, waits for them, and re-layouts  0.92 us
  transfers between devices with their start and end apart: 12, of which 7 were waited for; matrix products, arithmetic and copies ran while one was open for 0% of the time, Pallas kernels for 3%

profile of v8, /device:TPU:13, one launch (start us, length us, event | category | flops | bytes accessed | tf_op | source)
XLA Modules:
  0.0 38.3 jit_solution(9095641171954434079)
XLA Ops:
  0.0 2.1 %pack.1 = (f32[64,128]{1,0:T(8,128)}, f32[336,128]{1,0:T(8,128)}, f32[10,24,128]{2,1,0:T(8,128)}) custom-call(f32[1,9,2,16,128]{4,3,2,1,0:T(8,128)} %fields_in.1, s32[1,2,16,128]{3,2,1,0:T(8,128)} %ids_in.1, f32[6,1024]{1,0:T(8,128)} %moments_in.1, s32[8,128]{1,0:T(8,128)} %bitcast.4, s32[8,128]{1,0:T(8,128)} %bitcast.5, s32[16,128]{1,0:T(8,128)} %bitcast.3, ...), custom_call_target="tpu_custom_call" | custom-call | flops 10000000 | bytes 1048576 | tf_op jit(solution)/shard_map/pack/pallas_call | solution.py:428
  2.1 0.7 %collective-permute-start = (f32[10,24,128]{2,1,0:T(8,128)}, f32[10,24,128]{2,1,0:T(8,128)S(1)}, u32[]{:S(2)}, u32[]{:S(2)}) collective-permute-start(f32[10,24,128]{2,1,0:T(8,128)} %get-tuple-element.31), channel_id=1, source_target_pairs={{0,1},{1,0},{2,3},{3,2},{4,5},{5,4},{6,7},{7,6},{8,9},{9,8},{10,11... | collective-permute-start | bytes 368648 | tf_op jit(solution)/shard_map/ppermute | solution.py:460
  2.8 1.3 %collective-permute-start.3 = (f32[64,128]{1,0:T(8,128)}, f32[64,128]{1,0:T(8,128)S(1)}, u32[]{:S(2)}, u32[]{:S(2)}) collective-permute-start(f32[64,128]{1,0:T(8,128)} %get-tuple-element.33), channel_id=1, source_target_pairs={{24,0},{16,8},{8,16},{0,24},{25,1},{17,9},{9,17},{1,25},{26,2},{18... | collective-permute-start | bytes 98312 | tf_op jit(solution)/shard_map/ppermute | solution.py:478
  4.1 1.0 %collective-permute-start.2 = (f32[64,128]{1,0:T(8,128)}, f32[64,128]{1,0:T(8,128)S(1)}, u32[]{:S(2)}, u32[]{:S(2)}) collective-permute-start(f32[64,128]{1,0:T(8,128)} %get-tuple-element.33), channel_id=1, source_target_pairs={{16,0},{24,8},{0,16},{8,24},{17,1},{25,9},{1,17},{9,25},{18,2},{26... | collective-permute-start | bytes 98312 | tf_op jit(solution)/shard_map/ppermute | solution.py:478
  5.1 1.2 %collective-permute-start.1 = (f32[64,128]{1,0:T(8,128)}, f32[64,128]{1,0:T(8,128)S(1)}, u32[]{:S(2)}, u32[]{:S(2)}) collective-permute-start(f32[64,128]{1,0:T(8,128)} %get-tuple-element.33), channel_id=1, source_target_pairs={{8,0},{0,8},{24,16},{16,24},{9,1},{1,9},{25,17},{17,25},{10,2},{2,... | collective-permute-start | bytes 98312 | tf_op jit(solution)/shard_map/ppermute | solution.py:478
  6.3 0.9 %copy-done = f32[336,128]{1,0:T(8,128)S(1)} copy-done((f32[336,128]{1,0:T(8,128)S(1)}, f32[336,128]{1,0:T(8,128)}, u32[]{:S(2)}) %copy-start) | copy-done | bytes 172056
  7.2 0.6 %own_moments.1 = (f32[11,24,128]{2,1,0:T(8,128)S(1)}, f32[8,128]{1,0:T(8,128)S(1)}, f32[96,256]{1,0:T(8,128)S(1)}) custom-call(f32[336,128]{1,0:T(8,128)S(1)} %copy-done), custom_call_target="tpu_custom_call" | custom-call | flops 1000000000 | bytes 1048576 | tf_op jit(solution)/shard_map/own_moments/pallas_call | solution.py:428
  8.0 1.2 %collective-permute-done.1.refs_3_ = f32[64,128]{1,0:T(8,128)S(1)} collective-permute-done((f32[64,128]{1,0:T(8,128)}, f32[64,128]{1,0:T(8,128)S(1)}, u32[]{:S(2)}, u32[]{:S(2)}) %collective-permute-start.1) | collective-permute-done | bytes 32800 | tf_op jit(solution)/shard_map/ppermute | solution.py:478
  9.1 1.7 %join_and_moments.1 = (f32[2,9,2,16,128]{4,3,2,1,0:T(8,128)S(1)}, f32[2,2,16,128]{3,2,1,0:T(8,128)S(1)}, f32[2,16,128]{2,1,0:T(8,128)S(1)}, f32[168,128]{1,0:T(8,128)S(1)}) custom-call(f32[11,24,128]{2,1,0:T(8,128)S(1)} %get-tuple-element.30.refs_0_, f32[10,24,128]{2,1,0:T(8,128)S(1)} %collective-permute-done.refs_1_, ...), custom_call_target="tpu_custom_call" | custom-call | flops 10000000 | bytes 1048576 | tf_op jit(solution)/shard_map/join_and_moments/pallas_call | solution.py:428
  10.9 4.1 %collective-permute-start.4 = (f32[168,128]{1,0:T(8,128)S(1)}, f32[168,128]{1,0:T(8,128)S(1)}, u32[]{:S(2)}, u32[]{:S(2)}) collective-permute-start(f32[168,128]{1,0:T(8,128)S(1)} %get-tuple-element.37), channel_id=1, source_target_pairs={{1,2},{3,4},{5,6},{2,1},{4,3},{6,5},{9,10},{11,12},{13,14},{10,9},... | collective-permute-start | bytes 258056 | tf_op jit(solution)/shard_map/ppermute | solution.py:457
  15.2 1.5 %collective-permute-start.5 = (f32[324,128]{1,0:T(8,128)S(1)}, f32[324,128]{1,0:T(8,128)S(1)}, u32[]{:S(2)}, u32[]{:S(2)}) collective-permute-start(f32[324,128]{1,0:T(8,128)S(1)} %get-tuple-element.42), channel_id=1, source_target_pairs={{0,8},{16,24},{8,0},{24,16},{1,9},{17,25},{9,1},{25,17},{2,10},{18... | collective-permute-start | bytes 497672 | tf_op jit(solution)/shard_map/ppermute | solution.py:450
  16.7 2.5 %collective-permute-start.6 = (f32[324,128]{1,0:T(8,128)S(1)}, f32[324,128]{1,0:T(8,128)S(1)}, u32[]{:S(2)}, u32[]{:S(2)}) collective-permute-start(f32[324,128]{1,0:T(8,128)S(1)} %get-tuple-element.43), channel_id=1, source_target_pairs={{8,16},{16,8},{9,17},{17,9},{10,18},{18,10},{11,19},{19,11},{12,20... | collective-permute-start | bytes 497672 | tf_op jit(solution)/shard_map/ppermute | solution.py:450
  19.2 0.3 outer_edges.1
  19.6 2.8 %collective-permute-start.8 = (f32[108,128]{1,0:T(8,128)S(1)}, f32[108,128]{1,0:T(8,128)S(1)}, u32[]{:S(2)}, u32[]{:S(2)}) collective-permute-start(f32[108,128]{1,0:T(8,128)S(1)} %get-tuple-element.45), channel_id=1, source_target_pairs={{8,16},{16,8},{9,17},{17,9},{10,18},{18,10},{11,19},{19,11},{12,20... | collective-permute-start | bytes 165896 | tf_op jit(solution)/shard_map/ppermute | solution.py:450
  22.3 0.8 %collective-permute-done.7.refs_5_ = f32[108,128]{1,0:T(8,128)S(1)} collective-permute-done((f32[108,128]{1,0:T(8,128)S(1)}, f32[108,128]{1,0:T(8,128)S(1)}, u32[]{:S(2)}, u32[]{:S(2)}) %collective-permute-start.7) | collective-permute-done | bytes 55328 | tf_op jit(solution)/shard_map/ppermute | solution.py:450
  23.2 2.0 %collective-permute-done.8.refs_6_ = f32[108,128]{1,0:T(8,128)S(1)} collective-permute-done((f32[108,128]{1,0:T(8,128)S(1)}, f32[108,128]{1,0:T(8,128)S(1)}, u32[]{:S(2)}, u32[]{:S(2)}) %collective-permute-start.8) | collective-permute-done | bytes 55328 | tf_op jit(solution)/shard_map/ppermute | solution.py:450
  25.2 1.5 %steps.2 = (f32[288,128]{1,0:T(8,128)S(1)}, f32[288,128]{1,0:T(8,128)S(1)}, f32[2,9,2,16,128]{4,3,2,1,0:T(8,128)S(1)}, f32[2,3,6,16,128]{4,3,2,1,0:T(8,128)S(1)}, f32[6,16,128]{2,1,0:T(8,128)S(1)}) custom-call(f32[2,9,2,16,128]{4,3,2,1,0:T(8,128)S(1)} %get-tuple-element.39.refs_0_, f32[2,3,2,16,128]{4,3,2,1,0:T(8,128)S(1)} %get-tuple-element.40.refs_1_, ...), custom_call_target="tpu_custom_call" | custom-call | flops 10000000 | bytes 1048576 | tf_op jit(solution)/shard_map/steps/pallas_call | solution.py:428
  26.7 2.5 %collective-permute-start.10 = (f32[288,128]{1,0:T(8,128)S(1)}, f32[288,128]{1,0:T(8,128)S(1)}, u32[]{:S(2)}, u32[]{:S(2)}) collective-permute-start(f32[288,128]{1,0:T(8,128)S(1)} %get-tuple-element.50), channel_id=1, source_target_pairs={{8,16},{16,8},{9,17},{17,9},{10,18},{18,10},{11,19},{19,11},{12,20... | collective-permute-start | bytes 442376 | tf_op jit(solution)/shard_map/ppermute | solution.py:450
  29.3 1.4 %collective-permute-done.9.refs_3_ = f32[288,128]{1,0:T(8,128)S(1)} collective-permute-done((f32[288,128]{1,0:T(8,128)S(1)}, f32[288,128]{1,0:T(8,128)S(1)}, u32[]{:S(2)}, u32[]{:S(2)}) %collective-permute-start.9) | collective-permute-done | bytes 147488 | tf_op jit(solution)/shard_map/ppermute | solution.py:450
  30.7 2.2 %collective-permute-done.10.refs_4_ = f32[288,128]{1,0:T(8,128)S(1)} collective-permute-done((f32[288,128]{1,0:T(8,128)S(1)}, f32[288,128]{1,0:T(8,128)S(1)}, u32[]{:S(2)}, u32[]{:S(2)}) %collective-permute-start.10) | collective-permute-done | bytes 147488 | tf_op jit(solution)/shard_map/ppermute | solution.py:450
  32.9 1.2 %steps.3 = (f32[9,2,8,128]{3,2,1,0:T(8,128)S(1)}, f32[9,2,8,128]{3,2,1,0:T(8,128)S(1)}) custom-call(f32[2,9,2,16,128]{4,3,2,1,0:T(8,128)S(1)} %get-tuple-element.46.refs_0_, f32[2,3,6,16,128]{4,3,2,1,0:T(8,128)S(1)} %get-tuple-element.47.refs_1_, f32[6,16,128]{2,1,0:T(8,128)S(1)} %get-tuple-element.48.refs_2_, ...), custom_call_target="tpu_custom_call" | custom-call | flops 10000000 | bytes 1048576 | tf_op jit(solution)/shard_map/steps/pallas_call | solution.py:428
  34.1 2.6 %collective-permute-start.11 = (f32[9,2,8,128]{3,2,1,0:T(8,128)S(1)}, f32[9,2,8,128]{3,2,1,0:T(8,128)S(1)}, u32[]{:S(2)}, u32[]{:S(2)}) collective-permute-start(f32[9,2,8,128]{3,2,1,0:T(8,128)S(1)} %get-tuple-element.52), channel_id=1, source_target_pairs={{0,1},{1,0},{2,3},{3,2},{4,5},{5,4},{6,7},{7,6},{8,9},{9,8},{10,11... | collective-permute-start | bytes 221192 | tf_op jit(solution)/shard_map/ppermute | solution.py:460
  36.7 0.9 %collective-permute-done.11.brought = f32[9,2,8,128]{3,2,1,0:T(8,128)S(1)} collective-permute-done((f32[9,2,8,128]{3,2,1,0:T(8,128)S(1)}, f32[9,2,8,128]{3,2,1,0:T(8,128)S(1)}, u32[]{:S(2)}, u32[]{:S(2)}) %collective-permute-start.11) | collective-permute-done | bytes 73760 | tf_op jit(solution)/shard_map/ppermute | solution.py:460
  37.6 0.7 %home.1 = f32[1,9,2,16,128]{4,3,2,1,0:T(8,128)} custom-call(f32[9,2,8,128]{3,2,1,0:T(8,128)S(1)} %get-tuple-element.51.mine, f32[9,2,8,128]{3,2,1,0:T(8,128)S(1)} %collective-permute-done.11.brought), custom_call_target="tpu_custom_call" | custom-call | flops 10000000 | bytes 1048576 | tf_op jit(solution)/shard_map/home/pallas_call | solution.py:428
  (10 shorter events, 0.5 us)
Async XLA Ops:
  2.1 7.1 %collective-permute-start = (f32[10,24,128]{2,1,0:T(8,128)}, f32[10,24,128]{2,1,0:T(8,128)S(1)}, u32[]{:S(2)}, u32[]{:S(2)}) collective-permute-start(f32[10,24,128]{2,1,0:T(8,128)} %get-tuple-element.31), channel_id=1, source_target_pairs={{0,1},{1,0},{2,3},{3,2},{4,5},{5,4},{6,7},{7,6},{8,9},{9,8},{10,11... | collective-permute-start | bytes 368648 | tf_op jit(solution)/shard_map/ppermute | solution.py:460
  2.8 5.1 %collective-permute-start.3 = (f32[64,128]{1,0:T(8,128)}, f32[64,128]{1,0:T(8,128)S(1)}, u32[]{:S(2)}, u32[]{:S(2)}) collective-permute-start(f32[64,128]{1,0:T(8,128)} %get-tuple-element.33), channel_id=1, source_target_pairs={{24,0},{16,8},{8,16},{0,24},{25,1},{17,9},{9,17},{1,25},{26,2},{18... | collective-permute-start | bytes 98312 | tf_op jit(solution)/shard_map/ppermute | solution.py:478
  4.1 3.9 %collective-permute-start.2 = (f32[64,128]{1,0:T(8,128)}, f32[64,128]{1,0:T(8,128)S(1)}, u32[]{:S(2)}, u32[]{:S(2)}) collective-permute-start(f32[64,128]{1,0:T(8,128)} %get-tuple-element.33), channel_id=1, source_target_pairs={{16,0},{24,8},{0,16},{8,24},{17,1},{25,9},{1,17},{9,25},{18,2},{26... | collective-permute-start | bytes 98312 | tf_op jit(solution)/shard_map/ppermute | solution.py:478
  5.1 4.0 %collective-permute-start.1 = (f32[64,128]{1,0:T(8,128)}, f32[64,128]{1,0:T(8,128)S(1)}, u32[]{:S(2)}, u32[]{:S(2)}) collective-permute-start(f32[64,128]{1,0:T(8,128)} %get-tuple-element.33), channel_id=1, source_target_pairs={{8,0},{0,8},{24,16},{16,24},{9,1},{1,9},{25,17},{17,25},{10,2},{2,... | collective-permute-start | bytes 98312 | tf_op jit(solution)/shard_map/ppermute | solution.py:478
  6.3 0.9 %copy-start = (f32[336,128]{1,0:T(8,128)S(1)}, f32[336,128]{1,0:T(8,128)}, u32[]{:S(2)}) copy-start(f32[336,128]{1,0:T(8,128)} %get-tuple-element.29.kept) | copy-start | bytes 516100
  10.9 8.3 %collective-permute-start.4 = (f32[168,128]{1,0:T(8,128)S(1)}, f32[168,128]{1,0:T(8,128)S(1)}, u32[]{:S(2)}, u32[]{:S(2)}) collective-permute-start(f32[168,128]{1,0:T(8,128)S(1)} %get-tuple-element.37), channel_id=1, source_target_pairs={{1,2},{3,4},{5,6},{2,1},{4,3},{6,5},{9,10},{11,12},{13,14},{10,9},... | collective-permute-start | bytes 258056 | tf_op jit(solution)/shard_map/ppermute | solution.py:457
  15.2 9.9 %collective-permute-start.5 = (f32[324,128]{1,0:T(8,128)S(1)}, f32[324,128]{1,0:T(8,128)S(1)}, u32[]{:S(2)}, u32[]{:S(2)}) collective-permute-start(f32[324,128]{1,0:T(8,128)S(1)} %get-tuple-element.42), channel_id=1, source_target_pairs={{0,8},{16,24},{8,0},{24,16},{1,9},{17,25},{9,1},{25,17},{2,10},{18... | collective-permute-start | bytes 497672 | tf_op jit(solution)/shard_map/ppermute | solution.py:450
  16.7 8.5 %collective-permute-start.6 = (f32[324,128]{1,0:T(8,128)S(1)}, f32[324,128]{1,0:T(8,128)S(1)}, u32[]{:S(2)}, u32[]{:S(2)}) collective-permute-start(f32[324,128]{1,0:T(8,128)S(1)} %get-tuple-element.43), channel_id=1, source_target_pairs={{8,16},{16,8},{9,17},{17,9},{10,18},{18,10},{11,19},{19,11},{12,20... | collective-permute-start | bytes 497672 | tf_op jit(solution)/shard_map/ppermute | solution.py:450
  19.5 3.7 %collective-permute-start.7 = (f32[108,128]{1,0:T(8,128)S(1)}, f32[108,128]{1,0:T(8,128)S(1)}, u32[]{:S(2)}, u32[]{:S(2)}) collective-permute-start(f32[108,128]{1,0:T(8,128)S(1)} %get-tuple-element.44), channel_id=1, source_target_pairs={{0,8},{16,24},{8,0},{24,16},{1,9},{17,25},{9,1},{25,17},{2,10},{18... | collective-permute-start | bytes 165896 | tf_op jit(solution)/shard_map/ppermute | solution.py:450
  19.6 5.6 %collective-permute-start.8 = (f32[108,128]{1,0:T(8,128)S(1)}, f32[108,128]{1,0:T(8,128)S(1)}, u32[]{:S(2)}, u32[]{:S(2)}) collective-permute-start(f32[108,128]{1,0:T(8,128)S(1)} %get-tuple-element.45), channel_id=1, source_target_pairs={{8,16},{16,8},{9,17},{17,9},{10,18},{18,10},{11,19},{19,11},{12,20... | collective-permute-start | bytes 165896 | tf_op jit(solution)/shard_map/ppermute | solution.py:450
  26.7 4.1 %collective-permute-start.9 = (f32[288,128]{1,0:T(8,128)S(1)}, f32[288,128]{1,0:T(8,128)S(1)}, u32[]{:S(2)}, u32[]{:S(2)}) collective-permute-start(f32[288,128]{1,0:T(8,128)S(1)} %get-tuple-element.49), channel_id=1, source_target_pairs={{0,8},{16,24},{8,0},{24,16},{1,9},{17,25},{9,1},{25,17},{2,10},{18... | collective-permute-start | bytes 442376 | tf_op jit(solution)/shard_map/ppermute | solution.py:450
  26.7 6.2 %collective-permute-start.10 = (f32[288,128]{1,0:T(8,128)S(1)}, f32[288,128]{1,0:T(8,128)S(1)}, u32[]{:S(2)}, u32[]{:S(2)}) collective-permute-start(f32[288,128]{1,0:T(8,128)S(1)} %get-tuple-element.50), channel_id=1, source_target_pairs={{8,16},{16,8},{9,17},{17,9},{10,18},{18,10},{11,19},{19,11},{12,20... | collective-permute-start | bytes 442376 | tf_op jit(solution)/shard_map/ppermute | solution.py:450
  34.1 3.5 %collective-permute-start.11 = (f32[9,2,8,128]{3,2,1,0:T(8,128)S(1)}, f32[9,2,8,128]{3,2,1,0:T(8,128)S(1)}, u32[]{:S(2)}, u32[]{:S(2)}) collective-permute-start(f32[9,2,8,128]{3,2,1,0:T(8,128)S(1)} %get-tuple-element.52), channel_id=1, source_target_pairs={{0,1},{1,0},{2,3},{3,2},{4,5},{5,4},{6,7},{7,6},{8,9},{9,8},{10,11... | collective-permute-start | bytes 221192 | tf_op jit(solution)/shard_map/ppermute | solution.py:460

commit v9 on v8

--- a/solution.py
+++ b/solution.py
@@ -41,20 +41,24 @@
     return cz // 2 + STEPS
 
 
-def pack_kernel(
-    fields_in, ids_in, moments_in, owner_in, cells_in, rows_in, buoyancy, lame_lambda, lame_mu,
-    entries, kept, given, fields, ids, moments, owner, cells, rows, wide, tables, sem,
-):
-    cx, cz, cy = ids.shape[1:]
-    arguments = [(fields_in, fields), (ids_in, ids), (moments_in, moments), (owner_in, owner)]
-    arguments += [(cells_in, cells), (rows_in, rows)]
-    arguments += [(t, tables.at[i]) for i, t in enumerate((buoyancy, lame_lambda, lame_mu))]
-    copy_all(sem, arguments)
+def entries_kernel(moments_in, owner_in, cells_in, entries, moments, owner, cells, sem):
+    copy_all(sem, [(moments_in, moments), (owner_in, owner), (cells_in, cells)])
+    cy = cells.shape[1]
     for i in range(cells.shape[0]):
         at = 8 * i
         entries[at : at + 6] = moments[:, i * cy : (i + 1) * cy]
         entries[at + 6 : at + 7] = owner[i : i + 1, :].astype(F32)
         entries[at + 7 : at + 8] = cells[i : i + 1, :].astype(F32)
+
+
+def pack_kernel(
+    fields_in, ids_in, rows_in, entries_in, buoyancy, lame_lambda, lame_mu,
+    kept, given, fields, ids, rows, entries, wide, tables, sem,
+):
+    cx, cz, cy = ids.shape[1:]
+    arguments = [(fields_in, fields), (ids_in, ids), (rows_in, rows), (entries_in, entries)]
+    arguments += [(t, tables.at[i]) for i, t in enumerate((buoyancy, lame_lambda, lame_mu))]
+    copy_all(sem, arguments)
     wide[0] = (ids[0] + 1).astype(F32)
     line = in_line(rows[...])
     high = one_hot(line // cy, cx * cz).astype(BF16)
@@ -91,32 +95,34 @@
         cut(cz - reach, 0)
 
 
-def add_moments(layout, blocks, acc):
+def moments_of(layout, entries):
     cx, cz, cy = layout
     section = lax.axis_index("sec")
     half = cx * cz // 2
-    for entries in blocks:
-        chunk = [entries[8 * i : 8 * i + 8] for i in range(entries.shape[0] // 8)]
-        entry = jnp.concatenate(chunk, axis=1)
-        owner = entry[6:7].astype(jnp.int32)
-        cell = entry[7:8].astype(jnp.int32)
-        line = jnp.where(owner == section, cell // cy, -1)
-        upper = line >= half
-        high = one_hot(jnp.where(upper, line - half, line), half)
-        low = one_hot(jnp.where(upper, cell % cy + cy, cell % cy), 2 * cy).astype(BF16)
-        for part in split3(entry[0:6]):
-            spread = [(high * part[c : c + 1]).astype(BF16) for c in range(6)]
-            acc[...] += lax.dot_general(
-                jnp.concatenate(spread, axis=0), low, NT, preferred_element_type=F32
-            )
+    chunk = [entries[8 * i : 8 * i + 8] for i in range(entries.shape[0] // 8)]
+    entry = jnp.concatenate(chunk, axis=1)
+    owner = entry[6:7].astype(jnp.int32)
+    cell = entry[7:8].astype(jnp.int32)
+    line = jnp.where(owner == section, cell // cy, -1)
+    upper = line >= half
+    high = one_hot(jnp.where(upper, line - half, line), half)
+    low = one_hot(jnp.where(upper, cell % cy + cy, cell % cy), 2 * cy).astype(BF16)
+    total = jnp.zeros((6 * half, 2 * cy), F32)
+    for part in split3(entry[0:6]):
+        spread = jnp.concatenate([(high * part[c : c + 1]).astype(BF16) for c in range(6)], axis=0)
+        total = total + lax.dot_general(spread, low, NT, preferred_element_type=F32)
+    return total
 
 
 def own_kernel(layout, kept, out, tables, acc):
     lines = out.shape[0] * out.shape[1]
     out[...] = kept[0:lines].reshape(out.shape)
     tables[...] = kept[lines : lines + 8]
-    acc[...] = jnp.zeros_like(acc)
-    add_moments(layout, [kept.at[pl.ds(lines + 8, kept.shape[0] - lines - 8)]], acc)
+    acc[...] = moments_of(layout, kept[lines + 8 :])
+
+
+def more_kernel(layout, started, entries, acc):
+    acc[...] = started[...] + moments_of(layout, entries[...])
 
 
 def by_core(act):
@@ -133,15 +139,13 @@
 
 def join_kernel(layout, *refs):
     cx, cz, cy = layout
-    kept, got, started, blocks = refs[0], refs[1], refs[2], refs[3:-6]
-    state, ids, times, edge, acc, dense = refs[-6:]
+    kept, got, started, entries, state, ids, times, edge, dense = refs
     reach = reach_of(cz)
     half = cx * cz // 2
-    acc[...] = started[...]
-    add_moments(layout, blocks, acc)
+    total = started[...] + moments_of(layout, entries[...])
     for c in range(6):
         for k in range(2):
-            added = acc[c * half : (c + 1) * half, k * cy : (k + 1) * cy]
+            added = total[c * half : (c + 1) * half, k * cy : (k + 1) * cy]
             dense[c, k * half : (k + 1) * half] = added
 
     def join(mine, main, outer):
@@ -220,10 +224,9 @@
     for step in range(steps):
         left = steps - 1 - step
         low, high = cx - left, 2 * cx + left
-        pl.loop(low, high + 1 - (given_top and step == 0))(velocity)
-
-        @pl.loop(low, high)
-        def _(x):
+        for x in range(low, high + 1 - (given_top and step == 0)):
+            velocity(x)
+        for x in range(low, high):
             for model in range(2):
                 vx, vy, vz = (state[model, k, x] for k in range(3))
                 vx_n, vy_n, vz_n = (state[model, k, x + 1] for k in range(3))
@@ -262,11 +265,11 @@
 def cut_edges(cx, rows_of, with_ids, velocity, state, ids, times, to_first, to_second):
     right_units, left_units = edge_units(cx, with_ids)
 
-    def put(to, units, new_plane):
-        for i, (model, what, x) in enumerate(units):
-            at = rows_of(x == new_plane)
-            count = at.stop - at.start
-            line = slice(i * count, (i + 1) * count)
+    def put(to, units, far, right):
+        line = slice(0, 0)
+        for model, what, x in units:
+            at = rows_of(x == far, right)
+            line = slice(line.stop, line.stop + at.stop - at.start)
             if what == 10:
                 to[line] = times[cx + x, at]
             elif what == 9:
@@ -275,15 +278,25 @@
                 to[line] = state[model, what, cx + x, at]
 
     holders = (to_second, to_first), (to_first, to_second)
-    by_parity(*holders, lambda left, right: put(right, right_units, -1))
+    by_parity(*holders, lambda left, right: put(right, right_units, 0, True))
     velocity(2 * cx - 1)
-    by_parity(*holders, lambda left, right: put(left, left_units, cx - 1))
+    by_parity(*holders, lambda left, right: put(left, left_units, cx - 1, False))
 
 
 def outer_rows(mine, outer):
-    def rows_of(new):
-        shift = 1 if new and mine == 0 else 0
+    def rows_of(far, right):
+        shift = 1 if far and not right and mine == 0 else 0
         return slice(outer.start + shift, outer.stop + shift)
+
+    return rows_of
+
+
+def reached_rows(cx, done, rows):
+    def rows_of(far, right):
+        first, last = done, rows - done
+        if right:
+            return slice(first + (cx if far else 1), last)
+        return slice(first + far, last - (cx if far else 1))
 
     return rows_of
 
@@ -303,7 +316,7 @@
     velocity = advance(cx, 0, state, coef, times)
 
     def cut(mine, main, outer):
-        rows_of = lambda new: main(reach)
+        rows_of = lambda far, right: main(reach)
         cut_edges(cx, rows_of, True, velocity, state, ids, times, to_first, to_second)
 
     by_core(cut)
@@ -359,11 +372,12 @@
     state[:, :, own] = both_in[...]
     right_units, left_units = edge_units(cx, first)
 
-    def get(edge, units, start, rows_of, new_plane):
-        for i, (model, what, x) in enumerate(units):
-            at = rows_of(x == new_plane)
-            count = at.stop - at.start
-            line = edge[i * count : (i + 1) * count]
+    def get(edge, units, start, rows_of, far, right):
+        last = 0
+        for model, what, x in units:
+            at = rows_of(x == far, right)
+            first, last = last, last + at.stop - at.start
+            line = edge[first:last]
             if what == 10:
                 times[start + x, at] = line
             elif what == 9:
@@ -373,8 +387,8 @@
 
     def place(rows_of, pair):
         def put(left, right):
-            get(left, right_units, 0, rows_of, -1)
-            get(right, left_units, 2 * cx, rows_of, cx - 1)
+            get(left, right_units, 0, rows_of, 0, True)
+            get(right, left_units, 2 * cx, rows_of, cx - 1, False)
 
         by_parity((pair[1], pair[0]), pair, put)
 
@@ -382,7 +396,7 @@
 
         def place_both(mine, main, outer):
             reach = rows - STEPS
-            place(lambda new: main(reach), edges[0:2])
+            place(lambda far, right: main(reach), edges[0:2])
             place(outer_rows(mine, outer(reach)), edges[2:4])
 
         by_core(place_both)
@@ -390,7 +404,7 @@
         times[own] = times_in[...]
         coefficients(cx, (*range(1, cx), *range(2 * cx, 3 * cx - 1)), tables, ids, coef)
     else:
-        place(lambda new: slice(done, rows - done), edges)
+        place(reached_rows(cx, done, rows), edges)
     velocity = advance(cx, cx, state, coef, times, given_top=True)
     if done + cx == STEPS:
         outs[0][...] = state[segment, :, own, STEPS : rows - STEPS]
@@ -400,8 +414,8 @@
         if first:
             outs[3][...] = coef[...]
             outs[4][...] = times[...]
-        left = slice(done + cx, rows - done - cx)
-        cut_edges(cx, lambda new: left, False, velocity, state, None, times, outs[0], outs[1])
+        rows_of = reached_rows(cx, done + cx, rows)
+        cut_edges(cx, rows_of, False, velocity, state, None, times, outs[0], outs[1])
 
 
 def home_kernel(mine, brought, out):
@@ -461,23 +475,34 @@
 
     owner = moment_owner.reshape(-1, cy)
     cells = moment_cells.reshape(-1, cy)
-    arguments = (fields, block_ids, moments, owner, cells, drm_rows.reshape(-1, cy))
+    boundary = drm_rows.reshape(-1, cy)
     entry_lines = 8 * cells.shape[0]
-    entries, kept, given = call(
+    (entries,) = call(
+        entries_kernel,
+        "entries",
+        (),
+        (moments, owner, cells),
+        [(entry_lines, cy)],
+        [pltpu.VMEM(a.shape, a.dtype) for a in (moments, owner, cells)],
+        3,
+        limit=64 * 2**20,
+    )
+    blocks = [
+        lax.ppermute(entries, "sec", [(other(i, k), i) for i in range(sections)])
+        for k in range(1, sections)
+    ]
+    arguments = (fields, block_ids, boundary, entries)
+    kept, given = call(
         pack_kernel,
         "pack",
         (),
         (*arguments, buoyancy, lame_lambda, lame_mu),
-        [(entry_lines, cy), (11 * cx * reach + 8 + entry_lines, cy), (10, cx * reach, cy)],
+        [(11 * cx * reach + 8 + entry_lines, cy), (10, cx * reach, cy)],
         [pltpu.VMEM(a.shape, a.dtype) for a in arguments]
         + [(2, cx, cz, cy), pltpu.SMEM((3, buoyancy.shape[0]), F32)],
         len(arguments) + 3,
         limit=64 * 2**20,
     )
-    blocks = [
-        lax.ppermute(entries, "sec", [(other(i, k), i) for i in range(sections)])
-        for k in range(1, sections)
-    ]
     got = swap(given)
     acc_shape = (6 * cx * cz // 2, 2 * cy)
     kept, tables, started = call(
@@ -489,21 +514,37 @@
         [],
         flops=10**9,
     )
+    for block in blocks[:-1]:
+        (started,) = call(
+            functools.partial(more_kernel, layout),
+            "more_moments",
+            (started, block),
+            (),
+            [acc_shape],
+            [],
+            flops=10**9,
+        )
     own = (cx, rows, cy)
     window = (3 * cx, rows, cy)
     state, ids, times, edge = call(
         functools.partial(join_kernel, layout),
         "join_and_moments",
-        (kept, got, started, *blocks),
+        (kept, got, started, blocks[-1]),
         (),
         [(2, 9, *own), (2, *own), own, (21 * cx * STEPS, cy)],
-        [acc_shape, (6, cx * cz, cy)],
+        [(6, cx * cz, cy)],
     )
     halo = along_depth(edge)
     work = [(2, 9, *window), (2, *window), (2, 3, *window), window]
 
     def edges(count, with_ids):
         return [(len(edge_units(cx, with_ids)[0]) * count, cy)] * 2
+
+    def reached_edges(done):
+        rows_of = reached_rows(cx, done, rows)
+        whole, far = rows_of(False, True), rows_of(True, True)
+        lines = 18 * (cx - 1) * (whole.stop - whole.start) + 6 * (far.stop - far.start)
+        return [(-(-lines // 8) * 8, cy)] * 2
 
     def exchange(pair):
         return [pairs(pair[0], 0), pairs(pair[1], 1)]
@@ -533,7 +574,7 @@
         after = done + cx
         outs = [(9, cx, cz // 2, cy)] * 2
         if not last:
-            outs = edges(rows - 2 * after, False) + [(2, 9, *own)]
+            outs = reached_edges(after) + [(2, 9, *own)]
             outs += [(2, 3, *window), window] * first
         pair = call(
             functools.partial(next_kernel, cx, done),

time: 38.5 us -> 40.1 us (1.042)
  waiting for transfers between devices: 8.63 us -> 5.85 us
  Pallas kernels: 8.27 us -> 10.6 us
  starting transfers between devices: 20.3 us -> 22 us
    pallas_call x8 -> x11, Pallas kernels: 8.27 us -> 10.6 us  [call(): pl.pallas_call(kernel, out_shape=[jax.ShapeDtypeStruct(shape, F32) for sh...]
    ppermute x6, starting transfers between devices: 9.4 us -> 11.1 us  [pairs(): return lax.ppermute(block, 'sec', route + [(j, i) for i, j in route])]
    ppermute x6, waiting for transfers between devices: 6.46 us -> 4.93 us  [pairs(): return lax.ppermute(block, 'sec', route + [(j, i) for i, j in route])]
    ppermute x3, waiting for transfers between devices: 1.25 us -> 0.01 us  [on_device(): lax.ppermute(entries, 'sec', [(other(i, k), i) for i in range(sections)])]
    ppermute x1, starting transfers between devices: 4.14 us -> 3.01 us  [along_depth(): lax.ppermute(block, ('depth', 'segment'), down + [(j, i) for i, j in down])]
    ppermute x2, starting transfers between devices: 3.29 us -> 4.37 us  [swap(): return lax.ppermute(block, 'segment', [(0, 1), (1, 0)])]
  transfers between devices with their start and end apart: 12 -> 12, of which waited for: 7 -> 5; matrix products, arithmetic and copies ran while one was open for 0% -> 0% of each run, Pallas kernels for 3% -> 15%
where the time goes in v9:
time: 40.1 us; the launch traced here: 39.5 us
  starting transfers between devices  22 us (55%)
  Pallas kernels  10.6 us (26%)
  waiting for transfers between devices  5.85 us (15%)
  local copies, waits for them, and re-layouts  0.92 us (2%)
    ppermute x6, starting transfers between devices, pairs(): return lax.ppermute(block, 'sec', route + [(j, i) for i, j in route])  11.1 us
    pallas_call x11, Pallas kernels, call(): pl.pallas_call(kernel, out_shape=[jax.ShapeDtypeStruct(shape, F32) for sh...  10.6 us
    ppermute x6, waiting for transfers between devices, pairs(): return lax.ppermute(block, 'sec', route + [(j, i) for i, j in route])  4.93 us
    ppermute x2, starting transfers between devices, swap(): return lax.ppermute(block, 'segment', [(0, 1), (1, 0)])  4.37 us
    ppermute x3, starting transfers between devices, on_device(): lax.ppermute(entries, 'sec', [(other(i, k), i) for i in range(sections)])  3.56 us
    ppermute x1, starting transfers between devices, along_depth(): lax.ppermute(block, ('depth', 'segment'), down + [(j, i) for i, j in down])  3.01 us
    unnamed x2, local copies, waits for them, and re-layouts  0.92 us
    ppermute x2, waiting for transfers between devices, swap(): return lax.ppermute(block, 'segment', [(0, 1), (1, 0)])  0.92 us
  transfers between devices with their start and end apart: 12, of which 5 were waited for; matrix products, arithmetic and copies ran while one was open for 0% of the time, Pallas kernels for 15%

profile of v9, /device:TPU:13, one launch (start us, length us, event | category | flops | bytes accessed | tf_op | source)
XLA Modules:
  0.0 39.5 jit_solution(15517972400620581007)
XLA Ops:
  0.0 1.4 %entries.1.entries_in = f32[64,128]{1,0:T(8,128)} custom-call(f32[6,1024]{1,0:T(8,128)} %moments_in.1, s32[8,128]{1,0:T(8,128)} %bitcast.4, s32[8,128]{1,0:T(8,128)} %bitcast.5), custom_call_target="tpu_custom_call" | custom-call | flops 10000000 | bytes 1048576 | tf_op jit(solution)/shard_map/entries/pallas_call | solution.py:442
  1.4 1.4 %collective-permute-start.3 = (f32[64,128]{1,0:T(8,128)}, f32[64,128]{1,0:T(8,128)}, u32[]{:S(2)}, u32[]{:S(2)}) collective-permute-start(f32[64,128]{1,0:T(8,128)} %entries.1.entries_in), channel_id=1, source_target_pairs={{24,0},{16,8},{8,16},{0,24},{25,1},{17,9},{9,17},{1,25},{26,2},{18... | collective-permute-start | bytes 98312 | tf_op jit(solution)/shard_map/ppermute | solution.py:491
  2.8 1.1 %collective-permute-start.2 = (f32[64,128]{1,0:T(8,128)}, f32[64,128]{1,0:T(8,128)}, u32[]{:S(2)}, u32[]{:S(2)}) collective-permute-start(f32[64,128]{1,0:T(8,128)} %entries.1.entries_in), channel_id=1, source_target_pairs={{16,0},{24,8},{0,16},{8,24},{17,1},{25,9},{1,17},{9,25},{18,2},{26... | collective-permute-start | bytes 98312 | tf_op jit(solution)/shard_map/ppermute | solution.py:491
  3.9 1.1 %collective-permute-start.1 = (f32[64,128]{1,0:T(8,128)}, f32[64,128]{1,0:T(8,128)}, u32[]{:S(2)}, u32[]{:S(2)}) collective-permute-start(f32[64,128]{1,0:T(8,128)} %entries.1.entries_in), channel_id=1, source_target_pairs={{8,0},{0,8},{24,16},{16,24},{9,1},{1,9},{25,17},{17,25},{10,2},{2,... | collective-permute-start | bytes 98312 | tf_op jit(solution)/shard_map/ppermute | solution.py:491
  5.0 2.0 %pack.1 = (f32[336,128]{1,0:T(8,128)}, f32[10,24,128]{2,1,0:T(8,128)}) custom-call(f32[1,9,2,16,128]{4,3,2,1,0:T(8,128)} %fields_in.1, s32[1,2,16,128]{3,2,1,0:T(8,128)} %ids_in.1, s32[16,128]{1,0:T(8,128)} %bitcast.3, f32[64,128]{1,0:T(8,128)} %entries.1.entries_in, f32[16]{0:T(128)} %buoyancy.1, f32[16]{0:T(128)} %lame_lambda.1, f32[16]{0:T(128)} %lame_mu.1), custom_call_target="tpu_custom_call" | custom-call | flops 10000000 | bytes 1048576 | tf_op jit(solution)/shard_map/pack/pallas_call | solution.py:442
  7.0 1.3 %collective-permute-start = (f32[10,24,128]{2,1,0:T(8,128)}, f32[10,24,128]{2,1,0:T(8,128)S(1)}, u32[]{:S(2)}, u32[]{:S(2)}) collective-permute-start(f32[10,24,128]{2,1,0:T(8,128)} %get-tuple-element.30), channel_id=1, source_target_pairs={{0,1},{1,0},{2,3},{3,2},{4,5},{5,4},{6,7},{7,6},{8,9},{9,8},{10,11... | collective-permute-start | bytes 368648 | tf_op jit(solution)/shard_map/ppermute | solution.py:474
  8.3 0.9 %copy-done = f32[336,128]{1,0:T(8,128)S(1)} copy-done((f32[336,128]{1,0:T(8,128)S(1)}, f32[336,128]{1,0:T(8,128)}, u32[]{:S(2)}) %copy-start) | copy-done | bytes 172056
  9.2 0.7 %own_moments.1 = (f32[11,24,128]{2,1,0:T(8,128)S(1)}, f32[8,128]{1,0:T(8,128)S(1)}, f32[96,256]{1,0:T(8,128)S(1)}) custom-call(f32[336,128]{1,0:T(8,128)S(1)} %copy-done), custom_call_target="tpu_custom_call" | custom-call | flops 1000000000 | bytes 1048576 | tf_op jit(solution)/shard_map/own_moments/pallas_call | solution.py:442
  9.9 1.4 %more_moments.2.started = f32[96,256]{1,0:T(8,128)S(1)} custom-call(f32[96,256]{1,0:T(8,128)S(1)} %get-tuple-element.31.started, f32[64,128]{1,0:T(8,128)} %collective-permute-done.1.entries), custom_call_target="tpu_custom_call" | custom-call | flops 1000000000 | bytes 1048576 | tf_op jit(solution)/shard_map/more_moments/pallas_call | solution.py:442
  11.3 1.4 %more_moments.3.refs_2_ = f32[96,256]{1,0:T(8,128)S(1)} custom-call(f32[96,256]{1,0:T(8,128)S(1)} %more_moments.2.started, f32[64,128]{1,0:T(8,128)} %collective-permute-done.2.entries), custom_call_target="tpu_custom_call" | custom-call | flops 1000000000 | bytes 1048576 | tf_op jit(solution)/shard_map/more_moments/pallas_call | solution.py:442
  12.7 1.5 %join_and_moments.1 = (f32[2,9,2,16,128]{4,3,2,1,0:T(8,128)S(1)}, f32[2,2,16,128]{3,2,1,0:T(8,128)S(1)}, f32[2,16,128]{2,1,0:T(8,128)S(1)}, f32[168,128]{1,0:T(8,128)S(1)}) custom-call(f32[11,24,128]{2,1,0:T(8,128)S(1)} %get-tuple-element.29.refs_0_, f32[10,24,128]{2,1,0:T(8,128)S(1)} %collective-permute-done.refs_1_, f32[96,256]{1,0:T(8,128)S(1)} %more_moments.3.refs_2_, ...), custom_call_target="tpu_custom_call" | custom-call | flops 10000000 | bytes 1048576 | tf_op jit(solution)/shard_map/join_and_moments/pallas_call | solution.py:442
  14.2 3.0 %collective-permute-start.4 = (f32[168,128]{1,0:T(8,128)S(1)}, f32[168,128]{1,0:T(8,128)S(1)}, u32[]{:S(2)}, u32[]{:S(2)}) collective-permute-start(f32[168,128]{1,0:T(8,128)S(1)} %get-tuple-element.35), channel_id=1, source_target_pairs={{1,2},{3,4},{5,6},{2,1},{4,3},{6,5},{9,10},{11,12},{13,14},{10,9},... | collective-permute-start | bytes 258056 | tf_op jit(solution)/shard_map/ppermute | solution.py:471
  17.5 0.6 %collective-permute-start.5 = (f32[324,128]{1,0:T(8,128)S(1)}, f32[324,128]{1,0:T(8,128)S(1)}, u32[]{:S(2)}, u32[]{:S(2)}) collective-permute-start(f32[324,128]{1,0:T(8,128)S(1)} %get-tuple-element.40), channel_id=1, source_target_pairs={{0,8},{16,24},{8,0},{24,16},{1,9},{17,25},{9,1},{25,17},{2,10},{18... | collective-permute-start | bytes 497672 | tf_op jit(solution)/shard_map/ppermute | solution.py:464
  18.0 4.3 %collective-permute-start.6 = (f32[324,128]{1,0:T(8,128)S(1)}, f32[324,128]{1,0:T(8,128)S(1)}, u32[]{:S(2)}, u32[]{:S(2)}) collective-permute-start(f32[324,128]{1,0:T(8,128)S(1)} %get-tuple-element.41), channel_id=1, source_target_pairs={{8,16},{16,8},{9,17},{17,9},{10,18},{18,10},{11,19},{19,11},{12,20... | collective-permute-start | bytes 497672 | tf_op jit(solution)/shard_map/ppermute | solution.py:464
  22.7 2.8 %collective-permute-start.8 = (f32[108,128]{1,0:T(8,128)S(1)}, f32[108,128]{1,0:T(8,128)S(1)}, u32[]{:S(2)}, u32[]{:S(2)}) collective-permute-start(f32[108,128]{1,0:T(8,128)S(1)} %get-tuple-element.43), channel_id=1, source_target_pairs={{8,16},{16,8},{9,17},{17,9},{10,18},{18,10},{11,19},{19,11},{12,20... | collective-permute-start | bytes 165896 | tf_op jit(solution)/shard_map/ppermute | solution.py:464
  25.5 0.5 %collective-permute-done.7.refs_5_ = f32[108,128]{1,0:T(8,128)S(1)} collective-permute-done((f32[108,128]{1,0:T(8,128)S(1)}, f32[108,128]{1,0:T(8,128)S(1)}, u32[]{:S(2)}, u32[]{:S(2)}) %collective-permute-start.7) | collective-permute-done | bytes 55328 | tf_op jit(solution)/shard_map/ppermute | solution.py:464
  26.0 1.6 %collective-permute-done.8.refs_6_ = f32[108,128]{1,0:T(8,128)S(1)} collective-permute-done((f32[108,128]{1,0:T(8,128)S(1)}, f32[108,128]{1,0:T(8,128)S(1)}, u32[]{:S(2)}, u32[]{:S(2)}) %collective-permute-start.8) | collective-permute-done | bytes 55328 | tf_op jit(solution)/shard_map/ppermute | solution.py:464
  27.7 0.6 %steps.2 = (f32[264,128]{1,0:T(8,128)S(1)}, f32[264,128]{1,0:T(8,128)S(1)}, f32[2,9,2,16,128]{4,3,2,1,0:T(8,128)S(1)}, f32[2,3,6,16,128]{4,3,2,1,0:T(8,128)S(1)}, f32[6,16,128]{2,1,0:T(8,128)S(1)}) custom-call(f32[2,9,2,16,128]{4,3,2,1,0:T(8,128)S(1)} %get-tuple-element.37.refs_0_, f32[2,3,2,16,128]{4,3,2,1,0:T(8,128)S(1)} %get-tuple-element.38.refs_1_, ...), custom_call_target="tpu_custom_call" | custom-call | flops 10000000 | bytes 1048576 | tf_op jit(solution)/shard_map/steps/pallas_call | solution.py:442
  28.4 3.3 %collective-permute-start.10 = (f32[264,128]{1,0:T(8,128)S(1)}, f32[264,128]{1,0:T(8,128)S(1)}, u32[]{:S(2)}, u32[]{:S(2)}) collective-permute-start(f32[264,128]{1,0:T(8,128)S(1)} %get-tuple-element.48), channel_id=1, source_target_pairs={{8,16},{16,8},{9,17},{17,9},{10,18},{18,10},{11,19},{19,11},{12,20... | collective-permute-start | bytes 405512 | tf_op jit(solution)/shard_map/ppermute | solution.py:464
  31.6 0.6 %collective-permute-done.9.refs_3_ = f32[264,128]{1,0:T(8,128)S(1)} collective-permute-done((f32[264,128]{1,0:T(8,128)S(1)}, f32[264,128]{1,0:T(8,128)S(1)}, u32[]{:S(2)}, u32[]{:S(2)}) %collective-permute-start.9) | collective-permute-done | bytes 135200 | tf_op jit(solution)/shard_map/ppermute | solution.py:464
  32.2 2.2 %collective-permute-done.10.refs_4_ = f32[264,128]{1,0:T(8,128)S(1)} collective-permute-done((f32[264,128]{1,0:T(8,128)S(1)}, f32[264,128]{1,0:T(8,128)S(1)}, u32[]{:S(2)}, u32[]{:S(2)}) %collective-permute-start.10) | collective-permute-done | bytes 135200 | tf_op jit(solution)/shard_map/ppermute | solution.py:464
  34.9 3.1 %collective-permute-start.11 = (f32[9,2,8,128]{3,2,1,0:T(8,128)S(1)}, f32[9,2,8,128]{3,2,1,0:T(8,128)S(1)}, u32[]{:S(2)}, u32[]{:S(2)}) collective-permute-start(f32[9,2,8,128]{3,2,1,0:T(8,128)S(1)} %get-tuple-element.50), channel_id=1, source_target_pairs={{0,1},{1,0},{2,3},{3,2},{4,5},{5,4},{6,7},{7,6},{8,9},{9,8},{10,11... | collective-permute-start | bytes 221192 | tf_op jit(solution)/shard_map/ppermute | solution.py:474
  37.9 0.9 %collective-permute-done.11.brought = f32[9,2,8,128]{3,2,1,0:T(8,128)S(1)} collective-permute-done((f32[9,2,8,128]{3,2,1,0:T(8,128)S(1)}, f32[9,2,8,128]{3,2,1,0:T(8,128)S(1)}, u32[]{:S(2)}, u32[]{:S(2)}) %collective-permute-start.11) | collective-permute-done | bytes 73760 | tf_op jit(solution)/shard_map/ppermute | solution.py:474
  38.9 0.7 %home.1 = f32[1,9,2,16,128]{4,3,2,1,0:T(8,128)} custom-call(f32[9,2,8,128]{3,2,1,0:T(8,128)S(1)} %get-tuple-element.49.mine, f32[9,2,8,128]{3,2,1,0:T(8,128)S(1)} %collective-permute-done.11.brought), custom_call_target="tpu_custom_call" | custom-call | flops 10000000 | bytes 1048576 | tf_op jit(solution)/shard_map/home/pallas_call | solution.py:442
  (13 shorter events, 1.1 us)
Async XLA Ops:
  1.4 11.3 %collective-permute-start.3 = (f32[64,128]{1,0:T(8,128)}, f32[64,128]{1,0:T(8,128)}, u32[]{:S(2)}, u32[]{:S(2)}) collective-permute-start(f32[64,128]{1,0:T(8,128)} %entries.1.entries_in), channel_id=1, source_target_pairs={{24,0},{16,8},{8,16},{0,24},{25,1},{17,9},{9,17},{1,25},{26,2},{18... | collective-permute-start | bytes 98312 | tf_op jit(solution)/shard_map/ppermute | solution.py:491
  2.8 8.5 %collective-permute-start.2 = (f32[64,128]{1,0:T(8,128)}, f32[64,128]{1,0:T(8,128)}, u32[]{:S(2)}, u32[]{:S(2)}) collective-permute-start(f32[64,128]{1,0:T(8,128)} %entries.1.entries_in), channel_id=1, source_target_pairs={{16,0},{24,8},{0,16},{8,24},{17,1},{25,9},{1,17},{9,25},{18,2},{26... | collective-permute-start | bytes 98312 | tf_op jit(solution)/shard_map/ppermute | solution.py:491
  3.9 6.0 %collective-permute-start.1 = (f32[64,128]{1,0:T(8,128)}, f32[64,128]{1,0:T(8,128)}, u32[]{:S(2)}, u32[]{:S(2)}) collective-permute-start(f32[64,128]{1,0:T(8,128)} %entries.1.entries_in), channel_id=1, source_target_pairs={{8,0},{0,8},{24,16},{16,24},{9,1},{1,9},{25,17},{17,25},{10,2},{2,... | collective-permute-start | bytes 98312 | tf_op jit(solution)/shard_map/ppermute | solution.py:491
  7.0 5.7 %collective-permute-start = (f32[10,24,128]{2,1,0:T(8,128)}, f32[10,24,128]{2,1,0:T(8,128)S(1)}, u32[]{:S(2)}, u32[]{:S(2)}) collective-permute-start(f32[10,24,128]{2,1,0:T(8,128)} %get-tuple-element.30), channel_id=1, source_target_pairs={{0,1},{1,0},{2,3},{3,2},{4,5},{5,4},{6,7},{7,6},{8,9},{9,8},{10,11... | collective-permute-start | bytes 368648 | tf_op jit(solution)/shard_map/ppermute | solution.py:474
  8.3 0.9 %copy-start = (f32[336,128]{1,0:T(8,128)S(1)}, f32[336,128]{1,0:T(8,128)}, u32[]{:S(2)}) copy-start(f32[336,128]{1,0:T(8,128)} %get-tuple-element.28.kept) | copy-start | bytes 516100
  14.2 8.1 %collective-permute-start.4 = (f32[168,128]{1,0:T(8,128)S(1)}, f32[168,128]{1,0:T(8,128)S(1)}, u32[]{:S(2)}, u32[]{:S(2)}) collective-permute-start(f32[168,128]{1,0:T(8,128)S(1)} %get-tuple-element.35), channel_id=1, source_target_pairs={{1,2},{3,4},{5,6},{2,1},{4,3},{6,5},{9,10},{11,12},{13,14},{10,9},... | collective-permute-start | bytes 258056 | tf_op jit(solution)/shard_map/ppermute | solution.py:471
  17.5 10.2 %collective-permute-start.5 = (f32[324,128]{1,0:T(8,128)S(1)}, f32[324,128]{1,0:T(8,128)S(1)}, u32[]{:S(2)}, u32[]{:S(2)}) collective-permute-start(f32[324,128]{1,0:T(8,128)S(1)} %get-tuple-element.40), channel_id=1, source_target_pairs={{0,8},{16,24},{8,0},{24,16},{1,9},{17,25},{9,1},{25,17},{2,10},{18... | collective-permute-start | bytes 497672 | tf_op jit(solution)/shard_map/ppermute | solution.py:464
  18.0 9.6 %collective-permute-start.6 = (f32[324,128]{1,0:T(8,128)S(1)}, f32[324,128]{1,0:T(8,128)S(1)}, u32[]{:S(2)}, u32[]{:S(2)}) collective-permute-start(f32[324,128]{1,0:T(8,128)S(1)} %get-tuple-element.41), channel_id=1, source_target_pairs={{8,16},{16,8},{9,17},{17,9},{10,18},{18,10},{11,19},{19,11},{12,20... | collective-permute-start | bytes 497672 | tf_op jit(solution)/shard_map/ppermute | solution.py:464
  22.7 3.4 %collective-permute-start.7 = (f32[108,128]{1,0:T(8,128)S(1)}, f32[108,128]{1,0:T(8,128)S(1)}, u32[]{:S(2)}, u32[]{:S(2)}) collective-permute-start(f32[108,128]{1,0:T(8,128)S(1)} %get-tuple-element.42), channel_id=1, source_target_pairs={{0,8},{16,24},{8,0},{24,16},{1,9},{17,25},{9,1},{25,17},{2,10},{18... | collective-permute-start | bytes 165896 | tf_op jit(solution)/shard_map/ppermute | solution.py:464
  22.7 4.9 %collective-permute-start.8 = (f32[108,128]{1,0:T(8,128)S(1)}, f32[108,128]{1,0:T(8,128)S(1)}, u32[]{:S(2)}, u32[]{:S(2)}) collective-permute-start(f32[108,128]{1,0:T(8,128)S(1)} %get-tuple-element.43), channel_id=1, source_target_pairs={{8,16},{16,8},{9,17},{17,9},{10,18},{18,10},{11,19},{19,11},{12,20... | collective-permute-start | bytes 165896 | tf_op jit(solution)/shard_map/ppermute | solution.py:464
  28.3 3.9 %collective-permute-start.9 = (f32[264,128]{1,0:T(8,128)S(1)}, f32[264,128]{1,0:T(8,128)S(1)}, u32[]{:S(2)}, u32[]{:S(2)}) collective-permute-start(f32[264,128]{1,0:T(8,128)S(1)} %get-tuple-element.47), channel_id=1, source_target_pairs={{0,8},{16,24},{8,0},{24,16},{1,9},{17,25},{9,1},{25,17},{2,10},{18... | collective-permute-start | bytes 405512 | tf_op jit(solution)/shard_map/ppermute | solution.py:464
  28.4 6.1 %collective-permute-start.10 = (f32[264,128]{1,0:T(8,128)S(1)}, f32[264,128]{1,0:T(8,128)S(1)}, u32[]{:S(2)}, u32[]{:S(2)}) collective-permute-start(f32[264,128]{1,0:T(8,128)S(1)} %get-tuple-element.48), channel_id=1, source_target_pairs={{8,16},{16,8},{9,17},{17,9},{10,18},{18,10},{11,19},{19,11},{12,20... | collective-permute-start | bytes 405512 | tf_op jit(solution)/shard_map/ppermute | solution.py:464
  34.9 4.0 %collective-permute-start.11 = (f32[9,2,8,128]{3,2,1,0:T(8,128)S(1)}, f32[9,2,8,128]{3,2,1,0:T(8,128)S(1)}, u32[]{:S(2)}, u32[]{:S(2)}) collective-permute-start(f32[9,2,8,128]{3,2,1,0:T(8,128)S(1)} %get-tuple-element.50), channel_id=1, source_target_pairs={{0,1},{1,0},{2,3},{3,2},{4,5},{5,4},{6,7},{7,6},{8,9},{9,8},{10,11... | collective-permute-start | bytes 221192 | tf_op jit(solution)/shard_map/ppermute | solution.py:474

commit v10 on v9

--- a/solution.py
+++ b/solution.py
@@ -41,24 +41,20 @@
     return cz // 2 + STEPS
 
 
-def entries_kernel(moments_in, owner_in, cells_in, entries, moments, owner, cells, sem):
-    copy_all(sem, [(moments_in, moments), (owner_in, owner), (cells_in, cells)])
-    cy = cells.shape[1]
+def pack_kernel(
+    fields_in, ids_in, moments_in, owner_in, cells_in, rows_in, buoyancy, lame_lambda, lame_mu,
+    entries, kept, given, fields, ids, moments, owner, cells, rows, wide, tables, sem,
+):
+    cx, cz, cy = ids.shape[1:]
+    arguments = [(fields_in, fields), (ids_in, ids), (moments_in, moments), (owner_in, owner)]
+    arguments += [(cells_in, cells), (rows_in, rows)]
+    arguments += [(t, tables.at[i]) for i, t in enumerate((buoyancy, lame_lambda, lame_mu))]
+    copy_all(sem, arguments)
     for i in range(cells.shape[0]):
         at = 8 * i
         entries[at : at + 6] = moments[:, i * cy : (i + 1) * cy]
         entries[at + 6 : at + 7] = owner[i : i + 1, :].astype(F32)
         entries[at + 7 : at + 8] = cells[i : i + 1, :].astype(F32)
-
-
-def pack_kernel(
-    fields_in, ids_in, rows_in, entries_in, buoyancy, lame_lambda, lame_mu,
-    kept, given, fields, ids, rows, entries, wide, tables, sem,
-):
-    cx, cz, cy = ids.shape[1:]
-    arguments = [(fields_in, fields), (ids_in, ids), (rows_in, rows), (entries_in, entries)]
-    arguments += [(t, tables.at[i]) for i, t in enumerate((buoyancy, lame_lambda, lame_mu))]
-    copy_all(sem, arguments)
     wide[0] = (ids[0] + 1).astype(F32)
     line = in_line(rows[...])
     high = one_hot(line // cy, cx * cz).astype(BF16)
@@ -475,34 +471,23 @@
 
     owner = moment_owner.reshape(-1, cy)
     cells = moment_cells.reshape(-1, cy)
-    boundary = drm_rows.reshape(-1, cy)
+    arguments = (fields, block_ids, moments, owner, cells, drm_rows.reshape(-1, cy))
     entry_lines = 8 * cells.shape[0]
-    (entries,) = call(
-        entries_kernel,
-        "entries",
+    entries, kept, given = call(
+        pack_kernel,
+        "pack",
         (),
-        (moments, owner, cells),
-        [(entry_lines, cy)],
-        [pltpu.VMEM(a.shape, a.dtype) for a in (moments, owner, cells)],
-        3,
+        (*arguments, buoyancy, lame_lambda, lame_mu),
+        [(entry_lines, cy), (11 * cx * reach + 8 + entry_lines, cy), (10, cx * reach, cy)],
+        [pltpu.VMEM(a.shape, a.dtype) for a in arguments]
+        + [(2, cx, cz, cy), pltpu.SMEM((3, buoyancy.shape[0]), F32)],
+        len(arguments) + 3,
         limit=64 * 2**20,
     )
     blocks = [
         lax.ppermute(entries, "sec", [(other(i, k), i) for i in range(sections)])
         for k in range(1, sections)
     ]
-    arguments = (fields, block_ids, boundary, entries)
-    kept, given = call(
-        pack_kernel,
-        "pack",
-        (),
-        (*arguments, buoyancy, lame_lambda, lame_mu),
-        [(11 * cx * reach + 8 + entry_lines, cy), (10, cx * reach, cy)],
-        [pltpu.VMEM(a.shape, a.dtype) for a in arguments]
-        + [(2, cx, cz, cy), pltpu.SMEM((3, buoyancy.shape[0]), F32)],
-        len(arguments) + 3,
-        limit=64 * 2**20,
-    )
     got = swap(given)
     acc_shape = (6 * cx * cz // 2, 2 * cy)
     kept, tables, started = call(

time: 40.1 us -> 36.6 us (0.913)
  Pallas kernels: 10.6 us -> 6.96 us
  waiting for transfers between devices: 5.85 us -> 6.55 us
  starting transfers between devices: 22 us -> 21.5 us
    pallas_call x11 -> x10, Pallas kernels: 10.6 us -> 6.96 us  [call(): pl.pallas_call(kernel, out_shape=[jax.ShapeDtypeStruct(shape, F32) for sh...]
    ppermute x1, starting transfers between devices: 3.01 us -> 4.29 us  [along_depth(): lax.ppermute(block, ('depth', 'segment'), down + [(j, i) for i, j in down])]
    ppermute x6, starting transfers between devices: 11.1 us -> 9.89 us  [pairs(): return lax.ppermute(block, 'sec', route + [(j, i) for i, j in route])]
    ppermute x6, waiting for transfers between devices: 4.93 us -> 5.63 us  [pairs(): return lax.ppermute(block, 'sec', route + [(j, i) for i, j in route])]
    ppermute x2, starting transfers between devices: 4.37 us -> 3.79 us  [swap(): return lax.ppermute(block, 'segment', [(0, 1), (1, 0)])]
  transfers between devices with their start and end apart: 12 -> 12, of which waited for: 5 -> 5; matrix products, arithmetic and copies ran while one was open for 0% -> 0% of each run, Pallas kernels for 15% -> 7%
where the time goes in v10:
time: 36.6 us; the launch traced here: 36.1 us
  starting transfers between devices  21.5 us (59%)
  Pallas kernels  6.96 us (19%)
  waiting for transfers between devices  6.55 us (18%)
  local copies, waits for them, and re-layouts  0.92 us (3%)
    ppermute x6, starting transfers between devices, pairs(): return lax.ppermute(block, 'sec', route + [(j, i) for i, j in route])  9.89 us
    pallas_call x10, Pallas kernels, call(): pl.pallas_call(kernel, out_shape=[jax.ShapeDtypeStruct(shape, F32) for sh...  6.96 us
    ppermute x6, waiting for transfers between devices, pairs(): return lax.ppermute(block, 'sec', route + [(j, i) for i, j in route])  5.63 us
    ppermute x1, starting transfers between devices, along_depth(): lax.ppermute(block, ('depth', 'segment'), down + [(j, i) for i, j in down])  4.29 us
    ppermute x2, starting transfers between devices, swap(): return lax.ppermute(block, 'segment', [(0, 1), (1, 0)])  3.79 us
    ppermute x3, starting transfers between devices, on_device(): lax.ppermute(entries, 'sec', [(other(i, k), i) for i in range(sections)])  3.56 us
    unnamed x2, local copies, waits for them, and re-layouts  0.92 us
    ppermute x2, waiting for transfers between devices, swap(): return lax.ppermute(block, 'segment', [(0, 1), (1, 0)])  0.92 us
  transfers between devices with their start and end apart: 12, of which 5 were waited for; matrix products, arithmetic and copies ran while one was open for 0% of the time, Pallas kernels for 7%

profile of v10, /device:TPU:13, one launch (start us, length us, event | category | flops | bytes accessed | tf_op | source)
XLA Modules:
  0.0 36.1 jit_solution(17891211417150851237)
XLA Ops:
  0.0 2.1 %pack.1 = (f32[64,128]{1,0:T(8,128)}, f32[336,128]{1,0:T(8,128)}, f32[10,24,128]{2,1,0:T(8,128)}) custom-call(f32[1,9,2,16,128]{4,3,2,1,0:T(8,128)} %fields_in.1, s32[1,2,16,128]{3,2,1,0:T(8,128)} %ids_in.1, f32[6,1024]{1,0:T(8,128)} %moments_in.1, s32[8,128]{1,0:T(8,128)} %bitcast.4, s32[8,128]{1,0:T(8,128)} %bitcast.5, s32[16,128]{1,0:T(8,128)} %bitcast.3, ...), custom_call_target="tpu_custom_call" | custom-call | flops 10000000 | bytes 1048576 | tf_op jit(solution)/shard_map/pack/pallas_call | solution.py:438
  2.1 1.4 %collective-permute-start.3 = (f32[64,128]{1,0:T(8,128)}, f32[64,128]{1,0:T(8,128)S(1)}, u32[]{:S(2)}, u32[]{:S(2)}) collective-permute-start(f32[64,128]{1,0:T(8,128)} %get-tuple-element.33), channel_id=1, source_target_pairs={{24,0},{16,8},{8,16},{0,24},{25,1},{17,9},{9,17},{1,25},{26,2},{18... | collective-permute-start | bytes 98312 | tf_op jit(solution)/shard_map/ppermute | solution.py:488
  3.4 1.1 %collective-permute-start.2 = (f32[64,128]{1,0:T(8,128)}, f32[64,128]{1,0:T(8,128)S(1)}, u32[]{:S(2)}, u32[]{:S(2)}) collective-permute-start(f32[64,128]{1,0:T(8,128)} %get-tuple-element.33), channel_id=1, source_target_pairs={{16,0},{24,8},{0,16},{8,24},{17,1},{25,9},{1,17},{9,25},{18,2},{26... | collective-permute-start | bytes 98312 | tf_op jit(solution)/shard_map/ppermute | solution.py:488
  4.5 1.1 %collective-permute-start.1 = (f32[64,128]{1,0:T(8,128)}, f32[64,128]{1,0:T(8,128)S(1)}, u32[]{:S(2)}, u32[]{:S(2)}) collective-permute-start(f32[64,128]{1,0:T(8,128)} %get-tuple-element.33), channel_id=1, source_target_pairs={{8,0},{0,8},{24,16},{16,24},{9,1},{1,9},{25,17},{17,25},{10,2},{2,... | collective-permute-start | bytes 98312 | tf_op jit(solution)/shard_map/ppermute | solution.py:488
  5.6 1.2 %collective-permute-start = (f32[10,24,128]{2,1,0:T(8,128)}, f32[10,24,128]{2,1,0:T(8,128)S(1)}, u32[]{:S(2)}, u32[]{:S(2)}) collective-permute-start(f32[10,24,128]{2,1,0:T(8,128)} %get-tuple-element.31), channel_id=1, source_target_pairs={{0,1},{1,0},{2,3},{3,2},{4,5},{5,4},{6,7},{7,6},{8,9},{9,8},{10,11... | collective-permute-start | bytes 368648 | tf_op jit(solution)/shard_map/ppermute | solution.py:470
  6.9 0.9 %copy-done = f32[336,128]{1,0:T(8,128)S(1)} copy-done((f32[336,128]{1,0:T(8,128)S(1)}, f32[336,128]{1,0:T(8,128)}, u32[]{:S(2)}) %copy-start) | copy-done | bytes 172056
  7.8 0.7 %own_moments.1 = (f32[11,24,128]{2,1,0:T(8,128)S(1)}, f32[8,128]{1,0:T(8,128)S(1)}, f32[96,256]{1,0:T(8,128)S(1)}) custom-call(f32[336,128]{1,0:T(8,128)S(1)} %copy-done), custom_call_target="tpu_custom_call" | custom-call | flops 1000000000 | bytes 1048576 | tf_op jit(solution)/shard_map/own_moments/pallas_call | solution.py:438
  8.4 0.7 %more_moments.2.started = f32[96,256]{1,0:T(8,128)S(1)} custom-call(f32[96,256]{1,0:T(8,128)S(1)} %get-tuple-element.32.started, f32[64,128]{1,0:T(8,128)S(1)} %collective-permute-done.1.entries), custom_call_target="tpu_custom_call" | custom-call | flops 1000000000 | bytes 1048576 | tf_op jit(solution)/shard_map/more_moments/pallas_call | solution.py:438
  9.1 0.7 %more_moments.3.refs_2_ = f32[96,256]{1,0:T(8,128)S(1)} custom-call(f32[96,256]{1,0:T(8,128)S(1)} %more_moments.2.started, f32[64,128]{1,0:T(8,128)S(1)} %collective-permute-done.2.entries), custom_call_target="tpu_custom_call" | custom-call | flops 1000000000 | bytes 1048576 | tf_op jit(solution)/shard_map/more_moments/pallas_call | solution.py:438
  9.8 0.7 %join_and_moments.1 = (f32[2,9,2,16,128]{4,3,2,1,0:T(8,128)S(1)}, f32[2,2,16,128]{3,2,1,0:T(8,128)S(1)}, f32[2,16,128]{2,1,0:T(8,128)S(1)}, f32[168,128]{1,0:T(8,128)S(1)}) custom-call(f32[11,24,128]{2,1,0:T(8,128)S(1)} %get-tuple-element.30.refs_0_, f32[10,24,128]{2,1,0:T(8,128)S(1)} %collective-permute-done.refs_1_, f32[96,256]{1,0:T(8,128)S(1)} %more_moments.3.refs_2_, ...), custom_call_target="tpu_custom_call" | custom-call | flops 10000000 | bytes 1048576 | tf_op jit(solution)/shard_map/join_and_moments/pallas_call | solution.py:438
  10.5 4.3 %collective-permute-start.4 = (f32[168,128]{1,0:T(8,128)S(1)}, f32[168,128]{1,0:T(8,128)S(1)}, u32[]{:S(2)}, u32[]{:S(2)}) collective-permute-start(f32[168,128]{1,0:T(8,128)S(1)} %get-tuple-element.37), channel_id=1, source_target_pairs={{1,2},{3,4},{5,6},{2,1},{4,3},{6,5},{9,10},{11,12},{13,14},{10,9},... | collective-permute-start | bytes 258056 | tf_op jit(solution)/shard_map/ppermute | solution.py:467
  15.0 1.3 %collective-permute-start.5 = (f32[324,128]{1,0:T(8,128)S(1)}, f32[324,128]{1,0:T(8,128)S(1)}, u32[]{:S(2)}, u32[]{:S(2)}) collective-permute-start(f32[324,128]{1,0:T(8,128)S(1)} %get-tuple-element.42), channel_id=1, source_target_pairs={{0,8},{16,24},{8,0},{24,16},{1,9},{17,25},{9,1},{25,17},{2,10},{18... | collective-permute-start | bytes 497672 | tf_op jit(solution)/shard_map/ppermute | solution.py:460
  16.3 3.2 %collective-permute-start.6 = (f32[324,128]{1,0:T(8,128)S(1)}, f32[324,128]{1,0:T(8,128)S(1)}, u32[]{:S(2)}, u32[]{:S(2)}) collective-permute-start(f32[324,128]{1,0:T(8,128)S(1)} %get-tuple-element.43), channel_id=1, source_target_pairs={{8,16},{16,8},{9,17},{17,9},{10,18},{18,10},{11,19},{19,11},{12,20... | collective-permute-start | bytes 497672 | tf_op jit(solution)/shard_map/ppermute | solution.py:460
  19.8 2.1 %collective-permute-start.8 = (f32[108,128]{1,0:T(8,128)S(1)}, f32[108,128]{1,0:T(8,128)S(1)}, u32[]{:S(2)}, u32[]{:S(2)}) collective-permute-start(f32[108,128]{1,0:T(8,128)S(1)} %get-tuple-element.45), channel_id=1, source_target_pairs={{8,16},{16,8},{9,17},{17,9},{10,18},{18,10},{11,19},{19,11},{12,20... | collective-permute-start | bytes 165896 | tf_op jit(solution)/shard_map/ppermute | solution.py:460
  22.0 1.2 %collective-permute-done.7.refs_5_ = f32[108,128]{1,0:T(8,128)S(1)} collective-permute-done((f32[108,128]{1,0:T(8,128)S(1)}, f32[108,128]{1,0:T(8,128)S(1)}, u32[]{:S(2)}, u32[]{:S(2)}) %collective-permute-start.7) | collective-permute-done | bytes 55328 | tf_op jit(solution)/shard_map/ppermute | solution.py:460
  23.1 1.6 %collective-permute-done.8.refs_6_ = f32[108,128]{1,0:T(8,128)S(1)} collective-permute-done((f32[108,128]{1,0:T(8,128)S(1)}, f32[108,128]{1,0:T(8,128)S(1)}, u32[]{:S(2)}, u32[]{:S(2)}) %collective-permute-start.8) | collective-permute-done | bytes 55328 | tf_op jit(solution)/shard_map/ppermute | solution.py:460
  24.8 0.6 %steps.2 = (f32[264,128]{1,0:T(8,128)S(1)}, f32[264,128]{1,0:T(8,128)S(1)}, f32[2,9,2,16,128]{4,3,2,1,0:T(8,128)S(1)}, f32[2,3,6,16,128]{4,3,2,1,0:T(8,128)S(1)}, f32[6,16,128]{2,1,0:T(8,128)S(1)}) custom-call(f32[2,9,2,16,128]{4,3,2,1,0:T(8,128)S(1)} %get-tuple-element.39.refs_0_, f32[2,3,2,16,128]{4,3,2,1,0:T(8,128)S(1)} %get-tuple-element.40.refs_1_, ...), custom_call_target="tpu_custom_call" | custom-call | flops 10000000 | bytes 1048576 | tf_op jit(solution)/shard_map/steps/pallas_call | solution.py:438
  25.5 3.2 %collective-permute-start.10 = (f32[264,128]{1,0:T(8,128)S(1)}, f32[264,128]{1,0:T(8,128)S(1)}, u32[]{:S(2)}, u32[]{:S(2)}) collective-permute-start(f32[264,128]{1,0:T(8,128)S(1)} %get-tuple-element.50), channel_id=1, source_target_pairs={{8,16},{16,8},{9,17},{17,9},{10,18},{18,10},{11,19},{19,11},{12,20... | collective-permute-start | bytes 405512 | tf_op jit(solution)/shard_map/ppermute | solution.py:460
  28.7 0.6 %collective-permute-done.9.refs_3_ = f32[264,128]{1,0:T(8,128)S(1)} collective-permute-done((f32[264,128]{1,0:T(8,128)S(1)}, f32[264,128]{1,0:T(8,128)S(1)}, u32[]{:S(2)}, u32[]{:S(2)}) %collective-permute-start.9) | collective-permute-done | bytes 135200 | tf_op jit(solution)/shard_map/ppermute | solution.py:460
  29.3 2.2 %collective-permute-done.10.refs_4_ = f32[264,128]{1,0:T(8,128)S(1)} collective-permute-done((f32[264,128]{1,0:T(8,128)S(1)}, f32[264,128]{1,0:T(8,128)S(1)}, u32[]{:S(2)}, u32[]{:S(2)}) %collective-permute-start.10) | collective-permute-done | bytes 135200 | tf_op jit(solution)/shard_map/ppermute | solution.py:460
  31.5 0.4 %steps.3 = (f32[9,2,8,128]{3,2,1,0:T(8,128)S(1)}, f32[9,2,8,128]{3,2,1,0:T(8,128)S(1)}) custom-call(f32[2,9,2,16,128]{4,3,2,1,0:T(8,128)S(1)} %get-tuple-element.46.refs_0_, f32[2,3,6,16,128]{4,3,2,1,0:T(8,128)S(1)} %get-tuple-element.47.refs_1_, f32[6,16,128]{2,1,0:T(8,128)S(1)} %get-tuple-element.48.refs_2_, ...), custom_call_target="tpu_custom_call" | custom-call | flops 10000000 | bytes 1048576 | tf_op jit(solution)/shard_map/steps/pallas_call | solution.py:438
  32.0 2.6 %collective-permute-start.11 = (f32[9,2,8,128]{3,2,1,0:T(8,128)S(1)}, f32[9,2,8,128]{3,2,1,0:T(8,128)S(1)}, u32[]{:S(2)}, u32[]{:S(2)}) collective-permute-start(f32[9,2,8,128]{3,2,1,0:T(8,128)S(1)} %get-tuple-element.52), channel_id=1, source_target_pairs={{0,1},{1,0},{2,3},{3,2},{4,5},{5,4},{6,7},{7,6},{8,9},{9,8},{10,11... | collective-permute-start | bytes 221192 | tf_op jit(solution)/shard_map/ppermute | solution.py:470
  34.5 0.9 %collective-permute-done.11.brought = f32[9,2,8,128]{3,2,1,0:T(8,128)S(1)} collective-permute-done((f32[9,2,8,128]{3,2,1,0:T(8,128)S(1)}, f32[9,2,8,128]{3,2,1,0:T(8,128)S(1)}, u32[]{:S(2)}, u32[]{:S(2)}) %collective-permute-start.11) | collective-permute-done | bytes 73760 | tf_op jit(solution)/shard_map/ppermute | solution.py:470
  35.5 0.7 %home.1 = f32[1,9,2,16,128]{4,3,2,1,0:T(8,128)} custom-call(f32[9,2,8,128]{3,2,1,0:T(8,128)S(1)} %get-tuple-element.51.mine, f32[9,2,8,128]{3,2,1,0:T(8,128)S(1)} %collective-permute-done.11.brought), custom_call_target="tpu_custom_call" | custom-call | flops 10000000 | bytes 1048576 | tf_op jit(solution)/shard_map/home/pallas_call | solution.py:438
  (12 shorter events, 0.7 us)
Async XLA Ops:
  2.1 7.7 %collective-permute-start.3 = (f32[64,128]{1,0:T(8,128)}, f32[64,128]{1,0:T(8,128)S(1)}, u32[]{:S(2)}, u32[]{:S(2)}) collective-permute-start(f32[64,128]{1,0:T(8,128)} %get-tuple-element.33), channel_id=1, source_target_pairs={{24,0},{16,8},{8,16},{0,24},{25,1},{17,9},{9,17},{1,25},{26,2},{18... | collective-permute-start | bytes 98312 | tf_op jit(solution)/shard_map/ppermute | solution.py:488
  3.4 5.7 %collective-permute-start.2 = (f32[64,128]{1,0:T(8,128)}, f32[64,128]{1,0:T(8,128)S(1)}, u32[]{:S(2)}, u32[]{:S(2)}) collective-permute-start(f32[64,128]{1,0:T(8,128)} %get-tuple-element.33), channel_id=1, source_target_pairs={{16,0},{24,8},{0,16},{8,24},{17,1},{25,9},{1,17},{9,25},{18,2},{26... | collective-permute-start | bytes 98312 | tf_op jit(solution)/shard_map/ppermute | solution.py:488
  4.5 3.9 %collective-permute-start.1 = (f32[64,128]{1,0:T(8,128)}, f32[64,128]{1,0:T(8,128)S(1)}, u32[]{:S(2)}, u32[]{:S(2)}) collective-permute-start(f32[64,128]{1,0:T(8,128)} %get-tuple-element.33), channel_id=1, source_target_pairs={{8,0},{0,8},{24,16},{16,24},{9,1},{1,9},{25,17},{17,25},{10,2},{2,... | collective-permute-start | bytes 98312 | tf_op jit(solution)/shard_map/ppermute | solution.py:488
  5.6 4.2 %collective-permute-start = (f32[10,24,128]{2,1,0:T(8,128)}, f32[10,24,128]{2,1,0:T(8,128)S(1)}, u32[]{:S(2)}, u32[]{:S(2)}) collective-permute-start(f32[10,24,128]{2,1,0:T(8,128)} %get-tuple-element.31), channel_id=1, source_target_pairs={{0,1},{1,0},{2,3},{3,2},{4,5},{5,4},{6,7},{7,6},{8,9},{9,8},{10,11... | collective-permute-start | bytes 368648 | tf_op jit(solution)/shard_map/ppermute | solution.py:470
  6.9 0.9 %copy-start = (f32[336,128]{1,0:T(8,128)S(1)}, f32[336,128]{1,0:T(8,128)}, u32[]{:S(2)}) copy-start(f32[336,128]{1,0:T(8,128)} %get-tuple-element.29.kept) | copy-start | bytes 516100
  10.5 8.9 %collective-permute-start.4 = (f32[168,128]{1,0:T(8,128)S(1)}, f32[168,128]{1,0:T(8,128)S(1)}, u32[]{:S(2)}, u32[]{:S(2)}) collective-permute-start(f32[168,128]{1,0:T(8,128)S(1)} %get-tuple-element.37), channel_id=1, source_target_pairs={{1,2},{3,4},{5,6},{2,1},{4,3},{6,5},{9,10},{11,12},{13,14},{10,9},... | collective-permute-start | bytes 258056 | tf_op jit(solution)/shard_map/ppermute | solution.py:467
  15.0 9.7 %collective-permute-start.5 = (f32[324,128]{1,0:T(8,128)S(1)}, f32[324,128]{1,0:T(8,128)S(1)}, u32[]{:S(2)}, u32[]{:S(2)}) collective-permute-start(f32[324,128]{1,0:T(8,128)S(1)} %get-tuple-element.42), channel_id=1, source_target_pairs={{0,8},{16,24},{8,0},{24,16},{1,9},{17,25},{9,1},{25,17},{2,10},{18... | collective-permute-start | bytes 497672 | tf_op jit(solution)/shard_map/ppermute | solution.py:460
  16.3 8.5 %collective-permute-start.6 = (f32[324,128]{1,0:T(8,128)S(1)}, f32[324,128]{1,0:T(8,128)S(1)}, u32[]{:S(2)}, u32[]{:S(2)}) collective-permute-start(f32[324,128]{1,0:T(8,128)S(1)} %get-tuple-element.43), channel_id=1, source_target_pairs={{8,16},{16,8},{9,17},{17,9},{10,18},{18,10},{11,19},{19,11},{12,20... | collective-permute-start | bytes 497672 | tf_op jit(solution)/shard_map/ppermute | solution.py:460
  19.8 3.4 %collective-permute-start.7 = (f32[108,128]{1,0:T(8,128)S(1)}, f32[108,128]{1,0:T(8,128)S(1)}, u32[]{:S(2)}, u32[]{:S(2)}) collective-permute-start(f32[108,128]{1,0:T(8,128)S(1)} %get-tuple-element.44), channel_id=1, source_target_pairs={{0,8},{16,24},{8,0},{24,16},{1,9},{17,25},{9,1},{25,17},{2,10},{18... | collective-permute-start | bytes 165896 | tf_op jit(solution)/shard_map/ppermute | solution.py:460
  19.8 4.9 %collective-permute-start.8 = (f32[108,128]{1,0:T(8,128)S(1)}, f32[108,128]{1,0:T(8,128)S(1)}, u32[]{:S(2)}, u32[]{:S(2)}) collective-permute-start(f32[108,128]{1,0:T(8,128)S(1)} %get-tuple-element.45), channel_id=1, source_target_pairs={{8,16},{16,8},{9,17},{17,9},{10,18},{18,10},{11,19},{19,11},{12,20... | collective-permute-start | bytes 165896 | tf_op jit(solution)/shard_map/ppermute | solution.py:460
  25.4 3.9 %collective-permute-start.9 = (f32[264,128]{1,0:T(8,128)S(1)}, f32[264,128]{1,0:T(8,128)S(1)}, u32[]{:S(2)}, u32[]{:S(2)}) collective-permute-start(f32[264,128]{1,0:T(8,128)S(1)} %get-tuple-element.49), channel_id=1, source_target_pairs={{0,8},{16,24},{8,0},{24,16},{1,9},{17,25},{9,1},{25,17},{2,10},{18... | collective-permute-start | bytes 405512 | tf_op jit(solution)/shard_map/ppermute | solution.py:460
  25.5 6.1 %collective-permute-start.10 = (f32[264,128]{1,0:T(8,128)S(1)}, f32[264,128]{1,0:T(8,128)S(1)}, u32[]{:S(2)}, u32[]{:S(2)}) collective-permute-start(f32[264,128]{1,0:T(8,128)S(1)} %get-tuple-element.50), channel_id=1, source_target_pairs={{8,16},{16,8},{9,17},{17,9},{10,18},{18,10},{11,19},{19,11},{12,20... | collective-permute-start | bytes 405512 | tf_op jit(solution)/shard_map/ppermute | solution.py:460
  32.0 3.5 %collective-permute-start.11 = (f32[9,2,8,128]{3,2,1,0:T(8,128)S(1)}, f32[9,2,8,128]{3,2,1,0:T(8,128)S(1)}, u32[]{:S(2)}, u32[]{:S(2)}) collective-permute-start(f32[9,2,8,128]{3,2,1,0:T(8,128)S(1)} %get-tuple-element.52), channel_id=1, source_target_pairs={{0,1},{1,0},{2,3},{3,2},{4,5},{5,4},{6,7},{7,6},{8,9},{9,8},{10,11... | collective-permute-start | bytes 221192 | tf_op jit(solution)/shard_map/ppermute | solution.py:470

commit v11 on v10

--- a/solution.py
+++ b/solution.py
@@ -103,11 +103,12 @@
     upper = line >= half
     high = one_hot(jnp.where(upper, line - half, line), half)
     low = one_hot(jnp.where(upper, cell % cy + cy, cell % cy), 2 * cy).astype(BF16)
-    total = jnp.zeros((6 * half, 2 * cy), F32)
-    for part in split3(entry[0:6]):
-        spread = jnp.concatenate([(high * part[c : c + 1]).astype(BF16) for c in range(6)], axis=0)
-        total = total + lax.dot_general(spread, low, NT, preferred_element_type=F32)
-    return total
+    parts = split3(entry[0:6])
+    spread = [(high * part[c : c + 1]).astype(BF16) for part in parts for c in range(6)]
+    spread = jnp.concatenate(spread, axis=0)
+    got = lax.dot_general(spread, low, NT, preferred_element_type=F32)
+    lines = 6 * half
+    return got[0:lines] + got[lines : 2 * lines] + got[2 * lines :]
 
 
 def own_kernel(layout, kept, out, tables, acc):
@@ -486,7 +487,7 @@
     )
     blocks = [
         lax.ppermute(entries, "sec", [(other(i, k), i) for i in range(sections)])
-        for k in range(1, sections)
+        for k in (sections - 1, *range(1, sections - 1))
     ]
     got = swap(given)
     acc_shape = (6 * cx * cz // 2, 2 * cy)
@@ -497,7 +498,7 @@
         (),
         [(11, cx * reach, cy), (8, cy), acc_shape],
         [],
-        flops=10**9,
+        flops=10**8,
     )
     for block in blocks[:-1]:
         (started,) = call(
@@ -507,7 +508,7 @@
             (),
             [acc_shape],
             [],
-            flops=10**9,
+            flops=6 * 10**9,
         )
     own = (cx, rows, cy)
     window = (3 * cx, rows, cy)

time: 36.6 us -> 35.4 us (0.967)
  Pallas kernels: 6.96 us -> 5.92 us
    pallas_call x10, Pallas kernels: 6.96 us -> 5.92 us  [call(): pl.pallas_call(kernel, out_shape=[jax.ShapeDtypeStruct(shape, F32) for sh...]
  transfers between devices with their start and end apart: 12 -> 12, of which waited for: 5 -> 5; matrix products, arithmetic and copies ran while one was open for 0% -> 0% of each run, Pallas kernels for 7% -> 5%
where the time goes in v11:
time: 35.4 us; the launch traced here: 35.2 us
  starting transfers between devices  21.8 us (62%)
  waiting for transfers between devices  6.38 us (18%)
  Pallas kernels  5.92 us (17%)
  local copies, waits for them, and re-layouts  0.92 us (3%)
    ppermute x6, starting transfers between devices, pairs(): return lax.ppermute(block, 'sec', route + [(j, i) for i, j in route])  10.2 us
    pallas_call x10, Pallas kernels, call(): pl.pallas_call(kernel, out_shape=[jax.ShapeDtypeStruct(shape, F32) for sh...  5.92 us
    ppermute x6, waiting for transfers between devices, pairs(): return lax.ppermute(block, 'sec', route + [(j, i) for i, j in route])  5.45 us
    ppermute x1, starting transfers between devices, along_depth(): lax.ppermute(block, ('depth', 'segment'), down + [(j, i) for i, j in down])  4.14 us
    ppermute x2, starting transfers between devices, swap(): return lax.ppermute(block, 'segment', [(0, 1), (1, 0)])  3.94 us
    ppermute x3, starting transfers between devices, on_device(): lax.ppermute(entries, 'sec', [(other(i, k), i) for i in range(sections)])  3.56 us
    unnamed x2, local copies, waits for them, and re-layouts  0.92 us
    ppermute x2, waiting for transfers between devices, swap(): return lax.ppermute(block, 'segment', [(0, 1), (1, 0)])  0.92 us
  transfers between devices with their start and end apart: 12, of which 5 were waited for; matrix products, arithmetic and copies ran while one was open for 0% of the time, Pallas kernels for 5%

profile of v11, /device:TPU:13, one launch (start us, length us, event | category | flops | bytes accessed | tf_op | source)
XLA Modules:
  0.0 35.2 jit_solution(7494195310244159704)
XLA Ops:
  0.0 2.1 %pack.1 = (f32[64,128]{1,0:T(8,128)}, f32[336,128]{1,0:T(8,128)}, f32[10,24,128]{2,1,0:T(8,128)}) custom-call(f32[1,9,2,16,128]{4,3,2,1,0:T(8,128)} %fields_in.1, s32[1,2,16,128]{3,2,1,0:T(8,128)} %ids_in.1, f32[6,1024]{1,0:T(8,128)} %moments_in.1, s32[8,128]{1,0:T(8,128)} %bitcast.4, s32[8,128]{1,0:T(8,128)} %bitcast.5, s32[16,128]{1,0:T(8,128)} %bitcast.3, ...), custom_call_target="tpu_custom_call" | custom-call | flops 10000000 | bytes 1048576 | tf_op jit(solution)/shard_map/pack/pallas_call | solution.py:439
  2.1 1.4 %collective-permute-start.1 = (f32[64,128]{1,0:T(8,128)}, f32[64,128]{1,0:T(8,128)S(1)}, u32[]{:S(2)}, u32[]{:S(2)}) collective-permute-start(f32[64,128]{1,0:T(8,128)} %get-tuple-element.33), channel_id=1, source_target_pairs={{24,0},{16,8},{8,16},{0,24},{25,1},{17,9},{9,17},{1,25},{26,2},{18... | collective-permute-start | bytes 98312 | tf_op jit(solution)/shard_map/ppermute | solution.py:489
  3.4 1.1 %collective-permute-start.3 = (f32[64,128]{1,0:T(8,128)}, f32[64,128]{1,0:T(8,128)S(1)}, u32[]{:S(2)}, u32[]{:S(2)}) collective-permute-start(f32[64,128]{1,0:T(8,128)} %get-tuple-element.33), channel_id=1, source_target_pairs={{16,0},{24,8},{0,16},{8,24},{17,1},{25,9},{1,17},{9,25},{18,2},{26... | collective-permute-start | bytes 98312 | tf_op jit(solution)/shard_map/ppermute | solution.py:489
  4.5 1.1 %collective-permute-start.2 = (f32[64,128]{1,0:T(8,128)}, f32[64,128]{1,0:T(8,128)S(1)}, u32[]{:S(2)}, u32[]{:S(2)}) collective-permute-start(f32[64,128]{1,0:T(8,128)} %get-tuple-element.33), channel_id=1, source_target_pairs={{8,0},{0,8},{24,16},{16,24},{9,1},{1,9},{25,17},{17,25},{10,2},{2,... | collective-permute-start | bytes 98312 | tf_op jit(solution)/shard_map/ppermute | solution.py:489
  5.6 1.2 %collective-permute-start = (f32[10,24,128]{2,1,0:T(8,128)}, f32[10,24,128]{2,1,0:T(8,128)S(1)}, u32[]{:S(2)}, u32[]{:S(2)}) collective-permute-start(f32[10,24,128]{2,1,0:T(8,128)} %get-tuple-element.31), channel_id=1, source_target_pairs={{0,1},{1,0},{2,3},{3,2},{4,5},{5,4},{6,7},{7,6},{8,9},{9,8},{10,11... | collective-permute-start | bytes 368648 | tf_op jit(solution)/shard_map/ppermute | solution.py:471
  6.9 0.9 %copy-done = f32[336,128]{1,0:T(8,128)S(1)} copy-done((f32[336,128]{1,0:T(8,128)S(1)}, f32[336,128]{1,0:T(8,128)}, u32[]{:S(2)}) %copy-start) | copy-done | bytes 172056
  7.8 0.4 %own_moments.1 = (f32[11,24,128]{2,1,0:T(8,128)S(1)}, f32[8,128]{1,0:T(8,128)S(1)}, f32[96,256]{1,0:T(8,128)S(1)}) custom-call(f32[336,128]{1,0:T(8,128)S(1)} %copy-done), custom_call_target="tpu_custom_call" | custom-call | flops 100000000 | bytes 1048576 | tf_op jit(solution)/shard_map/own_moments/pallas_call | solution.py:439
  8.2 0.4 %more_moments.2.started = f32[96,256]{1,0:T(8,128)S(1)} custom-call(f32[96,256]{1,0:T(8,128)S(1)} %get-tuple-element.32.started, f32[64,128]{1,0:T(8,128)S(1)} %collective-permute-done.1.entries), custom_call_target="tpu_custom_call" | custom-call | flops 6000000000 | bytes 1048576 | tf_op jit(solution)/shard_map/more_moments/pallas_call | solution.py:439
  8.6 0.4 %more_moments.3.refs_2_ = f32[96,256]{1,0:T(8,128)S(1)} custom-call(f32[96,256]{1,0:T(8,128)S(1)} %more_moments.2.started, f32[64,128]{1,0:T(8,128)S(1)} %collective-permute-done.2.entries), custom_call_target="tpu_custom_call" | custom-call | flops 6000000000 | bytes 1048576 | tf_op jit(solution)/shard_map/more_moments/pallas_call | solution.py:439
  9.0 0.5 %join_and_moments.1 = (f32[2,9,2,16,128]{4,3,2,1,0:T(8,128)S(1)}, f32[2,2,16,128]{3,2,1,0:T(8,128)S(1)}, f32[2,16,128]{2,1,0:T(8,128)S(1)}, f32[168,128]{1,0:T(8,128)S(1)}) custom-call(f32[11,24,128]{2,1,0:T(8,128)S(1)} %get-tuple-element.30.refs_0_, f32[10,24,128]{2,1,0:T(8,128)S(1)} %collective-permute-done.refs_1_, f32[96,256]{1,0:T(8,128)S(1)} %more_moments.3.refs_2_, ...), custom_call_target="tpu_custom_call" | custom-call | flops 10000000 | bytes 1048576 | tf_op jit(solution)/shard_map/join_and_moments/pallas_call | solution.py:439
  9.5 4.1 %collective-permute-start.4 = (f32[168,128]{1,0:T(8,128)S(1)}, f32[168,128]{1,0:T(8,128)S(1)}, u32[]{:S(2)}, u32[]{:S(2)}) collective-permute-start(f32[168,128]{1,0:T(8,128)S(1)} %get-tuple-element.37), channel_id=1, source_target_pairs={{1,2},{3,4},{5,6},{2,1},{4,3},{6,5},{9,10},{11,12},{13,14},{10,9},... | collective-permute-start | bytes 258056 | tf_op jit(solution)/shard_map/ppermute | solution.py:468
  13.9 1.5 %collective-permute-start.5 = (f32[324,128]{1,0:T(8,128)S(1)}, f32[324,128]{1,0:T(8,128)S(1)}, u32[]{:S(2)}, u32[]{:S(2)}) collective-permute-start(f32[324,128]{1,0:T(8,128)S(1)} %get-tuple-element.42), channel_id=1, source_target_pairs={{0,8},{16,24},{8,0},{24,16},{1,9},{17,25},{9,1},{25,17},{2,10},{18... | collective-permute-start | bytes 497672 | tf_op jit(solution)/shard_map/ppermute | solution.py:461
  15.4 2.9 %collective-permute-start.6 = (f32[324,128]{1,0:T(8,128)S(1)}, f32[324,128]{1,0:T(8,128)S(1)}, u32[]{:S(2)}, u32[]{:S(2)}) collective-permute-start(f32[324,128]{1,0:T(8,128)S(1)} %get-tuple-element.43), channel_id=1, source_target_pairs={{8,16},{16,8},{9,17},{17,9},{10,18},{18,10},{11,19},{19,11},{12,20... | collective-permute-start | bytes 497672 | tf_op jit(solution)/shard_map/ppermute | solution.py:461
  18.6 2.4 %collective-permute-start.8 = (f32[108,128]{1,0:T(8,128)S(1)}, f32[108,128]{1,0:T(8,128)S(1)}, u32[]{:S(2)}, u32[]{:S(2)}) collective-permute-start(f32[108,128]{1,0:T(8,128)S(1)} %get-tuple-element.45), channel_id=1, source_target_pairs={{8,16},{16,8},{9,17},{17,9},{10,18},{18,10},{11,19},{19,11},{12,20... | collective-permute-start | bytes 165896 | tf_op jit(solution)/shard_map/ppermute | solution.py:461
  21.0 0.9 %collective-permute-done.7.refs_5_ = f32[108,128]{1,0:T(8,128)S(1)} collective-permute-done((f32[108,128]{1,0:T(8,128)S(1)}, f32[108,128]{1,0:T(8,128)S(1)}, u32[]{:S(2)}, u32[]{:S(2)}) %collective-permute-start.7) | collective-permute-done | bytes 55328 | tf_op jit(solution)/shard_map/ppermute | solution.py:461
  22.0 1.7 %collective-permute-done.8.refs_6_ = f32[108,128]{1,0:T(8,128)S(1)} collective-permute-done((f32[108,128]{1,0:T(8,128)S(1)}, f32[108,128]{1,0:T(8,128)S(1)}, u32[]{:S(2)}, u32[]{:S(2)}) %collective-permute-start.8) | collective-permute-done | bytes 55328 | tf_op jit(solution)/shard_map/ppermute | solution.py:461
  23.7 0.6 %steps.2 = (f32[264,128]{1,0:T(8,128)S(1)}, f32[264,128]{1,0:T(8,128)S(1)}, f32[2,9,2,16,128]{4,3,2,1,0:T(8,128)S(1)}, f32[2,3,6,16,128]{4,3,2,1,0:T(8,128)S(1)}, f32[6,16,128]{2,1,0:T(8,128)S(1)}) custom-call(f32[2,9,2,16,128]{4,3,2,1,0:T(8,128)S(1)} %get-tuple-element.39.refs_0_, f32[2,3,2,16,128]{4,3,2,1,0:T(8,128)S(1)} %get-tuple-element.40.refs_1_, ...), custom_call_target="tpu_custom_call" | custom-call | flops 10000000 | bytes 1048576 | tf_op jit(solution)/shard_map/steps/pallas_call | solution.py:439
  24.4 3.2 %collective-permute-start.10 = (f32[264,128]{1,0:T(8,128)S(1)}, f32[264,128]{1,0:T(8,128)S(1)}, u32[]{:S(2)}, u32[]{:S(2)}) collective-permute-start(f32[264,128]{1,0:T(8,128)S(1)} %get-tuple-element.50), channel_id=1, source_target_pairs={{8,16},{16,8},{9,17},{17,9},{10,18},{18,10},{11,19},{19,11},{12,20... | collective-permute-start | bytes 405512 | tf_op jit(solution)/shard_map/ppermute | solution.py:461
  27.6 0.6 %collective-permute-done.9.refs_3_ = f32[264,128]{1,0:T(8,128)S(1)} collective-permute-done((f32[264,128]{1,0:T(8,128)S(1)}, f32[264,128]{1,0:T(8,128)S(1)}, u32[]{:S(2)}, u32[]{:S(2)}) %collective-permute-start.9) | collective-permute-done | bytes 135200 | tf_op jit(solution)/shard_map/ppermute | solution.py:461
  28.2 2.2 %collective-permute-done.10.refs_4_ = f32[264,128]{1,0:T(8,128)S(1)} collective-permute-done((f32[264,128]{1,0:T(8,128)S(1)}, f32[264,128]{1,0:T(8,128)S(1)}, u32[]{:S(2)}, u32[]{:S(2)}) %collective-permute-start.10) | collective-permute-done | bytes 135200 | tf_op jit(solution)/shard_map/ppermute | solution.py:461
  30.4 0.4 %steps.3 = (f32[9,2,8,128]{3,2,1,0:T(8,128)S(1)}, f32[9,2,8,128]{3,2,1,0:T(8,128)S(1)}) custom-call(f32[2,9,2,16,128]{4,3,2,1,0:T(8,128)S(1)} %get-tuple-element.46.refs_0_, f32[2,3,6,16,128]{4,3,2,1,0:T(8,128)S(1)} %get-tuple-element.47.refs_1_, f32[6,16,128]{2,1,0:T(8,128)S(1)} %get-tuple-element.48.refs_2_, ...), custom_call_target="tpu_custom_call" | custom-call | flops 10000000 | bytes 1048576 | tf_op jit(solution)/shard_map/steps/pallas_call | solution.py:439
  30.9 2.7 %collective-permute-start.11 = (f32[9,2,8,128]{3,2,1,0:T(8,128)S(1)}, f32[9,2,8,128]{3,2,1,0:T(8,128)S(1)}, u32[]{:S(2)}, u32[]{:S(2)}) collective-permute-start(f32[9,2,8,128]{3,2,1,0:T(8,128)S(1)} %get-tuple-element.52), channel_id=1, source_target_pairs={{0,1},{1,0},{2,3},{3,2},{4,5},{5,4},{6,7},{7,6},{8,9},{9,8},{10,11... | collective-permute-start | bytes 221192 | tf_op jit(solution)/shard_map/ppermute | solution.py:471
  33.6 0.9 %collective-permute-done.11.brought = f32[9,2,8,128]{3,2,1,0:T(8,128)S(1)} collective-permute-done((f32[9,2,8,128]{3,2,1,0:T(8,128)S(1)}, f32[9,2,8,128]{3,2,1,0:T(8,128)S(1)}, u32[]{:S(2)}, u32[]{:S(2)}) %collective-permute-start.11) | collective-permute-done | bytes 73760 | tf_op jit(solution)/shard_map/ppermute | solution.py:471
  34.5 0.7 %home.1 = f32[1,9,2,16,128]{4,3,2,1,0:T(8,128)} custom-call(f32[9,2,8,128]{3,2,1,0:T(8,128)S(1)} %get-tuple-element.51.mine, f32[9,2,8,128]{3,2,1,0:T(8,128)S(1)} %collective-permute-done.11.brought), custom_call_target="tpu_custom_call" | custom-call | flops 10000000 | bytes 1048576 | tf_op jit(solution)/shard_map/home/pallas_call | solution.py:439
  (12 shorter events, 0.7 us)
Async XLA Ops:
  2.1 6.1 %collective-permute-start.1 = (f32[64,128]{1,0:T(8,128)}, f32[64,128]{1,0:T(8,128)S(1)}, u32[]{:S(2)}, u32[]{:S(2)}) collective-permute-start(f32[64,128]{1,0:T(8,128)} %get-tuple-element.33), channel_id=1, source_target_pairs={{24,0},{16,8},{8,16},{0,24},{25,1},{17,9},{9,17},{1,25},{26,2},{18... | collective-permute-start | bytes 98312 | tf_op jit(solution)/shard_map/ppermute | solution.py:489
  3.4 5.6 %collective-permute-start.3 = (f32[64,128]{1,0:T(8,128)}, f32[64,128]{1,0:T(8,128)S(1)}, u32[]{:S(2)}, u32[]{:S(2)}) collective-permute-start(f32[64,128]{1,0:T(8,128)} %get-tuple-element.33), channel_id=1, source_target_pairs={{16,0},{24,8},{0,16},{8,24},{17,1},{25,9},{1,17},{9,25},{18,2},{26... | collective-permute-start | bytes 98312 | tf_op jit(solution)/shard_map/ppermute | solution.py:489
  4.5 4.1 %collective-permute-start.2 = (f32[64,128]{1,0:T(8,128)}, f32[64,128]{1,0:T(8,128)S(1)}, u32[]{:S(2)}, u32[]{:S(2)}) collective-permute-start(f32[64,128]{1,0:T(8,128)} %get-tuple-element.33), channel_id=1, source_target_pairs={{8,0},{0,8},{24,16},{16,24},{9,1},{1,9},{25,17},{17,25},{10,2},{2,... | collective-permute-start | bytes 98312 | tf_op jit(solution)/shard_map/ppermute | solution.py:489
  5.6 3.4 %collective-permute-start = (f32[10,24,128]{2,1,0:T(8,128)}, f32[10,24,128]{2,1,0:T(8,128)S(1)}, u32[]{:S(2)}, u32[]{:S(2)}) collective-permute-start(f32[10,24,128]{2,1,0:T(8,128)} %get-tuple-element.31), channel_id=1, source_target_pairs={{0,1},{1,0},{2,3},{3,2},{4,5},{5,4},{6,7},{7,6},{8,9},{9,8},{10,11... | collective-permute-start | bytes 368648 | tf_op jit(solution)/shard_map/ppermute | solution.py:471
  6.9 0.9 %copy-start = (f32[336,128]{1,0:T(8,128)S(1)}, f32[336,128]{1,0:T(8,128)}, u32[]{:S(2)}) copy-start(f32[336,128]{1,0:T(8,128)} %get-tuple-element.29.kept) | copy-start | bytes 516100
  9.5 8.8 %collective-permute-start.4 = (f32[168,128]{1,0:T(8,128)S(1)}, f32[168,128]{1,0:T(8,128)S(1)}, u32[]{:S(2)}, u32[]{:S(2)}) collective-permute-start(f32[168,128]{1,0:T(8,128)S(1)} %get-tuple-element.37), channel_id=1, source_target_pairs={{1,2},{3,4},{5,6},{2,1},{4,3},{6,5},{9,10},{11,12},{13,14},{10,9},... | collective-permute-start | bytes 258056 | tf_op jit(solution)/shard_map/ppermute | solution.py:468
  13.9 9.8 %collective-permute-start.5 = (f32[324,128]{1,0:T(8,128)S(1)}, f32[324,128]{1,0:T(8,128)S(1)}, u32[]{:S(2)}, u32[]{:S(2)}) collective-permute-start(f32[324,128]{1,0:T(8,128)S(1)} %get-tuple-element.42), channel_id=1, source_target_pairs={{0,8},{16,24},{8,0},{24,16},{1,9},{17,25},{9,1},{25,17},{2,10},{18... | collective-permute-start | bytes 497672 | tf_op jit(solution)/shard_map/ppermute | solution.py:461
  15.4 8.3 %collective-permute-start.6 = (f32[324,128]{1,0:T(8,128)S(1)}, f32[324,128]{1,0:T(8,128)S(1)}, u32[]{:S(2)}, u32[]{:S(2)}) collective-permute-start(f32[324,128]{1,0:T(8,128)S(1)} %get-tuple-element.43), channel_id=1, source_target_pairs={{8,16},{16,8},{9,17},{17,9},{10,18},{18,10},{11,19},{19,11},{12,20... | collective-permute-start | bytes 497672 | tf_op jit(solution)/shard_map/ppermute | solution.py:461
  18.6 3.4 %collective-permute-start.7 = (f32[108,128]{1,0:T(8,128)S(1)}, f32[108,128]{1,0:T(8,128)S(1)}, u32[]{:S(2)}, u32[]{:S(2)}) collective-permute-start(f32[108,128]{1,0:T(8,128)S(1)} %get-tuple-element.44), channel_id=1, source_target_pairs={{0,8},{16,24},{8,0},{24,16},{1,9},{17,25},{9,1},{25,17},{2,10},{18... | collective-permute-start | bytes 165896 | tf_op jit(solution)/shard_map/ppermute | solution.py:461
  18.6 5.0 %collective-permute-start.8 = (f32[108,128]{1,0:T(8,128)S(1)}, f32[108,128]{1,0:T(8,128)S(1)}, u32[]{:S(2)}, u32[]{:S(2)}) collective-permute-start(f32[108,128]{1,0:T(8,128)S(1)} %get-tuple-element.45), channel_id=1, source_target_pairs={{8,16},{16,8},{9,17},{17,9},{10,18},{18,10},{11,19},{19,11},{12,20... | collective-permute-start | bytes 165896 | tf_op jit(solution)/shard_map/ppermute | solution.py:461
  24.3 3.9 %collective-permute-start.9 = (f32[264,128]{1,0:T(8,128)S(1)}, f32[264,128]{1,0:T(8,128)S(1)}, u32[]{:S(2)}, u32[]{:S(2)}) collective-permute-start(f32[264,128]{1,0:T(8,128)S(1)} %get-tuple-element.49), channel_id=1, source_target_pairs={{0,8},{16,24},{8,0},{24,16},{1,9},{17,25},{9,1},{25,17},{2,10},{18... | collective-permute-start | bytes 405512 | tf_op jit(solution)/shard_map/ppermute | solution.py:461
  24.4 6.1 %collective-permute-start.10 = (f32[264,128]{1,0:T(8,128)S(1)}, f32[264,128]{1,0:T(8,128)S(1)}, u32[]{:S(2)}, u32[]{:S(2)}) collective-permute-start(f32[264,128]{1,0:T(8,128)S(1)} %get-tuple-element.50), channel_id=1, source_target_pairs={{8,16},{16,8},{9,17},{17,9},{10,18},{18,10},{11,19},{19,11},{12,20... | collective-permute-start | bytes 405512 | tf_op jit(solution)/shard_map/ppermute | solution.py:461
  30.9 3.6 %collective-permute-start.11 = (f32[9,2,8,128]{3,2,1,0:T(8,128)S(1)}, f32[9,2,8,128]{3,2,1,0:T(8,128)S(1)}, u32[]{:S(2)}, u32[]{:S(2)}) collective-permute-start(f32[9,2,8,128]{3,2,1,0:T(8,128)S(1)} %get-tuple-element.52), channel_id=1, source_target_pairs={{0,1},{1,0},{2,3},{3,2},{4,5},{5,4},{6,7},{7,6},{8,9},{9,8},{10,11... | collective-permute-start | bytes 221192 | tf_op jit(solution)/shard_map/ppermute | solution.py:471

commit v12 on v11

--- a/solution.py
+++ b/solution.py
@@ -264,7 +264,7 @@
 
     def put(to, units, far, right):
         line = slice(0, 0)
-        for model, what, x in units:
+        for model, what, x in units if to is not None else ():
             at = rows_of(x == far, right)
             line = slice(line.stop, line.stop + at.stop - at.start)
             if what == 10:
@@ -280,6 +280,10 @@
     by_parity(*holders, lambda left, right: put(left, left_units, cx - 1, False))
 
 
+def arrived_kernel(edge, out):
+    out[...] = edge[...]
+
+
 def outer_rows(mine, outer):
     def rows_of(far, right):
         shift = 1 if far and not right and mine == 0 else 0
@@ -305,7 +309,7 @@
                 coef[model, i, x] = found
 
 
-def inner_kernel(cx, own_state, own_ids, own_times, tables, to_first, to_second, state, ids, coef, times):
+def inner_kernel(cx, pairing, own_state, own_ids, own_times, tables, to, state, ids, coef, times):
     own = slice(cx, 2 * cx)
     reach = state.shape[3] - STEPS
     state[:, :, own], ids[:, own], times[own] = own_state[...], own_ids[...], own_times[...]
@@ -314,7 +318,8 @@
 
     def cut(mine, main, outer):
         rows_of = lambda far, right: main(reach)
-        cut_edges(cx, rows_of, True, velocity, state, ids, times, to_first, to_second)
+        both = (to, None) if pairing == 0 else (None, to)
+        cut_edges(cx, rows_of, True, velocity, state, ids, times, *both)
 
     by_core(cut)
 
@@ -535,16 +540,21 @@
     def exchange(pair):
         return [pairs(pair[0], 0), pairs(pair[1], 1)]
 
-    inner = call(
-        functools.partial(inner_kernel, cx),
-        "inner_edges",
-        (state, ids, times, tables),
-        (),
-        edges(reach, True),
-        work,
-        flops=10**9,
+    got_edges = []
+    for pairing, flops in enumerate((10**7, 10**7)):
+        (inner,) = call(
+            functools.partial(inner_kernel, cx, pairing),
+            "inner_edges",
+            (state, ids, times, tables),
+            (),
+            edges(reach, True)[0:1],
+            work,
+            flops=flops,
+        )
+        got_edges.append(pairs(inner, pairing))
+    (got_edges[0],) = call(
+        arrived_kernel, "arrived", got_edges[0:1], (), edges(reach, True)[0:1], [], flops=10**10
     )
-    got_edges = exchange(inner)
     *outer, both, coef, times = call(
         functools.partial(outer_kernel, cx),
         "outer_edges",
@@ -552,7 +562,7 @@
         (),
         edges(STEPS, True) + [(2, 9, *own), (2, 3, *own), own],
         work,
-        flops=4 * 10**9,
+        flops=10**8,
     )
     got_edges += exchange(outer)
     for done in range(0, STEPS, cx):

time: 35.4 us -> 37.1 us (1.048); the launches traced: 35.2 us -> 36.4 us
  starting transfers between devices: 21.8 us -> 24.1 us
  waiting for transfers between devices: 6.38 us -> 5.13 us
    ppermute x6, waiting for transfers between devices: 5.45 us -> 4.2 us  [pairs(): return lax.ppermute(block, 'sec', route + [(j, i) for i, j in route])]
    ppermute x1, starting transfers between devices: 4.14 us -> 5.35 us  [along_depth(): lax.ppermute(block, ('depth', 'segment'), down + [(j, i) for i, j in down])]
    ppermute x2, starting transfers between devices: 3.94 us -> 4.55 us  [swap(): return lax.ppermute(block, 'segment', [(0, 1), (1, 0)])]
    ppermute x6, starting transfers between devices: 10.2 us -> 10.6 us  [pairs(): return lax.ppermute(block, 'sec', route + [(j, i) for i, j in route])]
    pallas_call x10 -> x12, Pallas kernels: 5.92 us -> 6.1 us  [call(): pl.pallas_call(kernel, out_shape=[jax.ShapeDtypeStruct(shape, F32) for sh...]
  transfers between devices with their start and end apart: 12 -> 12, of which waited for: 5 -> 4; matrix products, arithmetic and copies ran while one was open for 0% -> 0% of each run, Pallas kernels for 5% -> 5%
where the time goes in v12:
time: 37.1 us; the launch traced here: 36.4 us
  starting transfers between devices  24.1 us (65%)
  Pallas kernels  6.1 us (16%)
  waiting for transfers between devices  5.13 us (14%)
  local copies, waits for them, and re-layouts  0.92 us (2%)
    ppermute x6, starting transfers between devices, pairs(): return lax.ppermute(block, 'sec', route + [(j, i) for i, j in route])  10.6 us
    pallas_call x12, Pallas kernels, call(): pl.pallas_call(kernel, out_shape=[jax.ShapeDtypeStruct(shape, F32) for sh...  6.1 us
    ppermute x1, starting transfers between devices, along_depth(): lax.ppermute(block, ('depth', 'segment'), down + [(j, i) for i, j in down])  5.35 us
    ppermute x2, starting transfers between devices, swap(): return lax.ppermute(block, 'segment', [(0, 1), (1, 0)])  4.55 us
    ppermute x6, waiting for transfers between devices, pairs(): return lax.ppermute(block, 'sec', route + [(j, i) for i, j in route])  4.2 us
    ppermute x3, starting transfers between devices, on_device(): lax.ppermute(entries, 'sec', [(other(i, k), i) for i in range(sections)])  3.56 us
    unnamed x2, local copies, waits for them, and re-layouts  0.92 us
    ppermute x2, waiting for transfers between devices, swap(): return lax.ppermute(block, 'segment', [(0, 1), (1, 0)])  0.92 us
  transfers between devices with their start and end apart: 12, of which 4 were waited for; matrix products, arithmetic and copies ran while one was open for 0% of the time, Pallas kernels for 5%

profile of v12, /device:TPU:13, one launch (start us, length us, event | category | flops | bytes accessed | tf_op | source)
XLA Modules:
  0.0 36.4 jit_solution(15053940236022958808)
XLA Ops:
  0.0 2.1 %pack.1 = (f32[64,128]{1,0:T(8,128)}, f32[336,128]{1,0:T(8,128)}, f32[10,24,128]{2,1,0:T(8,128)}) custom-call(f32[1,9,2,16,128]{4,3,2,1,0:T(8,128)} %fields_in.1, s32[1,2,16,128]{3,2,1,0:T(8,128)} %ids_in.1, f32[6,1024]{1,0:T(8,128)} %moments_in.1, s32[8,128]{1,0:T(8,128)} %bitcast.4, s32[8,128]{1,0:T(8,128)} %bitcast.5, s32[16,128]{1,0:T(8,128)} %bitcast.3, ...), custom_call_target="tpu_custom_call" | custom-call | flops 10000000 | bytes 1048576 | tf_op jit(solution)/shard_map/pack/pallas_call | solution.py:444
  2.1 1.4 %collective-permute-start.1 = (f32[64,128]{1,0:T(8,128)}, f32[64,128]{1,0:T(8,128)S(1)}, u32[]{:S(2)}, u32[]{:S(2)}) collective-permute-start(f32[64,128]{1,0:T(8,128)} %get-tuple-element.31), channel_id=1, source_target_pairs={{24,0},{16,8},{8,16},{0,24},{25,1},{17,9},{9,17},{1,25},{26,2},{18... | collective-permute-start | bytes 98312 | tf_op jit(solution)/shard_map/ppermute | solution.py:494
  3.4 1.1 %collective-permute-start.3 = (f32[64,128]{1,0:T(8,128)}, f32[64,128]{1,0:T(8,128)S(1)}, u32[]{:S(2)}, u32[]{:S(2)}) collective-permute-start(f32[64,128]{1,0:T(8,128)} %get-tuple-element.31), channel_id=1, source_target_pairs={{16,0},{24,8},{0,16},{8,24},{17,1},{25,9},{1,17},{9,25},{18,2},{26... | collective-permute-start | bytes 98312 | tf_op jit(solution)/shard_map/ppermute | solution.py:494
  4.5 1.1 %collective-permute-start.2 = (f32[64,128]{1,0:T(8,128)}, f32[64,128]{1,0:T(8,128)S(1)}, u32[]{:S(2)}, u32[]{:S(2)}) collective-permute-start(f32[64,128]{1,0:T(8,128)} %get-tuple-element.31), channel_id=1, source_target_pairs={{8,0},{0,8},{24,16},{16,24},{9,1},{1,9},{25,17},{17,25},{10,2},{2,... | collective-permute-start | bytes 98312 | tf_op jit(solution)/shard_map/ppermute | solution.py:494
  5.6 1.2 %collective-permute-start = (f32[10,24,128]{2,1,0:T(8,128)}, f32[10,24,128]{2,1,0:T(8,128)S(1)}, u32[]{:S(2)}, u32[]{:S(2)}) collective-permute-start(f32[10,24,128]{2,1,0:T(8,128)} %get-tuple-element.29), channel_id=1, source_target_pairs={{0,1},{1,0},{2,3},{3,2},{4,5},{5,4},{6,7},{7,6},{8,9},{9,8},{10,11... | collective-permute-start | bytes 368648 | tf_op jit(solution)/shard_map/ppermute | solution.py:476
  6.9 0.9 %copy-done = f32[336,128]{1,0:T(8,128)S(1)} copy-done((f32[336,128]{1,0:T(8,128)S(1)}, f32[336,128]{1,0:T(8,128)}, u32[]{:S(2)}) %copy-start) | copy-done | bytes 172056
  7.8 0.4 %own_moments.1 = (f32[11,24,128]{2,1,0:T(8,128)S(1)}, f32[8,128]{1,0:T(8,128)S(1)}, f32[96,256]{1,0:T(8,128)S(1)}) custom-call(f32[336,128]{1,0:T(8,128)S(1)} %copy-done), custom_call_target="tpu_custom_call" | custom-call | flops 100000000 | bytes 1048576 | tf_op jit(solution)/shard_map/own_moments/pallas_call | solution.py:444
  8.2 0.4 %more_moments.2.started = f32[96,256]{1,0:T(8,128)S(1)} custom-call(f32[96,256]{1,0:T(8,128)S(1)} %get-tuple-element.30.started, f32[64,128]{1,0:T(8,128)S(1)} %collective-permute-done.1.entries), custom_call_target="tpu_custom_call" | custom-call | flops 6000000000 | bytes 1048576 | tf_op jit(solution)/shard_map/more_moments/pallas_call | solution.py:444
  8.6 0.4 %more_moments.3.refs_2_ = f32[96,256]{1,0:T(8,128)S(1)} custom-call(f32[96,256]{1,0:T(8,128)S(1)} %more_moments.2.started, f32[64,128]{1,0:T(8,128)S(1)} %collective-permute-done.2.entries), custom_call_target="tpu_custom_call" | custom-call | flops 6000000000 | bytes 1048576 | tf_op jit(solution)/shard_map/more_moments/pallas_call | solution.py:444
  9.0 0.5 %join_and_moments.1 = (f32[2,9,2,16,128]{4,3,2,1,0:T(8,128)S(1)}, f32[2,2,16,128]{3,2,1,0:T(8,128)S(1)}, f32[2,16,128]{2,1,0:T(8,128)S(1)}, f32[168,128]{1,0:T(8,128)S(1)}) custom-call(f32[11,24,128]{2,1,0:T(8,128)S(1)} %get-tuple-element.28.refs_0_, f32[10,24,128]{2,1,0:T(8,128)S(1)} %collective-permute-done.refs_1_, f32[96,256]{1,0:T(8,128)S(1)} %more_moments.3.refs_2_, ...), custom_call_target="tpu_custom_call" | custom-call | flops 10000000 | bytes 1048576 | tf_op jit(solution)/shard_map/join_and_moments/pallas_call | solution.py:444
  9.7 0.6 %collective-permute-start.5 = (f32[324,128]{1,0:T(8,128)S(1)}, f32[324,128]{1,0:T(8,128)S(1)}, u32[]{:S(2)}, u32[]{:S(2)}) collective-permute-start(f32[324,128]{1,0:T(8,128)S(1)} %inner_edges.2), channel_id=1, source_target_pairs={{0,8},{16,24},{8,0},{24,16},{1,9},{17,25},{9,1},{25,17},{2,10},{18... | collective-permute-start | bytes 497672 | tf_op jit(solution)/shard_map/ppermute | solution.py:466
  10.3 5.4 %collective-permute-start.4 = (f32[168,128]{1,0:T(8,128)S(1)}, f32[168,128]{1,0:T(8,128)S(1)}, u32[]{:S(2)}, u32[]{:S(2)}) collective-permute-start(f32[168,128]{1,0:T(8,128)S(1)} %get-tuple-element.35), channel_id=1, source_target_pairs={{1,2},{3,4},{5,6},{2,1},{4,3},{6,5},{9,10},{11,12},{13,14},{10,9},... | collective-permute-start | bytes 258056 | tf_op jit(solution)/shard_map/ppermute | solution.py:473
  15.8 2.6 %collective-permute-start.6 = (f32[324,128]{1,0:T(8,128)S(1)}, f32[324,128]{1,0:T(8,128)S(1)}, u32[]{:S(2)}, u32[]{:S(2)}) collective-permute-start(f32[324,128]{1,0:T(8,128)S(1)} %inner_edges.3), channel_id=1, source_target_pairs={{8,16},{16,8},{9,17},{17,9},{10,18},{18,10},{11,19},{19,11},{12,20... | collective-permute-start | bytes 497672 | tf_op jit(solution)/shard_map/ppermute | solution.py:466
  18.5 0.3 outer_edges.1
  18.8 3.9 %collective-permute-start.8 = (f32[108,128]{1,0:T(8,128)S(1)}, f32[108,128]{1,0:T(8,128)S(1)}, u32[]{:S(2)}, u32[]{:S(2)}) collective-permute-start(f32[108,128]{1,0:T(8,128)S(1)} %get-tuple-element.41), channel_id=1, source_target_pairs={{8,16},{16,8},{9,17},{17,9},{10,18},{18,10},{11,19},{19,11},{12,20... | collective-permute-start | bytes 165896 | tf_op jit(solution)/shard_map/ppermute | solution.py:466
  22.8 1.5 %collective-permute-done.8.refs_6_ = f32[108,128]{1,0:T(8,128)S(1)} collective-permute-done((f32[108,128]{1,0:T(8,128)S(1)}, f32[108,128]{1,0:T(8,128)S(1)}, u32[]{:S(2)}, u32[]{:S(2)}) %collective-permute-start.8) | collective-permute-done | bytes 55328 | tf_op jit(solution)/shard_map/ppermute | solution.py:466
  24.3 0.6 %steps.2 = (f32[264,128]{1,0:T(8,128)S(1)}, f32[264,128]{1,0:T(8,128)S(1)}, f32[2,9,2,16,128]{4,3,2,1,0:T(8,128)S(1)}, f32[2,3,6,16,128]{4,3,2,1,0:T(8,128)S(1)}, f32[6,16,128]{2,1,0:T(8,128)S(1)}) custom-call(f32[2,9,2,16,128]{4,3,2,1,0:T(8,128)S(1)} %get-tuple-element.37.refs_0_, f32[2,3,2,16,128]{4,3,2,1,0:T(8,128)S(1)} %get-tuple-element.38.refs_1_, ...), custom_call_target="tpu_custom_call" | custom-call | flops 10000000 | bytes 1048576 | tf_op jit(solution)/shard_map/steps/pallas_call | solution.py:444
  25.0 3.4 %collective-permute-start.10 = (f32[264,128]{1,0:T(8,128)S(1)}, f32[264,128]{1,0:T(8,128)S(1)}, u32[]{:S(2)}, u32[]{:S(2)}) collective-permute-start(f32[264,128]{1,0:T(8,128)S(1)} %get-tuple-element.46), channel_id=1, source_target_pairs={{8,16},{16,8},{9,17},{17,9},{10,18},{18,10},{11,19},{19,11},{12,20... | collective-permute-start | bytes 405512 | tf_op jit(solution)/shard_map/ppermute | solution.py:466
  28.4 0.5 %collective-permute-done.9.refs_3_ = f32[264,128]{1,0:T(8,128)S(1)} collective-permute-done((f32[264,128]{1,0:T(8,128)S(1)}, f32[264,128]{1,0:T(8,128)S(1)}, u32[]{:S(2)}, u32[]{:S(2)}) %collective-permute-start.9) | collective-permute-done | bytes 135200 | tf_op jit(solution)/shard_map/ppermute | solution.py:466
  28.9 2.2 %collective-permute-done.10.refs_4_ = f32[264,128]{1,0:T(8,128)S(1)} collective-permute-done((f32[264,128]{1,0:T(8,128)S(1)}, f32[264,128]{1,0:T(8,128)S(1)}, u32[]{:S(2)}, u32[]{:S(2)}) %collective-permute-start.10) | collective-permute-done | bytes 135200 | tf_op jit(solution)/shard_map/ppermute | solution.py:466
  31.1 0.4 %steps.3 = (f32[9,2,8,128]{3,2,1,0:T(8,128)S(1)}, f32[9,2,8,128]{3,2,1,0:T(8,128)S(1)}) custom-call(f32[2,9,2,16,128]{4,3,2,1,0:T(8,128)S(1)} %get-tuple-element.42.refs_0_, f32[2,3,6,16,128]{4,3,2,1,0:T(8,128)S(1)} %get-tuple-element.43.refs_1_, f32[6,16,128]{2,1,0:T(8,128)S(1)} %get-tuple-element.44.refs_2_, ...), custom_call_target="tpu_custom_call" | custom-call | flops 10000000 | bytes 1048576 | tf_op jit(solution)/shard_map/steps/pallas_call | solution.py:444
  31.5 3.3 %collective-permute-start.11 = (f32[9,2,8,128]{3,2,1,0:T(8,128)S(1)}, f32[9,2,8,128]{3,2,1,0:T(8,128)S(1)}, u32[]{:S(2)}, u32[]{:S(2)}) collective-permute-start(f32[9,2,8,128]{3,2,1,0:T(8,128)S(1)} %get-tuple-element.48), channel_id=1, source_target_pairs={{0,1},{1,0},{2,3},{3,2},{4,5},{5,4},{6,7},{7,6},{8,9},{9,8},{10,11... | collective-permute-start | bytes 221192 | tf_op jit(solution)/shard_map/ppermute | solution.py:476
  34.8 0.9 %collective-permute-done.11.brought = f32[9,2,8,128]{3,2,1,0:T(8,128)S(1)} collective-permute-done((f32[9,2,8,128]{3,2,1,0:T(8,128)S(1)}, f32[9,2,8,128]{3,2,1,0:T(8,128)S(1)}, u32[]{:S(2)}, u32[]{:S(2)}) %collective-permute-start.11) | collective-permute-done | bytes 73760 | tf_op jit(solution)/shard_map/ppermute | solution.py:476
  35.8 0.7 %home.1 = f32[1,9,2,16,128]{4,3,2,1,0:T(8,128)} custom-call(f32[9,2,8,128]{3,2,1,0:T(8,128)S(1)} %get-tuple-element.47.mine, f32[9,2,8,128]{3,2,1,0:T(8,128)S(1)} %collective-permute-done.11.brought), custom_call_target="tpu_custom_call" | custom-call | flops 10000000 | bytes 1048576 | tf_op jit(solution)/shard_map/home/pallas_call | solution.py:444
  (14 shorter events, 0.6 us)
Async XLA Ops:
  2.1 6.1 %collective-permute-start.1 = (f32[64,128]{1,0:T(8,128)}, f32[64,128]{1,0:T(8,128)S(1)}, u32[]{:S(2)}, u32[]{:S(2)}) collective-permute-start(f32[64,128]{1,0:T(8,128)} %get-tuple-element.31), channel_id=1, source_target_pairs={{24,0},{16,8},{8,16},{0,24},{25,1},{17,9},{9,17},{1,25},{26,2},{18... | collective-permute-start | bytes 98312 | tf_op jit(solution)/shard_map/ppermute | solution.py:494
  3.4 5.6 %collective-permute-start.3 = (f32[64,128]{1,0:T(8,128)}, f32[64,128]{1,0:T(8,128)S(1)}, u32[]{:S(2)}, u32[]{:S(2)}) collective-permute-start(f32[64,128]{1,0:T(8,128)} %get-tuple-element.31), channel_id=1, source_target_pairs={{16,0},{24,8},{0,16},{8,24},{17,1},{25,9},{1,17},{9,25},{18,2},{26... | collective-permute-start | bytes 98312 | tf_op jit(solution)/shard_map/ppermute | solution.py:494
  4.5 4.1 %collective-permute-start.2 = (f32[64,128]{1,0:T(8,128)}, f32[64,128]{1,0:T(8,128)S(1)}, u32[]{:S(2)}, u32[]{:S(2)}) collective-permute-start(f32[64,128]{1,0:T(8,128)} %get-tuple-element.31), channel_id=1, source_target_pairs={{8,0},{0,8},{24,16},{16,24},{9,1},{1,9},{25,17},{17,25},{10,2},{2,... | collective-permute-start | bytes 98312 | tf_op jit(solution)/shard_map/ppermute | solution.py:494
  5.6 3.4 %collective-permute-start = (f32[10,24,128]{2,1,0:T(8,128)}, f32[10,24,128]{2,1,0:T(8,128)S(1)}, u32[]{:S(2)}, u32[]{:S(2)}) collective-permute-start(f32[10,24,128]{2,1,0:T(8,128)} %get-tuple-element.29), channel_id=1, source_target_pairs={{0,1},{1,0},{2,3},{3,2},{4,5},{5,4},{6,7},{7,6},{8,9},{9,8},{10,11... | collective-permute-start | bytes 368648 | tf_op jit(solution)/shard_map/ppermute | solution.py:476
  6.9 0.9 %copy-start = (f32[336,128]{1,0:T(8,128)S(1)}, f32[336,128]{1,0:T(8,128)}, u32[]{:S(2)}) copy-start(f32[336,128]{1,0:T(8,128)} %get-tuple-element.27.kept) | copy-start | bytes 516100
  9.7 13.1 %collective-permute-start.5 = (f32[324,128]{1,0:T(8,128)S(1)}, f32[324,128]{1,0:T(8,128)S(1)}, u32[]{:S(2)}, u32[]{:S(2)}) collective-permute-start(f32[324,128]{1,0:T(8,128)S(1)} %inner_edges.2), channel_id=1, source_target_pairs={{0,8},{16,24},{8,0},{24,16},{1,9},{17,25},{9,1},{25,17},{2,10},{18... | collective-permute-start | bytes 497672 | tf_op jit(solution)/shard_map/ppermute | solution.py:466
  10.3 8.2 %collective-permute-start.4 = (f32[168,128]{1,0:T(8,128)S(1)}, f32[168,128]{1,0:T(8,128)S(1)}, u32[]{:S(2)}, u32[]{:S(2)}) collective-permute-start(f32[168,128]{1,0:T(8,128)S(1)} %get-tuple-element.35), channel_id=1, source_target_pairs={{1,2},{3,4},{5,6},{2,1},{4,3},{6,5},{9,10},{11,12},{13,14},{10,9},... | collective-permute-start | bytes 258056 | tf_op jit(solution)/shard_map/ppermute | solution.py:473
  15.8 8.5 %collective-permute-start.6 = (f32[324,128]{1,0:T(8,128)S(1)}, f32[324,128]{1,0:T(8,128)S(1)}, u32[]{:S(2)}, u32[]{:S(2)}) collective-permute-start(f32[324,128]{1,0:T(8,128)S(1)} %inner_edges.3), channel_id=1, source_target_pairs={{8,16},{16,8},{9,17},{17,9},{10,18},{18,10},{11,19},{19,11},{12,20... | collective-permute-start | bytes 497672 | tf_op jit(solution)/shard_map/ppermute | solution.py:466
  18.8 4.0 %collective-permute-start.7 = (f32[108,128]{1,0:T(8,128)S(1)}, f32[108,128]{1,0:T(8,128)S(1)}, u32[]{:S(2)}, u32[]{:S(2)}) collective-permute-start(f32[108,128]{1,0:T(8,128)S(1)} %get-tuple-element.40), channel_id=1, source_target_pairs={{0,8},{16,24},{8,0},{24,16},{1,9},{17,25},{9,1},{25,17},{2,10},{18... | collective-permute-start | bytes 165896 | tf_op jit(solution)/shard_map/ppermute | solution.py:466
  18.8 5.5 %collective-permute-start.8 = (f32[108,128]{1,0:T(8,128)S(1)}, f32[108,128]{1,0:T(8,128)S(1)}, u32[]{:S(2)}, u32[]{:S(2)}) collective-permute-start(f32[108,128]{1,0:T(8,128)S(1)} %get-tuple-element.41), channel_id=1, source_target_pairs={{8,16},{16,8},{9,17},{17,9},{10,18},{18,10},{11,19},{19,11},{12,20... | collective-permute-start | bytes 165896 | tf_op jit(solution)/shard_map/ppermute | solution.py:466
  24.9 3.9 %collective-permute-start.9 = (f32[264,128]{1,0:T(8,128)S(1)}, f32[264,128]{1,0:T(8,128)S(1)}, u32[]{:S(2)}, u32[]{:S(2)}) collective-permute-start(f32[264,128]{1,0:T(8,128)S(1)} %get-tuple-element.45), channel_id=1, source_target_pairs={{0,8},{16,24},{8,0},{24,16},{1,9},{17,25},{9,1},{25,17},{2,10},{18... | collective-permute-start | bytes 405512 | tf_op jit(solution)/shard_map/ppermute | solution.py:466
  25.0 6.1 %collective-permute-start.10 = (f32[264,128]{1,0:T(8,128)S(1)}, f32[264,128]{1,0:T(8,128)S(1)}, u32[]{:S(2)}, u32[]{:S(2)}) collective-permute-start(f32[264,128]{1,0:T(8,128)S(1)} %get-tuple-element.46), channel_id=1, source_target_pairs={{8,16},{16,8},{9,17},{17,9},{10,18},{18,10},{11,19},{19,11},{12,20... | collective-permute-start | bytes 405512 | tf_op jit(solution)/shard_map/ppermute | solution.py:466
  31.5 4.2 %collective-permute-start.11 = (f32[9,2,8,128]{3,2,1,0:T(8,128)S(1)}, f32[9,2,8,128]{3,2,1,0:T(8,128)S(1)}, u32[]{:S(2)}, u32[]{:S(2)}) collective-permute-start(f32[9,2,8,128]{3,2,1,0:T(8,128)S(1)} %get-tuple-element.48), channel_id=1, source_target_pairs={{0,1},{1,0},{2,3},{3,2},{4,5},{5,4},{6,7},{7,6},{8,9},{9,8},{10,11... | collective-permute-start | bytes 221192 | tf_op jit(solution)/shard_map/ppermute | solution.py:476

commit v13 on v11

--- a/solution.py
+++ b/solution.py
@@ -320,7 +320,7 @@
 
 
 def outer_kernel(
-    cx, own_state, own_ids, own_times, halo, tables,
+    cx, own_state, own_ids, own_times, from_above, from_below, tables,
     to_first, to_second, both, coef_out, times_out, state, ids, coef, times,
 ):
     own = slice(cx, 2 * cx)
@@ -328,6 +328,7 @@
     state[:, :, own], ids[:, own], times[own] = own_state[...], own_ids[...], own_times[...]
 
     def join(mine, main, outer):
+        halo = from_above if mine == 0 else from_below
         for x in range(cx):
             for k in range(21):
                 line = halo[(k * cx + x) * STEPS : (k * cx + x + 1) * STEPS]
@@ -465,7 +466,8 @@
 
     def along_depth(block):
         down = [(2 * i + 1, 2 * (i + 1)) for i in range(slabs - 1)]
-        return lax.ppermute(block, ("depth", "segment"), down + [(j, i) for i, j in down])
+        routes = down, [(j, i) for i, j in down]
+        return [lax.ppermute(block, ("depth", "segment"), route) for route in routes]
 
     def swap(block):
         return lax.ppermute(block, "segment", [(0, 1), (1, 0)])
@@ -520,7 +522,7 @@
         [(2, 9, *own), (2, *own), own, (21 * cx * STEPS, cy)],
         [(6, cx * cz, cy)],
     )
-    halo = along_depth(edge)
+    halos = along_depth(edge)
     work = [(2, 9, *window), (2, *window), (2, 3, *window), window]
 
     def edges(count, with_ids):
@@ -548,7 +550,7 @@
     *outer, both, coef, times = call(
         functools.partial(outer_kernel, cx),
         "outer_edges",
-        (state, ids, times, halo, tables),
+        (state, ids, times, *halos, tables),
         (),
         edges(STEPS, True) + [(2, 9, *own), (2, 3, *own), own],
         work,

time: 35.4 us -> 37.9 us (1.071); the launches traced: 35.2 us -> 37.2 us
  starting transfers between devices: 21.8 us -> 23.4 us
  waiting for transfers between devices: 6.38 us -> 6.84 us
    ppermute x1 -> x2, starting transfers between devices: 4.14 us -> 5.56 us  [along_depth(): lax.ppermute(block, ('depth', 'segment'), route)]
    ppermute x6, waiting for transfers between devices: 5.45 us -> 5.92 us  [pairs(): return lax.ppermute(block, 'sec', route + [(j, i) for i, j in route])]
  transfers between devices with their start and end apart: 12 -> 13, of which waited for: 5 -> 5; matrix products, arithmetic and copies ran while one was open for 0% -> 0% of each run, Pallas kernels for 5% -> 4%
where the time goes in v13:
time: 37.9 us; the launch traced here: 37.2 us
  starting transfers between devices  23.4 us (62%)
  waiting for transfers between devices  6.84 us (18%)
  Pallas kernels  5.92 us (16%)
  local copies, waits for them, and re-layouts  0.92 us (2%)
    ppermute x6, starting transfers between devices, pairs(): return lax.ppermute(block, 'sec', route + [(j, i) for i, j in route])  10.1 us
    pallas_call x10, Pallas kernels, call(): pl.pallas_call(kernel, out_shape=[jax.ShapeDtypeStruct(shape, F32) for sh...  5.92 us
    ppermute x6, waiting for transfers between devices, pairs(): return lax.ppermute(block, 'sec', route + [(j, i) for i, j in route])  5.92 us
    ppermute x2, starting transfers between devices, along_depth(): lax.ppermute(block, ('depth', 'segment'), route)  5.56 us
    ppermute x2, starting transfers between devices, swap(): return lax.ppermute(block, 'segment', [(0, 1), (1, 0)])  4.19 us
    ppermute x3, starting transfers between devices, on_device(): lax.ppermute(entries, 'sec', [(other(i, k), i) for i in range(sections)])  3.56 us
    unnamed x2, local copies, waits for them, and re-layouts  0.92 us
    ppermute x2, waiting for transfers between devices, swap(): return lax.ppermute(block, 'segment', [(0, 1), (1, 0)])  0.92 us
  transfers between devices with their start and end apart: 13, of which 5 were waited for; matrix products, arithmetic and copies ran while one was open for 0% of the time, Pallas kernels for 4%

profile of v13, /device:TPU:13, one launch (start us, length us, event | category | flops | bytes accessed | tf_op | source)
XLA Modules:
  0.0 37.2 jit_solution(10027631740647268724)
XLA Ops:
  0.0 2.1 %pack.1 = (f32[64,128]{1,0:T(8,128)}, f32[336,128]{1,0:T(8,128)}, f32[10,24,128]{2,1,0:T(8,128)}) custom-call(f32[1,9,2,16,128]{4,3,2,1,0:T(8,128)} %fields_in.1, s32[1,2,16,128]{3,2,1,0:T(8,128)} %ids_in.1, f32[6,1024]{1,0:T(8,128)} %moments_in.1, s32[8,128]{1,0:T(8,128)} %bitcast.4, s32[8,128]{1,0:T(8,128)} %bitcast.5, s32[16,128]{1,0:T(8,128)} %bitcast.3, ...), custom_call_target="tpu_custom_call" | custom-call | flops 10000000 | bytes 1048576 | tf_op jit(solution)/shard_map/pack/pallas_call | solution.py:440
  2.1 1.4 %collective-permute-start.1 = (f32[64,128]{1,0:T(8,128)}, f32[64,128]{1,0:T(8,128)S(1)}, u32[]{:S(2)}, u32[]{:S(2)}) collective-permute-start(f32[64,128]{1,0:T(8,128)} %get-tuple-element.33), channel_id=1, source_target_pairs={{24,0},{16,8},{8,16},{0,24},{25,1},{17,9},{9,17},{1,25},{26,2},{18... | collective-permute-start | bytes 98312 | tf_op jit(solution)/shard_map/ppermute | solution.py:491
  3.4 1.1 %collective-permute-start.3 = (f32[64,128]{1,0:T(8,128)}, f32[64,128]{1,0:T(8,128)S(1)}, u32[]{:S(2)}, u32[]{:S(2)}) collective-permute-start(f32[64,128]{1,0:T(8,128)} %get-tuple-element.33), channel_id=1, source_target_pairs={{16,0},{24,8},{0,16},{8,24},{17,1},{25,9},{1,17},{9,25},{18,2},{26... | collective-permute-start | bytes 98312 | tf_op jit(solution)/shard_map/ppermute | solution.py:491
  4.5 1.1 %collective-permute-start.2 = (f32[64,128]{1,0:T(8,128)}, f32[64,128]{1,0:T(8,128)S(1)}, u32[]{:S(2)}, u32[]{:S(2)}) collective-permute-start(f32[64,128]{1,0:T(8,128)} %get-tuple-element.33), channel_id=1, source_target_pairs={{8,0},{0,8},{24,16},{16,24},{9,1},{1,9},{25,17},{17,25},{10,2},{2,... | collective-permute-start | bytes 98312 | tf_op jit(solution)/shard_map/ppermute | solution.py:491
  5.6 1.2 %collective-permute-start = (f32[10,24,128]{2,1,0:T(8,128)}, f32[10,24,128]{2,1,0:T(8,128)S(1)}, u32[]{:S(2)}, u32[]{:S(2)}) collective-permute-start(f32[10,24,128]{2,1,0:T(8,128)} %get-tuple-element.31), channel_id=1, source_target_pairs={{0,1},{1,0},{2,3},{3,2},{4,5},{5,4},{6,7},{7,6},{8,9},{9,8},{10,11... | collective-permute-start | bytes 368648 | tf_op jit(solution)/shard_map/ppermute | solution.py:473
  6.9 0.9 %copy-done = f32[336,128]{1,0:T(8,128)S(1)} copy-done((f32[336,128]{1,0:T(8,128)S(1)}, f32[336,128]{1,0:T(8,128)}, u32[]{:S(2)}) %copy-start) | copy-done | bytes 172056
  7.8 0.4 %own_moments.1 = (f32[11,24,128]{2,1,0:T(8,128)S(1)}, f32[8,128]{1,0:T(8,128)S(1)}, f32[96,256]{1,0:T(8,128)S(1)}) custom-call(f32[336,128]{1,0:T(8,128)S(1)} %copy-done), custom_call_target="tpu_custom_call" | custom-call | flops 100000000 | bytes 1048576 | tf_op jit(solution)/shard_map/own_moments/pallas_call | solution.py:440
  8.6 0.4 %more_moments.3.refs_2_ = f32[96,256]{1,0:T(8,128)S(1)} custom-call(f32[96,256]{1,0:T(8,128)S(1)} %more_moments.2.started, f32[64,128]{1,0:T(8,128)S(1)} %collective-permute-done.2.entries), custom_call_target="tpu_custom_call" | custom-call | flops 6000000000 | bytes 1048576 | tf_op jit(solution)/shard_map/more_moments/pallas_call | solution.py:440
  9.0 0.5 %join_and_moments.1 = (f32[2,9,2,16,128]{4,3,2,1,0:T(8,128)S(1)}, f32[2,2,16,128]{3,2,1,0:T(8,128)S(1)}, f32[2,16,128]{2,1,0:T(8,128)S(1)}, f32[168,128]{1,0:T(8,128)S(1)}) custom-call(f32[11,24,128]{2,1,0:T(8,128)S(1)} %get-tuple-element.30.refs_0_, f32[10,24,128]{2,1,0:T(8,128)S(1)} %collective-permute-done.refs_1_, f32[96,256]{1,0:T(8,128)S(1)} %more_moments.3.refs_2_, ...), custom_call_target="tpu_custom_call" | custom-call | flops 10000000 | bytes 1048576 | tf_op jit(solution)/shard_map/join_and_moments/pallas_call | solution.py:440
  9.5 1.3 %collective-permute-start.5 = (f32[168,128]{1,0:T(8,128)S(1)}, f32[168,128]{1,0:T(8,128)S(1)}, u32[]{:S(2)}, u32[]{:S(2)}) collective-permute-start(f32[168,128]{1,0:T(8,128)S(1)} %get-tuple-element.37), channel_id=1, source_target_pairs={{2,1},{4,3},{6,5},{10,9},{12,11},{14,13},{18,17},{20,19},{22,21},{... | collective-permute-start | bytes 258056 | tf_op jit(solution)/shard_map/ppermute | solution.py:470
  10.8 4.3 %collective-permute-start.4 = (f32[168,128]{1,0:T(8,128)S(1)}, f32[168,128]{1,0:T(8,128)S(1)}, u32[]{:S(2)}, u32[]{:S(2)}) collective-permute-start(f32[168,128]{1,0:T(8,128)S(1)} %get-tuple-element.37), channel_id=1, source_target_pairs={{1,2},{3,4},{5,6},{9,10},{11,12},{13,14},{17,18},{19,20},{21,22},{... | collective-permute-start | bytes 258056 | tf_op jit(solution)/shard_map/ppermute | solution.py:470
  15.3 1.4 %collective-permute-start.6 = (f32[324,128]{1,0:T(8,128)S(1)}, f32[324,128]{1,0:T(8,128)S(1)}, u32[]{:S(2)}, u32[]{:S(2)}) collective-permute-start(f32[324,128]{1,0:T(8,128)S(1)} %get-tuple-element.42), channel_id=1, source_target_pairs={{0,8},{16,24},{8,0},{24,16},{1,9},{17,25},{9,1},{25,17},{2,10},{18... | collective-permute-start | bytes 497672 | tf_op jit(solution)/shard_map/ppermute | solution.py:462
  16.7 3.5 %collective-permute-start.7 = (f32[324,128]{1,0:T(8,128)S(1)}, f32[324,128]{1,0:T(8,128)S(1)}, u32[]{:S(2)}, u32[]{:S(2)}) collective-permute-start(f32[324,128]{1,0:T(8,128)S(1)} %get-tuple-element.43), channel_id=1, source_target_pairs={{8,16},{16,8},{9,17},{17,9},{10,18},{18,10},{11,19},{19,11},{12,20... | collective-permute-start | bytes 497672 | tf_op jit(solution)/shard_map/ppermute | solution.py:462
  20.6 1.9 %collective-permute-start.9 = (f32[108,128]{1,0:T(8,128)S(1)}, f32[108,128]{1,0:T(8,128)S(1)}, u32[]{:S(2)}, u32[]{:S(2)}) collective-permute-start(f32[108,128]{1,0:T(8,128)S(1)} %get-tuple-element.45), channel_id=1, source_target_pairs={{8,16},{16,8},{9,17},{17,9},{10,18},{18,10},{11,19},{19,11},{12,20... | collective-permute-start | bytes 165896 | tf_op jit(solution)/shard_map/ppermute | solution.py:462
  22.5 1.8 %collective-permute-done.8.refs_5_ = f32[108,128]{1,0:T(8,128)S(1)} collective-permute-done((f32[108,128]{1,0:T(8,128)S(1)}, f32[108,128]{1,0:T(8,128)S(1)}, u32[]{:S(2)}, u32[]{:S(2)}) %collective-permute-start.8) | collective-permute-done | bytes 55328 | tf_op jit(solution)/shard_map/ppermute | solution.py:462
  24.3 1.2 %collective-permute-done.9.refs_6_ = f32[108,128]{1,0:T(8,128)S(1)} collective-permute-done((f32[108,128]{1,0:T(8,128)S(1)}, f32[108,128]{1,0:T(8,128)S(1)}, u32[]{:S(2)}, u32[]{:S(2)}) %collective-permute-start.9) | collective-permute-done | bytes 55328 | tf_op jit(solution)/shard_map/ppermute | solution.py:462
  25.5 0.6 %steps.2 = (f32[264,128]{1,0:T(8,128)S(1)}, f32[264,128]{1,0:T(8,128)S(1)}, f32[2,9,2,16,128]{4,3,2,1,0:T(8,128)S(1)}, f32[2,3,6,16,128]{4,3,2,1,0:T(8,128)S(1)}, f32[6,16,128]{2,1,0:T(8,128)S(1)}) custom-call(f32[2,9,2,16,128]{4,3,2,1,0:T(8,128)S(1)} %get-tuple-element.39.refs_0_, f32[2,3,2,16,128]{4,3,2,1,0:T(8,128)S(1)} %get-tuple-element.40.refs_1_, ...), custom_call_target="tpu_custom_call" | custom-call | flops 10000000 | bytes 1048576 | tf_op jit(solution)/shard_map/steps/pallas_call | solution.py:440
  26.2 3.1 %collective-permute-start.11 = (f32[264,128]{1,0:T(8,128)S(1)}, f32[264,128]{1,0:T(8,128)S(1)}, u32[]{:S(2)}, u32[]{:S(2)}) collective-permute-start(f32[264,128]{1,0:T(8,128)S(1)} %get-tuple-element.50), channel_id=1, source_target_pairs={{8,16},{16,8},{9,17},{17,9},{10,18},{18,10},{11,19},{19,11},{12,20... | collective-permute-start | bytes 405512 | tf_op jit(solution)/shard_map/ppermute | solution.py:462
  29.3 0.7 %collective-permute-done.10.refs_3_ = f32[264,128]{1,0:T(8,128)S(1)} collective-permute-done((f32[264,128]{1,0:T(8,128)S(1)}, f32[264,128]{1,0:T(8,128)S(1)}, u32[]{:S(2)}, u32[]{:S(2)}) %collective-permute-start.10) | collective-permute-done | bytes 135200 | tf_op jit(solution)/shard_map/ppermute | solution.py:462
  30.0 2.2 %collective-permute-done.11.refs_4_ = f32[264,128]{1,0:T(8,128)S(1)} collective-permute-done((f32[264,128]{1,0:T(8,128)S(1)}, f32[264,128]{1,0:T(8,128)S(1)}, u32[]{:S(2)}, u32[]{:S(2)}) %collective-permute-start.11) | collective-permute-done | bytes 135200 | tf_op jit(solution)/shard_map/ppermute | solution.py:462
  32.2 0.4 %steps.3 = (f32[9,2,8,128]{3,2,1,0:T(8,128)S(1)}, f32[9,2,8,128]{3,2,1,0:T(8,128)S(1)}) custom-call(f32[2,9,2,16,128]{4,3,2,1,0:T(8,128)S(1)} %get-tuple-element.46.refs_0_, f32[2,3,6,16,128]{4,3,2,1,0:T(8,128)S(1)} %get-tuple-element.47.refs_1_, f32[6,16,128]{2,1,0:T(8,128)S(1)} %get-tuple-element.48.refs_2_, ...), custom_call_target="tpu_custom_call" | custom-call | flops 10000000 | bytes 1048576 | tf_op jit(solution)/shard_map/steps/pallas_call | solution.py:440
  32.7 3.0 %collective-permute-start.12 = (f32[9,2,8,128]{3,2,1,0:T(8,128)S(1)}, f32[9,2,8,128]{3,2,1,0:T(8,128)S(1)}, u32[]{:S(2)}, u32[]{:S(2)}) collective-permute-start(f32[9,2,8,128]{3,2,1,0:T(8,128)S(1)} %get-tuple-element.52), channel_id=1, source_target_pairs={{0,1},{1,0},{2,3},{3,2},{4,5},{5,4},{6,7},{7,6},{8,9},{9,8},{10,11... | collective-permute-start | bytes 221192 | tf_op jit(solution)/shard_map/ppermute | solution.py:473
  35.7 0.9 %collective-permute-done.12.brought = f32[9,2,8,128]{3,2,1,0:T(8,128)S(1)} collective-permute-done((f32[9,2,8,128]{3,2,1,0:T(8,128)S(1)}, f32[9,2,8,128]{3,2,1,0:T(8,128)S(1)}, u32[]{:S(2)}, u32[]{:S(2)}) %collective-permute-start.12) | collective-permute-done | bytes 73760 | tf_op jit(solution)/shard_map/ppermute | solution.py:473
  36.6 0.7 %home.1 = f32[1,9,2,16,128]{4,3,2,1,0:T(8,128)} custom-call(f32[9,2,8,128]{3,2,1,0:T(8,128)S(1)} %get-tuple-element.51.mine, f32[9,2,8,128]{3,2,1,0:T(8,128)S(1)} %collective-permute-done.12.brought), custom_call_target="tpu_custom_call" | custom-call | flops 10000000 | bytes 1048576 | tf_op jit(solution)/shard_map/home/pallas_call | solution.py:440
  (14 shorter events, 1.0 us)
Async XLA Ops:
  2.1 6.1 %collective-permute-start.1 = (f32[64,128]{1,0:T(8,128)}, f32[64,128]{1,0:T(8,128)S(1)}, u32[]{:S(2)}, u32[]{:S(2)}) collective-permute-start(f32[64,128]{1,0:T(8,128)} %get-tuple-element.33), channel_id=1, source_target_pairs={{24,0},{16,8},{8,16},{0,24},{25,1},{17,9},{9,17},{1,25},{26,2},{18... | collective-permute-start | bytes 98312 | tf_op jit(solution)/shard_map/ppermute | solution.py:491
  3.4 5.6 %collective-permute-start.3 = (f32[64,128]{1,0:T(8,128)}, f32[64,128]{1,0:T(8,128)S(1)}, u32[]{:S(2)}, u32[]{:S(2)}) collective-permute-start(f32[64,128]{1,0:T(8,128)} %get-tuple-element.33), channel_id=1, source_target_pairs={{16,0},{24,8},{0,16},{8,24},{17,1},{25,9},{1,17},{9,25},{18,2},{26... | collective-permute-start | bytes 98312 | tf_op jit(solution)/shard_map/ppermute | solution.py:491
  4.5 4.1 %collective-permute-start.2 = (f32[64,128]{1,0:T(8,128)}, f32[64,128]{1,0:T(8,128)S(1)}, u32[]{:S(2)}, u32[]{:S(2)}) collective-permute-start(f32[64,128]{1,0:T(8,128)} %get-tuple-element.33), channel_id=1, source_target_pairs={{8,0},{0,8},{24,16},{16,24},{9,1},{1,9},{25,17},{17,25},{10,2},{2,... | collective-permute-start | bytes 98312 | tf_op jit(solution)/shard_map/ppermute | solution.py:491
  5.6 3.4 %collective-permute-start = (f32[10,24,128]{2,1,0:T(8,128)}, f32[10,24,128]{2,1,0:T(8,128)S(1)}, u32[]{:S(2)}, u32[]{:S(2)}) collective-permute-start(f32[10,24,128]{2,1,0:T(8,128)} %get-tuple-element.31), channel_id=1, source_target_pairs={{0,1},{1,0},{2,3},{3,2},{4,5},{5,4},{6,7},{7,6},{8,9},{9,8},{10,11... | collective-permute-start | bytes 368648 | tf_op jit(solution)/shard_map/ppermute | solution.py:473
  6.9 0.9 %copy-start = (f32[336,128]{1,0:T(8,128)S(1)}, f32[336,128]{1,0:T(8,128)}, u32[]{:S(2)}) copy-start(f32[336,128]{1,0:T(8,128)} %get-tuple-element.29.kept) | copy-start | bytes 516100
  9.5 10.7 %collective-permute-start.5 = (f32[168,128]{1,0:T(8,128)S(1)}, f32[168,128]{1,0:T(8,128)S(1)}, u32[]{:S(2)}, u32[]{:S(2)}) collective-permute-start(f32[168,128]{1,0:T(8,128)S(1)} %get-tuple-element.37), channel_id=1, source_target_pairs={{2,1},{4,3},{6,5},{10,9},{12,11},{14,13},{18,17},{20,19},{22,21},{... | collective-permute-start | bytes 258056 | tf_op jit(solution)/shard_map/ppermute | solution.py:470
  10.8 9.4 %collective-permute-start.4 = (f32[168,128]{1,0:T(8,128)S(1)}, f32[168,128]{1,0:T(8,128)S(1)}, u32[]{:S(2)}, u32[]{:S(2)}) collective-permute-start(f32[168,128]{1,0:T(8,128)S(1)} %get-tuple-element.37), channel_id=1, source_target_pairs={{1,2},{3,4},{5,6},{9,10},{11,12},{13,14},{17,18},{19,20},{21,22},{... | collective-permute-start | bytes 258056 | tf_op jit(solution)/shard_map/ppermute | solution.py:470
  15.3 10.2 %collective-permute-start.6 = (f32[324,128]{1,0:T(8,128)S(1)}, f32[324,128]{1,0:T(8,128)S(1)}, u32[]{:S(2)}, u32[]{:S(2)}) collective-permute-start(f32[324,128]{1,0:T(8,128)S(1)} %get-tuple-element.42), channel_id=1, source_target_pairs={{0,8},{16,24},{8,0},{24,16},{1,9},{17,25},{9,1},{25,17},{2,10},{18... | collective-permute-start | bytes 497672 | tf_op jit(solution)/shard_map/ppermute | solution.py:462
  16.7 8.8 %collective-permute-start.7 = (f32[324,128]{1,0:T(8,128)S(1)}, f32[324,128]{1,0:T(8,128)S(1)}, u32[]{:S(2)}, u32[]{:S(2)}) collective-permute-start(f32[324,128]{1,0:T(8,128)S(1)} %get-tuple-element.43), channel_id=1, source_target_pairs={{8,16},{16,8},{9,17},{17,9},{10,18},{18,10},{11,19},{19,11},{12,20... | collective-permute-start | bytes 497672 | tf_op jit(solution)/shard_map/ppermute | solution.py:462
  20.5 3.8 %collective-permute-start.8 = (f32[108,128]{1,0:T(8,128)S(1)}, f32[108,128]{1,0:T(8,128)S(1)}, u32[]{:S(2)}, u32[]{:S(2)}) collective-permute-start(f32[108,128]{1,0:T(8,128)S(1)} %get-tuple-element.44), channel_id=1, source_target_pairs={{0,8},{16,24},{8,0},{24,16},{1,9},{17,25},{9,1},{25,17},{2,10},{18... | collective-permute-start | bytes 165896 | tf_op jit(solution)/shard_map/ppermute | solution.py:462
  20.6 4.9 %collective-permute-start.9 = (f32[108,128]{1,0:T(8,128)S(1)}, f32[108,128]{1,0:T(8,128)S(1)}, u32[]{:S(2)}, u32[]{:S(2)}) collective-permute-start(f32[108,128]{1,0:T(8,128)S(1)} %get-tuple-element.45), channel_id=1, source_target_pairs={{8,16},{16,8},{9,17},{17,9},{10,18},{18,10},{11,19},{19,11},{12,20... | collective-permute-start | bytes 165896 | tf_op jit(solution)/shard_map/ppermute | solution.py:462
  26.1 3.9 %collective-permute-start.10 = (f32[264,128]{1,0:T(8,128)S(1)}, f32[264,128]{1,0:T(8,128)S(1)}, u32[]{:S(2)}, u32[]{:S(2)}) collective-permute-start(f32[264,128]{1,0:T(8,128)S(1)} %get-tuple-element.49), channel_id=1, source_target_pairs={{0,8},{16,24},{8,0},{24,16},{1,9},{17,25},{9,1},{25,17},{2,10},{18... | collective-permute-start | bytes 405512 | tf_op jit(solution)/shard_map/ppermute | solution.py:462
  26.2 6.1 %collective-permute-start.11 = (f32[264,128]{1,0:T(8,128)S(1)}, f32[264,128]{1,0:T(8,128)S(1)}, u32[]{:S(2)}, u32[]{:S(2)}) collective-permute-start(f32[264,128]{1,0:T(8,128)S(1)} %get-tuple-element.50), channel_id=1, source_target_pairs={{8,16},{16,8},{9,17},{17,9},{10,18},{18,10},{11,19},{19,11},{12,20... | collective-permute-start | bytes 405512 | tf_op jit(solution)/shard_map/ppermute | solution.py:462
  32.7 3.9 %collective-permute-start.12 = (f32[9,2,8,128]{3,2,1,0:T(8,128)S(1)}, f32[9,2,8,128]{3,2,1,0:T(8,128)S(1)}, u32[]{:S(2)}, u32[]{:S(2)}) collective-permute-start(f32[9,2,8,128]{3,2,1,0:T(8,128)S(1)} %get-tuple-element.52), channel_id=1, source_target_pairs={{0,1},{1,0},{2,3},{3,2},{4,5},{5,4},{6,7},{7,6},{8,9},{9,8},{10,11... | collective-permute-start | bytes 221192 | tf_op jit(solution)/shard_map/ppermute | solution.py:473

commit v14 on v11

--- a/solution.py
+++ b/solution.py
@@ -487,7 +487,7 @@
     )
     blocks = [
         lax.ppermute(entries, "sec", [(other(i, k), i) for i in range(sections)])
-        for k in (sections - 1, *range(1, sections - 1))
+        for k in reversed(range(1, sections))
     ]
     got = swap(given)
     acc_shape = (6 * cx * cz // 2, 2 * cy)
@@ -500,7 +500,7 @@
         [],
         flops=10**8,
     )
-    for block in blocks[:-1]:
+    for block, flops in zip(blocks[:-1], (10**8,) + (6 * 10**9,) * sections):
         (started,) = call(
             functools.partial(more_kernel, layout),
             "more_moments",
@@ -508,7 +508,7 @@
             (),
             [acc_shape],
             [],
-            flops=6 * 10**9,
+            flops=flops,
         )
     own = (cx, rows, cy)
     window = (3 * cx, rows, cy)

time: 35.4 us -> 35.8 us (1.011)
  waiting for transfers between devices: 6.38 us -> 7.06 us
    ppermute x6, waiting for transfers between devices: 5.45 us -> 6.14 us  [pairs(): return lax.ppermute(block, 'sec', route + [(j, i) for i, j in route])]
where the time goes in v14:
time: 35.8 us; the launch traced here: 35.6 us
  starting transfers between devices  21.5 us (60%)
  waiting for transfers between devices  7.06 us (20%)
  Pallas kernels  5.92 us (17%)
  local copies, waits for them, and re-layouts  0.92 us (3%)
    ppermute x6, starting transfers between devices, pairs(): return lax.ppermute(block, 'sec', route + [(j, i) for i, j in route])  10.1 us
    ppermute x6, waiting for transfers between devices, pairs(): return lax.ppermute(block, 'sec', route + [(j, i) for i, j in route])  6.14 us
    pallas_call x10, Pallas kernels, call(): pl.pallas_call(kernel, out_shape=[jax.ShapeDtypeStruct(shape, F32) for sh...  5.92 us
    ppermute x2, starting transfers between devices, swap(): return lax.ppermute(block, 'segment', [(0, 1), (1, 0)])  4.08 us
    ppermute x1, starting transfers between devices, along_depth(): lax.ppermute(block, ('depth', 'segment'), down + [(j, i) for i, j in down])  3.81 us
    ppermute x3, starting transfers between devices, on_device(): lax.ppermute(entries, 'sec', [(other(i, k), i) for i in range(sections)])  3.56 us
    unnamed x2, local copies, waits for them, and re-layouts  0.92 us
    ppermute x2, waiting for transfers between devices, swap(): return lax.ppermute(block, 'segment', [(0, 1), (1, 0)])  0.92 us
  transfers between devices with their start and end apart: 12, of which 5 were waited for; matrix products, arithmetic and copies ran while one was open for 0% of the time, Pallas kernels for 5%

profile of v14, /device:TPU:13, one launch (start us, length us, event | category | flops | bytes accessed | tf_op | source)
XLA Modules:
  0.0 35.6 jit_solution(8849199896564153096)
XLA Ops:
  0.0 2.1 %pack.1 = (f32[64,128]{1,0:T(8,128)}, f32[336,128]{1,0:T(8,128)}, f32[10,24,128]{2,1,0:T(8,128)}) custom-call(f32[1,9,2,16,128]{4,3,2,1,0:T(8,128)} %fields_in.1, s32[1,2,16,128]{3,2,1,0:T(8,128)} %ids_in.1, f32[6,1024]{1,0:T(8,128)} %moments_in.1, s32[8,128]{1,0:T(8,128)} %bitcast.4, s32[8,128]{1,0:T(8,128)} %bitcast.5, s32[16,128]{1,0:T(8,128)} %bitcast.3, ...), custom_call_target="tpu_custom_call" | custom-call | flops 10000000 | bytes 1048576 | tf_op jit(solution)/shard_map/pack/pallas_call | solution.py:439
  2.1 1.4 %collective-permute-start.1 = (f32[64,128]{1,0:T(8,128)}, f32[64,128]{1,0:T(8,128)S(1)}, u32[]{:S(2)}, u32[]{:S(2)}) collective-permute-start(f32[64,128]{1,0:T(8,128)} %get-tuple-element.33), channel_id=1, source_target_pairs={{24,0},{16,8},{8,16},{0,24},{25,1},{17,9},{9,17},{1,25},{26,2},{18... | collective-permute-start | bytes 98312 | tf_op jit(solution)/shard_map/ppermute | solution.py:489
  3.4 1.1 %collective-permute-start.2 = (f32[64,128]{1,0:T(8,128)}, f32[64,128]{1,0:T(8,128)S(1)}, u32[]{:S(2)}, u32[]{:S(2)}) collective-permute-start(f32[64,128]{1,0:T(8,128)} %get-tuple-element.33), channel_id=1, source_target_pairs={{16,0},{24,8},{0,16},{8,24},{17,1},{25,9},{1,17},{9,25},{18,2},{26... | collective-permute-start | bytes 98312 | tf_op jit(solution)/shard_map/ppermute | solution.py:489
  4.5 1.1 %collective-permute-start.3 = (f32[64,128]{1,0:T(8,128)}, f32[64,128]{1,0:T(8,128)S(1)}, u32[]{:S(2)}, u32[]{:S(2)}) collective-permute-start(f32[64,128]{1,0:T(8,128)} %get-tuple-element.33), channel_id=1, source_target_pairs={{8,0},{0,8},{24,16},{16,24},{9,1},{1,9},{25,17},{17,25},{10,2},{2,... | collective-permute-start | bytes 98312 | tf_op jit(solution)/shard_map/ppermute | solution.py:489
  5.6 1.2 %collective-permute-start = (f32[10,24,128]{2,1,0:T(8,128)}, f32[10,24,128]{2,1,0:T(8,128)S(1)}, u32[]{:S(2)}, u32[]{:S(2)}) collective-permute-start(f32[10,24,128]{2,1,0:T(8,128)} %get-tuple-element.31), channel_id=1, source_target_pairs={{0,1},{1,0},{2,3},{3,2},{4,5},{5,4},{6,7},{7,6},{8,9},{9,8},{10,11... | collective-permute-start | bytes 368648 | tf_op jit(solution)/shard_map/ppermute | solution.py:471
  6.9 0.9 %copy-done = f32[336,128]{1,0:T(8,128)S(1)} copy-done((f32[336,128]{1,0:T(8,128)S(1)}, f32[336,128]{1,0:T(8,128)}, u32[]{:S(2)}) %copy-start) | copy-done | bytes 172056
  7.8 0.4 %own_moments.1 = (f32[11,24,128]{2,1,0:T(8,128)S(1)}, f32[8,128]{1,0:T(8,128)S(1)}, f32[96,256]{1,0:T(8,128)S(1)}) custom-call(f32[336,128]{1,0:T(8,128)S(1)} %copy-done), custom_call_target="tpu_custom_call" | custom-call | flops 100000000 | bytes 1048576 | tf_op jit(solution)/shard_map/own_moments/pallas_call | solution.py:439
  8.2 0.4 %more_moments.2.started = f32[96,256]{1,0:T(8,128)S(1)} custom-call(f32[96,256]{1,0:T(8,128)S(1)} %get-tuple-element.32.started, f32[64,128]{1,0:T(8,128)S(1)} %collective-permute-done.1.entries), custom_call_target="tpu_custom_call" | custom-call | flops 100000000 | bytes 1048576 | tf_op jit(solution)/shard_map/more_moments/pallas_call | solution.py:439
  8.6 0.4 %more_moments.3.refs_2_ = f32[96,256]{1,0:T(8,128)S(1)} custom-call(f32[96,256]{1,0:T(8,128)S(1)} %more_moments.2.started, f32[64,128]{1,0:T(8,128)S(1)} %collective-permute-done.2.entries), custom_call_target="tpu_custom_call" | custom-call | flops 6000000000 | bytes 1048576 | tf_op jit(solution)/shard_map/more_moments/pallas_call | solution.py:439
  9.0 0.5 %join_and_moments.1 = (f32[2,9,2,16,128]{4,3,2,1,0:T(8,128)S(1)}, f32[2,2,16,128]{3,2,1,0:T(8,128)S(1)}, f32[2,16,128]{2,1,0:T(8,128)S(1)}, f32[168,128]{1,0:T(8,128)S(1)}) custom-call(f32[11,24,128]{2,1,0:T(8,128)S(1)} %get-tuple-element.30.refs_0_, f32[10,24,128]{2,1,0:T(8,128)S(1)} %collective-permute-done.refs_1_, f32[96,256]{1,0:T(8,128)S(1)} %more_moments.3.refs_2_, ...), custom_call_target="tpu_custom_call" | custom-call | flops 10000000 | bytes 1048576 | tf_op jit(solution)/shard_map/join_and_moments/pallas_call | solution.py:439
  9.5 3.8 %collective-permute-start.4 = (f32[168,128]{1,0:T(8,128)S(1)}, f32[168,128]{1,0:T(8,128)S(1)}, u32[]{:S(2)}, u32[]{:S(2)}) collective-permute-start(f32[168,128]{1,0:T(8,128)S(1)} %get-tuple-element.37), channel_id=1, source_target_pairs={{1,2},{3,4},{5,6},{2,1},{4,3},{6,5},{9,10},{11,12},{13,14},{10,9},... | collective-permute-start | bytes 258056 | tf_op jit(solution)/shard_map/ppermute | solution.py:468
  13.5 2.3 %collective-permute-start.5 = (f32[324,128]{1,0:T(8,128)S(1)}, f32[324,128]{1,0:T(8,128)S(1)}, u32[]{:S(2)}, u32[]{:S(2)}) collective-permute-start(f32[324,128]{1,0:T(8,128)S(1)} %get-tuple-element.42), channel_id=1, source_target_pairs={{0,8},{16,24},{8,0},{24,16},{1,9},{17,25},{9,1},{25,17},{2,10},{18... | collective-permute-start | bytes 497672 | tf_op jit(solution)/shard_map/ppermute | solution.py:461
  15.8 2.1 %collective-permute-start.6 = (f32[324,128]{1,0:T(8,128)S(1)}, f32[324,128]{1,0:T(8,128)S(1)}, u32[]{:S(2)}, u32[]{:S(2)}) collective-permute-start(f32[324,128]{1,0:T(8,128)S(1)} %get-tuple-element.43), channel_id=1, source_target_pairs={{8,16},{16,8},{9,17},{17,9},{10,18},{18,10},{11,19},{19,11},{12,20... | collective-permute-start | bytes 497672 | tf_op jit(solution)/shard_map/ppermute | solution.py:461
  17.9 0.3 outer_edges.1
  18.3 3.1 %collective-permute-start.8 = (f32[108,128]{1,0:T(8,128)S(1)}, f32[108,128]{1,0:T(8,128)S(1)}, u32[]{:S(2)}, u32[]{:S(2)}) collective-permute-start(f32[108,128]{1,0:T(8,128)S(1)} %get-tuple-element.45), channel_id=1, source_target_pairs={{8,16},{16,8},{9,17},{17,9},{10,18},{18,10},{11,19},{19,11},{12,20... | collective-permute-start | bytes 165896 | tf_op jit(solution)/shard_map/ppermute | solution.py:461
  21.5 2.4 %collective-permute-done.8.refs_6_ = f32[108,128]{1,0:T(8,128)S(1)} collective-permute-done((f32[108,128]{1,0:T(8,128)S(1)}, f32[108,128]{1,0:T(8,128)S(1)}, u32[]{:S(2)}, u32[]{:S(2)}) %collective-permute-start.8) | collective-permute-done | bytes 55328 | tf_op jit(solution)/shard_map/ppermute | solution.py:461
  23.9 0.6 %steps.2 = (f32[264,128]{1,0:T(8,128)S(1)}, f32[264,128]{1,0:T(8,128)S(1)}, f32[2,9,2,16,128]{4,3,2,1,0:T(8,128)S(1)}, f32[2,3,6,16,128]{4,3,2,1,0:T(8,128)S(1)}, f32[6,16,128]{2,1,0:T(8,128)S(1)}) custom-call(f32[2,9,2,16,128]{4,3,2,1,0:T(8,128)S(1)} %get-tuple-element.39.refs_0_, f32[2,3,2,16,128]{4,3,2,1,0:T(8,128)S(1)} %get-tuple-element.40.refs_1_, ...), custom_call_target="tpu_custom_call" | custom-call | flops 10000000 | bytes 1048576 | tf_op jit(solution)/shard_map/steps/pallas_call | solution.py:439
  24.6 2.4 %collective-permute-start.10 = (f32[264,128]{1,0:T(8,128)S(1)}, f32[264,128]{1,0:T(8,128)S(1)}, u32[]{:S(2)}, u32[]{:S(2)}) collective-permute-start(f32[264,128]{1,0:T(8,128)S(1)} %get-tuple-element.50), channel_id=1, source_target_pairs={{8,16},{16,8},{9,17},{17,9},{10,18},{18,10},{11,19},{19,11},{12,20... | collective-permute-start | bytes 405512 | tf_op jit(solution)/shard_map/ppermute | solution.py:461
  27.1 1.4 %collective-permute-done.9.refs_3_ = f32[264,128]{1,0:T(8,128)S(1)} collective-permute-done((f32[264,128]{1,0:T(8,128)S(1)}, f32[264,128]{1,0:T(8,128)S(1)}, u32[]{:S(2)}, u32[]{:S(2)}) %collective-permute-start.9) | collective-permute-done | bytes 135200 | tf_op jit(solution)/shard_map/ppermute | solution.py:461
  28.5 2.2 %collective-permute-done.10.refs_4_ = f32[264,128]{1,0:T(8,128)S(1)} collective-permute-done((f32[264,128]{1,0:T(8,128)S(1)}, f32[264,128]{1,0:T(8,128)S(1)}, u32[]{:S(2)}, u32[]{:S(2)}) %collective-permute-start.10) | collective-permute-done | bytes 135200 | tf_op jit(solution)/shard_map/ppermute | solution.py:461
  30.7 0.4 %steps.3 = (f32[9,2,8,128]{3,2,1,0:T(8,128)S(1)}, f32[9,2,8,128]{3,2,1,0:T(8,128)S(1)}) custom-call(f32[2,9,2,16,128]{4,3,2,1,0:T(8,128)S(1)} %get-tuple-element.46.refs_0_, f32[2,3,6,16,128]{4,3,2,1,0:T(8,128)S(1)} %get-tuple-element.47.refs_1_, f32[6,16,128]{2,1,0:T(8,128)S(1)} %get-tuple-element.48.refs_2_, ...), custom_call_target="tpu_custom_call" | custom-call | flops 10000000 | bytes 1048576 | tf_op jit(solution)/shard_map/steps/pallas_call | solution.py:439
  31.2 2.9 %collective-permute-start.11 = (f32[9,2,8,128]{3,2,1,0:T(8,128)S(1)}, f32[9,2,8,128]{3,2,1,0:T(8,128)S(1)}, u32[]{:S(2)}, u32[]{:S(2)}) collective-permute-start(f32[9,2,8,128]{3,2,1,0:T(8,128)S(1)} %get-tuple-element.52), channel_id=1, source_target_pairs={{0,1},{1,0},{2,3},{3,2},{4,5},{5,4},{6,7},{7,6},{8,9},{9,8},{10,11... | collective-permute-start | bytes 221192 | tf_op jit(solution)/shard_map/ppermute | solution.py:471
  34.0 0.9 %collective-permute-done.11.brought = f32[9,2,8,128]{3,2,1,0:T(8,128)S(1)} collective-permute-done((f32[9,2,8,128]{3,2,1,0:T(8,128)S(1)}, f32[9,2,8,128]{3,2,1,0:T(8,128)S(1)}, u32[]{:S(2)}, u32[]{:S(2)}) %collective-permute-start.11) | collective-permute-done | bytes 73760 | tf_op jit(solution)/shard_map/ppermute | solution.py:471
  34.9 0.7 %home.1 = f32[1,9,2,16,128]{4,3,2,1,0:T(8,128)} custom-call(f32[9,2,8,128]{3,2,1,0:T(8,128)S(1)} %get-tuple-element.51.mine, f32[9,2,8,128]{3,2,1,0:T(8,128)S(1)} %collective-permute-done.11.brought), custom_call_target="tpu_custom_call" | custom-call | flops 10000000 | bytes 1048576 | tf_op jit(solution)/shard_map/home/pallas_call | solution.py:439
  (12 shorter events, 0.5 us)
Async XLA Ops:
  2.1 6.1 %collective-permute-start.1 = (f32[64,128]{1,0:T(8,128)}, f32[64,128]{1,0:T(8,128)S(1)}, u32[]{:S(2)}, u32[]{:S(2)}) collective-permute-start(f32[64,128]{1,0:T(8,128)} %get-tuple-element.33), channel_id=1, source_target_pairs={{24,0},{16,8},{8,16},{0,24},{25,1},{17,9},{9,17},{1,25},{26,2},{18... | collective-permute-start | bytes 98312 | tf_op jit(solution)/shard_map/ppermute | solution.py:489
  3.4 5.1 %collective-permute-start.2 = (f32[64,128]{1,0:T(8,128)}, f32[64,128]{1,0:T(8,128)S(1)}, u32[]{:S(2)}, u32[]{:S(2)}) collective-permute-start(f32[64,128]{1,0:T(8,128)} %get-tuple-element.33), channel_id=1, source_target_pairs={{16,0},{24,8},{0,16},{8,24},{17,1},{25,9},{1,17},{9,25},{18,2},{26... | collective-permute-start | bytes 98312 | tf_op jit(solution)/shard_map/ppermute | solution.py:489
  4.5 4.5 %collective-permute-start.3 = (f32[64,128]{1,0:T(8,128)}, f32[64,128]{1,0:T(8,128)S(1)}, u32[]{:S(2)}, u32[]{:S(2)}) collective-permute-start(f32[64,128]{1,0:T(8,128)} %get-tuple-element.33), channel_id=1, source_target_pairs={{8,0},{0,8},{24,16},{16,24},{9,1},{1,9},{25,17},{17,25},{10,2},{2,... | collective-permute-start | bytes 98312 | tf_op jit(solution)/shard_map/ppermute | solution.py:489
  5.6 3.4 %collective-permute-start = (f32[10,24,128]{2,1,0:T(8,128)}, f32[10,24,128]{2,1,0:T(8,128)S(1)}, u32[]{:S(2)}, u32[]{:S(2)}) collective-permute-start(f32[10,24,128]{2,1,0:T(8,128)} %get-tuple-element.31), channel_id=1, source_target_pairs={{0,1},{1,0},{2,3},{3,2},{4,5},{5,4},{6,7},{7,6},{8,9},{9,8},{10,11... | collective-permute-start | bytes 368648 | tf_op jit(solution)/shard_map/ppermute | solution.py:471
  6.9 0.9 %copy-start = (f32[336,128]{1,0:T(8,128)S(1)}, f32[336,128]{1,0:T(8,128)}, u32[]{:S(2)}) copy-start(f32[336,128]{1,0:T(8,128)} %get-tuple-element.29.kept) | copy-start | bytes 516100
  9.5 8.4 %collective-permute-start.4 = (f32[168,128]{1,0:T(8,128)S(1)}, f32[168,128]{1,0:T(8,128)S(1)}, u32[]{:S(2)}, u32[]{:S(2)}) collective-permute-start(f32[168,128]{1,0:T(8,128)S(1)} %get-tuple-element.37), channel_id=1, source_target_pairs={{1,2},{3,4},{5,6},{2,1},{4,3},{6,5},{9,10},{11,12},{13,14},{10,9},... | collective-permute-start | bytes 258056 | tf_op jit(solution)/shard_map/ppermute | solution.py:468
  13.5 10.4 %collective-permute-start.5 = (f32[324,128]{1,0:T(8,128)S(1)}, f32[324,128]{1,0:T(8,128)S(1)}, u32[]{:S(2)}, u32[]{:S(2)}) collective-permute-start(f32[324,128]{1,0:T(8,128)S(1)} %get-tuple-element.42), channel_id=1, source_target_pairs={{0,8},{16,24},{8,0},{24,16},{1,9},{17,25},{9,1},{25,17},{2,10},{18... | collective-permute-start | bytes 497672 | tf_op jit(solution)/shard_map/ppermute | solution.py:461
  15.8 8.2 %collective-permute-start.6 = (f32[324,128]{1,0:T(8,128)S(1)}, f32[324,128]{1,0:T(8,128)S(1)}, u32[]{:S(2)}, u32[]{:S(2)}) collective-permute-start(f32[324,128]{1,0:T(8,128)S(1)} %get-tuple-element.43), channel_id=1, source_target_pairs={{8,16},{16,8},{9,17},{17,9},{10,18},{18,10},{11,19},{19,11},{12,20... | collective-permute-start | bytes 497672 | tf_op jit(solution)/shard_map/ppermute | solution.py:461
  18.2 3.4 %collective-permute-start.7 = (f32[108,128]{1,0:T(8,128)S(1)}, f32[108,128]{1,0:T(8,128)S(1)}, u32[]{:S(2)}, u32[]{:S(2)}) collective-permute-start(f32[108,128]{1,0:T(8,128)S(1)} %get-tuple-element.44), channel_id=1, source_target_pairs={{0,8},{16,24},{8,0},{24,16},{1,9},{17,25},{9,1},{25,17},{2,10},{18... | collective-permute-start | bytes 165896 | tf_op jit(solution)/shard_map/ppermute | solution.py:461
  18.3 5.7 %collective-permute-start.8 = (f32[108,128]{1,0:T(8,128)S(1)}, f32[108,128]{1,0:T(8,128)S(1)}, u32[]{:S(2)}, u32[]{:S(2)}) collective-permute-start(f32[108,128]{1,0:T(8,128)S(1)} %get-tuple-element.45), channel_id=1, source_target_pairs={{8,16},{16,8},{9,17},{17,9},{10,18},{18,10},{11,19},{19,11},{12,20... | collective-permute-start | bytes 165896 | tf_op jit(solution)/shard_map/ppermute | solution.py:461
  24.6 3.9 %collective-permute-start.9 = (f32[264,128]{1,0:T(8,128)S(1)}, f32[264,128]{1,0:T(8,128)S(1)}, u32[]{:S(2)}, u32[]{:S(2)}) collective-permute-start(f32[264,128]{1,0:T(8,128)S(1)} %get-tuple-element.49), channel_id=1, source_target_pairs={{0,8},{16,24},{8,0},{24,16},{1,9},{17,25},{9,1},{25,17},{2,10},{18... | collective-permute-start | bytes 405512 | tf_op jit(solution)/shard_map/ppermute | solution.py:461
  24.6 6.1 %collective-permute-start.10 = (f32[264,128]{1,0:T(8,128)S(1)}, f32[264,128]{1,0:T(8,128)S(1)}, u32[]{:S(2)}, u32[]{:S(2)}) collective-permute-start(f32[264,128]{1,0:T(8,128)S(1)} %get-tuple-element.50), channel_id=1, source_target_pairs={{8,16},{16,8},{9,17},{17,9},{10,18},{18,10},{11,19},{19,11},{12,20... | collective-permute-start | bytes 405512 | tf_op jit(solution)/shard_map/ppermute | solution.py:461
  31.2 3.8 %collective-permute-start.11 = (f32[9,2,8,128]{3,2,1,0:T(8,128)S(1)}, f32[9,2,8,128]{3,2,1,0:T(8,128)S(1)}, u32[]{:S(2)}, u32[]{:S(2)}) collective-permute-start(f32[9,2,8,128]{3,2,1,0:T(8,128)S(1)} %get-tuple-element.52), channel_id=1, source_target_pairs={{0,1},{1,0},{2,3},{3,2},{4,5},{5,4},{6,7},{7,6},{8,9},{9,8},{10,11... | collective-permute-start | bytes 221192 | tf_op jit(solution)/shard_map/ppermute | solution.py:471

commit v15 on v14

--- a/solution.py
+++ b/solution.py
@@ -487,7 +487,7 @@
     )
     blocks = [
         lax.ppermute(entries, "sec", [(other(i, k), i) for i in range(sections)])
-        for k in reversed(range(1, sections))
+        for k in (*range(2, sections), 1)[: sections - 1]
     ]
     got = swap(given)
     acc_shape = (6 * cx * cz // 2, 2 * cy)

time: 35.8 us -> 35.7 us (level)
  no operation moved by 1% of the time
where the time goes in v15:
time: 35.7 us; the launch traced here: 35.5 us
  starting transfers between devices  21.6 us (61%)
  waiting for transfers between devices  6.9 us (19%)
  Pallas kernels  5.91 us (17%)
  local copies, waits for them, and re-layouts  0.92 us (3%)
    ppermute x6, starting transfers between devices, pairs(): return lax.ppermute(block, 'sec', route + [(j, i) for i, j in route])  10 us
    ppermute x6, waiting for transfers between devices, pairs(): return lax.ppermute(block, 'sec', route + [(j, i) for i, j in route])  5.98 us
    pallas_call x10, Pallas kernels, call(): pl.pallas_call(kernel, out_shape=[jax.ShapeDtypeStruct(shape, F32) for sh...  5.91 us
    ppermute x2, starting transfers between devices, swap(): return lax.ppermute(block, 'segment', [(0, 1), (1, 0)])  4.34 us
    ppermute x3, starting transfers between devices, on_device(): lax.ppermute(entries, 'sec', [(other(i, k), i) for i in range(sections)])  3.64 us
    ppermute x1, starting transfers between devices, along_depth(): lax.ppermute(block, ('depth', 'segment'), down + [(j, i) for i, j in down])  3.59 us
    unnamed x2, local copies, waits for them, and re-layouts  0.92 us
    ppermute x2, waiting for transfers between devices, swap(): return lax.ppermute(block, 'segment', [(0, 1), (1, 0)])  0.92 us
  transfers between devices with their start and end apart: 12, of which 5 were waited for; matrix products, arithmetic and copies ran while one was open for 0% of the time, Pallas kernels for 5%

profile of v15, /device:TPU:13, one launch (start us, length us, event | category | flops | bytes accessed | tf_op | source)
XLA Modules:
  0.0 35.5 jit_solution(5356771965618843205)
XLA Ops:
  0.0 2.1 %pack.1 = (f32[64,128]{1,0:T(8,128)}, f32[336,128]{1,0:T(8,128)}, f32[10,24,128]{2,1,0:T(8,128)}) custom-call(f32[1,9,2,16,128]{4,3,2,1,0:T(8,128)} %fields_in.1, s32[1,2,16,128]{3,2,1,0:T(8,128)} %ids_in.1, f32[6,1024]{1,0:T(8,128)} %moments_in.1, s32[8,128]{1,0:T(8,128)} %bitcast.4, s32[8,128]{1,0:T(8,128)} %bitcast.5, s32[16,128]{1,0:T(8,128)} %bitcast.3, ...), custom_call_target="tpu_custom_call" | custom-call | flops 10000000 | bytes 1048576 | tf_op jit(solution)/shard_map/pack/pallas_call | solution.py:439
  2.1 2.4 %collective-permute-start.1 = (f32[64,128]{1,0:T(8,128)}, f32[64,128]{1,0:T(8,128)S(1)}, u32[]{:S(2)}, u32[]{:S(2)}) collective-permute-start(f32[64,128]{1,0:T(8,128)} %get-tuple-element.33), channel_id=1, source_target_pairs={{16,0},{24,8},{0,16},{8,24},{17,1},{25,9},{1,17},{9,25},{18,2},{26... | collective-permute-start | bytes 98312 | tf_op jit(solution)/shard_map/ppermute | solution.py:489
  4.5 1.3 %collective-permute-start.3 = (f32[64,128]{1,0:T(8,128)}, f32[64,128]{1,0:T(8,128)S(1)}, u32[]{:S(2)}, u32[]{:S(2)}) collective-permute-start(f32[64,128]{1,0:T(8,128)} %get-tuple-element.33), channel_id=1, source_target_pairs={{8,0},{0,8},{24,16},{16,24},{9,1},{1,9},{25,17},{17,25},{10,2},{2,... | collective-permute-start | bytes 98312 | tf_op jit(solution)/shard_map/ppermute | solution.py:489
  5.7 1.5 %collective-permute-start = (f32[10,24,128]{2,1,0:T(8,128)}, f32[10,24,128]{2,1,0:T(8,128)S(1)}, u32[]{:S(2)}, u32[]{:S(2)}) collective-permute-start(f32[10,24,128]{2,1,0:T(8,128)} %get-tuple-element.31), channel_id=1, source_target_pairs={{0,1},{1,0},{2,3},{3,2},{4,5},{5,4},{6,7},{7,6},{8,9},{9,8},{10,11... | collective-permute-start | bytes 368648 | tf_op jit(solution)/shard_map/ppermute | solution.py:471
  7.2 0.9 %copy-done = f32[336,128]{1,0:T(8,128)S(1)} copy-done((f32[336,128]{1,0:T(8,128)S(1)}, f32[336,128]{1,0:T(8,128)}, u32[]{:S(2)}) %copy-start) | copy-done | bytes 172056
  8.1 0.4 %own_moments.1 = (f32[11,24,128]{2,1,0:T(8,128)S(1)}, f32[8,128]{1,0:T(8,128)S(1)}, f32[96,256]{1,0:T(8,128)S(1)}) custom-call(f32[336,128]{1,0:T(8,128)S(1)} %copy-done), custom_call_target="tpu_custom_call" | custom-call | flops 100000000 | bytes 1048576 | tf_op jit(solution)/shard_map/own_moments/pallas_call | solution.py:439
  8.5 0.4 %more_moments.2.started = f32[96,256]{1,0:T(8,128)S(1)} custom-call(f32[96,256]{1,0:T(8,128)S(1)} %get-tuple-element.32.started, f32[64,128]{1,0:T(8,128)S(1)} %collective-permute-done.1.entries), custom_call_target="tpu_custom_call" | custom-call | flops 100000000 | bytes 1048576 | tf_op jit(solution)/shard_map/more_moments/pallas_call | solution.py:439
  8.9 0.4 %more_moments.3.refs_2_ = f32[96,256]{1,0:T(8,128)S(1)} custom-call(f32[96,256]{1,0:T(8,128)S(1)} %more_moments.2.started, f32[64,128]{1,0:T(8,128)S(1)} %collective-permute-done.2.entries), custom_call_target="tpu_custom_call" | custom-call | flops 6000000000 | bytes 1048576 | tf_op jit(solution)/shard_map/more_moments/pallas_call | solution.py:439
  9.3 0.5 %join_and_moments.1 = (f32[2,9,2,16,128]{4,3,2,1,0:T(8,128)S(1)}, f32[2,2,16,128]{3,2,1,0:T(8,128)S(1)}, f32[2,16,128]{2,1,0:T(8,128)S(1)}, f32[168,128]{1,0:T(8,128)S(1)}) custom-call(f32[11,24,128]{2,1,0:T(8,128)S(1)} %get-tuple-element.30.refs_0_, f32[10,24,128]{2,1,0:T(8,128)S(1)} %collective-permute-done.refs_1_, f32[96,256]{1,0:T(8,128)S(1)} %more_moments.3.refs_2_, ...), custom_call_target="tpu_custom_call" | custom-call | flops 10000000 | bytes 1048576 | tf_op jit(solution)/shard_map/join_and_moments/pallas_call | solution.py:439
  9.8 3.6 %collective-permute-start.4 = (f32[168,128]{1,0:T(8,128)S(1)}, f32[168,128]{1,0:T(8,128)S(1)}, u32[]{:S(2)}, u32[]{:S(2)}) collective-permute-start(f32[168,128]{1,0:T(8,128)S(1)} %get-tuple-element.37), channel_id=1, source_target_pairs={{1,2},{3,4},{5,6},{2,1},{4,3},{6,5},{9,10},{11,12},{13,14},{10,9},... | collective-permute-start | bytes 258056 | tf_op jit(solution)/shard_map/ppermute | solution.py:468
  13.6 2.0 %collective-permute-start.5 = (f32[324,128]{1,0:T(8,128)S(1)}, f32[324,128]{1,0:T(8,128)S(1)}, u32[]{:S(2)}, u32[]{:S(2)}) collective-permute-start(f32[324,128]{1,0:T(8,128)S(1)} %get-tuple-element.42), channel_id=1, source_target_pairs={{0,8},{16,24},{8,0},{24,16},{1,9},{17,25},{9,1},{25,17},{2,10},{18... | collective-permute-start | bytes 497672 | tf_op jit(solution)/shard_map/ppermute | solution.py:461
  15.7 2.3 %collective-permute-start.6 = (f32[324,128]{1,0:T(8,128)S(1)}, f32[324,128]{1,0:T(8,128)S(1)}, u32[]{:S(2)}, u32[]{:S(2)}) collective-permute-start(f32[324,128]{1,0:T(8,128)S(1)} %get-tuple-element.43), channel_id=1, source_target_pairs={{8,16},{16,8},{9,17},{17,9},{10,18},{18,10},{11,19},{19,11},{12,20... | collective-permute-start | bytes 497672 | tf_op jit(solution)/shard_map/ppermute | solution.py:461
  18.0 0.3 outer_edges.1
  18.4 2.9 %collective-permute-start.8 = (f32[108,128]{1,0:T(8,128)S(1)}, f32[108,128]{1,0:T(8,128)S(1)}, u32[]{:S(2)}, u32[]{:S(2)}) collective-permute-start(f32[108,128]{1,0:T(8,128)S(1)} %get-tuple-element.45), channel_id=1, source_target_pairs={{8,16},{16,8},{9,17},{17,9},{10,18},{18,10},{11,19},{19,11},{12,20... | collective-permute-start | bytes 165896 | tf_op jit(solution)/shard_map/ppermute | solution.py:461
  21.3 0.8 %collective-permute-done.7.refs_5_ = f32[108,128]{1,0:T(8,128)S(1)} collective-permute-done((f32[108,128]{1,0:T(8,128)S(1)}, f32[108,128]{1,0:T(8,128)S(1)}, u32[]{:S(2)}, u32[]{:S(2)}) %collective-permute-start.7) | collective-permute-done | bytes 55328 | tf_op jit(solution)/shard_map/ppermute | solution.py:461
  22.1 1.7 %collective-permute-done.8.refs_6_ = f32[108,128]{1,0:T(8,128)S(1)} collective-permute-done((f32[108,128]{1,0:T(8,128)S(1)}, f32[108,128]{1,0:T(8,128)S(1)}, u32[]{:S(2)}, u32[]{:S(2)}) %collective-permute-start.8) | collective-permute-done | bytes 55328 | tf_op jit(solution)/shard_map/ppermute | solution.py:461
  23.8 0.6 %steps.2 = (f32[264,128]{1,0:T(8,128)S(1)}, f32[264,128]{1,0:T(8,128)S(1)}, f32[2,9,2,16,128]{4,3,2,1,0:T(8,128)S(1)}, f32[2,3,6,16,128]{4,3,2,1,0:T(8,128)S(1)}, f32[6,16,128]{2,1,0:T(8,128)S(1)}) custom-call(f32[2,9,2,16,128]{4,3,2,1,0:T(8,128)S(1)} %get-tuple-element.39.refs_0_, f32[2,3,2,16,128]{4,3,2,1,0:T(8,128)S(1)} %get-tuple-element.40.refs_1_, ...), custom_call_target="tpu_custom_call" | custom-call | flops 10000000 | bytes 1048576 | tf_op jit(solution)/shard_map/steps/pallas_call | solution.py:439
  24.5 2.6 %collective-permute-start.10 = (f32[264,128]{1,0:T(8,128)S(1)}, f32[264,128]{1,0:T(8,128)S(1)}, u32[]{:S(2)}, u32[]{:S(2)}) collective-permute-start(f32[264,128]{1,0:T(8,128)S(1)} %get-tuple-element.50), channel_id=1, source_target_pairs={{8,16},{16,8},{9,17},{17,9},{10,18},{18,10},{11,19},{19,11},{12,20... | collective-permute-start | bytes 405512 | tf_op jit(solution)/shard_map/ppermute | solution.py:461
  27.1 1.3 %collective-permute-done.9.refs_3_ = f32[264,128]{1,0:T(8,128)S(1)} collective-permute-done((f32[264,128]{1,0:T(8,128)S(1)}, f32[264,128]{1,0:T(8,128)S(1)}, u32[]{:S(2)}, u32[]{:S(2)}) %collective-permute-start.9) | collective-permute-done | bytes 135200 | tf_op jit(solution)/shard_map/ppermute | solution.py:461
  28.4 2.2 %collective-permute-done.10.refs_4_ = f32[264,128]{1,0:T(8,128)S(1)} collective-permute-done((f32[264,128]{1,0:T(8,128)S(1)}, f32[264,128]{1,0:T(8,128)S(1)}, u32[]{:S(2)}, u32[]{:S(2)}) %collective-permute-start.10) | collective-permute-done | bytes 135200 | tf_op jit(solution)/shard_map/ppermute | solution.py:461
  30.6 0.4 %steps.3 = (f32[9,2,8,128]{3,2,1,0:T(8,128)S(1)}, f32[9,2,8,128]{3,2,1,0:T(8,128)S(1)}) custom-call(f32[2,9,2,16,128]{4,3,2,1,0:T(8,128)S(1)} %get-tuple-element.46.refs_0_, f32[2,3,6,16,128]{4,3,2,1,0:T(8,128)S(1)} %get-tuple-element.47.refs_1_, f32[6,16,128]{2,1,0:T(8,128)S(1)} %get-tuple-element.48.refs_2_, ...), custom_call_target="tpu_custom_call" | custom-call | flops 10000000 | bytes 1048576 | tf_op jit(solution)/shard_map/steps/pallas_call | solution.py:439
  31.0 2.9 %collective-permute-start.11 = (f32[9,2,8,128]{3,2,1,0:T(8,128)S(1)}, f32[9,2,8,128]{3,2,1,0:T(8,128)S(1)}, u32[]{:S(2)}, u32[]{:S(2)}) collective-permute-start(f32[9,2,8,128]{3,2,1,0:T(8,128)S(1)} %get-tuple-element.52), channel_id=1, source_target_pairs={{0,1},{1,0},{2,3},{3,2},{4,5},{5,4},{6,7},{7,6},{8,9},{9,8},{10,11... | collective-permute-start | bytes 221192 | tf_op jit(solution)/shard_map/ppermute | solution.py:471
  33.9 0.9 %collective-permute-done.11.brought = f32[9,2,8,128]{3,2,1,0:T(8,128)S(1)} collective-permute-done((f32[9,2,8,128]{3,2,1,0:T(8,128)S(1)}, f32[9,2,8,128]{3,2,1,0:T(8,128)S(1)}, u32[]{:S(2)}, u32[]{:S(2)}) %collective-permute-start.11) | collective-permute-done | bytes 73760 | tf_op jit(solution)/shard_map/ppermute | solution.py:471
  34.8 0.7 %home.1 = f32[1,9,2,16,128]{4,3,2,1,0:T(8,128)} custom-call(f32[9,2,8,128]{3,2,1,0:T(8,128)S(1)} %get-tuple-element.51.mine, f32[9,2,8,128]{3,2,1,0:T(8,128)S(1)} %collective-permute-done.11.brought), custom_call_target="tpu_custom_call" | custom-call | flops 10000000 | bytes 1048576 | tf_op jit(solution)/shard_map/home/pallas_call | solution.py:439
  (12 shorter events, 0.4 us)
Async XLA Ops:
  2.1 6.4 %collective-permute-start.1 = (f32[64,128]{1,0:T(8,128)}, f32[64,128]{1,0:T(8,128)S(1)}, u32[]{:S(2)}, u32[]{:S(2)}) collective-permute-start(f32[64,128]{1,0:T(8,128)} %get-tuple-element.33), channel_id=1, source_target_pairs={{16,0},{24,8},{0,16},{8,24},{17,1},{25,9},{1,17},{9,25},{18,2},{26... | collective-permute-start | bytes 98312 | tf_op jit(solution)/shard_map/ppermute | solution.py:489
  4.4 4.5 %collective-permute-start.2 = (f32[64,128]{1,0:T(8,128)}, f32[64,128]{1,0:T(8,128)S(1)}, u32[]{:S(2)}, u32[]{:S(2)}) collective-permute-start(f32[64,128]{1,0:T(8,128)} %get-tuple-element.33), channel_id=1, source_target_pairs={{24,0},{16,8},{8,16},{0,24},{25,1},{17,9},{9,17},{1,25},{26,2},{18... | collective-permute-start | bytes 98312 | tf_op jit(solution)/shard_map/ppermute | solution.py:489
  4.5 4.9 %collective-permute-start.3 = (f32[64,128]{1,0:T(8,128)}, f32[64,128]{1,0:T(8,128)S(1)}, u32[]{:S(2)}, u32[]{:S(2)}) collective-permute-start(f32[64,128]{1,0:T(8,128)} %get-tuple-element.33), channel_id=1, source_target_pairs={{8,0},{0,8},{24,16},{16,24},{9,1},{1,9},{25,17},{17,25},{10,2},{2,... | collective-permute-start | bytes 98312 | tf_op jit(solution)/shard_map/ppermute | solution.py:489
  5.7 3.6 %collective-permute-start = (f32[10,24,128]{2,1,0:T(8,128)}, f32[10,24,128]{2,1,0:T(8,128)S(1)}, u32[]{:S(2)}, u32[]{:S(2)}) collective-permute-start(f32[10,24,128]{2,1,0:T(8,128)} %get-tuple-element.31), channel_id=1, source_target_pairs={{0,1},{1,0},{2,3},{3,2},{4,5},{5,4},{6,7},{7,6},{8,9},{9,8},{10,11... | collective-permute-start | bytes 368648 | tf_op jit(solution)/shard_map/ppermute | solution.py:471
  7.2 0.9 %copy-start = (f32[336,128]{1,0:T(8,128)S(1)}, f32[336,128]{1,0:T(8,128)}, u32[]{:S(2)}) copy-start(f32[336,128]{1,0:T(8,128)} %get-tuple-element.29.kept) | copy-start | bytes 516100
  9.8 8.2 %collective-permute-start.4 = (f32[168,128]{1,0:T(8,128)S(1)}, f32[168,128]{1,0:T(8,128)S(1)}, u32[]{:S(2)}, u32[]{:S(2)}) collective-permute-start(f32[168,128]{1,0:T(8,128)S(1)} %get-tuple-element.37), channel_id=1, source_target_pairs={{1,2},{3,4},{5,6},{2,1},{4,3},{6,5},{9,10},{11,12},{13,14},{10,9},... | collective-permute-start | bytes 258056 | tf_op jit(solution)/shard_map/ppermute | solution.py:468
  13.6 10.2 %collective-permute-start.5 = (f32[324,128]{1,0:T(8,128)S(1)}, f32[324,128]{1,0:T(8,128)S(1)}, u32[]{:S(2)}, u32[]{:S(2)}) collective-permute-start(f32[324,128]{1,0:T(8,128)S(1)} %get-tuple-element.42), channel_id=1, source_target_pairs={{0,8},{16,24},{8,0},{24,16},{1,9},{17,25},{9,1},{25,17},{2,10},{18... | collective-permute-start | bytes 497672 | tf_op jit(solution)/shard_map/ppermute | solution.py:461
  15.7 8.2 %collective-permute-start.6 = (f32[324,128]{1,0:T(8,128)S(1)}, f32[324,128]{1,0:T(8,128)S(1)}, u32[]{:S(2)}, u32[]{:S(2)}) collective-permute-start(f32[324,128]{1,0:T(8,128)S(1)} %get-tuple-element.43), channel_id=1, source_target_pairs={{8,16},{16,8},{9,17},{17,9},{10,18},{18,10},{11,19},{19,11},{12,20... | collective-permute-start | bytes 497672 | tf_op jit(solution)/shard_map/ppermute | solution.py:461
  18.3 3.8 %collective-permute-start.7 = (f32[108,128]{1,0:T(8,128)S(1)}, f32[108,128]{1,0:T(8,128)S(1)}, u32[]{:S(2)}, u32[]{:S(2)}) collective-permute-start(f32[108,128]{1,0:T(8,128)S(1)} %get-tuple-element.44), channel_id=1, source_target_pairs={{0,8},{16,24},{8,0},{24,16},{1,9},{17,25},{9,1},{25,17},{2,10},{18... | collective-permute-start | bytes 165896 | tf_op jit(solution)/shard_map/ppermute | solution.py:461
  18.4 5.5 %collective-permute-start.8 = (f32[108,128]{1,0:T(8,128)S(1)}, f32[108,128]{1,0:T(8,128)S(1)}, u32[]{:S(2)}, u32[]{:S(2)}) collective-permute-start(f32[108,128]{1,0:T(8,128)S(1)} %get-tuple-element.45), channel_id=1, source_target_pairs={{8,16},{16,8},{9,17},{17,9},{10,18},{18,10},{11,19},{19,11},{12,20... | collective-permute-start | bytes 165896 | tf_op jit(solution)/shard_map/ppermute | solution.py:461
  24.5 3.9 %collective-permute-start.9 = (f32[264,128]{1,0:T(8,128)S(1)}, f32[264,128]{1,0:T(8,128)S(1)}, u32[]{:S(2)}, u32[]{:S(2)}) collective-permute-start(f32[264,128]{1,0:T(8,128)S(1)} %get-tuple-element.49), channel_id=1, source_target_pairs={{0,8},{16,24},{8,0},{24,16},{1,9},{17,25},{9,1},{25,17},{2,10},{18... | collective-permute-start | bytes 405512 | tf_op jit(solution)/shard_map/ppermute | solution.py:461
  24.5 6.1 %collective-permute-start.10 = (f32[264,128]{1,0:T(8,128)S(1)}, f32[264,128]{1,0:T(8,128)S(1)}, u32[]{:S(2)}, u32[]{:S(2)}) collective-permute-start(f32[264,128]{1,0:T(8,128)S(1)} %get-tuple-element.50), channel_id=1, source_target_pairs={{8,16},{16,8},{9,17},{17,9},{10,18},{18,10},{11,19},{19,11},{12,20... | collective-permute-start | bytes 405512 | tf_op jit(solution)/shard_map/ppermute | solution.py:461
  31.0 3.8 %collective-permute-start.11 = (f32[9,2,8,128]{3,2,1,0:T(8,128)S(1)}, f32[9,2,8,128]{3,2,1,0:T(8,128)S(1)}, u32[]{:S(2)}, u32[]{:S(2)}) collective-permute-start(f32[9,2,8,128]{3,2,1,0:T(8,128)S(1)} %get-tuple-element.52), channel_id=1, source_target_pairs={{0,1},{1,0},{2,3},{3,2},{4,5},{5,4},{6,7},{7,6},{8,9},{9,8},{10,11... | collective-permute-start | bytes 221192 | tf_op jit(solution)/shard_map/ppermute | solution.py:471

commit v16 on v11

--- a/solution.py
+++ b/solution.py
@@ -263,9 +263,10 @@
     right_units, left_units = edge_units(cx, with_ids)
 
     def put(to, units, far, right):
+        to, pairing = to
         line = slice(0, 0)
         for model, what, x in units:
-            at = rows_of(x == far, right)
+            at = rows_of(x == far, right, pairing)
             line = slice(line.stop, line.stop + at.stop - at.start)
             if what == 10:
                 to[line] = times[cx + x, at]
@@ -274,22 +275,36 @@
             else:
                 to[line] = state[model, what, cx + x, at]
 
-    holders = (to_second, to_first), (to_first, to_second)
+    first, second = (to_first, 0), (to_second, 1)
+    holders = (second, first), (first, second)
     by_parity(*holders, lambda left, right: put(right, right_units, 0, True))
     velocity(2 * cx - 1)
     by_parity(*holders, lambda left, right: put(left, left_units, cx - 1, False))
 
 
+def inner_rows(mine, main):
+    def rows_of(far, right, pairing):
+        short = STEPS * (pairing == 0)
+        if mine == 0:
+            return slice(main.start + short, main.stop)
+        return slice(main.start, main.stop - short)
+
+    return rows_of
+
+
 def outer_rows(mine, outer):
-    def rows_of(far, right):
-        shift = 1 if far and not right and mine == 0 else 0
-        return slice(outer.start + shift, outer.stop + shift)
+    def rows_of(far, right, pairing):
+        more = STEPS * (pairing == 0)
+        if mine == 1:
+            return slice(outer.start - more, outer.stop)
+        shift = 1 if far and not right else 0
+        return slice(outer.start + shift, outer.stop + more + shift)
 
     return rows_of
 
 
 def reached_rows(cx, done, rows):
-    def rows_of(far, right):
+    def rows_of(far, right, pairing=0):
         first, last = done, rows - done
         if right:
             return slice(first + (cx if far else 1), last)
@@ -313,7 +328,7 @@
     velocity = advance(cx, 0, state, coef, times)
 
     def cut(mine, main, outer):
-        rows_of = lambda far, right: main(reach)
+        rows_of = inner_rows(mine, main(reach))
         cut_edges(cx, rows_of, True, velocity, state, ids, times, to_first, to_second)
 
     by_core(cut)
@@ -370,9 +385,10 @@
     right_units, left_units = edge_units(cx, first)
 
     def get(edge, units, start, rows_of, far, right):
+        edge, pairing = edge
         last = 0
         for model, what, x in units:
-            at = rows_of(x == far, right)
+            at = rows_of(x == far, right, pairing)
             first, last = last, last + at.stop - at.start
             line = edge[first:last]
             if what == 10:
@@ -387,13 +403,14 @@
             get(left, right_units, 0, rows_of, 0, True)
             get(right, left_units, 2 * cx, rows_of, cx - 1, False)
 
-        by_parity((pair[1], pair[0]), pair, put)
+        early, late = (pair[0], 0), (pair[1], 1)
+        by_parity((late, early), (early, late), put)
 
     if first:
 
         def place_both(mine, main, outer):
             reach = rows - STEPS
-            place(lambda far, right: main(reach), edges[0:2])
+            place(inner_rows(mine, main(reach)), edges[0:2])
             place(outer_rows(mine, outer(reach)), edges[2:4])
 
         by_core(place_both)
@@ -523,8 +540,8 @@
     halo = along_depth(edge)
     work = [(2, 9, *window), (2, *window), (2, 3, *window), window]
 
-    def edges(count, with_ids):
-        return [(len(edge_units(cx, with_ids)[0]) * count, cy)] * 2
+    def edges(*counts):
+        return [(len(edge_units(cx, True)[0]) * count, cy) for count in counts]
 
     def reached_edges(done):
         rows_of = reached_rows(cx, done, rows)
@@ -540,7 +557,7 @@
         "inner_edges",
         (state, ids, times, tables),
         (),
-        edges(reach, True),
+        edges(reach - STEPS, reach),
         work,
         flops=10**9,
     )
@@ -550,7 +567,7 @@
         "outer_edges",
         (state, ids, times, halo, tables),
         (),
-        edges(STEPS, True) + [(2, 9, *own), (2, 3, *own), own],
+        edges(2 * STEPS, STEPS) + [(2, 9, *own), (2, 3, *own), own],
         work,
         flops=4 * 10**9,
     )

time: 35.4 us -> 35.4 us (level)
  transfers between devices with their start and end apart: 12 -> 12, of which waited for: 5 -> 4; matrix products, arithmetic and copies ran while one was open for 0% -> 0% of each run, Pallas kernels for 5% -> 5%
where the time goes in v16:
time: 35.4 us; the launch traced here: 35.2 us
  starting transfers between devices  21.7 us (61%)
  waiting for transfers between devices  6.48 us (18%)
  Pallas kernels  5.9 us (17%)
  local copies, waits for them, and re-layouts  0.92 us (3%)
    ppermute x6, starting transfers between devices, pairs(): return lax.ppermute(block, 'sec', route + [(j, i) for i, j in route])  10.1 us
    pallas_call x10, Pallas kernels, call(): pl.pallas_call(kernel, out_shape=[jax.ShapeDtypeStruct(shape, F32) for sh...  5.9 us
    ppermute x6, waiting for transfers between devices, pairs(): return lax.ppermute(block, 'sec', route + [(j, i) for i, j in route])  5.55 us
    ppermute x1, starting transfers between devices, along_depth(): lax.ppermute(block, ('depth', 'segment'), down + [(j, i) for i, j in down])  4.14 us
    ppermute x2, starting transfers between devices, swap(): return lax.ppermute(block, 'segment', [(0, 1), (1, 0)])  3.89 us
    ppermute x3, starting transfers between devices, on_device(): lax.ppermute(entries, 'sec', [(other(i, k), i) for i in range(sections)])  3.56 us
    unnamed x2, local copies, waits for them, and re-layouts  0.92 us
    ppermute x2, waiting for transfers between devices, swap(): return lax.ppermute(block, 'segment', [(0, 1), (1, 0)])  0.92 us
  transfers between devices with their start and end apart: 12, of which 4 were waited for; matrix products, arithmetic and copies ran while one was open for 0% of the time, Pallas kernels for 5%

profile of v16, /device:TPU:13, one launch (start us, length us, event | category | flops | bytes accessed | tf_op | source)
XLA Modules:
  0.0 35.2 jit_solution(7972853807401679149)
XLA Ops:
  0.0 2.1 %pack.1 = (f32[64,128]{1,0:T(8,128)}, f32[336,128]{1,0:T(8,128)}, f32[10,24,128]{2,1,0:T(8,128)}) custom-call(f32[1,9,2,16,128]{4,3,2,1,0:T(8,128)} %fields_in.1, s32[1,2,16,128]{3,2,1,0:T(8,128)} %ids_in.1, f32[6,1024]{1,0:T(8,128)} %moments_in.1, s32[8,128]{1,0:T(8,128)} %bitcast.4, s32[8,128]{1,0:T(8,128)} %bitcast.5, s32[16,128]{1,0:T(8,128)} %bitcast.3, ...), custom_call_target="tpu_custom_call" | custom-call | flops 10000000 | bytes 1048576 | tf_op jit(solution)/shard_map/pack/pallas_call | solution.py:456
  2.1 1.4 %collective-permute-start.1 = (f32[64,128]{1,0:T(8,128)}, f32[64,128]{1,0:T(8,128)S(1)}, u32[]{:S(2)}, u32[]{:S(2)}) collective-permute-start(f32[64,128]{1,0:T(8,128)} %get-tuple-element.33), channel_id=1, source_target_pairs={{24,0},{16,8},{8,16},{0,24},{25,1},{17,9},{9,17},{1,25},{26,2},{18... | collective-permute-start | bytes 98312 | tf_op jit(solution)/shard_map/ppermute | solution.py:506
  3.4 1.1 %collective-permute-start.3 = (f32[64,128]{1,0:T(8,128)}, f32[64,128]{1,0:T(8,128)S(1)}, u32[]{:S(2)}, u32[]{:S(2)}) collective-permute-start(f32[64,128]{1,0:T(8,128)} %get-tuple-element.33), channel_id=1, source_target_pairs={{16,0},{24,8},{0,16},{8,24},{17,1},{25,9},{1,17},{9,25},{18,2},{26... | collective-permute-start | bytes 98312 | tf_op jit(solution)/shard_map/ppermute | solution.py:506
  4.5 1.1 %collective-permute-start.2 = (f32[64,128]{1,0:T(8,128)}, f32[64,128]{1,0:T(8,128)S(1)}, u32[]{:S(2)}, u32[]{:S(2)}) collective-permute-start(f32[64,128]{1,0:T(8,128)} %get-tuple-element.33), channel_id=1, source_target_pairs={{8,0},{0,8},{24,16},{16,24},{9,1},{1,9},{25,17},{17,25},{10,2},{2,... | collective-permute-start | bytes 98312 | tf_op jit(solution)/shard_map/ppermute | solution.py:506
  5.6 1.2 %collective-permute-start = (f32[10,24,128]{2,1,0:T(8,128)}, f32[10,24,128]{2,1,0:T(8,128)S(1)}, u32[]{:S(2)}, u32[]{:S(2)}) collective-permute-start(f32[10,24,128]{2,1,0:T(8,128)} %get-tuple-element.31), channel_id=1, source_target_pairs={{0,1},{1,0},{2,3},{3,2},{4,5},{5,4},{6,7},{7,6},{8,9},{9,8},{10,11... | collective-permute-start | bytes 368648 | tf_op jit(solution)/shard_map/ppermute | solution.py:488
  6.9 0.9 %copy-done = f32[336,128]{1,0:T(8,128)S(1)} copy-done((f32[336,128]{1,0:T(8,128)S(1)}, f32[336,128]{1,0:T(8,128)}, u32[]{:S(2)}) %copy-start) | copy-done | bytes 172056
  7.8 0.4 %own_moments.1 = (f32[11,24,128]{2,1,0:T(8,128)S(1)}, f32[8,128]{1,0:T(8,128)S(1)}, f32[96,256]{1,0:T(8,128)S(1)}) custom-call(f32[336,128]{1,0:T(8,128)S(1)} %copy-done), custom_call_target="tpu_custom_call" | custom-call | flops 100000000 | bytes 1048576 | tf_op jit(solution)/shard_map/own_moments/pallas_call | solution.py:456
  8.2 0.4 %more_moments.2.started = f32[96,256]{1,0:T(8,128)S(1)} custom-call(f32[96,256]{1,0:T(8,128)S(1)} %get-tuple-element.32.started, f32[64,128]{1,0:T(8,128)S(1)} %collective-permute-done.1.entries), custom_call_target="tpu_custom_call" | custom-call | flops 6000000000 | bytes 1048576 | tf_op jit(solution)/shard_map/more_moments/pallas_call | solution.py:456
  8.6 0.4 %more_moments.3.refs_2_ = f32[96,256]{1,0:T(8,128)S(1)} custom-call(f32[96,256]{1,0:T(8,128)S(1)} %more_moments.2.started, f32[64,128]{1,0:T(8,128)S(1)} %collective-permute-done.2.entries), custom_call_target="tpu_custom_call" | custom-call | flops 6000000000 | bytes 1048576 | tf_op jit(solution)/shard_map/more_moments/pallas_call | solution.py:456
  9.0 0.5 %join_and_moments.1 = (f32[2,9,2,16,128]{4,3,2,1,0:T(8,128)S(1)}, f32[2,2,16,128]{3,2,1,0:T(8,128)S(1)}, f32[2,16,128]{2,1,0:T(8,128)S(1)}, f32[168,128]{1,0:T(8,128)S(1)}) custom-call(f32[11,24,128]{2,1,0:T(8,128)S(1)} %get-tuple-element.30.refs_0_, f32[10,24,128]{2,1,0:T(8,128)S(1)} %collective-permute-done.refs_1_, f32[96,256]{1,0:T(8,128)S(1)} %more_moments.3.refs_2_, ...), custom_call_target="tpu_custom_call" | custom-call | flops 10000000 | bytes 1048576 | tf_op jit(solution)/shard_map/join_and_moments/pallas_call | solution.py:456
  9.5 4.1 %collective-permute-start.4 = (f32[168,128]{1,0:T(8,128)S(1)}, f32[168,128]{1,0:T(8,128)S(1)}, u32[]{:S(2)}, u32[]{:S(2)}) collective-permute-start(f32[168,128]{1,0:T(8,128)S(1)} %get-tuple-element.37), channel_id=1, source_target_pairs={{1,2},{3,4},{5,6},{2,1},{4,3},{6,5},{9,10},{11,12},{13,14},{10,9},... | collective-permute-start | bytes 258056 | tf_op jit(solution)/shard_map/ppermute | solution.py:485
  13.8 1.5 %collective-permute-start.5 = (f32[216,128]{1,0:T(8,128)S(1)}, f32[216,128]{1,0:T(8,128)S(1)}, u32[]{:S(2)}, u32[]{:S(2)}) collective-permute-start(f32[216,128]{1,0:T(8,128)S(1)} %get-tuple-element.42), channel_id=1, source_target_pairs={{0,8},{16,24},{8,0},{24,16},{1,9},{17,25},{9,1},{25,17},{2,10},{18... | collective-permute-start | bytes 331784 | tf_op jit(solution)/shard_map/ppermute | solution.py:478
  15.4 2.9 %collective-permute-start.6 = (f32[324,128]{1,0:T(8,128)S(1)}, f32[324,128]{1,0:T(8,128)S(1)}, u32[]{:S(2)}, u32[]{:S(2)}) collective-permute-start(f32[324,128]{1,0:T(8,128)S(1)} %get-tuple-element.43), channel_id=1, source_target_pairs={{8,16},{16,8},{9,17},{17,9},{10,18},{18,10},{11,19},{19,11},{12,20... | collective-permute-start | bytes 497672 | tf_op jit(solution)/shard_map/ppermute | solution.py:478
  18.3 0.3 outer_edges.1
  18.7 2.4 %collective-permute-start.8 = (f32[108,128]{1,0:T(8,128)S(1)}, f32[108,128]{1,0:T(8,128)S(1)}, u32[]{:S(2)}, u32[]{:S(2)}) collective-permute-start(f32[108,128]{1,0:T(8,128)S(1)} %get-tuple-element.45), channel_id=1, source_target_pairs={{8,16},{16,8},{9,17},{17,9},{10,18},{18,10},{11,19},{19,11},{12,20... | collective-permute-start | bytes 165896 | tf_op jit(solution)/shard_map/ppermute | solution.py:478
  21.0 2.7 %collective-permute-done.8.refs_6_ = f32[108,128]{1,0:T(8,128)S(1)} collective-permute-done((f32[108,128]{1,0:T(8,128)S(1)}, f32[108,128]{1,0:T(8,128)S(1)}, u32[]{:S(2)}, u32[]{:S(2)}) %collective-permute-start.8) | collective-permute-done | bytes 55328 | tf_op jit(solution)/shard_map/ppermute | solution.py:478
  23.7 0.6 %steps.2 = (f32[264,128]{1,0:T(8,128)S(1)}, f32[264,128]{1,0:T(8,128)S(1)}, f32[2,9,2,16,128]{4,3,2,1,0:T(8,128)S(1)}, f32[2,3,6,16,128]{4,3,2,1,0:T(8,128)S(1)}, f32[6,16,128]{2,1,0:T(8,128)S(1)}) custom-call(f32[2,9,2,16,128]{4,3,2,1,0:T(8,128)S(1)} %get-tuple-element.39.refs_0_, f32[2,3,2,16,128]{4,3,2,1,0:T(8,128)S(1)} %get-tuple-element.40.refs_1_, ...), custom_call_target="tpu_custom_call" | custom-call | flops 10000000 | bytes 1048576 | tf_op jit(solution)/shard_map/steps/pallas_call | solution.py:456
  24.4 3.2 %collective-permute-start.10 = (f32[264,128]{1,0:T(8,128)S(1)}, f32[264,128]{1,0:T(8,128)S(1)}, u32[]{:S(2)}, u32[]{:S(2)}) collective-permute-start(f32[264,128]{1,0:T(8,128)S(1)} %get-tuple-element.50), channel_id=1, source_target_pairs={{8,16},{16,8},{9,17},{17,9},{10,18},{18,10},{11,19},{19,11},{12,20... | collective-permute-start | bytes 405512 | tf_op jit(solution)/shard_map/ppermute | solution.py:478
  27.6 0.6 %collective-permute-done.9.refs_3_ = f32[264,128]{1,0:T(8,128)S(1)} collective-permute-done((f32[264,128]{1,0:T(8,128)S(1)}, f32[264,128]{1,0:T(8,128)S(1)}, u32[]{:S(2)}, u32[]{:S(2)}) %collective-permute-start.9) | collective-permute-done | bytes 135200 | tf_op jit(solution)/shard_map/ppermute | solution.py:478
  28.3 2.2 %collective-permute-done.10.refs_4_ = f32[264,128]{1,0:T(8,128)S(1)} collective-permute-done((f32[264,128]{1,0:T(8,128)S(1)}, f32[264,128]{1,0:T(8,128)S(1)}, u32[]{:S(2)}, u32[]{:S(2)}) %collective-permute-start.10) | collective-permute-done | bytes 135200 | tf_op jit(solution)/shard_map/ppermute | solution.py:478
  30.5 0.4 %steps.3 = (f32[9,2,8,128]{3,2,1,0:T(8,128)S(1)}, f32[9,2,8,128]{3,2,1,0:T(8,128)S(1)}) custom-call(f32[2,9,2,16,128]{4,3,2,1,0:T(8,128)S(1)} %get-tuple-element.46.refs_0_, f32[2,3,6,16,128]{4,3,2,1,0:T(8,128)S(1)} %get-tuple-element.47.refs_1_, f32[6,16,128]{2,1,0:T(8,128)S(1)} %get-tuple-element.48.refs_2_, ...), custom_call_target="tpu_custom_call" | custom-call | flops 10000000 | bytes 1048576 | tf_op jit(solution)/shard_map/steps/pallas_call | solution.py:456
  30.9 2.7 %collective-permute-start.11 = (f32[9,2,8,128]{3,2,1,0:T(8,128)S(1)}, f32[9,2,8,128]{3,2,1,0:T(8,128)S(1)}, u32[]{:S(2)}, u32[]{:S(2)}) collective-permute-start(f32[9,2,8,128]{3,2,1,0:T(8,128)S(1)} %get-tuple-element.52), channel_id=1, source_target_pairs={{0,1},{1,0},{2,3},{3,2},{4,5},{5,4},{6,7},{7,6},{8,9},{9,8},{10,11... | collective-permute-start | bytes 221192 | tf_op jit(solution)/shard_map/ppermute | solution.py:488
  33.6 0.9 %collective-permute-done.11.brought = f32[9,2,8,128]{3,2,1,0:T(8,128)S(1)} collective-permute-done((f32[9,2,8,128]{3,2,1,0:T(8,128)S(1)}, f32[9,2,8,128]{3,2,1,0:T(8,128)S(1)}, u32[]{:S(2)}, u32[]{:S(2)}) %collective-permute-start.11) | collective-permute-done | bytes 73760 | tf_op jit(solution)/shard_map/ppermute | solution.py:488
  34.5 0.7 %home.1 = f32[1,9,2,16,128]{4,3,2,1,0:T(8,128)} custom-call(f32[9,2,8,128]{3,2,1,0:T(8,128)S(1)} %get-tuple-element.51.mine, f32[9,2,8,128]{3,2,1,0:T(8,128)S(1)} %collective-permute-done.11.brought), custom_call_target="tpu_custom_call" | custom-call | flops 10000000 | bytes 1048576 | tf_op jit(solution)/shard_map/home/pallas_call | solution.py:456
  (12 shorter events, 0.4 us)
Async XLA Ops:
  2.1 6.1 %collective-permute-start.1 = (f32[64,128]{1,0:T(8,128)}, f32[64,128]{1,0:T(8,128)S(1)}, u32[]{:S(2)}, u32[]{:S(2)}) collective-permute-start(f32[64,128]{1,0:T(8,128)} %get-tuple-element.33), channel_id=1, source_target_pairs={{24,0},{16,8},{8,16},{0,24},{25,1},{17,9},{9,17},{1,25},{26,2},{18... | collective-permute-start | bytes 98312 | tf_op jit(solution)/shard_map/ppermute | solution.py:506
  3.4 5.6 %collective-permute-start.3 = (f32[64,128]{1,0:T(8,128)}, f32[64,128]{1,0:T(8,128)S(1)}, u32[]{:S(2)}, u32[]{:S(2)}) collective-permute-start(f32[64,128]{1,0:T(8,128)} %get-tuple-element.33), channel_id=1, source_target_pairs={{16,0},{24,8},{0,16},{8,24},{17,1},{25,9},{1,17},{9,25},{18,2},{26... | collective-permute-start | bytes 98312 | tf_op jit(solution)/shard_map/ppermute | solution.py:506
  4.5 4.1 %collective-permute-start.2 = (f32[64,128]{1,0:T(8,128)}, f32[64,128]{1,0:T(8,128)S(1)}, u32[]{:S(2)}, u32[]{:S(2)}) collective-permute-start(f32[64,128]{1,0:T(8,128)} %get-tuple-element.33), channel_id=1, source_target_pairs={{8,0},{0,8},{24,16},{16,24},{9,1},{1,9},{25,17},{17,25},{10,2},{2,... | collective-permute-start | bytes 98312 | tf_op jit(solution)/shard_map/ppermute | solution.py:506
  5.6 3.4 %collective-permute-start = (f32[10,24,128]{2,1,0:T(8,128)}, f32[10,24,128]{2,1,0:T(8,128)S(1)}, u32[]{:S(2)}, u32[]{:S(2)}) collective-permute-start(f32[10,24,128]{2,1,0:T(8,128)} %get-tuple-element.31), channel_id=1, source_target_pairs={{0,1},{1,0},{2,3},{3,2},{4,5},{5,4},{6,7},{7,6},{8,9},{9,8},{10,11... | collective-permute-start | bytes 368648 | tf_op jit(solution)/shard_map/ppermute | solution.py:488
  6.9 0.9 %copy-start = (f32[336,128]{1,0:T(8,128)S(1)}, f32[336,128]{1,0:T(8,128)}, u32[]{:S(2)}) copy-start(f32[336,128]{1,0:T(8,128)} %get-tuple-element.29.kept) | copy-start | bytes 516100
  9.5 8.8 %collective-permute-start.4 = (f32[168,128]{1,0:T(8,128)S(1)}, f32[168,128]{1,0:T(8,128)S(1)}, u32[]{:S(2)}, u32[]{:S(2)}) collective-permute-start(f32[168,128]{1,0:T(8,128)S(1)} %get-tuple-element.37), channel_id=1, source_target_pairs={{1,2},{3,4},{5,6},{2,1},{4,3},{6,5},{9,10},{11,12},{13,14},{10,9},... | collective-permute-start | bytes 258056 | tf_op jit(solution)/shard_map/ppermute | solution.py:485
  13.8 7.2 %collective-permute-start.5 = (f32[216,128]{1,0:T(8,128)S(1)}, f32[216,128]{1,0:T(8,128)S(1)}, u32[]{:S(2)}, u32[]{:S(2)}) collective-permute-start(f32[216,128]{1,0:T(8,128)S(1)} %get-tuple-element.42), channel_id=1, source_target_pairs={{0,8},{16,24},{8,0},{24,16},{1,9},{17,25},{9,1},{25,17},{2,10},{18... | collective-permute-start | bytes 331784 | tf_op jit(solution)/shard_map/ppermute | solution.py:478
  15.4 8.4 %collective-permute-start.6 = (f32[324,128]{1,0:T(8,128)S(1)}, f32[324,128]{1,0:T(8,128)S(1)}, u32[]{:S(2)}, u32[]{:S(2)}) collective-permute-start(f32[324,128]{1,0:T(8,128)S(1)} %get-tuple-element.43), channel_id=1, source_target_pairs={{8,16},{16,8},{9,17},{17,9},{10,18},{18,10},{11,19},{19,11},{12,20... | collective-permute-start | bytes 497672 | tf_op jit(solution)/shard_map/ppermute | solution.py:478
  18.6 5.2 %collective-permute-start.7 = (f32[216,128]{1,0:T(8,128)S(1)}, f32[216,128]{1,0:T(8,128)S(1)}, u32[]{:S(2)}, u32[]{:S(2)}) collective-permute-start(f32[216,128]{1,0:T(8,128)S(1)} %get-tuple-element.44), channel_id=1, source_target_pairs={{0,8},{16,24},{8,0},{24,16},{1,9},{17,25},{9,1},{25,17},{2,10},{18... | collective-permute-start | bytes 331784 | tf_op jit(solution)/shard_map/ppermute | solution.py:478
  18.7 5.1 %collective-permute-start.8 = (f32[108,128]{1,0:T(8,128)S(1)}, f32[108,128]{1,0:T(8,128)S(1)}, u32[]{:S(2)}, u32[]{:S(2)}) collective-permute-start(f32[108,128]{1,0:T(8,128)S(1)} %get-tuple-element.45), channel_id=1, source_target_pairs={{8,16},{16,8},{9,17},{17,9},{10,18},{18,10},{11,19},{19,11},{12,20... | collective-permute-start | bytes 165896 | tf_op jit(solution)/shard_map/ppermute | solution.py:478
  24.3 3.9 %collective-permute-start.9 = (f32[264,128]{1,0:T(8,128)S(1)}, f32[264,128]{1,0:T(8,128)S(1)}, u32[]{:S(2)}, u32[]{:S(2)}) collective-permute-start(f32[264,128]{1,0:T(8,128)S(1)} %get-tuple-element.49), channel_id=1, source_target_pairs={{0,8},{16,24},{8,0},{24,16},{1,9},{17,25},{9,1},{25,17},{2,10},{18... | collective-permute-start | bytes 405512 | tf_op jit(solution)/shard_map/ppermute | solution.py:478
  24.4 6.1 %collective-permute-start.10 = (f32[264,128]{1,0:T(8,128)S(1)}, f32[264,128]{1,0:T(8,128)S(1)}, u32[]{:S(2)}, u32[]{:S(2)}) collective-permute-start(f32[264,128]{1,0:T(8,128)S(1)} %get-tuple-element.50), channel_id=1, source_target_pairs={{8,16},{16,8},{9,17},{17,9},{10,18},{18,10},{11,19},{19,11},{12,20... | collective-permute-start | bytes 405512 | tf_op jit(solution)/shard_map/ppermute | solution.py:478
  30.9 3.6 %collective-permute-start.11 = (f32[9,2,8,128]{3,2,1,0:T(8,128)S(1)}, f32[9,2,8,128]{3,2,1,0:T(8,128)S(1)}, u32[]{:S(2)}, u32[]{:S(2)}) collective-permute-start(f32[9,2,8,128]{3,2,1,0:T(8,128)S(1)} %get-tuple-element.52), channel_id=1, source_target_pairs={{0,1},{1,0},{2,3},{3,2},{4,5},{5,4},{6,7},{7,6},{8,9},{9,8},{10,11... | collective-permute-start | bytes 221192 | tf_op jit(solution)/shard_map/ppermute | solution.py:488

commit v17 on v11

--- a/solution.py
+++ b/solution.py
@@ -327,10 +327,14 @@
     reach = state.shape[3] - STEPS
     state[:, :, own], ids[:, own], times[own] = own_state[...], own_ids[...], own_times[...]
 
+    slab = lax.axis_index("depth")
+
     def join(mine, main, outer):
+        inside = slab > 0 if mine == 0 else slab < lax.axis_size("depth") - 1
+        inside = jnp.where(inside, F32(1.0), F32(0.0))
         for x in range(cx):
             for k in range(21):
-                line = halo[(k * cx + x) * STEPS : (k * cx + x + 1) * STEPS]
+                line = inside * halo[(k * cx + x) * STEPS : (k * cx + x + 1) * STEPS]
                 if k == 20:
                     times[cx + x, outer(reach)] = line
                 elif k % 10 == 9:
@@ -369,12 +373,17 @@
     state[:, :, own] = both_in[...]
     right_units, left_units = edge_units(cx, first)
 
+    section = lax.axis_index("sec")
+    has_left = jnp.where(section > 0, F32(1.0), F32(0.0))
+    has_right = jnp.where(section < lax.axis_size("sec") - 1, F32(1.0), F32(0.0))
+
     def get(edge, units, start, rows_of, far, right):
+        inside = has_left if right else has_right
         last = 0
         for model, what, x in units:
             at = rows_of(x == far, right)
             first, last = last, last + at.stop - at.start
-            line = edge[first:last]
+            line = inside * edge[first:last]
             if what == 10:
                 times[start + x, at] = line
             elif what == 9:
@@ -430,6 +439,13 @@
         out[0, :, :, 0:half] = brought[...]
 
 
+def swaps(start, count):
+    route = {i: i for i in range(count)}
+    for i in range(start, count - 1, 2):
+        route[i], route[i + 1] = i + 1, i
+    return list(route.items())
+
+
 VMEM = pl.BlockSpec(memory_space=pltpu.VMEM)
 HBM = pl.BlockSpec(memory_space=pltpu.HBM)
 
@@ -457,15 +473,13 @@
     assert cx > 1 and STEPS % cx == 0
 
     def pairs(block, start):
-        route = [(i, i + 1) for i in range(start, sections - 1, 2)]
-        return lax.ppermute(block, "sec", route + [(j, i) for i, j in route])
+        return lax.ppermute(block, "sec", swaps(start, sections))
 
     def other(section, k):
         return section ^ k if sections & (sections - 1) == 0 else (section + k) % sections
 
     def along_depth(block):
-        down = [(2 * i + 1, 2 * (i + 1)) for i in range(slabs - 1)]
-        return lax.ppermute(block, ("depth", "segment"), down + [(j, i) for i, j in down])
+        return lax.ppermute(block, ("depth", "segment"), swaps(1, 2 * slabs))
 
     def swap(block):
         return lax.ppermute(block, "segment", [(0, 1), (1, 0)])

time: 35.4 us -> 35.4 us (level)
  no operation moved by 1% of the time
where the time goes in v17:
time: 35.4 us; the launch traced here: 35.2 us
  starting transfers between devices  21.8 us (62%)
  waiting for transfers between devices  6.38 us (18%)
  Pallas kernels  5.92 us (17%)
  local copies, waits for them, and re-layouts  0.92 us (3%)
    ppermute x6, starting transfers between devices, pairs(): return lax.ppermute(block, 'sec', swaps(start, sections))  10.2 us
    pallas_call x10, Pallas kernels, call(): pl.pallas_call(kernel, out_shape=[jax.ShapeDtypeStruct(shape, F32) for sh...  5.92 us
    ppermute x6, waiting for transfers between devices, pairs(): return lax.ppermute(block, 'sec', swaps(start, sections))  5.45 us
    ppermute x1, starting transfers between devices, along_depth(): return lax.ppermute(block, ('depth', 'segment'), swaps(1, 2 * slabs))  4.14 us
    ppermute x2, starting transfers between devices, swap(): return lax.ppermute(block, 'segment', [(0, 1), (1, 0)])  3.94 us
    ppermute x3, starting transfers between devices, on_device(): lax.ppermute(entries, 'sec', [(other(i, k), i) for i in range(sections)])  3.56 us
    unnamed x2, local copies, waits for them, and re-layouts  0.92 us
    ppermute x2, waiting for transfers between devices, swap(): return lax.ppermute(block, 'segment', [(0, 1), (1, 0)])  0.92 us
  transfers between devices with their start and end apart: 12, of which 5 were waited for; matrix products, arithmetic and copies ran while one was open for 0% of the time, Pallas kernels for 5%

profile of v17, /device:TPU:13, one launch (start us, length us, event | category | flops | bytes accessed | tf_op | source)
XLA Modules:
  0.0 35.2 jit_solution(9146709537639355748)
XLA Ops:
  0.0 2.1 %pack.1 = (f32[64,128]{1,0:T(8,128)}, f32[336,128]{1,0:T(8,128)}, f32[10,24,128]{2,1,0:T(8,128)}) custom-call(f32[1,9,2,16,128]{4,3,2,1,0:T(8,128)} %fields_in.1, s32[1,2,16,128]{3,2,1,0:T(8,128)} %ids_in.1, f32[6,1024]{1,0:T(8,128)} %moments_in.1, s32[8,128]{1,0:T(8,128)} %bitcast.4, s32[8,128]{1,0:T(8,128)} %bitcast.5, s32[16,128]{1,0:T(8,128)} %bitcast.3, ...), custom_call_target="tpu_custom_call" | custom-call | flops 10000000 | bytes 1048576 | tf_op jit(solution)/shard_map/pack/pallas_call | solution.py:455
  2.1 1.4 %collective-permute-start.1 = (f32[64,128]{1,0:T(8,128)}, f32[64,128]{1,0:T(8,128)S(1)}, u32[]{:S(2)}, u32[]{:S(2)}) collective-permute-start(f32[64,128]{1,0:T(8,128)} %get-tuple-element.33), channel_id=1, source_target_pairs={{24,0},{16,8},{8,16},{0,24},{25,1},{17,9},{9,17},{1,25},{26,2},{18... | collective-permute-start | bytes 98312 | tf_op jit(solution)/shard_map/ppermute | solution.py:503
  3.4 1.1 %collective-permute-start.3 = (f32[64,128]{1,0:T(8,128)}, f32[64,128]{1,0:T(8,128)S(1)}, u32[]{:S(2)}, u32[]{:S(2)}) collective-permute-start(f32[64,128]{1,0:T(8,128)} %get-tuple-element.33), channel_id=1, source_target_pairs={{16,0},{24,8},{0,16},{8,24},{17,1},{25,9},{1,17},{9,25},{18,2},{26... | collective-permute-start | bytes 98312 | tf_op jit(solution)/shard_map/ppermute | solution.py:503
  4.5 1.1 %collective-permute-start.2 = (f32[64,128]{1,0:T(8,128)}, f32[64,128]{1,0:T(8,128)S(1)}, u32[]{:S(2)}, u32[]{:S(2)}) collective-permute-start(f32[64,128]{1,0:T(8,128)} %get-tuple-element.33), channel_id=1, source_target_pairs={{8,0},{0,8},{24,16},{16,24},{9,1},{1,9},{25,17},{17,25},{10,2},{2,... | collective-permute-start | bytes 98312 | tf_op jit(solution)/shard_map/ppermute | solution.py:503
  5.6 1.2 %collective-permute-start = (f32[10,24,128]{2,1,0:T(8,128)}, f32[10,24,128]{2,1,0:T(8,128)S(1)}, u32[]{:S(2)}, u32[]{:S(2)}) collective-permute-start(f32[10,24,128]{2,1,0:T(8,128)} %get-tuple-element.31), channel_id=1, source_target_pairs={{0,1},{1,0},{2,3},{3,2},{4,5},{5,4},{6,7},{7,6},{8,9},{9,8},{10,11... | collective-permute-start | bytes 368648 | tf_op jit(solution)/shard_map/ppermute | solution.py:485
  6.9 0.9 %copy-done = f32[336,128]{1,0:T(8,128)S(1)} copy-done((f32[336,128]{1,0:T(8,128)S(1)}, f32[336,128]{1,0:T(8,128)}, u32[]{:S(2)}) %copy-start) | copy-done | bytes 172056
  7.8 0.4 %own_moments.1 = (f32[11,24,128]{2,1,0:T(8,128)S(1)}, f32[8,128]{1,0:T(8,128)S(1)}, f32[96,256]{1,0:T(8,128)S(1)}) custom-call(f32[336,128]{1,0:T(8,128)S(1)} %copy-done), custom_call_target="tpu_custom_call" | custom-call | flops 100000000 | bytes 1048576 | tf_op jit(solution)/shard_map/own_moments/pallas_call | solution.py:455
  8.2 0.4 %more_moments.2.started = f32[96,256]{1,0:T(8,128)S(1)} custom-call(f32[96,256]{1,0:T(8,128)S(1)} %get-tuple-element.32.started, f32[64,128]{1,0:T(8,128)S(1)} %collective-permute-done.1.entries), custom_call_target="tpu_custom_call" | custom-call | flops 6000000000 | bytes 1048576 | tf_op jit(solution)/shard_map/more_moments/pallas_call | solution.py:455
  8.6 0.4 %more_moments.3.refs_2_ = f32[96,256]{1,0:T(8,128)S(1)} custom-call(f32[96,256]{1,0:T(8,128)S(1)} %more_moments.2.started, f32[64,128]{1,0:T(8,128)S(1)} %collective-permute-done.2.entries), custom_call_target="tpu_custom_call" | custom-call | flops 6000000000 | bytes 1048576 | tf_op jit(solution)/shard_map/more_moments/pallas_call | solution.py:455
  9.0 0.5 %join_and_moments.1 = (f32[2,9,2,16,128]{4,3,2,1,0:T(8,128)S(1)}, f32[2,2,16,128]{3,2,1,0:T(8,128)S(1)}, f32[2,16,128]{2,1,0:T(8,128)S(1)}, f32[168,128]{1,0:T(8,128)S(1)}) custom-call(f32[11,24,128]{2,1,0:T(8,128)S(1)} %get-tuple-element.30.refs_0_, f32[10,24,128]{2,1,0:T(8,128)S(1)} %collective-permute-done.refs_1_, f32[96,256]{1,0:T(8,128)S(1)} %more_moments.3.refs_2_, ...), custom_call_target="tpu_custom_call" | custom-call | flops 10000000 | bytes 1048576 | tf_op jit(solution)/shard_map/join_and_moments/pallas_call | solution.py:455
  9.5 4.1 %collective-permute-start.4 = (f32[168,128]{1,0:T(8,128)S(1)}, f32[168,128]{1,0:T(8,128)S(1)}, u32[]{:S(2)}, u32[]{:S(2)}) collective-permute-start(f32[168,128]{1,0:T(8,128)S(1)} %get-tuple-element.37), channel_id=1, source_target_pairs={{0,0},{1,2},{2,1},{3,4},{4,3},{5,6},{6,5},{7,7},{8,8},{9,10},{10,9... | collective-permute-start | bytes 258056 | tf_op jit(solution)/shard_map/ppermute | solution.py:482
  13.9 1.5 %collective-permute-start.5 = (f32[324,128]{1,0:T(8,128)S(1)}, f32[324,128]{1,0:T(8,128)S(1)}, u32[]{:S(2)}, u32[]{:S(2)}) collective-permute-start(f32[324,128]{1,0:T(8,128)S(1)} %get-tuple-element.42), channel_id=1, source_target_pairs={{0,8},{8,0},{16,24},{24,16},{1,9},{9,1},{17,25},{25,17},{2,10},{10... | collective-permute-start | bytes 497672 | tf_op jit(solution)/shard_map/ppermute | solution.py:476
  15.4 2.9 %collective-permute-start.6 = (f32[324,128]{1,0:T(8,128)S(1)}, f32[324,128]{1,0:T(8,128)S(1)}, u32[]{:S(2)}, u32[]{:S(2)}) collective-permute-start(f32[324,128]{1,0:T(8,128)S(1)} %get-tuple-element.43), channel_id=1, source_target_pairs={{0,0},{8,16},{16,8},{24,24},{1,1},{9,17},{17,9},{25,25},{2,2},{10,... | collective-permute-start | bytes 497672 | tf_op jit(solution)/shard_map/ppermute | solution.py:476
  18.6 2.4 %collective-permute-start.8 = (f32[108,128]{1,0:T(8,128)S(1)}, f32[108,128]{1,0:T(8,128)S(1)}, u32[]{:S(2)}, u32[]{:S(2)}) collective-permute-start(f32[108,128]{1,0:T(8,128)S(1)} %get-tuple-element.45), channel_id=1, source_target_pairs={{0,0},{8,16},{16,8},{24,24},{1,1},{9,17},{17,9},{25,25},{2,2},{10,... | collective-permute-start | bytes 165896 | tf_op jit(solution)/shard_map/ppermute | solution.py:476
  21.0 0.9 %collective-permute-done.7.refs_5_ = f32[108,128]{1,0:T(8,128)S(1)} collective-permute-done((f32[108,128]{1,0:T(8,128)S(1)}, f32[108,128]{1,0:T(8,128)S(1)}, u32[]{:S(2)}, u32[]{:S(2)}) %collective-permute-start.7) | collective-permute-done | bytes 55328 | tf_op jit(solution)/shard_map/ppermute | solution.py:476
  22.0 1.7 %collective-permute-done.8.refs_6_ = f32[108,128]{1,0:T(8,128)S(1)} collective-permute-done((f32[108,128]{1,0:T(8,128)S(1)}, f32[108,128]{1,0:T(8,128)S(1)}, u32[]{:S(2)}, u32[]{:S(2)}) %collective-permute-start.8) | collective-permute-done | bytes 55328 | tf_op jit(solution)/shard_map/ppermute | solution.py:476
  23.7 0.6 %steps.2 = (f32[264,128]{1,0:T(8,128)S(1)}, f32[264,128]{1,0:T(8,128)S(1)}, f32[2,9,2,16,128]{4,3,2,1,0:T(8,128)S(1)}, f32[2,3,6,16,128]{4,3,2,1,0:T(8,128)S(1)}, f32[6,16,128]{2,1,0:T(8,128)S(1)}) custom-call(f32[2,9,2,16,128]{4,3,2,1,0:T(8,128)S(1)} %get-tuple-element.39.refs_0_, f32[2,3,2,16,128]{4,3,2,1,0:T(8,128)S(1)} %get-tuple-element.40.refs_1_, ...), custom_call_target="tpu_custom_call" | custom-call | flops 10000000 | bytes 1048576 | tf_op jit(solution)/shard_map/steps/pallas_call | solution.py:455
  24.4 3.2 %collective-permute-start.10 = (f32[264,128]{1,0:T(8,128)S(1)}, f32[264,128]{1,0:T(8,128)S(1)}, u32[]{:S(2)}, u32[]{:S(2)}) collective-permute-start(f32[264,128]{1,0:T(8,128)S(1)} %get-tuple-element.50), channel_id=1, source_target_pairs={{0,0},{8,16},{16,8},{24,24},{1,1},{9,17},{17,9},{25,25},{2,2},{10,... | collective-permute-start | bytes 405512 | tf_op jit(solution)/shard_map/ppermute | solution.py:476
  27.6 0.6 %collective-permute-done.9.refs_3_ = f32[264,128]{1,0:T(8,128)S(1)} collective-permute-done((f32[264,128]{1,0:T(8,128)S(1)}, f32[264,128]{1,0:T(8,128)S(1)}, u32[]{:S(2)}, u32[]{:S(2)}) %collective-permute-start.9) | collective-permute-done | bytes 135200 | tf_op jit(solution)/shard_map/ppermute | solution.py:476
  28.2 2.2 %collective-permute-done.10.refs_4_ = f32[264,128]{1,0:T(8,128)S(1)} collective-permute-done((f32[264,128]{1,0:T(8,128)S(1)}, f32[264,128]{1,0:T(8,128)S(1)}, u32[]{:S(2)}, u32[]{:S(2)}) %collective-permute-start.10) | collective-permute-done | bytes 135200 | tf_op jit(solution)/shard_map/ppermute | solution.py:476
  30.4 0.4 %steps.3 = (f32[9,2,8,128]{3,2,1,0:T(8,128)S(1)}, f32[9,2,8,128]{3,2,1,0:T(8,128)S(1)}) custom-call(f32[2,9,2,16,128]{4,3,2,1,0:T(8,128)S(1)} %get-tuple-element.46.refs_0_, f32[2,3,6,16,128]{4,3,2,1,0:T(8,128)S(1)} %get-tuple-element.47.refs_1_, f32[6,16,128]{2,1,0:T(8,128)S(1)} %get-tuple-element.48.refs_2_, ...), custom_call_target="tpu_custom_call" | custom-call | flops 10000000 | bytes 1048576 | tf_op jit(solution)/shard_map/steps/pallas_call | solution.py:455
  30.9 2.7 %collective-permute-start.11 = (f32[9,2,8,128]{3,2,1,0:T(8,128)S(1)}, f32[9,2,8,128]{3,2,1,0:T(8,128)S(1)}, u32[]{:S(2)}, u32[]{:S(2)}) collective-permute-start(f32[9,2,8,128]{3,2,1,0:T(8,128)S(1)} %get-tuple-element.52), channel_id=1, source_target_pairs={{0,1},{1,0},{2,3},{3,2},{4,5},{5,4},{6,7},{7,6},{8,9},{9,8},{10,11... | collective-permute-start | bytes 221192 | tf_op jit(solution)/shard_map/ppermute | solution.py:485
  33.6 0.9 %collective-permute-done.11.brought = f32[9,2,8,128]{3,2,1,0:T(8,128)S(1)} collective-permute-done((f32[9,2,8,128]{3,2,1,0:T(8,128)S(1)}, f32[9,2,8,128]{3,2,1,0:T(8,128)S(1)}, u32[]{:S(2)}, u32[]{:S(2)}) %collective-permute-start.11) | collective-permute-done | bytes 73760 | tf_op jit(solution)/shard_map/ppermute | solution.py:485
  34.5 0.7 %home.1 = f32[1,9,2,16,128]{4,3,2,1,0:T(8,128)} custom-call(f32[9,2,8,128]{3,2,1,0:T(8,128)S(1)} %get-tuple-element.51.mine, f32[9,2,8,128]{3,2,1,0:T(8,128)S(1)} %collective-permute-done.11.brought), custom_call_target="tpu_custom_call" | custom-call | flops 10000000 | bytes 1048576 | tf_op jit(solution)/shard_map/home/pallas_call | solution.py:455
  (12 shorter events, 0.7 us)
Async XLA Ops:
  2.1 6.1 %collective-permute-start.1 = (f32[64,128]{1,0:T(8,128)}, f32[64,128]{1,0:T(8,128)S(1)}, u32[]{:S(2)}, u32[]{:S(2)}) collective-permute-start(f32[64,128]{1,0:T(8,128)} %get-tuple-element.33), channel_id=1, source_target_pairs={{24,0},{16,8},{8,16},{0,24},{25,1},{17,9},{9,17},{1,25},{26,2},{18... | collective-permute-start | bytes 98312 | tf_op jit(solution)/shard_map/ppermute | solution.py:503
  3.4 5.6 %collective-permute-start.3 = (f32[64,128]{1,0:T(8,128)}, f32[64,128]{1,0:T(8,128)S(1)}, u32[]{:S(2)}, u32[]{:S(2)}) collective-permute-start(f32[64,128]{1,0:T(8,128)} %get-tuple-element.33), channel_id=1, source_target_pairs={{16,0},{24,8},{0,16},{8,24},{17,1},{25,9},{1,17},{9,25},{18,2},{26... | collective-permute-start | bytes 98312 | tf_op jit(solution)/shard_map/ppermute | solution.py:503
  4.5 4.1 %collective-permute-start.2 = (f32[64,128]{1,0:T(8,128)}, f32[64,128]{1,0:T(8,128)S(1)}, u32[]{:S(2)}, u32[]{:S(2)}) collective-permute-start(f32[64,128]{1,0:T(8,128)} %get-tuple-element.33), channel_id=1, source_target_pairs={{8,0},{0,8},{24,16},{16,24},{9,1},{1,9},{25,17},{17,25},{10,2},{2,... | collective-permute-start | bytes 98312 | tf_op jit(solution)/shard_map/ppermute | solution.py:503
  5.6 3.4 %collective-permute-start = (f32[10,24,128]{2,1,0:T(8,128)}, f32[10,24,128]{2,1,0:T(8,128)S(1)}, u32[]{:S(2)}, u32[]{:S(2)}) collective-permute-start(f32[10,24,128]{2,1,0:T(8,128)} %get-tuple-element.31), channel_id=1, source_target_pairs={{0,1},{1,0},{2,3},{3,2},{4,5},{5,4},{6,7},{7,6},{8,9},{9,8},{10,11... | collective-permute-start | bytes 368648 | tf_op jit(solution)/shard_map/ppermute | solution.py:485
  6.9 0.9 %copy-start = (f32[336,128]{1,0:T(8,128)S(1)}, f32[336,128]{1,0:T(8,128)}, u32[]{:S(2)}) copy-start(f32[336,128]{1,0:T(8,128)} %get-tuple-element.29.kept) | copy-start | bytes 516100
  9.5 8.8 %collective-permute-start.4 = (f32[168,128]{1,0:T(8,128)S(1)}, f32[168,128]{1,0:T(8,128)S(1)}, u32[]{:S(2)}, u32[]{:S(2)}) collective-permute-start(f32[168,128]{1,0:T(8,128)S(1)} %get-tuple-element.37), channel_id=1, source_target_pairs={{0,0},{1,2},{2,1},{3,4},{4,3},{5,6},{6,5},{7,7},{8,8},{9,10},{10,9... | collective-permute-start | bytes 258056 | tf_op jit(solution)/shard_map/ppermute | solution.py:482
  13.9 9.8 %collective-permute-start.5 = (f32[324,128]{1,0:T(8,128)S(1)}, f32[324,128]{1,0:T(8,128)S(1)}, u32[]{:S(2)}, u32[]{:S(2)}) collective-permute-start(f32[324,128]{1,0:T(8,128)S(1)} %get-tuple-element.42), channel_id=1, source_target_pairs={{0,8},{8,0},{16,24},{24,16},{1,9},{9,1},{17,25},{25,17},{2,10},{10... | collective-permute-start | bytes 497672 | tf_op jit(solution)/shard_map/ppermute | solution.py:476
  15.4 8.3 %collective-permute-start.6 = (f32[324,128]{1,0:T(8,128)S(1)}, f32[324,128]{1,0:T(8,128)S(1)}, u32[]{:S(2)}, u32[]{:S(2)}) collective-permute-start(f32[324,128]{1,0:T(8,128)S(1)} %get-tuple-element.43), channel_id=1, source_target_pairs={{0,0},{8,16},{16,8},{24,24},{1,1},{9,17},{17,9},{25,25},{2,2},{10,... | collective-permute-start | bytes 497672 | tf_op jit(solution)/shard_map/ppermute | solution.py:476
  18.6 3.4 %collective-permute-start.7 = (f32[108,128]{1,0:T(8,128)S(1)}, f32[108,128]{1,0:T(8,128)S(1)}, u32[]{:S(2)}, u32[]{:S(2)}) collective-permute-start(f32[108,128]{1,0:T(8,128)S(1)} %get-tuple-element.44), channel_id=1, source_target_pairs={{0,8},{8,0},{16,24},{24,16},{1,9},{9,1},{17,25},{25,17},{2,10},{10... | collective-permute-start | bytes 165896 | tf_op jit(solution)/shard_map/ppermute | solution.py:476
  18.6 5.0 %collective-permute-start.8 = (f32[108,128]{1,0:T(8,128)S(1)}, f32[108,128]{1,0:T(8,128)S(1)}, u32[]{:S(2)}, u32[]{:S(2)}) collective-permute-start(f32[108,128]{1,0:T(8,128)S(1)} %get-tuple-element.45), channel_id=1, source_target_pairs={{0,0},{8,16},{16,8},{24,24},{1,1},{9,17},{17,9},{25,25},{2,2},{10,... | collective-permute-start | bytes 165896 | tf_op jit(solution)/shard_map/ppermute | solution.py:476
  24.3 3.9 %collective-permute-start.9 = (f32[264,128]{1,0:T(8,128)S(1)}, f32[264,128]{1,0:T(8,128)S(1)}, u32[]{:S(2)}, u32[]{:S(2)}) collective-permute-start(f32[264,128]{1,0:T(8,128)S(1)} %get-tuple-element.49), channel_id=1, source_target_pairs={{0,8},{8,0},{16,24},{24,16},{1,9},{9,1},{17,25},{25,17},{2,10},{10... | collective-permute-start | bytes 405512 | tf_op jit(solution)/shard_map/ppermute | solution.py:476
  24.4 6.1 %collective-permute-start.10 = (f32[264,128]{1,0:T(8,128)S(1)}, f32[264,128]{1,0:T(8,128)S(1)}, u32[]{:S(2)}, u32[]{:S(2)}) collective-permute-start(f32[264,128]{1,0:T(8,128)S(1)} %get-tuple-element.50), channel_id=1, source_target_pairs={{0,0},{8,16},{16,8},{24,24},{1,1},{9,17},{17,9},{25,25},{2,2},{10,... | collective-permute-start | bytes 405512 | tf_op jit(solution)/shard_map/ppermute | solution.py:476
  30.9 3.6 %collective-permute-start.11 = (f32[9,2,8,128]{3,2,1,0:T(8,128)S(1)}, f32[9,2,8,128]{3,2,1,0:T(8,128)S(1)}, u32[]{:S(2)}, u32[]{:S(2)}) collective-permute-start(f32[9,2,8,128]{3,2,1,0:T(8,128)S(1)} %get-tuple-element.52), channel_id=1, source_target_pairs={{0,1},{1,0},{2,3},{3,2},{4,5},{5,4},{6,7},{7,6},{8,9},{9,8},{10,11... | collective-permute-start | bytes 221192 | tf_op jit(solution)/shard_map/ppermute | solution.py:485

commit v18 on v17

--- a/solution.py
+++ b/solution.py
@@ -473,13 +473,18 @@
     assert cx > 1 and STEPS % cx == 0
 
     def pairs(block, start):
-        return lax.ppermute(block, "sec", swaps(start, sections))
+        route = []
+        for i, j in swaps(start, sections):
+            route += [(2 * i + k, 2 * j + (k if i != j else 1 - k)) for k in range(2)]
+        return lax.ppermute(block, ("sec", "segment"), route)
 
     def other(section, k):
         return section ^ k if sections & (sections - 1) == 0 else (section + k) % sections
 
     def along_depth(block):
-        return lax.ppermute(block, ("depth", "segment"), swaps(1, 2 * slabs))
+        ends = [(0, 2 * slabs - 1), (2 * slabs - 1, 0)]
+        route = [(i, j) for i, j in swaps(1, 2 * slabs) if i != j] + ends
+        return lax.ppermute(block, ("depth", "segment"), route)
 
     def swap(block):
         return lax.ppermute(block, "segment", [(0, 1), (1, 0)])

time: 35.4 us -> 31.2 us (0.88)
  the two profiles are of different devices: /device:TPU:13 before, /device:TPU:0 now
where the time goes in v18:
time: 31.2 us; the launch traced here: 31.1 us
  waiting for transfers between devices  14.2 us (46%)
  starting transfers between devices  9.97 us (32%)
  Pallas kernels  5.89 us (19%)
  local copies, waits for them, and re-layouts  0.92 us (3%)
    ppermute x6, waiting for transfers between devices, pairs(): return lax.ppermute(block, ('sec', 'segment'), route)  7.04 us
    pallas_call x10, Pallas kernels, call(): pl.pallas_call(kernel, out_shape=[jax.ShapeDtypeStruct(shape, F32) for sh...  5.89 us
    ppermute x3, starting transfers between devices, on_device(): lax.ppermute(entries, 'sec', [(other(i, k), i) for i in range(sections)])  5.76 us
    ppermute x1, waiting for transfers between devices, along_depth(): return lax.ppermute(block, ('depth', 'segment'), route)  3.61 us
    ppermute x6, starting transfers between devices, pairs(): return lax.ppermute(block, ('sec', 'segment'), route)  3.6 us
    ppermute x3, waiting for transfers between devices, on_device(): lax.ppermute(entries, 'sec', [(other(i, k), i) for i in range(sections)])  2.26 us
    ppermute x2, waiting for transfers between devices, swap(): return lax.ppermute(block, 'segment', [(0, 1), (1, 0)])  1.26 us
    unnamed x2, local copies, waits for them, and re-layouts  0.92 us
  transfers between devices with their start and end apart: 12, of which 7 were waited for; matrix products, arithmetic and copies ran while one was open for 0% of the time, Pallas kernels for 5%

profile of v18, /device:TPU:0, one launch (start us, length us, event | category | flops | bytes accessed | tf_op | source)
XLA Modules:
  0.0 31.1 jit_solution(568551106097559919)
XLA Ops:
  0.0 2.1 %pack.1 = (f32[64,128]{1,0:T(8,128)}, f32[336,128]{1,0:T(8,128)}, f32[10,24,128]{2,1,0:T(8,128)}) custom-call(f32[1,9,2,16,128]{4,3,2,1,0:T(8,128)} %fields_in.1, s32[1,2,16,128]{3,2,1,0:T(8,128)} %ids_in.1, f32[6,1024]{1,0:T(8,128)} %moments_in.1, s32[8,128]{1,0:T(8,128)} %bitcast.4, s32[8,128]{1,0:T(8,128)} %bitcast.5, s32[16,128]{1,0:T(8,128)} %bitcast.3, ...), custom_call_target="tpu_custom_call" | custom-call | flops 10000000 | bytes 1048576 | tf_op jit(solution)/shard_map/pack/pallas_call | solution.py:455
  2.1 5.1 %collective-permute-start.1 = (f32[64,128]{1,0:T(8,128)}, f32[64,128]{1,0:T(8,128)S(1)}, u32[]{:S(2)}, u32[]{:S(2)}) collective-permute-start(f32[64,128]{1,0:T(8,128)} %get-tuple-element.33), channel_id=1, source_target_pairs={{24,0},{16,8},{8,16},{0,24},{25,1},{17,9},{9,17},{1,25},{26,2},{18... | collective-permute-start | bytes 98312 | tf_op jit(solution)/shard_map/ppermute | solution.py:508
  7.2 0.6 %collective-permute-start.2 = (f32[64,128]{1,0:T(8,128)}, f32[64,128]{1,0:T(8,128)S(1)}, u32[]{:S(2)}, u32[]{:S(2)}) collective-permute-start(f32[64,128]{1,0:T(8,128)} %get-tuple-element.33), channel_id=1, source_target_pairs={{8,0},{0,8},{24,16},{16,24},{9,1},{1,9},{25,17},{17,25},{10,2},{2,... | collective-permute-start | bytes 98312 | tf_op jit(solution)/shard_map/ppermute | solution.py:508
  7.8 0.9 %copy-done = f32[336,128]{1,0:T(8,128)S(1)} copy-done((f32[336,128]{1,0:T(8,128)S(1)}, f32[336,128]{1,0:T(8,128)}, u32[]{:S(2)}) %copy-start) | copy-done | bytes 172056
  8.7 0.4 %own_moments.1 = (f32[11,24,128]{2,1,0:T(8,128)S(1)}, f32[8,128]{1,0:T(8,128)S(1)}, f32[96,256]{1,0:T(8,128)S(1)}) custom-call(f32[336,128]{1,0:T(8,128)S(1)} %copy-done), custom_call_target="tpu_custom_call" | custom-call | flops 100000000 | bytes 1048576 | tf_op jit(solution)/shard_map/own_moments/pallas_call | solution.py:455
  9.1 0.1 collective-permute-done.1.entries
  9.3 0.4 %more_moments.2.started = f32[96,256]{1,0:T(8,128)S(1)} custom-call(f32[96,256]{1,0:T(8,128)S(1)} %get-tuple-element.32.started, f32[64,128]{1,0:T(8,128)S(1)} %collective-permute-done.1.entries), custom_call_target="tpu_custom_call" | custom-call | flops 6000000000 | bytes 1048576 | tf_op jit(solution)/shard_map/more_moments/pallas_call | solution.py:455
  9.7 1.6 %collective-permute-done.2.entries = f32[64,128]{1,0:T(8,128)S(1)} collective-permute-done((f32[64,128]{1,0:T(8,128)}, f32[64,128]{1,0:T(8,128)S(1)}, u32[]{:S(2)}, u32[]{:S(2)}) %collective-permute-start.2) | collective-permute-done | bytes 32800 | tf_op jit(solution)/shard_map/ppermute | solution.py:508
  11.3 0.4 %more_moments.3.refs_2_ = f32[96,256]{1,0:T(8,128)S(1)} custom-call(f32[96,256]{1,0:T(8,128)S(1)} %more_moments.2.started, f32[64,128]{1,0:T(8,128)S(1)} %collective-permute-done.2.entries), custom_call_target="tpu_custom_call" | custom-call | flops 6000000000 | bytes 1048576 | tf_op jit(solution)/shard_map/more_moments/pallas_call | solution.py:455
  11.7 0.5 %collective-permute-done.3.refs_3_ = f32[64,128]{1,0:T(8,128)S(1)} collective-permute-done((f32[64,128]{1,0:T(8,128)}, f32[64,128]{1,0:T(8,128)S(1)}, u32[]{:S(2)}, u32[]{:S(2)}) %collective-permute-start.3) | collective-permute-done | bytes 32800 | tf_op jit(solution)/shard_map/ppermute | solution.py:508
  12.2 0.5 %join_and_moments.1 = (f32[2,9,2,16,128]{4,3,2,1,0:T(8,128)S(1)}, f32[2,2,16,128]{3,2,1,0:T(8,128)S(1)}, f32[2,16,128]{2,1,0:T(8,128)S(1)}, f32[168,128]{1,0:T(8,128)S(1)}) custom-call(f32[11,24,128]{2,1,0:T(8,128)S(1)} %get-tuple-element.30.refs_0_, f32[10,24,128]{2,1,0:T(8,128)S(1)} %collective-permute-done.refs_1_, f32[96,256]{1,0:T(8,128)S(1)} %more_moments.3.refs_2_, ...), custom_call_target="tpu_custom_call" | custom-call | flops 10000000 | bytes 1048576 | tf_op jit(solution)/shard_map/join_and_moments/pallas_call | solution.py:455
  12.7 0.6 %collective-permute-start.4 = (f32[168,128]{1,0:T(8,128)S(1)}, f32[168,128]{1,0:T(8,128)S(1)}, u32[]{:S(2)}, u32[]{:S(2)}) collective-permute-start(f32[168,128]{1,0:T(8,128)S(1)} %get-tuple-element.37), channel_id=1, source_target_pairs={{1,2},{2,1},{3,4},{4,3},{5,6},{6,5},{0,7},{7,0},{9,10},{10,9},{11,... | collective-permute-start | bytes 258056 | tf_op jit(solution)/shard_map/ppermute | solution.py:487
  13.2 0.2 inner_edges.1
  13.4 1.3 %collective-permute-start.5 = (f32[324,128]{1,0:T(8,128)S(1)}, f32[324,128]{1,0:T(8,128)S(1)}, u32[]{:S(2)}, u32[]{:S(2)}) collective-permute-start(f32[324,128]{1,0:T(8,128)S(1)} %get-tuple-element.42), channel_id=1, source_target_pairs={{0,8},{1,9},{8,0},{9,1},{16,24},{17,25},{24,16},{25,17},{2,10},{3,... | collective-permute-start | bytes 497672 | tf_op jit(solution)/shard_map/ppermute | solution.py:479
  14.7 3.6 %collective-permute-done.4.halo = f32[168,128]{1,0:T(8,128)S(1)} collective-permute-done((f32[168,128]{1,0:T(8,128)S(1)}, f32[168,128]{1,0:T(8,128)S(1)}, u32[]{:S(2)}, u32[]{:S(2)}) %collective-permute-start.4) | collective-permute-done | bytes 86048 | tf_op jit(solution)/shard_map/ppermute | solution.py:487
  18.4 0.3 outer_edges.1
  18.6 0.2 collective-permute-start.7
  18.8 4.0 %collective-permute-done.7.refs_5_ = f32[108,128]{1,0:T(8,128)S(1)} collective-permute-done((f32[108,128]{1,0:T(8,128)S(1)}, f32[108,128]{1,0:T(8,128)S(1)}, u32[]{:S(2)}, u32[]{:S(2)}) %collective-permute-start.7) | collective-permute-done | bytes 55328 | tf_op jit(solution)/shard_map/ppermute | solution.py:479
  22.9 0.6 %steps.2 = (f32[264,128]{1,0:T(8,128)S(1)}, f32[264,128]{1,0:T(8,128)S(1)}, f32[2,9,2,16,128]{4,3,2,1,0:T(8,128)S(1)}, f32[2,3,6,16,128]{4,3,2,1,0:T(8,128)S(1)}, f32[6,16,128]{2,1,0:T(8,128)S(1)}) custom-call(f32[2,9,2,16,128]{4,3,2,1,0:T(8,128)S(1)} %get-tuple-element.39.refs_0_, f32[2,3,2,16,128]{4,3,2,1,0:T(8,128)S(1)} %get-tuple-element.40.refs_1_, ...), custom_call_target="tpu_custom_call" | custom-call | flops 10000000 | bytes 1048576 | tf_op jit(solution)/shard_map/steps/pallas_call | solution.py:455
  23.5 2.1 %collective-permute-start.9 = (f32[264,128]{1,0:T(8,128)S(1)}, f32[264,128]{1,0:T(8,128)S(1)}, u32[]{:S(2)}, u32[]{:S(2)}) collective-permute-start(f32[264,128]{1,0:T(8,128)S(1)} %get-tuple-element.49), channel_id=1, source_target_pairs={{0,8},{1,9},{8,0},{9,1},{16,24},{17,25},{24,16},{25,17},{2,10},{3,... | collective-permute-start | bytes 405512 | tf_op jit(solution)/shard_map/ppermute | solution.py:479
  25.6 3.0 %collective-permute-done.9.refs_3_ = f32[264,128]{1,0:T(8,128)S(1)} collective-permute-done((f32[264,128]{1,0:T(8,128)S(1)}, f32[264,128]{1,0:T(8,128)S(1)}, u32[]{:S(2)}, u32[]{:S(2)}) %collective-permute-start.9) | collective-permute-done | bytes 135200 | tf_op jit(solution)/shard_map/ppermute | solution.py:479
  28.6 0.4 %steps.3 = (f32[9,2,8,128]{3,2,1,0:T(8,128)S(1)}, f32[9,2,8,128]{3,2,1,0:T(8,128)S(1)}) custom-call(f32[2,9,2,16,128]{4,3,2,1,0:T(8,128)S(1)} %get-tuple-element.46.refs_0_, f32[2,3,6,16,128]{4,3,2,1,0:T(8,128)S(1)} %get-tuple-element.47.refs_1_, f32[6,16,128]{2,1,0:T(8,128)S(1)} %get-tuple-element.48.refs_2_, ...), custom_call_target="tpu_custom_call" | custom-call | flops 10000000 | bytes 1048576 | tf_op jit(solution)/shard_map/steps/pallas_call | solution.py:455
  29.1 1.3 %collective-permute-done.11.brought = f32[9,2,8,128]{3,2,1,0:T(8,128)S(1)} collective-permute-done((f32[9,2,8,128]{3,2,1,0:T(8,128)S(1)}, f32[9,2,8,128]{3,2,1,0:T(8,128)S(1)}, u32[]{:S(2)}, u32[]{:S(2)}) %collective-permute-start.11) | collective-permute-done | bytes 73760 | tf_op jit(solution)/shard_map/ppermute | solution.py:490
  30.4 0.7 %home.1 = f32[1,9,2,16,128]{4,3,2,1,0:T(8,128)} custom-call(f32[9,2,8,128]{3,2,1,0:T(8,128)S(1)} %get-tuple-element.51.mine, f32[9,2,8,128]{3,2,1,0:T(8,128)S(1)} %collective-permute-done.11.brought), custom_call_target="tpu_custom_call" | custom-call | flops 10000000 | bytes 1048576 | tf_op jit(solution)/shard_map/home/pallas_call | solution.py:455
  (12 shorter events, 0.1 us)
Async XLA Ops:
  2.1 7.2 %collective-permute-start.1 = (f32[64,128]{1,0:T(8,128)}, f32[64,128]{1,0:T(8,128)S(1)}, u32[]{:S(2)}, u32[]{:S(2)}) collective-permute-start(f32[64,128]{1,0:T(8,128)} %get-tuple-element.33), channel_id=1, source_target_pairs={{24,0},{16,8},{8,16},{0,24},{25,1},{17,9},{9,17},{1,25},{26,2},{18... | collective-permute-start | bytes 98312 | tf_op jit(solution)/shard_map/ppermute | solution.py:508
  7.2 5.0 %collective-permute-start.3 = (f32[64,128]{1,0:T(8,128)}, f32[64,128]{1,0:T(8,128)S(1)}, u32[]{:S(2)}, u32[]{:S(2)}) collective-permute-start(f32[64,128]{1,0:T(8,128)} %get-tuple-element.33), channel_id=1, source_target_pairs={{16,0},{24,8},{0,16},{8,24},{17,1},{25,9},{1,17},{9,25},{18,2},{26... | collective-permute-start | bytes 98312 | tf_op jit(solution)/shard_map/ppermute | solution.py:508
  7.2 4.1 %collective-permute-start.2 = (f32[64,128]{1,0:T(8,128)}, f32[64,128]{1,0:T(8,128)S(1)}, u32[]{:S(2)}, u32[]{:S(2)}) collective-permute-start(f32[64,128]{1,0:T(8,128)} %get-tuple-element.33), channel_id=1, source_target_pairs={{8,0},{0,8},{24,16},{16,24},{9,1},{1,9},{25,17},{17,25},{10,2},{2,... | collective-permute-start | bytes 98312 | tf_op jit(solution)/shard_map/ppermute | solution.py:508
  7.8 4.4 %collective-permute-start = (f32[10,24,128]{2,1,0:T(8,128)}, f32[10,24,128]{2,1,0:T(8,128)S(1)}, u32[]{:S(2)}, u32[]{:S(2)}) collective-permute-start(f32[10,24,128]{2,1,0:T(8,128)} %get-tuple-element.31), channel_id=1, source_target_pairs={{0,1},{1,0},{2,3},{3,2},{4,5},{5,4},{6,7},{7,6},{8,9},{9,8},{10,11... | collective-permute-start | bytes 368648 | tf_op jit(solution)/shard_map/ppermute | solution.py:490
  7.8 0.9 %copy-start = (f32[336,128]{1,0:T(8,128)S(1)}, f32[336,128]{1,0:T(8,128)}, u32[]{:S(2)}) copy-start(f32[336,128]{1,0:T(8,128)} %get-tuple-element.29.kept) | copy-start | bytes 516100
  12.7 5.7 %collective-permute-start.4 = (f32[168,128]{1,0:T(8,128)S(1)}, f32[168,128]{1,0:T(8,128)S(1)}, u32[]{:S(2)}, u32[]{:S(2)}) collective-permute-start(f32[168,128]{1,0:T(8,128)S(1)} %get-tuple-element.37), channel_id=1, source_target_pairs={{1,2},{2,1},{3,4},{4,3},{5,6},{6,5},{0,7},{7,0},{9,10},{10,9},{11,... | collective-permute-start | bytes 258056 | tf_op jit(solution)/shard_map/ppermute | solution.py:487
  13.4 9.5 %collective-permute-start.5 = (f32[324,128]{1,0:T(8,128)S(1)}, f32[324,128]{1,0:T(8,128)S(1)}, u32[]{:S(2)}, u32[]{:S(2)}) collective-permute-start(f32[324,128]{1,0:T(8,128)S(1)} %get-tuple-element.42), channel_id=1, source_target_pairs={{0,8},{1,9},{8,0},{9,1},{16,24},{17,25},{24,16},{25,17},{2,10},{3,... | collective-permute-start | bytes 497672 | tf_op jit(solution)/shard_map/ppermute | solution.py:479
  14.7 8.2 %collective-permute-start.6 = (f32[324,128]{1,0:T(8,128)S(1)}, f32[324,128]{1,0:T(8,128)S(1)}, u32[]{:S(2)}, u32[]{:S(2)}) collective-permute-start(f32[324,128]{1,0:T(8,128)S(1)} %get-tuple-element.43), channel_id=1, source_target_pairs={{0,1},{1,0},{8,16},{9,17},{16,8},{17,9},{24,25},{25,24},{2,3},{3,2... | collective-permute-start | bytes 497672 | tf_op jit(solution)/shard_map/ppermute | solution.py:479
  18.6 4.2 %collective-permute-start.7 = (f32[108,128]{1,0:T(8,128)S(1)}, f32[108,128]{1,0:T(8,128)S(1)}, u32[]{:S(2)}, u32[]{:S(2)}) collective-permute-start(f32[108,128]{1,0:T(8,128)S(1)} %get-tuple-element.44), channel_id=1, source_target_pairs={{0,8},{1,9},{8,0},{9,1},{16,24},{17,25},{24,16},{25,17},{2,10},{3,... | collective-permute-start | bytes 165896 | tf_op jit(solution)/shard_map/ppermute | solution.py:479
  18.8 4.0 %collective-permute-start.8 = (f32[108,128]{1,0:T(8,128)S(1)}, f32[108,128]{1,0:T(8,128)S(1)}, u32[]{:S(2)}, u32[]{:S(2)}) collective-permute-start(f32[108,128]{1,0:T(8,128)S(1)} %get-tuple-element.45), channel_id=1, source_target_pairs={{0,1},{1,0},{8,16},{9,17},{16,8},{17,9},{24,25},{25,24},{2,3},{3,2... | collective-permute-start | bytes 165896 | tf_op jit(solution)/shard_map/ppermute | solution.py:479
  23.5 5.1 %collective-permute-start.9 = (f32[264,128]{1,0:T(8,128)S(1)}, f32[264,128]{1,0:T(8,128)S(1)}, u32[]{:S(2)}, u32[]{:S(2)}) collective-permute-start(f32[264,128]{1,0:T(8,128)S(1)} %get-tuple-element.49), channel_id=1, source_target_pairs={{0,8},{1,9},{8,0},{9,1},{16,24},{17,25},{24,16},{25,17},{2,10},{3,... | collective-permute-start | bytes 405512 | tf_op jit(solution)/shard_map/ppermute | solution.py:479
  25.6 3.0 %collective-permute-start.10 = (f32[264,128]{1,0:T(8,128)S(1)}, f32[264,128]{1,0:T(8,128)S(1)}, u32[]{:S(2)}, u32[]{:S(2)}) collective-permute-start(f32[264,128]{1,0:T(8,128)S(1)} %get-tuple-element.50), channel_id=1, source_target_pairs={{0,1},{1,0},{8,16},{9,17},{16,8},{17,9},{24,25},{25,24},{2,3},{3,2... | collective-permute-start | bytes 405512 | tf_op jit(solution)/shard_map/ppermute | solution.py:479
  29.0 1.3 %collective-permute-start.11 = (f32[9,2,8,128]{3,2,1,0:T(8,128)S(1)}, f32[9,2,8,128]{3,2,1,0:T(8,128)S(1)}, u32[]{:S(2)}, u32[]{:S(2)}) collective-permute-start(f32[9,2,8,128]{3,2,1,0:T(8,128)S(1)} %get-tuple-element.52), channel_id=1, source_target_pairs={{0,1},{1,0},{2,3},{3,2},{4,5},{5,4},{6,7},{7,6},{8,9},{9,8},{10,11... | collective-permute-start | bytes 221192 | tf_op jit(solution)/shard_map/ppermute | solution.py:490

commit v19 on v18

--- a/solution.py
+++ b/solution.py
@@ -482,9 +482,11 @@
         return section ^ k if sections & (sections - 1) == 0 else (section + k) % sections
 
     def along_depth(block):
-        ends = [(0, 2 * slabs - 1), (2 * slabs - 1, 0)]
-        route = [(i, j) for i, j in swaps(1, 2 * slabs) if i != j] + ends
-        return lax.ppermute(block, ("depth", "segment"), route)
+        line = 2 * slabs
+        route = []
+        for s, partner in swaps(0, sections):
+            route += [(s * line + i, (s if i != j else partner) * line + j) for i, j in swaps(1, line)]
+        return lax.ppermute(block, ("sec", "depth", "segment"), route)
 
     def swap(block):
         return lax.ppermute(block, "segment", [(0, 1), (1, 0)])

time: 31.2 us -> 30.6 us (0.981)
  waiting for transfers between devices: 14.2 us -> 12.8 us
  starting transfers between devices: 9.97 us -> 10.7 us
    ppermute x1, waiting for transfers between devices: 3.61 us -> 2.17 us  [along_depth(): return lax.ppermute(block, ('sec', 'depth', 'segment'), route)]
    ppermute x6, starting transfers between devices: 3.6 us -> 4.59 us  [pairs(): return lax.ppermute(block, ('sec', 'segment'), route)]
where the time goes in v19:
time: 30.6 us; the launch traced here: 30.4 us
  waiting for transfers between devices  12.8 us (42%)
  starting transfers between devices  10.7 us (35%)
  Pallas kernels  5.89 us (19%)
  local copies, waits for them, and re-layouts  0.92 us (3%)
    ppermute x6, waiting for transfers between devices, pairs(): return lax.ppermute(block, ('sec', 'segment'), route)  7.13 us
    pallas_call x10, Pallas kernels, call(): pl.pallas_call(kernel, out_shape=[jax.ShapeDtypeStruct(shape, F32) for sh...  5.89 us
    ppermute x3, starting transfers between devices, on_device(): lax.ppermute(entries, 'sec', [(other(i, k), i) for i in range(sections)])  5.76 us
    ppermute x6, starting transfers between devices, pairs(): return lax.ppermute(block, ('sec', 'segment'), route)  4.59 us
    ppermute x3, waiting for transfers between devices, on_device(): lax.ppermute(entries, 'sec', [(other(i, k), i) for i in range(sections)])  2.26 us
    ppermute x1, waiting for transfers between devices, along_depth(): return lax.ppermute(block, ('sec', 'depth', 'segment'), route)  2.17 us
    ppermute x2, waiting for transfers between devices, swap(): return lax.ppermute(block, 'segment', [(0, 1), (1, 0)])  1.26 us
    unnamed x2, local copies, waits for them, and re-layouts  0.92 us
  transfers between devices with their start and end apart: 12, of which 7 were waited for; matrix products, arithmetic and copies ran while one was open for 0% of the time, Pallas kernels for 5%

profile of v19, /device:TPU:0, one launch (start us, length us, event | category | flops | bytes accessed | tf_op | source)
XLA Modules:
  0.0 30.4 jit_solution(14488067885086352834)
XLA Ops:
  0.0 2.1 %pack.1 = (f32[64,128]{1,0:T(8,128)}, f32[336,128]{1,0:T(8,128)}, f32[10,24,128]{2,1,0:T(8,128)}) custom-call(f32[1,9,2,16,128]{4,3,2,1,0:T(8,128)} %fields_in.1, s32[1,2,16,128]{3,2,1,0:T(8,128)} %ids_in.1, f32[6,1024]{1,0:T(8,128)} %moments_in.1, s32[8,128]{1,0:T(8,128)} %bitcast.4, s32[8,128]{1,0:T(8,128)} %bitcast.5, s32[16,128]{1,0:T(8,128)} %bitcast.3, ...), custom_call_target="tpu_custom_call" | custom-call | flops 10000000 | bytes 1048576 | tf_op jit(solution)/shard_map/pack/pallas_call | solution.py:455
  2.1 5.1 %collective-permute-start.1 = (f32[64,128]{1,0:T(8,128)}, f32[64,128]{1,0:T(8,128)S(1)}, u32[]{:S(2)}, u32[]{:S(2)}) collective-permute-start(f32[64,128]{1,0:T(8,128)} %get-tuple-element.33), channel_id=1, source_target_pairs={{24,0},{16,8},{8,16},{0,24},{25,1},{17,9},{9,17},{1,25},{26,2},{18... | collective-permute-start | bytes 98312 | tf_op jit(solution)/shard_map/ppermute | solution.py:510
  7.2 0.6 %collective-permute-start.2 = (f32[64,128]{1,0:T(8,128)}, f32[64,128]{1,0:T(8,128)S(1)}, u32[]{:S(2)}, u32[]{:S(2)}) collective-permute-start(f32[64,128]{1,0:T(8,128)} %get-tuple-element.33), channel_id=1, source_target_pairs={{8,0},{0,8},{24,16},{16,24},{9,1},{1,9},{25,17},{17,25},{10,2},{2,... | collective-permute-start | bytes 98312 | tf_op jit(solution)/shard_map/ppermute | solution.py:510
  7.8 0.9 %copy-done = f32[336,128]{1,0:T(8,128)S(1)} copy-done((f32[336,128]{1,0:T(8,128)S(1)}, f32[336,128]{1,0:T(8,128)}, u32[]{:S(2)}) %copy-start) | copy-done | bytes 172056
  8.7 0.4 %own_moments.1 = (f32[11,24,128]{2,1,0:T(8,128)S(1)}, f32[8,128]{1,0:T(8,128)S(1)}, f32[96,256]{1,0:T(8,128)S(1)}) custom-call(f32[336,128]{1,0:T(8,128)S(1)} %copy-done), custom_call_target="tpu_custom_call" | custom-call | flops 100000000 | bytes 1048576 | tf_op jit(solution)/shard_map/own_moments/pallas_call | solution.py:455
  9.1 0.1 collective-permute-done.1.entries
  9.3 0.4 %more_moments.2.started = f32[96,256]{1,0:T(8,128)S(1)} custom-call(f32[96,256]{1,0:T(8,128)S(1)} %get-tuple-element.32.started, f32[64,128]{1,0:T(8,128)S(1)} %collective-permute-done.1.entries), custom_call_target="tpu_custom_call" | custom-call | flops 6000000000 | bytes 1048576 | tf_op jit(solution)/shard_map/more_moments/pallas_call | solution.py:455
  9.7 1.6 %collective-permute-done.2.entries = f32[64,128]{1,0:T(8,128)S(1)} collective-permute-done((f32[64,128]{1,0:T(8,128)}, f32[64,128]{1,0:T(8,128)S(1)}, u32[]{:S(2)}, u32[]{:S(2)}) %collective-permute-start.2) | collective-permute-done | bytes 32800 | tf_op jit(solution)/shard_map/ppermute | solution.py:510
  11.3 0.4 %more_moments.3.refs_2_ = f32[96,256]{1,0:T(8,128)S(1)} custom-call(f32[96,256]{1,0:T(8,128)S(1)} %more_moments.2.started, f32[64,128]{1,0:T(8,128)S(1)} %collective-permute-done.2.entries), custom_call_target="tpu_custom_call" | custom-call | flops 6000000000 | bytes 1048576 | tf_op jit(solution)/shard_map/more_moments/pallas_call | solution.py:455
  11.7 0.5 %collective-permute-done.3.refs_3_ = f32[64,128]{1,0:T(8,128)S(1)} collective-permute-done((f32[64,128]{1,0:T(8,128)}, f32[64,128]{1,0:T(8,128)S(1)}, u32[]{:S(2)}, u32[]{:S(2)}) %collective-permute-start.3) | collective-permute-done | bytes 32800 | tf_op jit(solution)/shard_map/ppermute | solution.py:510
  12.2 0.5 %join_and_moments.1 = (f32[2,9,2,16,128]{4,3,2,1,0:T(8,128)S(1)}, f32[2,2,16,128]{3,2,1,0:T(8,128)S(1)}, f32[2,16,128]{2,1,0:T(8,128)S(1)}, f32[168,128]{1,0:T(8,128)S(1)}) custom-call(f32[11,24,128]{2,1,0:T(8,128)S(1)} %get-tuple-element.30.refs_0_, f32[10,24,128]{2,1,0:T(8,128)S(1)} %collective-permute-done.refs_1_, f32[96,256]{1,0:T(8,128)S(1)} %more_moments.3.refs_2_, ...), custom_call_target="tpu_custom_call" | custom-call | flops 10000000 | bytes 1048576 | tf_op jit(solution)/shard_map/join_and_moments/pallas_call | solution.py:455
  12.7 0.3 collective-permute-start.4
  12.9 0.2 inner_edges.1
  13.2 1.9 %collective-permute-start.5 = (f32[324,128]{1,0:T(8,128)S(1)}, f32[324,128]{1,0:T(8,128)S(1)}, u32[]{:S(2)}, u32[]{:S(2)}) collective-permute-start(f32[324,128]{1,0:T(8,128)S(1)} %get-tuple-element.42), channel_id=1, source_target_pairs={{0,8},{1,9},{8,0},{9,1},{16,24},{17,25},{24,16},{25,17},{2,10},{3,... | collective-permute-start | bytes 497672 | tf_op jit(solution)/shard_map/ppermute | solution.py:479
  15.0 2.2 %collective-permute-done.4.halo = f32[168,128]{1,0:T(8,128)S(1)} collective-permute-done((f32[168,128]{1,0:T(8,128)S(1)}, f32[168,128]{1,0:T(8,128)S(1)}, u32[]{:S(2)}, u32[]{:S(2)}) %collective-permute-start.4) | collective-permute-done | bytes 86048 | tf_op jit(solution)/shard_map/ppermute | solution.py:489
  17.2 0.3 outer_edges.1
  17.5 0.9 %collective-permute-start.7 = (f32[108,128]{1,0:T(8,128)S(1)}, f32[108,128]{1,0:T(8,128)S(1)}, u32[]{:S(2)}, u32[]{:S(2)}) collective-permute-start(f32[108,128]{1,0:T(8,128)S(1)} %get-tuple-element.44), channel_id=1, source_target_pairs={{0,8},{1,9},{8,0},{9,1},{16,24},{17,25},{24,16},{25,17},{2,10},{3,... | collective-permute-start | bytes 165896 | tf_op jit(solution)/shard_map/ppermute | solution.py:479
  18.4 3.6 %collective-permute-done.7.refs_5_ = f32[108,128]{1,0:T(8,128)S(1)} collective-permute-done((f32[108,128]{1,0:T(8,128)S(1)}, f32[108,128]{1,0:T(8,128)S(1)}, u32[]{:S(2)}, u32[]{:S(2)}) %collective-permute-start.7) | collective-permute-done | bytes 55328 | tf_op jit(solution)/shard_map/ppermute | solution.py:479
  22.1 0.6 %steps.2 = (f32[264,128]{1,0:T(8,128)S(1)}, f32[264,128]{1,0:T(8,128)S(1)}, f32[2,9,2,16,128]{4,3,2,1,0:T(8,128)S(1)}, f32[2,3,6,16,128]{4,3,2,1,0:T(8,128)S(1)}, f32[6,16,128]{2,1,0:T(8,128)S(1)}) custom-call(f32[2,9,2,16,128]{4,3,2,1,0:T(8,128)S(1)} %get-tuple-element.39.refs_0_, f32[2,3,2,16,128]{4,3,2,1,0:T(8,128)S(1)} %get-tuple-element.40.refs_1_, ...), custom_call_target="tpu_custom_call" | custom-call | flops 10000000 | bytes 1048576 | tf_op jit(solution)/shard_map/steps/pallas_call | solution.py:455
  22.7 1.8 %collective-permute-start.9 = (f32[264,128]{1,0:T(8,128)S(1)}, f32[264,128]{1,0:T(8,128)S(1)}, u32[]{:S(2)}, u32[]{:S(2)}) collective-permute-start(f32[264,128]{1,0:T(8,128)S(1)} %get-tuple-element.49), channel_id=1, source_target_pairs={{0,8},{1,9},{8,0},{9,1},{16,24},{17,25},{24,16},{25,17},{2,10},{3,... | collective-permute-start | bytes 405512 | tf_op jit(solution)/shard_map/ppermute | solution.py:479
  24.5 3.5 %collective-permute-done.9.refs_3_ = f32[264,128]{1,0:T(8,128)S(1)} collective-permute-done((f32[264,128]{1,0:T(8,128)S(1)}, f32[264,128]{1,0:T(8,128)S(1)}, u32[]{:S(2)}, u32[]{:S(2)}) %collective-permute-start.9) | collective-permute-done | bytes 135200 | tf_op jit(solution)/shard_map/ppermute | solution.py:479
  28.0 0.4 %steps.3 = (f32[9,2,8,128]{3,2,1,0:T(8,128)S(1)}, f32[9,2,8,128]{3,2,1,0:T(8,128)S(1)}) custom-call(f32[2,9,2,16,128]{4,3,2,1,0:T(8,128)S(1)} %get-tuple-element.46.refs_0_, f32[2,3,6,16,128]{4,3,2,1,0:T(8,128)S(1)} %get-tuple-element.47.refs_1_, f32[6,16,128]{2,1,0:T(8,128)S(1)} %get-tuple-element.48.refs_2_, ...), custom_call_target="tpu_custom_call" | custom-call | flops 10000000 | bytes 1048576 | tf_op jit(solution)/shard_map/steps/pallas_call | solution.py:455
  28.5 1.3 %collective-permute-done.11.brought = f32[9,2,8,128]{3,2,1,0:T(8,128)S(1)} collective-permute-done((f32[9,2,8,128]{3,2,1,0:T(8,128)S(1)}, f32[9,2,8,128]{3,2,1,0:T(8,128)S(1)}, u32[]{:S(2)}, u32[]{:S(2)}) %collective-permute-start.11) | collective-permute-done | bytes 73760 | tf_op jit(solution)/shard_map/ppermute | solution.py:492
  29.7 0.7 %home.1 = f32[1,9,2,16,128]{4,3,2,1,0:T(8,128)} custom-call(f32[9,2,8,128]{3,2,1,0:T(8,128)S(1)} %get-tuple-element.51.mine, f32[9,2,8,128]{3,2,1,0:T(8,128)S(1)} %collective-permute-done.11.brought), custom_call_target="tpu_custom_call" | custom-call | flops 10000000 | bytes 1048576 | tf_op jit(solution)/shard_map/home/pallas_call | solution.py:455
  (12 shorter events, 0.1 us)
Async XLA Ops:
  2.1 7.2 %collective-permute-start.1 = (f32[64,128]{1,0:T(8,128)}, f32[64,128]{1,0:T(8,128)S(1)}, u32[]{:S(2)}, u32[]{:S(2)}) collective-permute-start(f32[64,128]{1,0:T(8,128)} %get-tuple-element.33), channel_id=1, source_target_pairs={{24,0},{16,8},{8,16},{0,24},{25,1},{17,9},{9,17},{1,25},{26,2},{18... | collective-permute-start | bytes 98312 | tf_op jit(solution)/shard_map/ppermute | solution.py:510
  7.2 5.0 %collective-permute-start.3 = (f32[64,128]{1,0:T(8,128)}, f32[64,128]{1,0:T(8,128)S(1)}, u32[]{:S(2)}, u32[]{:S(2)}) collective-permute-start(f32[64,128]{1,0:T(8,128)} %get-tuple-element.33), channel_id=1, source_target_pairs={{16,0},{24,8},{0,16},{8,24},{17,1},{25,9},{1,17},{9,25},{18,2},{26... | collective-permute-start | bytes 98312 | tf_op jit(solution)/shard_map/ppermute | solution.py:510
  7.2 4.1 %collective-permute-start.2 = (f32[64,128]{1,0:T(8,128)}, f32[64,128]{1,0:T(8,128)S(1)}, u32[]{:S(2)}, u32[]{:S(2)}) collective-permute-start(f32[64,128]{1,0:T(8,128)} %get-tuple-element.33), channel_id=1, source_target_pairs={{8,0},{0,8},{24,16},{16,24},{9,1},{1,9},{25,17},{17,25},{10,2},{2,... | collective-permute-start | bytes 98312 | tf_op jit(solution)/shard_map/ppermute | solution.py:510
  7.8 4.4 %collective-permute-start = (f32[10,24,128]{2,1,0:T(8,128)}, f32[10,24,128]{2,1,0:T(8,128)S(1)}, u32[]{:S(2)}, u32[]{:S(2)}) collective-permute-start(f32[10,24,128]{2,1,0:T(8,128)} %get-tuple-element.31), channel_id=1, source_target_pairs={{0,1},{1,0},{2,3},{3,2},{4,5},{5,4},{6,7},{7,6},{8,9},{9,8},{10,11... | collective-permute-start | bytes 368648 | tf_op jit(solution)/shard_map/ppermute | solution.py:492
  7.8 0.9 %copy-start = (f32[336,128]{1,0:T(8,128)S(1)}, f32[336,128]{1,0:T(8,128)}, u32[]{:S(2)}) copy-start(f32[336,128]{1,0:T(8,128)} %get-tuple-element.29.kept) | copy-start | bytes 516100
  12.7 4.5 %collective-permute-start.4 = (f32[168,128]{1,0:T(8,128)S(1)}, f32[168,128]{1,0:T(8,128)S(1)}, u32[]{:S(2)}, u32[]{:S(2)}) collective-permute-start(f32[168,128]{1,0:T(8,128)S(1)} %get-tuple-element.37), channel_id=1, source_target_pairs={{0,8},{1,2},{2,1},{3,4},{4,3},{5,6},{6,5},{7,15},{8,0},{9,10},{10,... | collective-permute-start | bytes 258056 | tf_op jit(solution)/shard_map/ppermute | solution.py:489
  13.2 8.9 %collective-permute-start.5 = (f32[324,128]{1,0:T(8,128)S(1)}, f32[324,128]{1,0:T(8,128)S(1)}, u32[]{:S(2)}, u32[]{:S(2)}) collective-permute-start(f32[324,128]{1,0:T(8,128)S(1)} %get-tuple-element.42), channel_id=1, source_target_pairs={{0,8},{1,9},{8,0},{9,1},{16,24},{17,25},{24,16},{25,17},{2,10},{3,... | collective-permute-start | bytes 497672 | tf_op jit(solution)/shard_map/ppermute | solution.py:479
  15.0 7.0 %collective-permute-start.6 = (f32[324,128]{1,0:T(8,128)S(1)}, f32[324,128]{1,0:T(8,128)S(1)}, u32[]{:S(2)}, u32[]{:S(2)}) collective-permute-start(f32[324,128]{1,0:T(8,128)S(1)} %get-tuple-element.43), channel_id=1, source_target_pairs={{0,1},{1,0},{8,16},{9,17},{16,8},{17,9},{24,25},{25,24},{2,3},{3,2... | collective-permute-start | bytes 497672 | tf_op jit(solution)/shard_map/ppermute | solution.py:479
  17.5 4.5 %collective-permute-start.7 = (f32[108,128]{1,0:T(8,128)S(1)}, f32[108,128]{1,0:T(8,128)S(1)}, u32[]{:S(2)}, u32[]{:S(2)}) collective-permute-start(f32[108,128]{1,0:T(8,128)S(1)} %get-tuple-element.44), channel_id=1, source_target_pairs={{0,8},{1,9},{8,0},{9,1},{16,24},{17,25},{24,16},{25,17},{2,10},{3,... | collective-permute-start | bytes 165896 | tf_op jit(solution)/shard_map/ppermute | solution.py:479
  18.4 3.6 %collective-permute-start.8 = (f32[108,128]{1,0:T(8,128)S(1)}, f32[108,128]{1,0:T(8,128)S(1)}, u32[]{:S(2)}, u32[]{:S(2)}) collective-permute-start(f32[108,128]{1,0:T(8,128)S(1)} %get-tuple-element.45), channel_id=1, source_target_pairs={{0,1},{1,0},{8,16},{9,17},{16,8},{17,9},{24,25},{25,24},{2,3},{3,2... | collective-permute-start | bytes 165896 | tf_op jit(solution)/shard_map/ppermute | solution.py:479
  22.7 5.3 %collective-permute-start.9 = (f32[264,128]{1,0:T(8,128)S(1)}, f32[264,128]{1,0:T(8,128)S(1)}, u32[]{:S(2)}, u32[]{:S(2)}) collective-permute-start(f32[264,128]{1,0:T(8,128)S(1)} %get-tuple-element.49), channel_id=1, source_target_pairs={{0,8},{1,9},{8,0},{9,1},{16,24},{17,25},{24,16},{25,17},{2,10},{3,... | collective-permute-start | bytes 405512 | tf_op jit(solution)/shard_map/ppermute | solution.py:479
  24.5 3.5 %collective-permute-start.10 = (f32[264,128]{1,0:T(8,128)S(1)}, f32[264,128]{1,0:T(8,128)S(1)}, u32[]{:S(2)}, u32[]{:S(2)}) collective-permute-start(f32[264,128]{1,0:T(8,128)S(1)} %get-tuple-element.50), channel_id=1, source_target_pairs={{0,1},{1,0},{8,16},{9,17},{16,8},{17,9},{24,25},{25,24},{2,3},{3,2... | collective-permute-start | bytes 405512 | tf_op jit(solution)/shard_map/ppermute | solution.py:479
  28.4 1.3 %collective-permute-start.11 = (f32[9,2,8,128]{3,2,1,0:T(8,128)S(1)}, f32[9,2,8,128]{3,2,1,0:T(8,128)S(1)}, u32[]{:S(2)}, u32[]{:S(2)}) collective-permute-start(f32[9,2,8,128]{3,2,1,0:T(8,128)S(1)} %get-tuple-element.52), channel_id=1, source_target_pairs={{0,1},{1,0},{2,3},{3,2},{4,5},{5,4},{6,7},{7,6},{8,9},{9,8},{10,11... | collective-permute-start | bytes 221192 | tf_op jit(solution)/shard_map/ppermute | solution.py:492

commit v20 on v12

--- a/solution.py
+++ b/solution.py
@@ -332,10 +332,14 @@
     reach = state.shape[3] - STEPS
     state[:, :, own], ids[:, own], times[own] = own_state[...], own_ids[...], own_times[...]
 
+    slab = lax.axis_index("depth")
+
     def join(mine, main, outer):
+        inside = slab > 0 if mine == 0 else slab < lax.axis_size("depth") - 1
+        inside = jnp.where(inside, F32(1.0), F32(0.0))
         for x in range(cx):
             for k in range(21):
-                line = halo[(k * cx + x) * STEPS : (k * cx + x + 1) * STEPS]
+                line = inside * halo[(k * cx + x) * STEPS : (k * cx + x + 1) * STEPS]
                 if k == 20:
                     times[cx + x, outer(reach)] = line
                 elif k % 10 == 9:
@@ -374,12 +378,17 @@
     state[:, :, own] = both_in[...]
     right_units, left_units = edge_units(cx, first)
 
+    section = lax.axis_index("sec")
+    has_left = jnp.where(section > 0, F32(1.0), F32(0.0))
+    has_right = jnp.where(section < lax.axis_size("sec") - 1, F32(1.0), F32(0.0))
+
     def get(edge, units, start, rows_of, far, right):
+        inside = has_left if right else has_right
         last = 0
         for model, what, x in units:
             at = rows_of(x == far, right)
             first, last = last, last + at.stop - at.start
-            line = edge[first:last]
+            line = inside * edge[first:last]
             if what == 10:
                 times[start + x, at] = line
             elif what == 9:
@@ -435,6 +444,13 @@
         out[0, :, :, 0:half] = brought[...]
 
 
+def swaps(start, count):
+    route = {i: i for i in range(count)}
+    for i in range(start, count - 1, 2):
+        route[i], route[i + 1] = i + 1, i
+    return list(route.items())
+
+
 VMEM = pl.BlockSpec(memory_space=pltpu.VMEM)
 HBM = pl.BlockSpec(memory_space=pltpu.HBM)
 
@@ -462,15 +478,20 @@
     assert cx > 1 and STEPS % cx == 0
 
     def pairs(block, start):
-        route = [(i, i + 1) for i in range(start, sections - 1, 2)]
-        return lax.ppermute(block, "sec", route + [(j, i) for i, j in route])
+        route = []
+        for i, j in swaps(start, sections):
+            route += [(2 * i + k, 2 * j + (k if i != j else 1 - k)) for k in range(2)]
+        return lax.ppermute(block, ("sec", "segment"), route)
 
     def other(section, k):
         return section ^ k if sections & (sections - 1) == 0 else (section + k) % sections
 
     def along_depth(block):
-        down = [(2 * i + 1, 2 * (i + 1)) for i in range(slabs - 1)]
-        return lax.ppermute(block, ("depth", "segment"), down + [(j, i) for i, j in down])
+        line = 2 * slabs
+        route = []
+        for s, partner in swaps(0, sections):
+            route += [(s * line + i, (s if i != j else partner) * line + j) for i, j in swaps(1, line)]
+        return lax.ppermute(block, ("sec", "depth", "segment"), route)
 
     def swap(block):
         return lax.ppermute(block, "segment", [(0, 1), (1, 0)])

time: 37.1 us -> 32.1 us (0.87)
  the two profiles are of different devices: /device:TPU:13 before, /device:TPU:0 now
where the time goes in v20:
time: 32.1 us; the launch traced here: 31.9 us
  waiting for transfers between devices  14.1 us (44%)
  starting transfers between devices  10.7 us (33%)
  Pallas kernels  6.07 us (19%)
  local copies, waits for them, and re-layouts  0.92 us (3%)
    ppermute x6, waiting for transfers between devices, pairs(): return lax.ppermute(block, ('sec', 'segment'), route)  6.65 us
    pallas_call x12, Pallas kernels, call(): pl.pallas_call(kernel, out_shape=[jax.ShapeDtypeStruct(shape, F32) for sh...  6.07 us
    ppermute x3, starting transfers between devices, on_device(): lax.ppermute(entries, 'sec', [(other(i, k), i) for i in range(sections)])  5.76 us
    ppermute x1, waiting for transfers between devices, along_depth(): return lax.ppermute(block, ('sec', 'depth', 'segment'), route)  3.98 us
    ppermute x6, starting transfers between devices, pairs(): return lax.ppermute(block, ('sec', 'segment'), route)  3.01 us
    ppermute x3, waiting for transfers between devices, on_device(): lax.ppermute(entries, 'sec', [(other(i, k), i) for i in range(sections)])  2.26 us
    ppermute x1, starting transfers between devices, along_depth(): return lax.ppermute(block, ('sec', 'depth', 'segment'), route)  1.81 us
    ppermute x2, waiting for transfers between devices, swap(): return lax.ppermute(block, 'segment', [(0, 1), (1, 0)])  1.26 us
  transfers between devices with their start and end apart: 12, of which 7 were waited for; matrix products, arithmetic and copies ran while one was open for 0% of the time, Pallas kernels for 5%

profile of v20, /device:TPU:0, one launch (start us, length us, event | category | flops | bytes accessed | tf_op | source)
XLA Modules:
  0.0 31.9 jit_solution(17963862244657895615)
XLA Ops:
  0.0 2.1 %pack.1 = (f32[64,128]{1,0:T(8,128)}, f32[336,128]{1,0:T(8,128)}, f32[10,24,128]{2,1,0:T(8,128)}) custom-call(f32[1,9,2,16,128]{4,3,2,1,0:T(8,128)} %fields_in.1, s32[1,2,16,128]{3,2,1,0:T(8,128)} %ids_in.1, f32[6,1024]{1,0:T(8,128)} %moments_in.1, s32[8,128]{1,0:T(8,128)} %bitcast.4, s32[8,128]{1,0:T(8,128)} %bitcast.5, s32[16,128]{1,0:T(8,128)} %bitcast.3, ...), custom_call_target="tpu_custom_call" | custom-call | flops 10000000 | bytes 1048576 | tf_op jit(solution)/shard_map/pack/pallas_call | solution.py:460
  2.1 5.1 %collective-permute-start.1 = (f32[64,128]{1,0:T(8,128)}, f32[64,128]{1,0:T(8,128)S(1)}, u32[]{:S(2)}, u32[]{:S(2)}) collective-permute-start(f32[64,128]{1,0:T(8,128)} %get-tuple-element.31), channel_id=1, source_target_pairs={{24,0},{16,8},{8,16},{0,24},{25,1},{17,9},{9,17},{1,25},{26,2},{18... | collective-permute-start | bytes 98312 | tf_op jit(solution)/shard_map/ppermute | solution.py:515
  7.2 0.6 %collective-permute-start.2 = (f32[64,128]{1,0:T(8,128)}, f32[64,128]{1,0:T(8,128)S(1)}, u32[]{:S(2)}, u32[]{:S(2)}) collective-permute-start(f32[64,128]{1,0:T(8,128)} %get-tuple-element.31), channel_id=1, source_target_pairs={{8,0},{0,8},{24,16},{16,24},{9,1},{1,9},{25,17},{17,25},{10,2},{2,... | collective-permute-start | bytes 98312 | tf_op jit(solution)/shard_map/ppermute | solution.py:515
  7.8 0.9 %copy-done = f32[336,128]{1,0:T(8,128)S(1)} copy-done((f32[336,128]{1,0:T(8,128)S(1)}, f32[336,128]{1,0:T(8,128)}, u32[]{:S(2)}) %copy-start) | copy-done | bytes 172056
  8.7 0.4 %own_moments.1 = (f32[11,24,128]{2,1,0:T(8,128)S(1)}, f32[8,128]{1,0:T(8,128)S(1)}, f32[96,256]{1,0:T(8,128)S(1)}) custom-call(f32[336,128]{1,0:T(8,128)S(1)} %copy-done), custom_call_target="tpu_custom_call" | custom-call | flops 100000000 | bytes 1048576 | tf_op jit(solution)/shard_map/own_moments/pallas_call | solution.py:460
  9.3 0.4 %more_moments.2.started = f32[96,256]{1,0:T(8,128)S(1)} custom-call(f32[96,256]{1,0:T(8,128)S(1)} %get-tuple-element.30.started, f32[64,128]{1,0:T(8,128)S(1)} %collective-permute-done.1.entries), custom_call_target="tpu_custom_call" | custom-call | flops 6000000000 | bytes 1048576 | tf_op jit(solution)/shard_map/more_moments/pallas_call | solution.py:460
  9.7 1.6 %collective-permute-done.2.entries = f32[64,128]{1,0:T(8,128)S(1)} collective-permute-done((f32[64,128]{1,0:T(8,128)}, f32[64,128]{1,0:T(8,128)S(1)}, u32[]{:S(2)}, u32[]{:S(2)}) %collective-permute-start.2) | collective-permute-done | bytes 32800 | tf_op jit(solution)/shard_map/ppermute | solution.py:515
  11.3 0.4 %more_moments.3.refs_2_ = f32[96,256]{1,0:T(8,128)S(1)} custom-call(f32[96,256]{1,0:T(8,128)S(1)} %more_moments.2.started, f32[64,128]{1,0:T(8,128)S(1)} %collective-permute-done.2.entries), custom_call_target="tpu_custom_call" | custom-call | flops 6000000000 | bytes 1048576 | tf_op jit(solution)/shard_map/more_moments/pallas_call | solution.py:460
  11.7 0.5 %collective-permute-done.3.refs_3_ = f32[64,128]{1,0:T(8,128)S(1)} collective-permute-done((f32[64,128]{1,0:T(8,128)}, f32[64,128]{1,0:T(8,128)S(1)}, u32[]{:S(2)}, u32[]{:S(2)}) %collective-permute-start.3) | collective-permute-done | bytes 32800 | tf_op jit(solution)/shard_map/ppermute | solution.py:515
  12.2 0.5 %join_and_moments.1 = (f32[2,9,2,16,128]{4,3,2,1,0:T(8,128)S(1)}, f32[2,2,16,128]{3,2,1,0:T(8,128)S(1)}, f32[2,16,128]{2,1,0:T(8,128)S(1)}, f32[168,128]{1,0:T(8,128)S(1)}) custom-call(f32[11,24,128]{2,1,0:T(8,128)S(1)} %get-tuple-element.28.refs_0_, f32[10,24,128]{2,1,0:T(8,128)S(1)} %collective-permute-done.refs_1_, f32[96,256]{1,0:T(8,128)S(1)} %more_moments.3.refs_2_, ...), custom_call_target="tpu_custom_call" | custom-call | flops 10000000 | bytes 1048576 | tf_op jit(solution)/shard_map/join_and_moments/pallas_call | solution.py:460
  12.7 0.2 inner_edges.2
  12.9 0.3 collective-permute-start.5
  13.2 1.8 %collective-permute-start.4 = (f32[168,128]{1,0:T(8,128)S(1)}, f32[168,128]{1,0:T(8,128)S(1)}, u32[]{:S(2)}, u32[]{:S(2)}) collective-permute-start(f32[168,128]{1,0:T(8,128)S(1)} %get-tuple-element.35), channel_id=1, source_target_pairs={{0,8},{1,2},{2,1},{3,4},{4,3},{5,6},{6,5},{7,15},{8,0},{9,10},{10,... | collective-permute-start | bytes 258056 | tf_op jit(solution)/shard_map/ppermute | solution.py:494
  15.0 0.2 inner_edges.3
  15.2 4.0 %collective-permute-done.4.halo = f32[168,128]{1,0:T(8,128)S(1)} collective-permute-done((f32[168,128]{1,0:T(8,128)S(1)}, f32[168,128]{1,0:T(8,128)S(1)}, u32[]{:S(2)}, u32[]{:S(2)}) %collective-permute-start.4) | collective-permute-done | bytes 86048 | tf_op jit(solution)/shard_map/ppermute | solution.py:494
  19.2 0.3 outer_edges.1
  19.5 0.6 %collective-permute-start.7 = (f32[108,128]{1,0:T(8,128)S(1)}, f32[108,128]{1,0:T(8,128)S(1)}, u32[]{:S(2)}, u32[]{:S(2)}) collective-permute-start(f32[108,128]{1,0:T(8,128)S(1)} %get-tuple-element.40), channel_id=1, source_target_pairs={{0,8},{1,9},{8,0},{9,1},{16,24},{17,25},{24,16},{25,17},{2,10},{3,... | collective-permute-start | bytes 165896 | tf_op jit(solution)/shard_map/ppermute | solution.py:484
  20.1 3.7 %collective-permute-done.7.refs_5_ = f32[108,128]{1,0:T(8,128)S(1)} collective-permute-done((f32[108,128]{1,0:T(8,128)S(1)}, f32[108,128]{1,0:T(8,128)S(1)}, u32[]{:S(2)}, u32[]{:S(2)}) %collective-permute-start.7) | collective-permute-done | bytes 55328 | tf_op jit(solution)/shard_map/ppermute | solution.py:484
  23.8 0.6 %steps.2 = (f32[264,128]{1,0:T(8,128)S(1)}, f32[264,128]{1,0:T(8,128)S(1)}, f32[2,9,2,16,128]{4,3,2,1,0:T(8,128)S(1)}, f32[2,3,6,16,128]{4,3,2,1,0:T(8,128)S(1)}, f32[6,16,128]{2,1,0:T(8,128)S(1)}) custom-call(f32[2,9,2,16,128]{4,3,2,1,0:T(8,128)S(1)} %get-tuple-element.37.refs_0_, f32[2,3,2,16,128]{4,3,2,1,0:T(8,128)S(1)} %get-tuple-element.38.refs_1_, ...), custom_call_target="tpu_custom_call" | custom-call | flops 10000000 | bytes 1048576 | tf_op jit(solution)/shard_map/steps/pallas_call | solution.py:460
  24.4 2.1 %collective-permute-start.9 = (f32[264,128]{1,0:T(8,128)S(1)}, f32[264,128]{1,0:T(8,128)S(1)}, u32[]{:S(2)}, u32[]{:S(2)}) collective-permute-start(f32[264,128]{1,0:T(8,128)S(1)} %get-tuple-element.45), channel_id=1, source_target_pairs={{0,8},{1,9},{8,0},{9,1},{16,24},{17,25},{24,16},{25,17},{2,10},{3,... | collective-permute-start | bytes 405512 | tf_op jit(solution)/shard_map/ppermute | solution.py:484
  26.5 3.0 %collective-permute-done.9.refs_3_ = f32[264,128]{1,0:T(8,128)S(1)} collective-permute-done((f32[264,128]{1,0:T(8,128)S(1)}, f32[264,128]{1,0:T(8,128)S(1)}, u32[]{:S(2)}, u32[]{:S(2)}) %collective-permute-start.9) | collective-permute-done | bytes 135200 | tf_op jit(solution)/shard_map/ppermute | solution.py:484
  29.5 0.4 %steps.3 = (f32[9,2,8,128]{3,2,1,0:T(8,128)S(1)}, f32[9,2,8,128]{3,2,1,0:T(8,128)S(1)}) custom-call(f32[2,9,2,16,128]{4,3,2,1,0:T(8,128)S(1)} %get-tuple-element.42.refs_0_, f32[2,3,6,16,128]{4,3,2,1,0:T(8,128)S(1)} %get-tuple-element.43.refs_1_, f32[6,16,128]{2,1,0:T(8,128)S(1)} %get-tuple-element.44.refs_2_, ...), custom_call_target="tpu_custom_call" | custom-call | flops 10000000 | bytes 1048576 | tf_op jit(solution)/shard_map/steps/pallas_call | solution.py:460
  30.0 1.3 %collective-permute-done.11.brought = f32[9,2,8,128]{3,2,1,0:T(8,128)S(1)} collective-permute-done((f32[9,2,8,128]{3,2,1,0:T(8,128)S(1)}, f32[9,2,8,128]{3,2,1,0:T(8,128)S(1)}, u32[]{:S(2)}, u32[]{:S(2)}) %collective-permute-start.11) | collective-permute-done | bytes 73760 | tf_op jit(solution)/shard_map/ppermute | solution.py:497
  31.2 0.7 %home.1 = f32[1,9,2,16,128]{4,3,2,1,0:T(8,128)} custom-call(f32[9,2,8,128]{3,2,1,0:T(8,128)S(1)} %get-tuple-element.47.mine, f32[9,2,8,128]{3,2,1,0:T(8,128)S(1)} %collective-permute-done.11.brought), custom_call_target="tpu_custom_call" | custom-call | flops 10000000 | bytes 1048576 | tf_op jit(solution)/shard_map/home/pallas_call | solution.py:460
  (14 shorter events, 0.3 us)
Async XLA Ops:
  2.1 7.2 %collective-permute-start.1 = (f32[64,128]{1,0:T(8,128)}, f32[64,128]{1,0:T(8,128)S(1)}, u32[]{:S(2)}, u32[]{:S(2)}) collective-permute-start(f32[64,128]{1,0:T(8,128)} %get-tuple-element.31), channel_id=1, source_target_pairs={{24,0},{16,8},{8,16},{0,24},{25,1},{17,9},{9,17},{1,25},{26,2},{18... | collective-permute-start | bytes 98312 | tf_op jit(solution)/shard_map/ppermute | solution.py:515
  7.2 5.0 %collective-permute-start.3 = (f32[64,128]{1,0:T(8,128)}, f32[64,128]{1,0:T(8,128)S(1)}, u32[]{:S(2)}, u32[]{:S(2)}) collective-permute-start(f32[64,128]{1,0:T(8,128)} %get-tuple-element.31), channel_id=1, source_target_pairs={{16,0},{24,8},{0,16},{8,24},{17,1},{25,9},{1,17},{9,25},{18,2},{26... | collective-permute-start | bytes 98312 | tf_op jit(solution)/shard_map/ppermute | solution.py:515
  7.2 4.1 %collective-permute-start.2 = (f32[64,128]{1,0:T(8,128)}, f32[64,128]{1,0:T(8,128)S(1)}, u32[]{:S(2)}, u32[]{:S(2)}) collective-permute-start(f32[64,128]{1,0:T(8,128)} %get-tuple-element.31), channel_id=1, source_target_pairs={{8,0},{0,8},{24,16},{16,24},{9,1},{1,9},{25,17},{17,25},{10,2},{2,... | collective-permute-start | bytes 98312 | tf_op jit(solution)/shard_map/ppermute | solution.py:515
  7.8 4.4 %collective-permute-start = (f32[10,24,128]{2,1,0:T(8,128)}, f32[10,24,128]{2,1,0:T(8,128)S(1)}, u32[]{:S(2)}, u32[]{:S(2)}) collective-permute-start(f32[10,24,128]{2,1,0:T(8,128)} %get-tuple-element.29), channel_id=1, source_target_pairs={{0,1},{1,0},{2,3},{3,2},{4,5},{5,4},{6,7},{7,6},{8,9},{9,8},{10,11... | collective-permute-start | bytes 368648 | tf_op jit(solution)/shard_map/ppermute | solution.py:497
  7.8 0.9 %copy-start = (f32[336,128]{1,0:T(8,128)S(1)}, f32[336,128]{1,0:T(8,128)}, u32[]{:S(2)}) copy-start(f32[336,128]{1,0:T(8,128)} %get-tuple-element.27.kept) | copy-start | bytes 516100
  12.9 7.2 %collective-permute-start.5 = (f32[324,128]{1,0:T(8,128)S(1)}, f32[324,128]{1,0:T(8,128)S(1)}, u32[]{:S(2)}, u32[]{:S(2)}) collective-permute-start(f32[324,128]{1,0:T(8,128)S(1)} %inner_edges.2), channel_id=1, source_target_pairs={{0,8},{1,9},{8,0},{9,1},{16,24},{17,25},{24,16},{25,17},{2,10},{3,... | collective-permute-start | bytes 497672 | tf_op jit(solution)/shard_map/ppermute | solution.py:484
  13.2 6.1 %collective-permute-start.4 = (f32[168,128]{1,0:T(8,128)S(1)}, f32[168,128]{1,0:T(8,128)S(1)}, u32[]{:S(2)}, u32[]{:S(2)}) collective-permute-start(f32[168,128]{1,0:T(8,128)S(1)} %get-tuple-element.35), channel_id=1, source_target_pairs={{0,8},{1,2},{2,1},{3,4},{4,3},{5,6},{6,5},{7,15},{8,0},{9,10},{10,... | collective-permute-start | bytes 258056 | tf_op jit(solution)/shard_map/ppermute | solution.py:494
  15.2 8.6 %collective-permute-start.6 = (f32[324,128]{1,0:T(8,128)S(1)}, f32[324,128]{1,0:T(8,128)S(1)}, u32[]{:S(2)}, u32[]{:S(2)}) collective-permute-start(f32[324,128]{1,0:T(8,128)S(1)} %inner_edges.3), channel_id=1, source_target_pairs={{0,1},{1,0},{8,16},{9,17},{16,8},{17,9},{24,25},{25,24},{2,3},{3,2... | collective-permute-start | bytes 497672 | tf_op jit(solution)/shard_map/ppermute | solution.py:484
  19.5 4.2 %collective-permute-start.7 = (f32[108,128]{1,0:T(8,128)S(1)}, f32[108,128]{1,0:T(8,128)S(1)}, u32[]{:S(2)}, u32[]{:S(2)}) collective-permute-start(f32[108,128]{1,0:T(8,128)S(1)} %get-tuple-element.40), channel_id=1, source_target_pairs={{0,8},{1,9},{8,0},{9,1},{16,24},{17,25},{24,16},{25,17},{2,10},{3,... | collective-permute-start | bytes 165896 | tf_op jit(solution)/shard_map/ppermute | solution.py:484
  20.1 3.7 %collective-permute-start.8 = (f32[108,128]{1,0:T(8,128)S(1)}, f32[108,128]{1,0:T(8,128)S(1)}, u32[]{:S(2)}, u32[]{:S(2)}) collective-permute-start(f32[108,128]{1,0:T(8,128)S(1)} %get-tuple-element.41), channel_id=1, source_target_pairs={{0,1},{1,0},{8,16},{9,17},{16,8},{17,9},{24,25},{25,24},{2,3},{3,2... | collective-permute-start | bytes 165896 | tf_op jit(solution)/shard_map/ppermute | solution.py:484
  24.4 5.1 %collective-permute-start.9 = (f32[264,128]{1,0:T(8,128)S(1)}, f32[264,128]{1,0:T(8,128)S(1)}, u32[]{:S(2)}, u32[]{:S(2)}) collective-permute-start(f32[264,128]{1,0:T(8,128)S(1)} %get-tuple-element.45), channel_id=1, source_target_pairs={{0,8},{1,9},{8,0},{9,1},{16,24},{17,25},{24,16},{25,17},{2,10},{3,... | collective-permute-start | bytes 405512 | tf_op jit(solution)/shard_map/ppermute | solution.py:484
  26.5 3.0 %collective-permute-start.10 = (f32[264,128]{1,0:T(8,128)S(1)}, f32[264,128]{1,0:T(8,128)S(1)}, u32[]{:S(2)}, u32[]{:S(2)}) collective-permute-start(f32[264,128]{1,0:T(8,128)S(1)} %get-tuple-element.46), channel_id=1, source_target_pairs={{0,1},{1,0},{8,16},{9,17},{16,8},{17,9},{24,25},{25,24},{2,3},{3,2... | collective-permute-start | bytes 405512 | tf_op jit(solution)/shard_map/ppermute | solution.py:484
  29.9 1.3 %collective-permute-start.11 = (f32[9,2,8,128]{3,2,1,0:T(8,128)S(1)}, f32[9,2,8,128]{3,2,1,0:T(8,128)S(1)}, u32[]{:S(2)}, u32[]{:S(2)}) collective-permute-start(f32[9,2,8,128]{3,2,1,0:T(8,128)S(1)} %get-tuple-element.48), channel_id=1, source_target_pairs={{0,1},{1,0},{2,3},{3,2},{4,5},{5,4},{6,7},{7,6},{8,9},{9,8},{10,11... | collective-permute-start | bytes 221192 | tf_op jit(solution)/shard_map/ppermute | solution.py:497

commit v21 on v19

--- a/solution.py
+++ b/solution.py
@@ -508,7 +508,7 @@
     )
     blocks = [
         lax.ppermute(entries, "sec", [(other(i, k), i) for i in range(sections)])
-        for k in (sections - 1, *range(1, sections - 1))
+        for k in dict.fromkeys((*range(2, sections - 1), 1, sections - 1))
     ]
     got = swap(given)
     acc_shape = (6 * cx * cz // 2, 2 * cy)

time: 30.6 us -> 30.5 us (level)
  starting transfers between devices: 10.7 us -> 10.1 us
  waiting for transfers between devices: 12.8 us -> 13.3 us
    ppermute x6, starting transfers between devices: 4.59 us -> 3.95 us  [pairs(): return lax.ppermute(block, ('sec', 'segment'), route)]
    ppermute x6, waiting for transfers between devices: 7.13 us -> 7.67 us  [pairs(): return lax.ppermute(block, ('sec', 'segment'), route)]
  transfers between devices with their start and end apart: 12 -> 12, of which waited for: 7 -> 6; matrix products, arithmetic and copies ran while one was open for 0% -> 0% of each run, Pallas kernels for 5% -> 5%
where the time goes in v21:
time: 30.5 us; the launch traced here: 30.3 us
  waiting for transfers between devices  13.3 us (44%)
  starting transfers between devices  10.1 us (33%)
  Pallas kernels  5.89 us (19%)
  local copies, waits for them, and re-layouts  0.92 us (3%)
    ppermute x6, waiting for transfers between devices, pairs(): return lax.ppermute(block, ('sec', 'segment'), route)  7.67 us
    pallas_call x10, Pallas kernels, call(): pl.pallas_call(kernel, out_shape=[jax.ShapeDtypeStruct(shape, F32) for sh...  5.89 us
    ppermute x3, starting transfers between devices, on_device(): lax.ppermute(entries, 'sec', [(other(i, k), i) for i in range(sections)])  5.68 us
    ppermute x6, starting transfers between devices, pairs(): return lax.ppermute(block, ('sec', 'segment'), route)  3.95 us
    ppermute x3, waiting for transfers between devices, on_device(): lax.ppermute(entries, 'sec', [(other(i, k), i) for i in range(sections)])  2.22 us
    ppermute x1, waiting for transfers between devices, along_depth(): return lax.ppermute(block, ('sec', 'depth', 'segment'), route)  2.17 us
    ppermute x2, waiting for transfers between devices, swap(): return lax.ppermute(block, 'segment', [(0, 1), (1, 0)])  1.26 us
    unnamed x2, local copies, waits for them, and re-layouts  0.92 us
  transfers between devices with their start and end apart: 12, of which 6 were waited for; matrix products, arithmetic and copies ran while one was open for 0% of the time, Pallas kernels for 5%

profile of v21, /device:TPU:0, one launch (start us, length us, event | category | flops | bytes accessed | tf_op | source)
XLA Modules:
  0.0 30.3 jit_solution(9496474657249626414)
XLA Ops:
  0.0 2.1 %pack.1 = (f32[64,128]{1,0:T(8,128)}, f32[336,128]{1,0:T(8,128)}, f32[10,24,128]{2,1,0:T(8,128)}) custom-call(f32[1,9,2,16,128]{4,3,2,1,0:T(8,128)} %fields_in.1, s32[1,2,16,128]{3,2,1,0:T(8,128)} %ids_in.1, f32[6,1024]{1,0:T(8,128)} %moments_in.1, s32[8,128]{1,0:T(8,128)} %bitcast.4, s32[8,128]{1,0:T(8,128)} %bitcast.5, s32[16,128]{1,0:T(8,128)} %bitcast.3, ...), custom_call_target="tpu_custom_call" | custom-call | flops 10000000 | bytes 1048576 | tf_op jit(solution)/shard_map/pack/pallas_call | solution.py:455
  2.1 4.1 %collective-permute-start.1 = (f32[64,128]{1,0:T(8,128)}, f32[64,128]{1,0:T(8,128)S(1)}, u32[]{:S(2)}, u32[]{:S(2)}) collective-permute-start(f32[64,128]{1,0:T(8,128)} %get-tuple-element.33), channel_id=1, source_target_pairs={{16,0},{24,8},{0,16},{8,24},{17,1},{25,9},{1,17},{9,25},{18,2},{26... | collective-permute-start | bytes 98312 | tf_op jit(solution)/shard_map/ppermute | solution.py:510
  6.2 1.3 %collective-permute-start.3 = (f32[64,128]{1,0:T(8,128)}, f32[64,128]{1,0:T(8,128)S(1)}, u32[]{:S(2)}, u32[]{:S(2)}) collective-permute-start(f32[64,128]{1,0:T(8,128)} %get-tuple-element.33), channel_id=1, source_target_pairs={{24,0},{16,8},{8,16},{0,24},{25,1},{17,9},{9,17},{1,25},{26,2},{18... | collective-permute-start | bytes 98312 | tf_op jit(solution)/shard_map/ppermute | solution.py:510
  7.5 0.2 collective-permute-start.2
  7.7 0.9 %copy-done = f32[336,128]{1,0:T(8,128)S(1)} copy-done((f32[336,128]{1,0:T(8,128)S(1)}, f32[336,128]{1,0:T(8,128)}, u32[]{:S(2)}) %copy-start) | copy-done | bytes 172056
  8.7 0.4 %own_moments.1 = (f32[11,24,128]{2,1,0:T(8,128)S(1)}, f32[8,128]{1,0:T(8,128)S(1)}, f32[96,256]{1,0:T(8,128)S(1)}) custom-call(f32[336,128]{1,0:T(8,128)S(1)} %copy-done), custom_call_target="tpu_custom_call" | custom-call | flops 100000000 | bytes 1048576 | tf_op jit(solution)/shard_map/own_moments/pallas_call | solution.py:455
  9.1 0.4 %more_moments.2.started = f32[96,256]{1,0:T(8,128)S(1)} custom-call(f32[96,256]{1,0:T(8,128)S(1)} %get-tuple-element.32.started, f32[64,128]{1,0:T(8,128)S(1)} %collective-permute-done.1.entries), custom_call_target="tpu_custom_call" | custom-call | flops 6000000000 | bytes 1048576 | tf_op jit(solution)/shard_map/more_moments/pallas_call | solution.py:455
  9.5 2.2 %collective-permute-done.2.entries = f32[64,128]{1,0:T(8,128)S(1)} collective-permute-done((f32[64,128]{1,0:T(8,128)}, f32[64,128]{1,0:T(8,128)S(1)}, u32[]{:S(2)}, u32[]{:S(2)}) %collective-permute-start.2) | collective-permute-done | bytes 32800 | tf_op jit(solution)/shard_map/ppermute | solution.py:510
  11.6 0.4 %more_moments.3.refs_2_ = f32[96,256]{1,0:T(8,128)S(1)} custom-call(f32[96,256]{1,0:T(8,128)S(1)} %more_moments.2.started, f32[64,128]{1,0:T(8,128)S(1)} %collective-permute-done.2.entries), custom_call_target="tpu_custom_call" | custom-call | flops 6000000000 | bytes 1048576 | tf_op jit(solution)/shard_map/more_moments/pallas_call | solution.py:455
  12.1 0.5 %join_and_moments.1 = (f32[2,9,2,16,128]{4,3,2,1,0:T(8,128)S(1)}, f32[2,2,16,128]{3,2,1,0:T(8,128)S(1)}, f32[2,16,128]{2,1,0:T(8,128)S(1)}, f32[168,128]{1,0:T(8,128)S(1)}) custom-call(f32[11,24,128]{2,1,0:T(8,128)S(1)} %get-tuple-element.30.refs_0_, f32[10,24,128]{2,1,0:T(8,128)S(1)} %collective-permute-done.refs_1_, f32[96,256]{1,0:T(8,128)S(1)} %more_moments.3.refs_2_, ...), custom_call_target="tpu_custom_call" | custom-call | flops 10000000 | bytes 1048576 | tf_op jit(solution)/shard_map/join_and_moments/pallas_call | solution.py:455
  12.6 0.4 %collective-permute-start.4 = (f32[168,128]{1,0:T(8,128)S(1)}, f32[168,128]{1,0:T(8,128)S(1)}, u32[]{:S(2)}, u32[]{:S(2)}) collective-permute-start(f32[168,128]{1,0:T(8,128)S(1)} %get-tuple-element.37), channel_id=1, source_target_pairs={{0,8},{1,2},{2,1},{3,4},{4,3},{5,6},{6,5},{7,15},{8,0},{9,10},{10,... | collective-permute-start | bytes 258056 | tf_op jit(solution)/shard_map/ppermute | solution.py:489
  12.9 0.2 inner_edges.1
  13.2 1.8 %collective-permute-start.5 = (f32[324,128]{1,0:T(8,128)S(1)}, f32[324,128]{1,0:T(8,128)S(1)}, u32[]{:S(2)}, u32[]{:S(2)}) collective-permute-start(f32[324,128]{1,0:T(8,128)S(1)} %get-tuple-element.42), channel_id=1, source_target_pairs={{0,8},{1,9},{8,0},{9,1},{16,24},{17,25},{24,16},{25,17},{2,10},{3,... | collective-permute-start | bytes 497672 | tf_op jit(solution)/shard_map/ppermute | solution.py:479
  14.9 2.2 %collective-permute-done.4.halo = f32[168,128]{1,0:T(8,128)S(1)} collective-permute-done((f32[168,128]{1,0:T(8,128)S(1)}, f32[168,128]{1,0:T(8,128)S(1)}, u32[]{:S(2)}, u32[]{:S(2)}) %collective-permute-start.4) | collective-permute-done | bytes 86048 | tf_op jit(solution)/shard_map/ppermute | solution.py:489
  17.1 0.3 outer_edges.1
  17.4 0.4 %collective-permute-start.7 = (f32[108,128]{1,0:T(8,128)S(1)}, f32[108,128]{1,0:T(8,128)S(1)}, u32[]{:S(2)}, u32[]{:S(2)}) collective-permute-start(f32[108,128]{1,0:T(8,128)S(1)} %get-tuple-element.44), channel_id=1, source_target_pairs={{0,8},{1,9},{8,0},{9,1},{16,24},{17,25},{24,16},{25,17},{2,10},{3,... | collective-permute-start | bytes 165896 | tf_op jit(solution)/shard_map/ppermute | solution.py:479
  17.8 4.2 %collective-permute-done.7.refs_5_ = f32[108,128]{1,0:T(8,128)S(1)} collective-permute-done((f32[108,128]{1,0:T(8,128)S(1)}, f32[108,128]{1,0:T(8,128)S(1)}, u32[]{:S(2)}, u32[]{:S(2)}) %collective-permute-start.7) | collective-permute-done | bytes 55328 | tf_op jit(solution)/shard_map/ppermute | solution.py:479
  21.9 0.6 %steps.2 = (f32[264,128]{1,0:T(8,128)S(1)}, f32[264,128]{1,0:T(8,128)S(1)}, f32[2,9,2,16,128]{4,3,2,1,0:T(8,128)S(1)}, f32[2,3,6,16,128]{4,3,2,1,0:T(8,128)S(1)}, f32[6,16,128]{2,1,0:T(8,128)S(1)}) custom-call(f32[2,9,2,16,128]{4,3,2,1,0:T(8,128)S(1)} %get-tuple-element.39.refs_0_, f32[2,3,2,16,128]{4,3,2,1,0:T(8,128)S(1)} %get-tuple-element.40.refs_1_, ...), custom_call_target="tpu_custom_call" | custom-call | flops 10000000 | bytes 1048576 | tf_op jit(solution)/shard_map/steps/pallas_call | solution.py:455
  22.6 1.8 %collective-permute-start.9 = (f32[264,128]{1,0:T(8,128)S(1)}, f32[264,128]{1,0:T(8,128)S(1)}, u32[]{:S(2)}, u32[]{:S(2)}) collective-permute-start(f32[264,128]{1,0:T(8,128)S(1)} %get-tuple-element.49), channel_id=1, source_target_pairs={{0,8},{1,9},{8,0},{9,1},{16,24},{17,25},{24,16},{25,17},{2,10},{3,... | collective-permute-start | bytes 405512 | tf_op jit(solution)/shard_map/ppermute | solution.py:479
  24.3 3.5 %collective-permute-done.9.refs_3_ = f32[264,128]{1,0:T(8,128)S(1)} collective-permute-done((f32[264,128]{1,0:T(8,128)S(1)}, f32[264,128]{1,0:T(8,128)S(1)}, u32[]{:S(2)}, u32[]{:S(2)}) %collective-permute-start.9) | collective-permute-done | bytes 135200 | tf_op jit(solution)/shard_map/ppermute | solution.py:479
  27.8 0.4 %steps.3 = (f32[9,2,8,128]{3,2,1,0:T(8,128)S(1)}, f32[9,2,8,128]{3,2,1,0:T(8,128)S(1)}) custom-call(f32[2,9,2,16,128]{4,3,2,1,0:T(8,128)S(1)} %get-tuple-element.46.refs_0_, f32[2,3,6,16,128]{4,3,2,1,0:T(8,128)S(1)} %get-tuple-element.47.refs_1_, f32[6,16,128]{2,1,0:T(8,128)S(1)} %get-tuple-element.48.refs_2_, ...), custom_call_target="tpu_custom_call" | custom-call | flops 10000000 | bytes 1048576 | tf_op jit(solution)/shard_map/steps/pallas_call | solution.py:455
  28.3 0.1 collective-permute-start.11
  28.4 1.3 %collective-permute-done.11.brought = f32[9,2,8,128]{3,2,1,0:T(8,128)S(1)} collective-permute-done((f32[9,2,8,128]{3,2,1,0:T(8,128)S(1)}, f32[9,2,8,128]{3,2,1,0:T(8,128)S(1)}, u32[]{:S(2)}, u32[]{:S(2)}) %collective-permute-start.11) | collective-permute-done | bytes 73760 | tf_op jit(solution)/shard_map/ppermute | solution.py:492
  29.6 0.7 %home.1 = f32[1,9,2,16,128]{4,3,2,1,0:T(8,128)} custom-call(f32[9,2,8,128]{3,2,1,0:T(8,128)S(1)} %get-tuple-element.51.mine, f32[9,2,8,128]{3,2,1,0:T(8,128)S(1)} %collective-permute-done.11.brought), custom_call_target="tpu_custom_call" | custom-call | flops 10000000 | bytes 1048576 | tf_op jit(solution)/shard_map/home/pallas_call | solution.py:455
  (12 shorter events, 0.1 us)
Async XLA Ops:
  2.1 7.0 %collective-permute-start.1 = (f32[64,128]{1,0:T(8,128)}, f32[64,128]{1,0:T(8,128)S(1)}, u32[]{:S(2)}, u32[]{:S(2)}) collective-permute-start(f32[64,128]{1,0:T(8,128)} %get-tuple-element.33), channel_id=1, source_target_pairs={{16,0},{24,8},{0,16},{8,24},{17,1},{25,9},{1,17},{9,25},{18,2},{26... | collective-permute-start | bytes 98312 | tf_op jit(solution)/shard_map/ppermute | solution.py:510
  6.2 5.9 %collective-permute-start.3 = (f32[64,128]{1,0:T(8,128)}, f32[64,128]{1,0:T(8,128)S(1)}, u32[]{:S(2)}, u32[]{:S(2)}) collective-permute-start(f32[64,128]{1,0:T(8,128)} %get-tuple-element.33), channel_id=1, source_target_pairs={{24,0},{16,8},{8,16},{0,24},{25,1},{17,9},{9,17},{1,25},{26,2},{18... | collective-permute-start | bytes 98312 | tf_op jit(solution)/shard_map/ppermute | solution.py:510
  7.5 4.1 %collective-permute-start.2 = (f32[64,128]{1,0:T(8,128)}, f32[64,128]{1,0:T(8,128)S(1)}, u32[]{:S(2)}, u32[]{:S(2)}) collective-permute-start(f32[64,128]{1,0:T(8,128)} %get-tuple-element.33), channel_id=1, source_target_pairs={{8,0},{0,8},{24,16},{16,24},{9,1},{1,9},{25,17},{17,25},{10,2},{2,... | collective-permute-start | bytes 98312 | tf_op jit(solution)/shard_map/ppermute | solution.py:510
  7.7 4.3 %collective-permute-start = (f32[10,24,128]{2,1,0:T(8,128)}, f32[10,24,128]{2,1,0:T(8,128)S(1)}, u32[]{:S(2)}, u32[]{:S(2)}) collective-permute-start(f32[10,24,128]{2,1,0:T(8,128)} %get-tuple-element.31), channel_id=1, source_target_pairs={{0,1},{1,0},{2,3},{3,2},{4,5},{5,4},{6,7},{7,6},{8,9},{9,8},{10,11... | collective-permute-start | bytes 368648 | tf_op jit(solution)/shard_map/ppermute | solution.py:492
  7.7 0.9 %copy-start = (f32[336,128]{1,0:T(8,128)S(1)}, f32[336,128]{1,0:T(8,128)}, u32[]{:S(2)}) copy-start(f32[336,128]{1,0:T(8,128)} %get-tuple-element.29.kept) | copy-start | bytes 516100
  12.6 4.5 %collective-permute-start.4 = (f32[168,128]{1,0:T(8,128)S(1)}, f32[168,128]{1,0:T(8,128)S(1)}, u32[]{:S(2)}, u32[]{:S(2)}) collective-permute-start(f32[168,128]{1,0:T(8,128)S(1)} %get-tuple-element.37), channel_id=1, source_target_pairs={{0,8},{1,2},{2,1},{3,4},{4,3},{5,6},{6,5},{7,15},{8,0},{9,10},{10,... | collective-permute-start | bytes 258056 | tf_op jit(solution)/shard_map/ppermute | solution.py:489
  13.2 8.8 %collective-permute-start.5 = (f32[324,128]{1,0:T(8,128)S(1)}, f32[324,128]{1,0:T(8,128)S(1)}, u32[]{:S(2)}, u32[]{:S(2)}) collective-permute-start(f32[324,128]{1,0:T(8,128)S(1)} %get-tuple-element.42), channel_id=1, source_target_pairs={{0,8},{1,9},{8,0},{9,1},{16,24},{17,25},{24,16},{25,17},{2,10},{3,... | collective-permute-start | bytes 497672 | tf_op jit(solution)/shard_map/ppermute | solution.py:479
  14.9 7.0 %collective-permute-start.6 = (f32[324,128]{1,0:T(8,128)S(1)}, f32[324,128]{1,0:T(8,128)S(1)}, u32[]{:S(2)}, u32[]{:S(2)}) collective-permute-start(f32[324,128]{1,0:T(8,128)S(1)} %get-tuple-element.43), channel_id=1, source_target_pairs={{0,1},{1,0},{8,16},{9,17},{16,8},{17,9},{24,25},{25,24},{2,3},{3,2... | collective-permute-start | bytes 497672 | tf_op jit(solution)/shard_map/ppermute | solution.py:479
  17.4 4.5 %collective-permute-start.7 = (f32[108,128]{1,0:T(8,128)S(1)}, f32[108,128]{1,0:T(8,128)S(1)}, u32[]{:S(2)}, u32[]{:S(2)}) collective-permute-start(f32[108,128]{1,0:T(8,128)S(1)} %get-tuple-element.44), channel_id=1, source_target_pairs={{0,8},{1,9},{8,0},{9,1},{16,24},{17,25},{24,16},{25,17},{2,10},{3,... | collective-permute-start | bytes 165896 | tf_op jit(solution)/shard_map/ppermute | solution.py:479
  17.8 4.2 %collective-permute-start.8 = (f32[108,128]{1,0:T(8,128)S(1)}, f32[108,128]{1,0:T(8,128)S(1)}, u32[]{:S(2)}, u32[]{:S(2)}) collective-permute-start(f32[108,128]{1,0:T(8,128)S(1)} %get-tuple-element.45), channel_id=1, source_target_pairs={{0,1},{1,0},{8,16},{9,17},{16,8},{17,9},{24,25},{25,24},{2,3},{3,2... | collective-permute-start | bytes 165896 | tf_op jit(solution)/shard_map/ppermute | solution.py:479
  22.6 5.3 %collective-permute-start.9 = (f32[264,128]{1,0:T(8,128)S(1)}, f32[264,128]{1,0:T(8,128)S(1)}, u32[]{:S(2)}, u32[]{:S(2)}) collective-permute-start(f32[264,128]{1,0:T(8,128)S(1)} %get-tuple-element.49), channel_id=1, source_target_pairs={{0,8},{1,9},{8,0},{9,1},{16,24},{17,25},{24,16},{25,17},{2,10},{3,... | collective-permute-start | bytes 405512 | tf_op jit(solution)/shard_map/ppermute | solution.py:479
  24.3 3.5 %collective-permute-start.10 = (f32[264,128]{1,0:T(8,128)S(1)}, f32[264,128]{1,0:T(8,128)S(1)}, u32[]{:S(2)}, u32[]{:S(2)}) collective-permute-start(f32[264,128]{1,0:T(8,128)S(1)} %get-tuple-element.50), channel_id=1, source_target_pairs={{0,1},{1,0},{8,16},{9,17},{16,8},{17,9},{24,25},{25,24},{2,3},{3,2... | collective-permute-start | bytes 405512 | tf_op jit(solution)/shard_map/ppermute | solution.py:479
  28.3 1.3 %collective-permute-start.11 = (f32[9,2,8,128]{3,2,1,0:T(8,128)S(1)}, f32[9,2,8,128]{3,2,1,0:T(8,128)S(1)}, u32[]{:S(2)}, u32[]{:S(2)}) collective-permute-start(f32[9,2,8,128]{3,2,1,0:T(8,128)S(1)} %get-tuple-element.52), channel_id=1, source_target_pairs={{0,1},{1,0},{2,3},{3,2},{4,5},{5,4},{6,7},{7,6},{8,9},{9,8},{10,11... | collective-permute-start | bytes 221192 | tf_op jit(solution)/shard_map/ppermute | solution.py:492
